TPU v7x, 32 devices: a whole 2x2x4 slice. The times are simulated.
32 devices in a mesh: tm: 4 (over y, core), height: 8 (over z, x).
Axes of the slice: x: 2, y: 2, z: 4, core: 2. Of those that a mesh axis runs over, the one named last changes fastest.
Arguments:
- clip: bfloat16 [16, 8, 128, 256], P('tm', 'height'), may hold values from -6 to 6
- conv_weight: bfloat16 [3, 3, 3, 256, 256], replicated, may hold values from -0.078125 to 0.078125
- down_weight: bfloat16 [3, 256, 256], replicated, may hold values from -0.21875 to 0.21875
- grad_out: bfloat16 [8, 8, 128, 256], P('tm', 'height'), may hold values from -6 to 6
Outputs:
- grad_input: bfloat16 [16, 8, 128, 256], P('tm', 'height')
- grad_conv: float32 [6912, 256], P('height', 'tm')
- grad_down: float32 [768, 256], P('height', 'tm')
All inputs are finite; a program needn't handle non-finite values.
Results may differ from a plain program's by a relative error of at most 0.0051.
Values may be sent and summed in bfloat16 or wider, within the bound.
No kernel may reach another device: no remote copies, remote signals or barrier semaphores. Data moves between devices by JAX's collectives and lax.ppermute only.
A program may use at most 128 MiB of HBM per device.

v0:
```python
import jax
import jax.numpy as jnp
from jax import lax
from jax.sharding import PartitionSpec as P


def passed_along(value, axis, steps):
    count = lax.axis_size(axis)
    first, last = (max(0, -steps), min(count, count - steps))
    return lax.ppermute(value, axis, [(source, source + steps) for source in range(first, last)])


def padded(block, sides, width):
    for axis, dim in sides:
        count = lax.axis_size(axis)
        forward = [(i, i + 1) for i in range(count - 1)]
        backward = [(target, source) for source, target in forward]
        low = lax.ppermute(
            lax.slice_in_dim(block, block.shape[dim] - width, None, axis=dim), axis, forward
        )
        high = lax.ppermute(lax.slice_in_dim(block, 0, width, axis=dim), axis, backward)
        block = jnp.concatenate([low, block, high], axis=dim)
    return block


def silu_grad(value):
    sig = jax.nn.sigmoid(value)
    return sig * (1.0 + value * (1.0 - sig))


def spread_back(here, later, down_weight):
    chans = here.shape[-1]
    here_flat = here.reshape(-1, chans)
    later_flat = later.reshape(-1, chans)
    even = jnp.dot(later_flat, down_weight[0].T, preferred_element_type=jnp.float32) + jnp.dot(
        here_flat, down_weight[2].T, preferred_element_type=jnp.float32
    )
    odd = jnp.dot(later_flat, down_weight[1].T, preferred_element_type=jnp.float32)
    shape = here.shape
    stacked = jnp.stack([even.reshape(shape), odd.reshape(shape)], axis=1)
    return stacked.reshape((2 * shape[0],) + shape[1:]).astype(jnp.bfloat16)


def clip_edges(rimmed, first_dev, last_dev):
    total = rimmed.shape[1]
    position = jnp.arange(total, dtype=jnp.int32).reshape(1, total, 1, 1)
    drop = jnp.logical_or(
        jnp.logical_and(position == 0, first_dev), jnp.logical_and(position == total - 1, last_dev)
    )
    return jnp.where(drop, jnp.zeros_like(rimmed), rimmed)


def body(clip, conv_weight, down_weight, grad_out):
    nframes, nrows, ncols, chans = clip.shape
    half = grad_out.shape[0]
    cells = nframes * nrows * ncols
    split_count = lax.axis_size("height")
    place = lax.axis_index("height") % split_count
    first_dev = place == 0
    last_dev = place == split_count - 1
    inputs = clip.astype(jnp.float32)
    act = jax.nn.silu(inputs).astype(jnp.bfloat16)
    earlier = passed_along(act[nframes - 2 :], "tm", 1)
    act_ext = jnp.concatenate([earlier, act], axis=0)
    act_rim = padded(act_ext, (("height", 1),), 1)
    act_rim = clip_edges(act_rim, first_dev, last_dev)
    act_pad = jnp.pad(act_rim, ((0, 0), (0, 0), (1, 1), (0, 0)))
    patches = []
    conv = jnp.zeros((cells, chans), jnp.float32)
    for a in range(3):
        for b in range(3):
            patch = jnp.concatenate(
                [act_pad[a : a + nframes, b : b + nrows, c : c + ncols] for c in range(3)], axis=-1
            ).reshape(cells, 3 * chans)
            patches.append(patch)
            conv = conv + jnp.dot(
                patch,
                conv_weight[a, b].reshape(3 * chans, chans),
                preferred_element_type=jnp.float32,
            )
    summed = (inputs + conv.reshape(clip.shape)).astype(jnp.bfloat16)
    prior = passed_along(summed[nframes - 2 :], "tm", 1)
    sum_ext = jnp.concatenate([prior, summed], axis=0)
    following = passed_along(grad_out, "tm", -1)
    cot_rim = padded(jnp.concatenate([grad_out, following], axis=0), (("height", 1),), 1)
    cot_rim = clip_edges(cot_rim, first_dev, last_dev)
    grad_rim = spread_back(cot_rim[: half + 1], cot_rim[1 : half + 2], down_weight)
    grad_sum = grad_rim[:nframes, 1 : nrows + 1]
    out_flat = grad_out.reshape(-1, chans)
    down_terms = []
    for k in range(3):
        picked = sum_ext[k : k + 2 * half : 2].reshape(-1, chans)
        down_terms.append(jnp.dot(picked.T, out_flat, preferred_element_type=jnp.float32))
    term_down = jnp.concatenate(down_terms, axis=0)
    grad_pad = jnp.pad(grad_rim, ((0, 0), (0, 0), (1, 1), (0, 0)))
    grad_flat = grad_sum.reshape(cells, chans)
    grad_act = jnp.zeros((cells, chans), jnp.float32)
    conv_terms = []
    for a in range(3):
        for b in range(3):
            conv_terms.append(
                jnp.dot(patches[a * 3 + b].T, grad_flat, preferred_element_type=jnp.float32)
            )
            back = jnp.concatenate(
                [
                    grad_pad[2 - a : 2 - a + nframes, 2 - b : 2 - b + nrows, 2 - c : 2 - c + ncols]
                    for c in range(3)
                ],
                axis=-1,
            ).reshape(cells, 3 * chans)
            flipped = jnp.transpose(conv_weight[a, b], (0, 2, 1)).reshape(3 * chans, chans)
            grad_act = grad_act + jnp.dot(back, flipped, preferred_element_type=jnp.float32)
    term_conv = jnp.concatenate(conv_terms, axis=0)
    partial_sums = (
        lax.psum_scatter(term_conv, "height", scatter_dimension=0, tiled=True),
        lax.psum_scatter(term_down, "height", scatter_dimension=0, tiled=True),
    )
    grad_conv, grad_down = (
        lax.psum_scatter(partial_sums[0], "tm", scatter_dimension=1, tiled=True),
        lax.psum_scatter(partial_sums[1], "tm", scatter_dimension=1, tiled=True),
    )
    grad_input = (
        grad_sum.astype(jnp.float32) + grad_act.reshape(clip.shape) * silu_grad(inputs)
    ).astype(jnp.bfloat16)
    return (grad_input, grad_conv, grad_down)


def solution(mesh):
    placed = (P("tm", "height", None, None), P(), P(), P("tm", "height", None, None))
    return jax.shard_map(
        body,
        mesh=mesh,
        in_specs=placed,
        out_specs=(P("tm", "height", None, None), P("height", "tm"), P("height", "tm")),
        check_vma=False,
    )
```

profile of v0, /device:TPU:0, one launch (start us, length us, event | category | flops | bytes accessed | tf_op | source)
XLA Modules:
  0.0 325.6 jit_solution(4727178080388997754)
XLA Ops:
  7.2 1.3 collective-permute-start
  8.5 1.1 fusion.28
  9.6 0.7 slice.331
  10.3 3.7 %collective-permute-start.3 = (bf16[2,1,128,256]{3,2,0,1:T(8,128)(2,1)}, bf16[2,1,128,256]{3,2,0,1:T(8,128)(2,1)}, u32[]{:S(2)}, u32[]{:S(2)}) collective-permute-start(bf16[2,1,128,256]{3,2,0,1:T(8,128)(2,1)} %slice.331), channel_id=1, source_target_pairs={{0,8},{8,16},{16,24},{1,9},{9,17},{17,25},{2,10},{10,18},{18,26},{... | collective-permute-start | bytes 393224 | tf_op jit(solution)/shard_map/ppermute | solution.py:10
  14.0 1.6 constant_dynamic-update-slice_fusion.1
  16.2 5.5 %collective-permute-start.1 = (bf16[4,1,128,256]{3,2,1,0:T(8,128)(2,1)}, bf16[4,1,128,256]{3,2,1,0:T(8,128)(2,1)}, u32[]{:S(2)}, u32[]{:S(2)}) collective-permute-start(bf16[4,1,128,256]{3,2,1,0:T(8,128)(2,1)} %constant_dynamic-update-slice_fusion), channel_id=1, source_target_pairs={{0,1},{1,2},{2,3},{3,4},{4,5},{5,6},{6,7},{8,9},{9,10},{10,11},{11... | collective-permute-start | bytes 786440 | tf_op jit(solution)/shard_map/ppermute | solution.py:18
  21.8 1.3 collective-permute-start.2
  23.0 2.3 fusion.65
  25.4 1.1 copy.166
  26.5 0.9 copy.167
  27.5 0.9 copy.168
  28.4 0.9 copy.169
  29.3 0.9 copy.170
  30.2 0.9 copy.171
  31.2 0.9 copy.172
  32.1 0.9 copy.173
  33.0 0.9 copy.174
  34.0 0.9 pad_maximum_fusion.20
  34.9 4.6 %collective-permute-start.4 = (bf16[6,1,128,256]{3,2,0,1:T(8,128)(2,1)S(1)}, bf16[6,1,128,256]{3,2,0,1:T(8,128)(2,1)S(1)}, u32[]{:S(2)}, u32[]{:S(2)}) collective-permute-start(bf16[6,1,128,256]{3,2,0,1:T(8,128)(2,1)S(1)} %pad_maximum_fusion.20), channel_id=1, source_target_pairs={{0,1},{1,2},{2,3},{3,4},{4,5},{5,6},{6,7},{8,9},{9,10},{10,11},{11... | collective-permute-start | bytes 1179656 | tf_op jit(solution)/shard_map/ppermute | solution.py:18
  39.5 1.5 collective-permute-start.5
  41.0 1.3 maximum_select_fusion.1
  42.4 0.9 copy-done.62
  46.0 0.9 copy-done.18
  48.3 0.9 copy-done.16
  50.1 0.9 copy-done.14
  51.5 0.9 copy-done.13
  54.5 1.8 collective-permute-done.4
  56.3 1.1 maximum_select_fusion
  59.1 1.2 copy-done.5
  61.3 0.9 copy-done.1
  65.8 1.0 fusion.29
  66.8 1.3 collective-permute-start.6
  68.1 1.3 fusion.9
  69.4 1.3 fusion.8
  71.5 0.9 pad_maximum_fusion.19
  72.8 1.3 fusion.7
  74.1 1.3 fusion.6
  75.5 1.3 fusion.5
  76.8 1.3 fusion.4
  78.1 1.3 fusion.3
  79.5 1.3 fusion.2
  80.8 1.3 fusion.1
  82.2 55.7 %reduce-scatter.11.cloned.1.call-done = f32[96,256]{1,0:T(8,128)} async-done(((f32[768,256]{1,0:T(8,128)}), f32[96,256]{1,0:T(8,128)}) %reduce-scatter.11.cloned.1.call-update) | async-done | bytes 98320 | tf_op jit(solution)/shard_map/reduce_scatter | solution.py:116
  137.9 1.6 copy.164
  139.6 130.5 %reduce-scatter.9.cloned.1.call-done = f32[864,256]{1,0:T(8,128)} async-done(((f32[6912,256]{1,0:T(8,128)}), f32[864,256]{1,0:T(8,128)}) %reduce-scatter.9.cloned.1.call-update) | async-done | bytes 884752 | tf_op jit(solution)/shard_map/reduce_scatter | solution.py:115
  270.1 2.4 copy.162
  272.5 19.3 %reduce-scatter.15.cloned.1.call-done = f32[64,96]{1,0:T(8,128)} async-done(((f32[256,96]{1,0:T(8,128)}), f32[64,96]{1,0:T(8,128)}) %reduce-scatter.15.cloned.1.call-update) | async-done | bytes 24592
  291.8 27.3 %reduce-scatter.13.cloned.1.call-done = f32[64,864]{1,0:T(8,128)} async-done(((f32[256,864]{1,0:T(8,128)}), f32[64,864]{1,0:T(8,128)}) %reduce-scatter.13.cloned.1.call-update) | async-done | bytes 221200
  (180 shorter events, 15.5 us)
Async XLA Ops:
  7.2 130.7 %reduce-scatter.11.cloned.1.call-start = ((), (), s32[]{:S(2)}) async-start(), calls=%async_computation.5 | async-start | bytes 884736 | tf_op jit(solution)/shard_map/reduce_scatter | solution.py:116
  7.2 8.4 %collective-permute-start = (bf16[2,1,128,256]{3,2,1,0:T(8,128)(2,1)}, bf16[2,1,128,256]{3,2,1,0:T(8,128)(2,1)S(1)}, u32[]{:S(2)}, u32[]{:S(2)}) collective-permute-start(bf16[2,1,128,256]{3,2,1,0:T(8,128)(2,1)} %param.7), channel_id=1, source_target_pairs={{8,0},{16,8},{24,16},{9,1},{17,9},{25,17},{10,2},{18,10},{26,18},{... | collective-permute-start | bytes 393224 | tf_op jit(solution)/shard_map/ppermute | solution.py:10
  9.6 12.1 %copy-start.6 = (bf16[4,1,128,256]{3,2,0,1:T(8,128)(2,1)}, bf16[4,1,128,256]{3,2,0,1:T(8,128)(2,1)S(1)}, u32[]{:S(2)}) copy-start(bf16[4,1,128,256]{3,2,0,1:T(8,128)(2,1)S(1)} %fusion.28) | copy-start | bytes 786436
  10.3 23.6 %collective-permute-start.3 = (bf16[2,1,128,256]{3,2,0,1:T(8,128)(2,1)}, bf16[2,1,128,256]{3,2,0,1:T(8,128)(2,1)}, u32[]{:S(2)}, u32[]{:S(2)}) collective-permute-start(bf16[2,1,128,256]{3,2,0,1:T(8,128)(2,1)} %slice.331), channel_id=1, source_target_pairs={{0,8},{8,16},{16,24},{1,9},{9,17},{17,25},{2,10},{10,18},{18,26},{... | collective-permute-start | bytes 393224 | tf_op jit(solution)/shard_map/ppermute | solution.py:10
  16.2 24.7 %collective-permute-start.1 = (bf16[4,1,128,256]{3,2,1,0:T(8,128)(2,1)}, bf16[4,1,128,256]{3,2,1,0:T(8,128)(2,1)}, u32[]{:S(2)}, u32[]{:S(2)}) collective-permute-start(bf16[4,1,128,256]{3,2,1,0:T(8,128)(2,1)} %constant_dynamic-update-slice_fusion), channel_id=1, source_target_pairs={{0,1},{1,2},{2,3},{3,4},{4,5},{5,6},{6,7},{8,9},{9,10},{10,11},{11... | collective-permute-start | bytes 786440 | tf_op jit(solution)/shard_map/ppermute | solution.py:18
  21.8 19.2 %collective-permute-start.2 = (bf16[4,1,128,256]{3,2,1,0:T(8,128)(2,1)}, bf16[4,1,128,256]{3,2,1,0:T(8,128)(2,1)}, u32[]{:S(2)}, u32[]{:S(2)}) collective-permute-start(bf16[4,1,128,256]{3,2,1,0:T(8,128)(2,1)} %constant_dynamic-update-slice_fusion), channel_id=1, source_target_pairs={{1,0},{2,1},{3,2},{4,3},{5,4},{6,5},{7,6},{9,8},{10,9},{11,10},{12... | collective-permute-start | bytes 786440 | tf_op jit(solution)/shard_map/ppermute | solution.py:21
  25.4 3.9 %copy-start = (bf16[1,1,3,256,256]{4,3,2,1,0:T(8,128)(2,1)}, bf16[1,1,3,256,256]{4,3,2,1,0:T(8,128)(2,1)S(1)}, u32[]{:S(2)}) copy-start(bf16[1,1,3,256,256]{4,3,2,1,0:T(8,128)(2,1)S(1)} %get-tuple-element.21) | copy-start | bytes 1179652
  25.4 3.9 %copy-start.2 = (bf16[1,1,3,256,256]{4,3,2,1,0:T(8,128)(2,1)}, bf16[1,1,3,256,256]{4,3,2,1,0:T(8,128)(2,1)S(1)}, u32[]{:S(2)}) copy-start(bf16[1,1,3,256,256]{4,3,2,1,0:T(8,128)(2,1)S(1)} %get-tuple-element.22) | copy-start | bytes 1179652
  25.4 3.9 %copy-start.4 = (bf16[1,1,3,256,256]{4,3,2,1,0:T(8,128)(2,1)}, bf16[1,1,3,256,256]{4,3,2,1,0:T(8,128)(2,1)S(1)}, u32[]{:S(2)}) copy-start(bf16[1,1,3,256,256]{4,3,2,1,0:T(8,128)(2,1)S(1)} %get-tuple-element.23) | copy-start | bytes 1179652
  30.2 3.7 %copy-start.7 = (bf16[4,1,128,256]{3,2,0,1:T(8,128)(2,1)S(1)}, bf16[4,1,128,256]{3,2,0,1:T(8,128)(2,1)}, u32[]{:S(2)}) copy-start(bf16[4,1,128,256]{3,2,0,1:T(8,128)(2,1)} %copy-done.6) | copy-start | bytes 786436
  34.9 21.4 %collective-permute-start.4 = (bf16[6,1,128,256]{3,2,0,1:T(8,128)(2,1)S(1)}, bf16[6,1,128,256]{3,2,0,1:T(8,128)(2,1)S(1)}, u32[]{:S(2)}, u32[]{:S(2)}) collective-permute-start(bf16[6,1,128,256]{3,2,0,1:T(8,128)(2,1)S(1)} %pad_maximum_fusion.20), channel_id=1, source_target_pairs={{0,1},{1,2},{2,3},{3,4},{4,5},{5,6},{6,7},{8,9},{9,10},{10,11},{11... | collective-permute-start | bytes 1179656 | tf_op jit(solution)/shard_map/ppermute | solution.py:18
  39.5 16.9 %collective-permute-start.5 = (bf16[6,1,128,256]{3,2,0,1:T(8,128)(2,1)S(1)}, bf16[6,1,128,256]{3,2,0,1:T(8,128)(2,1)S(1)}, u32[]{:S(2)}, u32[]{:S(2)}) collective-permute-start(bf16[6,1,128,256]{3,2,0,1:T(8,128)(2,1)S(1)} %pad_maximum_fusion.20), channel_id=1, source_target_pairs={{1,0},{2,1},{3,2},{4,3},{5,4},{6,5},{7,6},{9,8},{10,9},{11,10},{12... | collective-permute-start | bytes 1179656 | tf_op jit(solution)/shard_map/ppermute | solution.py:21
  54.1 2.2 copy-start.8
  58.0 4.9 %copy-start.19 = (bf16[4,1,128,256]{3,2,0,1:T(8,128)(2,1)}, bf16[4,1,128,256]{3,2,0,1:T(8,128)(2,1)S(1)}, u32[]{:S(2)}) copy-start(bf16[4,1,128,256]{3,2,0,1:T(8,128)(2,1)S(1)} %get-tuple-element.34) | copy-start | bytes 786436
  58.1 4.9 %copy-start.37 = (bf16[4,1,128,256]{3,2,0,1:T(8,128)(2,1)}, bf16[4,1,128,256]{3,2,0,1:T(8,128)(2,1)S(1)}, u32[]{:S(2)}) copy-start(bf16[4,1,128,256]{3,2,0,1:T(8,128)(2,1)S(1)} %get-tuple-element.35) | copy-start | bytes 786436
  58.1 5.4 %copy-start.21 = (bf16[4,1,128,256]{3,2,0,1:T(8,128)(2,1)}, bf16[4,1,128,256]{3,2,0,1:T(8,128)(2,1)S(1)}, u32[]{:S(2)}) copy-start(bf16[4,1,128,256]{3,2,0,1:T(8,128)(2,1)S(1)} %get-tuple-element.38) | copy-start | bytes 786436
  58.1 5.4 %copy-start.23 = (bf16[4,1,128,256]{3,2,0,1:T(8,128)(2,1)}, bf16[4,1,128,256]{3,2,0,1:T(8,128)(2,1)S(1)}, u32[]{:S(2)}) copy-start(bf16[4,1,128,256]{3,2,0,1:T(8,128)(2,1)S(1)} %get-tuple-element.39) | copy-start | bytes 786436
  58.1 5.4 %copy-start.25 = (bf16[4,1,128,256]{3,2,0,1:T(8,128)(2,1)}, bf16[4,1,128,256]{3,2,0,1:T(8,128)(2,1)S(1)}, u32[]{:S(2)}) copy-start(bf16[4,1,128,256]{3,2,0,1:T(8,128)(2,1)S(1)} %get-tuple-element.43) | copy-start | bytes 786436
  58.1 5.4 %copy-start.27 = (bf16[4,1,128,256]{3,2,0,1:T(8,128)(2,1)}, bf16[4,1,128,256]{3,2,0,1:T(8,128)(2,1)S(1)}, u32[]{:S(2)}) copy-start(bf16[4,1,128,256]{3,2,0,1:T(8,128)(2,1)S(1)} %get-tuple-element.36) | copy-start | bytes 786436
  58.1 5.4 %copy-start.29 = (bf16[4,1,128,256]{3,2,0,1:T(8,128)(2,1)}, bf16[4,1,128,256]{3,2,0,1:T(8,128)(2,1)S(1)}, u32[]{:S(2)}) copy-start(bf16[4,1,128,256]{3,2,0,1:T(8,128)(2,1)S(1)} %get-tuple-element.37) | copy-start | bytes 786436
  58.1 5.4 %copy-start.31 = (bf16[4,1,128,256]{3,2,0,1:T(8,128)(2,1)}, bf16[4,1,128,256]{3,2,0,1:T(8,128)(2,1)S(1)}, u32[]{:S(2)}) copy-start(bf16[4,1,128,256]{3,2,0,1:T(8,128)(2,1)S(1)} %get-tuple-element.44) | copy-start | bytes 786436
  58.1 6.3 %copy-start.56 = (bf16[4,1,128,256]{3,2,0,1:T(8,128)(2,1)}, bf16[4,1,128,256]{3,2,0,1:T(8,128)(2,1)S(1)}, u32[]{:S(2)}) copy-start(bf16[4,1,128,256]{3,2,0,1:T(8,128)(2,1)S(1)} %get-tuple-element.40) | copy-start | bytes 786436
  58.1 6.3 %copy-start.58 = (bf16[4,1,128,256]{3,2,0,1:T(8,128)(2,1)}, bf16[4,1,128,256]{3,2,0,1:T(8,128)(2,1)S(1)}, u32[]{:S(2)}) copy-start(bf16[4,1,128,256]{3,2,0,1:T(8,128)(2,1)S(1)} %get-tuple-element.41) | copy-start | bytes 786436
  58.1 6.3 %copy-start.60 = (bf16[4,1,128,256]{3,2,0,1:T(8,128)(2,1)}, bf16[4,1,128,256]{3,2,0,1:T(8,128)(2,1)S(1)}, u32[]{:S(2)}) copy-start(bf16[4,1,128,256]{3,2,0,1:T(8,128)(2,1)S(1)} %get-tuple-element.42) | copy-start | bytes 786436
  58.7 2.3 copy-start.41
  58.8 2.3 copy-start.43
  58.8 2.3 copy-start.45
  58.8 2.3 copy-start.47
  58.8 4.1 %copy-start.33 = (bf16[4,1,128,256]{3,2,0,1:T(8,128)(2,1)}, bf16[4,1,128,256]{3,2,0,1:T(8,128)(2,1)S(1)}, u32[]{:S(2)}) copy-start(bf16[4,1,128,256]{3,2,0,1:T(8,128)(2,1)S(1)} %get-tuple-element.24) | copy-start | bytes 786436
  58.8 4.1 %copy-start.35 = (bf16[4,1,128,256]{3,2,0,1:T(8,128)(2,1)}, bf16[4,1,128,256]{3,2,0,1:T(8,128)(2,1)S(1)}, u32[]{:S(2)}) copy-start(bf16[4,1,128,256]{3,2,0,1:T(8,128)(2,1)S(1)} %get-tuple-element.33) | copy-start | bytes 786436
  58.8 4.1 %copy-start.39 = (bf16[4,1,128,256]{3,2,0,1:T(8,128)(2,1)}, bf16[4,1,128,256]{3,2,0,1:T(8,128)(2,1)S(1)}, u32[]{:S(2)}) copy-start(bf16[4,1,128,256]{3,2,0,1:T(8,128)(2,1)S(1)} %get-tuple-element.32) | copy-start | bytes 786436
  59.0 2.1 copy-start.51
  59.0 2.1 copy-start.53
  59.0 4.0 %copy-start.49 = (bf16[4,1,128,256]{3,2,0,1:T(8,128)(2,1)}, bf16[4,1,128,256]{3,2,0,1:T(8,128)(2,1)S(1)}, u32[]{:S(2)}) copy-start(bf16[4,1,128,256]{3,2,0,1:T(8,128)(2,1)S(1)} %get-tuple-element.45) | copy-start | bytes 786436
  59.1 1.6 copy-start.3
  66.8 4.2 %collective-permute-start.6 = (bf16[2,1,128,256]{3,2,0,1:T(8,128)(2,1)S(1)}, bf16[2,1,128,256]{3,2,0,1:T(8,128)(2,1)S(1)}, u32[]{:S(2)}, u32[]{:S(2)}) collective-permute-start(bf16[2,1,128,256]{3,2,0,1:T(8,128)(2,1)S(1)} %slice.341), channel_id=1, source_target_pairs={{0,8},{8,16},{16,24},{1,9},{9,17},{17,25},{2,10},{10,18},{18,26},{... | collective-permute-start | bytes 393224 | tf_op jit(solution)/shard_map/ppermute | solution.py:10
  71.2 1.5 copy-start.46
  71.3 1.5 copy-start.48
  71.3 1.5 copy-start.54
  72.5 1.6 copy-start.42
  72.5 1.6 copy-start.44
  72.5 1.6 copy-start.52
  72.5 197.6 %reduce-scatter.9.cloned.1.call-start = ((), (), s32[]{:S(2)}) async-start(), calls=%async_computation.4 | async-start | bytes 7962624 | tf_op jit(solution)/shard_map/reduce_scatter | solution.py:115
  76.8 1.3 copy-start.22
  76.8 1.3 copy-start.24
  76.8 1.3 copy-start.26
  82.1 209.7 %reduce-scatter.15.cloned.1.call-start = ((), (), s32[]{:S(2)}) async-start(), calls=%async_computation.7 | async-start | bytes 163840
  139.6 179.5 %reduce-scatter.13.cloned.1.call-start = ((), (), s32[]{:S(2)}) async-start(), calls=%async_computation.6 | async-start | bytes 1146880
  (26 other events, 30.9 us)
Sparse Core Ops, SparseCore 0:
  72.6 65.2 reduce-scatter.10
  142.0 128.0 reduce-scatter.8
  273.1 18.6 reduce-scatter.14
  295.0 24.0 reduce-scatter.12
where the time goes:
time: 326 us
  waiting for transfers between devices  235 us (72%)
  local copies, waits for them, and re-layouts  28.9 us (9%)
  matrix products  20.2 us (6%)
  starting transfers between devices  19.5 us (6%)
  between operations  14.9 us (5%)
  other arithmetic  7.46 us (2%)
    reduce_scatter x1, waiting for transfers between devices, body(): lax.psum_scatter(term_conv, 'height', scatter_dimension=0, tiled=True)  130 us
    reduce_scatter x1, waiting for transfers between devices, body(): lax.psum_scatter(term_down, 'height', scatter_dimension=0, tiled=True)  55.7 us
    unnamed x6, waiting for transfers between devices  46.6 us
    unnamed x138, local copies, waits for them, and re-layouts  22.5 us
    dot_general x9, matrix products, body(): jnp.dot(patches[a * 3 + b].T, grad_flat, preferred_element_type=jnp.float32)  11.7 us
    ppermute x2, starting transfers between devices, padded(): lax.ppermute(lax.slice_in_dim(block, block.shape[dim] - width, None, axis...  10.1 us
  transfers between devices with their start and end apart: 11, of which 5 were waited for; matrix products, arithmetic and copies ran while one was open for 12% of the time, Pallas kernels for 0%

commit v1 on v0

v1 whole, which is shorter than its diff:
```python
import functools

import jax
import jax.numpy as jnp
from jax import lax
from jax.experimental import pallas as pl
from jax.experimental.pallas import tpu as pltpu
from jax.sharding import PartitionSpec as P

F32 = jnp.float32
BF16 = jnp.bfloat16
VMEM_LIMIT = 56 * 1024 * 1024


def dot(left, right):
    return jnp.dot(left, right, preferred_element_type=F32)


def dot_nt(left, right):
    return lax.dot_general(left, right, (((1,), (1,)), ((), ())), preferred_element_type=F32)


def shifted_rows(value, step, period):
    if step == 0:
        return value
    rows = value.shape[0]
    moved = pltpu.roll(value, (-step) % rows, 0)
    place = lax.broadcasted_iota(jnp.int32, value.shape, 0) % period + step
    return jnp.where(jnp.logical_and(place >= 0, place < period), moved, 0.0)


def pack_halves(low, high, core):
    lane = lax.broadcasted_iota(jnp.int32, low.shape, 1)
    width = low.shape[1] // 2
    left = lane < width
    first = jnp.where(left, low, pltpu.roll(high, width, 1))
    second = jnp.where(left, pltpu.roll(low, width, 1), high)
    mine = core == 0
    return jnp.where(mine, second, first), jnp.where(mine, first, second)


def terms_kernel(dims, core_ref, clip_ref, up_ref, up_next_ref, here_ref, next_ref, low_ref, low_next_ref,
                 down_ref, grad_ref, act_ref, back_ref, send_ref, keep_ref, turned, total):
    frames, cols, chans, count = dims
    cells = frames * cols
    half = frames // 2
    core = core_ref[0]
    value = clip_ref[...].astype(F32)
    act = value / (1.0 + jnp.exp(-value))
    act = act.astype(BF16).astype(F32)
    for c in range(3):
        moved = shifted_rows(act, c - 1, cols)
        act_ref[:, c * chans : (c + 1) * chans] = moved.astype(BF16)
        turned[c * chans : (c + 1) * chans, :] = moved.T.astype(BF16)
    pairs = ((low_ref, low_next_ref), (here_ref, next_ref), (up_ref, up_next_ref))
    for b, (own, later) in enumerate(pairs):
        every = jnp.concatenate([own[...], later[...]], axis=0)
        back_ref[b] = every.T
        here = every[: (half + 1) * cols]
        after = every[cols : (half + 2) * cols]
        even = (dot_nt(after, down_ref[0]) + dot_nt(here, down_ref[2])).astype(BF16)
        odd = dot_nt(after, down_ref[1]).astype(BF16)
        for u in range(half + 1):
            grad_ref[b, 2 * u * cols : (2 * u + 1) * cols] = even[u * cols : (u + 1) * cols]
            grad_ref[b, (2 * u + 1) * cols : (2 * u + 2) * cols] = odd[u * cols : (u + 1) * cols]
    wide = 3 * chans
    lanes = chans // 2
    for a in range(3):
        for b in range(3):
            begin = (2 - a) * cols
            part = dot(turned[...], grad_ref[b, begin : begin + cells])
            row = (a * 3 + b) * wide
            for y in range(2):
                total[y, row : row + wide] = part[:, y * lanes : (y + 1) * lanes]
    block = 9 * wide // count
    for h in range(count):
        for y in range(2):
            low = total[y, h * block : h * block + block // 2]
            high = total[y, h * block + block // 2 : (h + 1) * block]
            send, keep = pack_halves(low, high, core)
            send_ref[y, h] = send.astype(BF16)
            keep_ref[y, h] = keep.astype(BF16)


def down_kernel(dims, core_ref, clip_ref, act_ref, back_ref, weight_ref, send_ref, keep_ref, cross, total):
    frames, cols, chans, count = dims
    half = frames // 2
    core = core_ref[0]
    wide = 3 * chans

    def pick(value, parity):
        return jnp.concatenate([value[(2 * u + parity) * cols : (2 * u + parity + 1) * cols] for u in range(half)], axis=0)

    sides = (pick(act_ref[...], 0), pick(act_ref[...], 1))
    clips = (pick(clip_ref[...], 0), pick(clip_ref[...], 1))
    for s in range(5):
        begin = ((4 - s + s % 2) // 2) * cols
        for b in range(3):
            cross[s, b] = dot(back_ref[b, :, begin : begin + half * cols], sides[s % 2]).astype(BF16)
    lanes = chans // 2
    for k in range(3):
        begin = ((2 - k + k % 2) // 2) * cols
        part = dot(back_ref[1, :, begin : begin + half * cols], clips[k % 2])
        for a in range(3):
            for b in range(3):
                part = part + dot(cross[a + k, b], weight_ref[a * 3 + b])
        flipped = part.T
        for y in range(2):
            total[y, k * chans : (k + 1) * chans] = flipped[:, y * lanes : (y + 1) * lanes]
    block = 3 * chans // count
    for h in range(count):
        for y in range(2):
            low = total[y, h * block : h * block + block // 2]
            high = total[y, h * block + block // 2 : (h + 1) * block]
            send, keep = pack_halves(low, high, core)
            send_ref[y, h] = send.astype(BF16)
            keep_ref[y, h] = keep.astype(BF16)


def input_kernel(dims, clip_ref, grad_ref, weight_ref, out_ref):
    frames, cols, chans, _ = dims
    cells = frames * cols
    acc = [jnp.zeros((cells, chans), F32) for _ in range(3)]
    for a in range(3):
        for b in range(3):
            begin = (2 - a) * cols
            grads = grad_ref[b, begin : begin + cells]
            for c in range(3):
                acc[c] = acc[c] + dot_nt(grads, weight_ref[a * 3 + b, c * chans : (c + 1) * chans])
    grad_act = acc[1]
    for c in (0, 2):
        grad_act = grad_act + shifted_rows(acc[c], 1 - c, cols)
    value = clip_ref[...].astype(F32)
    sig = 1.0 / (1.0 + jnp.exp(-value))
    own = grad_ref[1, :cells].astype(F32)
    out_ref[...] = (own + grad_act * (sig * (1.0 + value * (1.0 - sig)))).astype(BF16)


def vmem():
    return pl.BlockSpec(memory_space=pltpu.VMEM)


def smem():
    return pl.BlockSpec(memory_space=pltpu.SMEM)


def shape(dims, dtype):
    return jax.ShapeDtypeStruct(dims, dtype)


def call(kernel, scalars, args, outs, scratch=(), flops=0):
    size = sum(a.size * a.dtype.itemsize for a in args)
    return pl.pallas_call(
        kernel,
        out_shape=outs,
        in_specs=[smem()] * len(scalars) + [vmem()] * len(args),
        out_specs=jax.tree.map(lambda _: vmem(), outs),
        scratch_shapes=list(scratch),
        compiler_params=pltpu.CompilerParams(vmem_limit_bytes=VMEM_LIMIT),
        cost_estimate=pl.CostEstimate(flops=flops, bytes_accessed=size, transcendentals=0),
    )(*scalars, *args)


def halved(ref, axis, index):
    lead = ref.shape[:-2]
    rest = lead[:axis] + lead[axis + 1 :]
    for flat in range(functools.reduce(lambda p, q: p * q, rest, 1)):
        spot, left = [], flat
        for extent in reversed(rest):
            spot.insert(0, left % extent)
            left //= extent
        yield tuple(spot), tuple(spot[:axis]) + (index,) + tuple(spot[axis:])


def first_kernel(axes, cuts, bits_ref, conv_keep, conv_got, down_keep, down_got, *outs):
    rows = conv_keep.shape[-2]

    def summed(where, begin, end):
        parts = []
        if begin < rows:
            top = min(end, rows)
            parts.append(conv_keep[where + (slice(begin, top),)].astype(F32) + conv_got[where + (slice(begin, top),)].astype(F32))
        if end > rows:
            parts.append(down_keep[where].astype(F32) + down_got[where].astype(F32))
        return parts[0] if len(parts) == 1 else jnp.concatenate(parts, axis=0)

    for g, axis in enumerate(axes):
        mine = bits_ref[g]
        send, keep = outs[2 * g], outs[2 * g + 1]
        for to, where in halved(conv_keep, axis, 1 - mine):
            send[to] = summed(where, *cuts[g]).astype(BF16)
        for to, where in halved(conv_keep, axis, mine):
            keep[to] = summed(where, *cuts[g])


def fold_kernel(axes, bits_ref, *refs):
    count = len(axes)
    for g, axis in enumerate(axes):
        mine = bits_ref[g]
        held, got = refs[2 * g], refs[2 * g + 1]
        send, keep = refs[2 * count + 2 * g], refs[2 * count + 2 * g + 1]
        for to, where in halved(held, axis, 1 - mine):
            send[to] = (held[where] + got[where].astype(F32)).astype(BF16)
        for to, where in halved(held, axis, mine):
            keep[to] = held[where] + got[where].astype(F32)


def join_kernel(rows, *refs):
    groups = (len(refs) - 2) // 2
    conv_ref, down_ref = refs[-2:]
    parts = []
    for g in range(groups):
        parts.append(refs[2 * g][...] + refs[2 * g + 1][...].astype(F32))
    every = jnp.concatenate(parts, axis=0)
    width = every.shape[1] // 2
    for ref, begin, end in ((conv_ref, 0, rows), (down_ref, rows, every.shape[0])):
        piece = every[begin:end]
        ref[: end - begin] = piece[:, :width]
        ref[end - begin :] = pltpu.roll(piece, width, 1)[:, :width]


def swapped(value, axis, bit):
    count = lax.axis_size(axis)
    return lax.ppermute(value, axis, [(i, i ^ (1 << bit)) for i in range(count)])


def scattered(conv, down, tm_index, height_index):
    count = lax.axis_size("height")
    nbits = count.bit_length() - 1
    got = [swapped(send, "tm", 0) for send, _ in (conv, down)]
    rows = conv[0].shape[-2]
    total = rows + down[0].shape[-2]
    lead = (2,) * (1 + nbits)
    lanes = conv[0].shape[-1]

    def split(value):
        return value.reshape(lead + value.shape[-2:])

    links = [("tm", 1)] + [("height", i) for i in range(nbits)]
    position = {link: (0 if link[0] == "tm" else nbits - link[1]) for link in links}
    tops = links[:3]
    rest = links[3:]
    orders = [tops[g:] + tops[:g] + rest for g in range(3)]
    third = total // 3
    cuts = [(g * third, (g + 1) * third) for g in range(3)]

    def bit_of(link):
        index = tm_index if link[0] == "tm" else height_index
        return lax.shift_right_logical(index, link[1]) & 1

    left = [list(links) for _ in range(3)]

    def axis_of(g, link):
        ahead = [l for l in left[g] if position[l] < position[link]]
        return len(ahead)

    held = None
    for step in range(len(links)):
        now = [orders[g][step] for g in range(3)]
        axes = [axis_of(g, now[g]) for g in range(3)]
        bits = jnp.stack([bit_of(link) for link in now]).astype(jnp.int32)
        depth = len(links) - step - 1
        outs = []
        for g in range(3):
            dims = (2,) * depth + (third, lanes)
            outs += [shape(dims, BF16), shape(dims, F32)]
        if step == 0:
            args = [split(conv[1]), split(got[0]), split(down[1]), split(got[1])]
            kernel = functools.partial(first_kernel, axes, cuts)
        else:
            args = held
            kernel = functools.partial(fold_kernel, axes)
        result = call(kernel, [bits], args, outs)
        held = []
        for g in range(3):
            arrived = swapped(result[2 * g], *now[g])
            held += [result[2 * g + 1], arrived]
            left[g].remove(now[g])
    return call(
        functools.partial(join_kernel, rows), [], held,
        (shape((2 * rows, lanes // 2), F32), shape((2 * (total - rows), lanes // 2), F32)),
    )


def body(clip, conv_weight, down_weight, grad_out):
    nframes, nrows, ncols, chans = clip.shape
    half = grad_out.shape[0]
    cells = nframes * ncols
    outs = half * ncols
    tm_count, count = lax.axis_size("tm"), lax.axis_size("height")
    tm_index, height_index = lax.axis_index("tm"), lax.axis_index("height")
    mine = grad_out.reshape(outs, chans)

    def moved(rows, frames):
        pairs = []
        for t in range(tm_count):
            for h in range(count):
                to_t, to_h = t - frames, h + rows
                if 0 <= to_t < tm_count and 0 <= to_h < count:
                    pairs.append((t * count + h, to_t * count + to_h))
        return lax.ppermute(mine, ("tm", "height"), pairs)

    later = moved(0, 1)
    above, below = moved(1, 0), moved(-1, 0)
    above_later, below_later = moved(1, 1), moved(-1, 1)
    flat = clip.reshape(cells, chans)
    weight = conv_weight.reshape(9, 3 * chans, chans)
    core = (tm_index & 1).reshape(1).astype(jnp.int32)
    dims = (nframes, ncols, chans, count)
    wide = 3 * chans
    lanes = chans // 2
    grads, act, back, conv_send, conv_keep = call(
        functools.partial(terms_kernel, dims), [core],
        [flat, above, above_later, mine, later, below, below_later, down_weight],
        (
            shape((3, cells + 2 * ncols, chans), BF16),
            shape((cells, wide), BF16),
            shape((3, chans, 2 * outs), BF16),
            shape((2, count, 9 * wide // count // 2, lanes), BF16),
            shape((2, count, 9 * wide // count // 2, lanes), BF16),
        ),
        [pltpu.VMEM((wide, cells), BF16), pltpu.VMEM((2, 9 * wide, lanes), F32)],
        flops=2 * 9 * wide * cells * chans,
    )
    down_send, down_keep = call(
        functools.partial(down_kernel, dims), [core],
        [flat, act, back, weight],
        (
            shape((2, count, wide // count // 2, lanes), BF16),
            shape((2, count, wide // count // 2, lanes), BF16),
        ),
        [pltpu.VMEM((5, 3, chans, wide), BF16), pltpu.VMEM((2, wide, lanes), F32)],
        flops=4 * 9 * wide * cells * chans,
    )
    grad_conv, grad_down = scattered((conv_send, conv_keep), (down_send, down_keep), tm_index, height_index)
    grad_input = call(
        functools.partial(input_kernel, dims), [], [flat, grads, weight],
        shape((cells, chans), BF16),
        flops=2 * 9 * wide * cells * chans,
    )
    return (grad_input.reshape(clip.shape), grad_conv, grad_down)


def solution(mesh):
    placed = (P("tm", "height", None, None), P(), P(), P("tm", "height", None, None))
    return jax.shard_map(
        body,
        mesh=mesh,
        in_specs=placed,
        out_specs=(P("tm", "height", None, None), P("height", "tm"), P("height", "tm")),
        check_vma=False,
    )
```

time: 326 us -> 95.8 us (0.29)
  waiting for transfers between devices: 235 us -> 20.3 us
  Pallas kernels: 0 us -> 32.7 us
  local copies, waits for them, and re-layouts: 28.9 us -> 7.92 us
  matrix products: 20.2 us -> 0 us
  between operations: 14.9 us -> 0.81 us
  starting transfers between devices: 19.5 us -> 31.8 us
  other arithmetic: 7.46 us -> 1.79 us
    reduce_scatter x2 -> x0, waiting for transfers between devices: 186 us -> none  [the longest x1 130 us: body(): lax.psum_scatter(term_conv, 'height', scatter_dimension=0, tiled=True)]
    unnamed x6 -> x0, waiting for transfers between devices: 46.6 us -> none
    pallas_call x0 -> x8, Pallas kernels: none -> 32.7 us  [call(): pl.pallas_call(kernel, out_shape=outs, in_specs=[smem()] * len(scalars) +...]
    dot_general x33 -> x0, matrix products: 20.2 us -> none  [the longest x9 11.7 us: body(): jnp.dot(patches[a * 3 + b].T, grad_flat, preferred_element_type=jnp.float32)]
    ppermute x7 -> x19, waiting for transfers between devices: 1.81 us -> 20.3 us  [the longest x14 17 us: swapped(): return lax.ppermute(value, axis, [(i, i ^ 1 << bit) for i in range(count)])]
    unnamed x138 -> x40, local copies, waits for them, and re-layouts: 22.5 us -> 7.38 us
    ppermute x7 -> x19, starting transfers between devices: 19.1 us -> 31.8 us  [the longest x14 21.1 us: swapped(): return lax.ppermute(value, axis, [(i, i ^ 1 << bit) for i in range(count)])]
    slice x10 -> x0, local copies, waits for them, and re-layouts: 5.73 us -> none  [the longest x1 2.32 us: body(): conv_weight[a, b]]
  transfers between devices with their start and end apart: 11 -> 19, of which waited for: 5 -> 11; matrix products, arithmetic and copies ran while one was open for 12% -> 2% of each run, Pallas kernels for 0% -> 14%
where the time goes in v1:
time: 95.8 us; the launch traced here: 95.3 us
  Pallas kernels  32.7 us (34%)
  starting transfers between devices  31.8 us (33%)
  waiting for transfers between devices  20.3 us (21%)
  local copies, waits for them, and re-layouts  7.92 us (8%)
  other arithmetic  1.79 us (2%)
    pallas_call x8, Pallas kernels, call(): pl.pallas_call(kernel, out_shape=outs, in_specs=[smem()] * len(scalars) +...  32.7 us
    ppermute x14, starting transfers between devices, swapped(): return lax.ppermute(value, axis, [(i, i ^ 1 << bit) for i in range(count)])  21.1 us
    ppermute x14, waiting for transfers between devices, swapped(): return lax.ppermute(value, axis, [(i, i ^ 1 << bit) for i in range(count)])  17 us
    ppermute x5, starting transfers between devices, moved(): return lax.ppermute(mine, ('tm', 'height'), pairs)  10.6 us
    unnamed x40, local copies, waits for them, and re-layouts  7.38 us
    ppermute x5, waiting for transfers between devices, moved(): return lax.ppermute(mine, ('tm', 'height'), pairs)  3.28 us
  transfers between devices with their start and end apart: 19, of which 11 were waited for; matrix products, arithmetic and copies ran while one was open for 2% of the time, Pallas kernels for 14%

profile of v1, /device:TPU:0, one launch (start us, length us, event | category | flops | bytes accessed | tf_op | source)
XLA Modules:
  0.0 95.3 jit_solution(4425263502364021072)
XLA Ops:
  0.6 1.3 %collective-permute-start.4 = (bf16[256,256]{1,0:T(8,128)(2,1)}, bf16[256,256]{1,0:T(8,128)(2,1)S(1)}, u32[]{:S(2)}, u32[]{:S(2)}) collective-permute-start(bf16[256,256]{1,0:T(8,128)(2,1)} %bitcast.23), channel_id=1, source_target_pairs={{9,0},{10,1},{11,2},{12,3},{13,4},{14,5},{15,6},{17,8},{18,9},{19,... | collective-permute-start | bytes 393224 | tf_op jit(solution)/shard_map/ppermute | solution.py:301
  1.9 1.3 %collective-permute-start.3 = (bf16[256,256]{1,0:T(8,128)(2,1)}, bf16[256,256]{1,0:T(8,128)(2,1)S(1)}, u32[]{:S(2)}, u32[]{:S(2)}) collective-permute-start(bf16[256,256]{1,0:T(8,128)(2,1)} %bitcast.24), channel_id=1, source_target_pairs={{1,0},{2,1},{3,2},{4,3},{5,4},{6,5},{7,6},{9,8},{10,9},{11,10},{12... | collective-permute-start | bytes 393224 | tf_op jit(solution)/shard_map/ppermute | solution.py:301
  3.2 1.3 %collective-permute-start.2 = (bf16[256,256]{1,0:T(8,128)(2,1)}, bf16[256,256]{1,0:T(8,128)(2,1)S(1)}, u32[]{:S(2)}, u32[]{:S(2)}) collective-permute-start(bf16[256,256]{1,0:T(8,128)(2,1)} %bitcast.25), channel_id=1, source_target_pairs={{8,0},{9,1},{10,2},{11,3},{12,4},{13,5},{14,6},{15,7},{16,8},{17,9... | collective-permute-start | bytes 393224 | tf_op jit(solution)/shard_map/ppermute | solution.py:301
  4.5 0.7 collective-permute-start.1
  5.2 6.1 %collective-permute-start = (bf16[256,256]{1,0:T(8,128)(2,1)}, bf16[256,256]{1,0:T(8,128)(2,1)S(1)}, u32[]{:S(2)}, u32[]{:S(2)}) collective-permute-start(bf16[256,256]{1,0:T(8,128)(2,1)} %bitcast.27), channel_id=1, source_target_pairs={{0,1},{1,2},{2,3},{3,4},{4,5},{5,6},{6,7},{8,9},{9,10},{10,11},{11... | collective-permute-start | bytes 393224 | tf_op jit(solution)/shard_map/ppermute | solution.py:301
  11.4 3.3 %collective-permute-done.up_ref = bf16[256,256]{1,0:T(8,128)(2,1)S(1)} collective-permute-done((bf16[256,256]{1,0:T(8,128)(2,1)}, bf16[256,256]{1,0:T(8,128)(2,1)S(1)}, u32[]{:S(2)}, u32[]{:S(2)}) %collective-permute-start) | collective-permute-done | bytes 131104 | tf_op jit(solution)/shard_map/ppermute | solution.py:301
  14.7 0.6 copy-done.18
  15.3 6.0 %shard_map.67 = (bf16[3,768,256]{2,1,0:T(8,128)(2,1)}, bf16[512,768]{1,0:T(8,128)(2,1)}, bf16[3,256,512]{2,1,0:T(8,128)(2,1)}, bf16[2,8,432,128]{3,2,1,0:T(8,128)(2,1)}, bf16[2,8,432,128]{3,2,1,0:T(8,128)(2,1)}) custom-call(s32[1]{0:T(128)} %bitcast.1.core_ref, bf16[512,256]{1,0:T(8,128)(2,1)} %bitcast.20, bf16[256,256]{1,0:T(8,128)(2,1)} %copy-done.18, ...), custom_call_target="tpu_custom_call" | custom-call | flops 1811939328 | bytes 1441792 | tf_op jit(solution)/shard_map/pallas_call | solution.py:153
  21.4 2.2 %collective-permute-start.5 = (bf16[2,8,432,128]{3,2,1,0:T(8,128)(2,1)}, bf16[2,8,432,128]{3,2,1,0:T(8,128)(2,1)S(1)}, u32[]{:S(2)}, u32[]{:S(2)}) collective-permute-start(bf16[2,8,432,128]{3,2,1,0:T(8,128)(2,1)} %get-tuple-element.38), channel_id=1, source_target_pairs={{0,8},{8,0},{16,24},{24,16},{1,9},{9,1},{17,25},{25,17},{2,10},{10... | collective-permute-start | bytes 5308424 | tf_op jit(solution)/shard_map/ppermute | solution.py:224
  23.6 8.1 %shard_map.69 = (bf16[2,8,48,128]{3,2,1,0:T(8,128)(2,1)}, bf16[2,8,48,128]{3,2,1,0:T(8,128)(2,1)}) custom-call(s32[1]{0:T(128)} %bitcast.1.core_ref, bf16[512,256]{1,0:T(8,128)(2,1)} %bitcast.21, bf16[512,768]{1,0:T(8,128)(2,1)} %get-tuple-element.39.act_ref, bf16[3,256,512]{2,1,0:T(8,128)(2,1)} %get-tuple-element.40.back_ref, bf16[9,768,256]{2,1,0:T(8,128)(2,1)} %bitcast.18), custom_call_target="tpu_custom_call" | custom-call | flops 3623878656 | bytes 5373952 | tf_op jit(solution)/shard_map/pallas_call | solution.py:153
  31.7 0.6 pad_add_fusion.2.bits_ref
  32.3 1.1 %collective-permute-done.6 = bf16[2,8,48,128]{3,2,1,0:T(8,128)(2,1)S(1)} collective-permute-done((bf16[2,8,48,128]{3,2,1,0:T(8,128)(2,1)}, bf16[2,8,48,128]{3,2,1,0:T(8,128)(2,1)S(1)}, u32[]{:S(2)}, u32[]{:S(2)}) %collective-permute-start.6) | collective-permute-done | bytes 196640 | tf_op jit(solution)/shard_map/ppermute | solution.py:224
  33.3 0.7 copy-done.4
  34.0 0.6 copy-done
  34.6 4.0 %shard_map.70 = (bf16[2,2,2,160,128]{4,3,2,1,0:T(8,128)(2,1)}, f32[2,2,2,160,128]{4,3,2,1,0:T(8,128)}, bf16[2,2,2,160,128]{4,3,2,1,0:T(8,128)(2,1)}, f32[2,2,2,1...) custom-call(s32[3]{0:T(128)} %pad_add_fusion.2.bits_ref, ...), custom_call_target="tpu_custom_call" | custom-call | bytes 3932160 | tf_op jit(solution)/shard_map/pallas_call | solution.py:153
  38.6 4.4 %collective-permute-start.7 = (bf16[2,2,2,160,128]{4,3,2,1,0:T(8,128)(2,1)}, bf16[2,2,2,160,128]{4,3,2,1,0:T(8,128)(2,1)S(1)}, u32[]{:S(2)}, u32[]{:S(2)}) collective-permute-start(bf16[2,2,2,160,128]{4,3,2,1,0:T(8,128)(2,1)} %get-tuple-element.44), channel_id=1, source_target_pairs={{0,16},{8,24},{16,0},{24,8},{1,17},{9,25},{17,1},{25,9},{2,18},{10... | collective-permute-start | bytes 983048 | tf_op jit(solution)/shard_map/ppermute | solution.py:224
  43.0 2.4 %collective-permute-start.8 = (bf16[2,2,2,160,128]{4,3,2,1,0:T(8,128)(2,1)}, bf16[2,2,2,160,128]{4,3,2,1,0:T(8,128)(2,1)S(1)}, u32[]{:S(2)}, u32[]{:S(2)}) collective-permute-start(bf16[2,2,2,160,128]{4,3,2,1,0:T(8,128)(2,1)} %get-tuple-element.46), channel_id=1, source_target_pairs={{0,1},{1,0},{2,3},{3,2},{4,5},{5,4},{6,7},{7,6},{8,9},{9,8},{10,11... | collective-permute-start | bytes 983048 | tf_op jit(solution)/shard_map/ppermute | solution.py:224
  45.4 1.8 %collective-permute-start.9 = (bf16[2,2,2,160,128]{4,3,2,1,0:T(8,128)(2,1)}, bf16[2,2,2,160,128]{4,3,2,1,0:T(8,128)(2,1)S(1)}, u32[]{:S(2)}, u32[]{:S(2)}) collective-permute-start(bf16[2,2,2,160,128]{4,3,2,1,0:T(8,128)(2,1)} %get-tuple-element.48), channel_id=1, source_target_pairs={{0,2},{1,3},{2,0},{3,1},{4,6},{5,7},{6,4},{7,5},{8,10},{9,11},{10,... | collective-permute-start | bytes 983048 | tf_op jit(solution)/shard_map/ppermute | solution.py:224
  47.2 0.6 pad_add_fusion.1.bits_ref
  47.8 3.7 %collective-permute-done.7.refs_1_ = bf16[2,2,2,160,128]{4,3,2,1,0:T(8,128)(2,1)S(1)} collective-permute-done((bf16[2,2,2,160,128]{4,3,2,1,0:T(8,128)(2,1)}, bf16[2,2,2,160,128]{4,3,2,1,0:T(8,128)(2,1)S(1)}, u32[]{:S(2)}, u32[]{:S(2)}) %collective-permute-start.7) | collective-permute-done | bytes 327712 | tf_op jit(solution)/shard_map/ppermute | solution.py:224
  51.4 2.1 %collective-permute-done.8.refs_3_ = bf16[2,2,2,160,128]{4,3,2,1,0:T(8,128)(2,1)S(1)} collective-permute-done((bf16[2,2,2,160,128]{4,3,2,1,0:T(8,128)(2,1)}, bf16[2,2,2,160,128]{4,3,2,1,0:T(8,128)(2,1)S(1)}, u32[]{:S(2)}, u32[]{:S(2)}) %collective-permute-start.8) | collective-permute-done | bytes 327712 | tf_op jit(solution)/shard_map/ppermute | solution.py:224
  53.5 1.5 %collective-permute-done.9.refs_5_ = bf16[2,2,2,160,128]{4,3,2,1,0:T(8,128)(2,1)S(1)} collective-permute-done((bf16[2,2,2,160,128]{4,3,2,1,0:T(8,128)(2,1)}, bf16[2,2,2,160,128]{4,3,2,1,0:T(8,128)(2,1)S(1)}, u32[]{:S(2)}, u32[]{:S(2)}) %collective-permute-start.9) | collective-permute-done | bytes 327712 | tf_op jit(solution)/shard_map/ppermute | solution.py:224
  55.1 0.7 copy-done.3
  55.8 3.0 %shard_map.71 = (bf16[2,2,160,128]{3,2,1,0:T(8,128)(2,1)}, f32[2,2,160,128]{3,2,1,0:T(8,128)}, bf16[2,2,160,128]{3,2,1,0:T(8,128)(2,1)}, f32[2,2,160,128]{3,2,1,...) custom-call(s32[3]{0:T(128)} %pad_add_fusion.1.bits_ref, ...), custom_call_target="tpu_custom_call" | custom-call | bytes 2949120 | tf_op jit(solution)/shard_map/pallas_call | solution.py:153
  58.8 1.4 %collective-permute-start.10 = (bf16[2,2,160,128]{3,2,1,0:T(8,128)(2,1)}, bf16[2,2,160,128]{3,2,1,0:T(8,128)(2,1)S(1)}, u32[]{:S(2)}, u32[]{:S(2)}) collective-permute-start(bf16[2,2,160,128]{3,2,1,0:T(8,128)(2,1)} %get-tuple-element.50), channel_id=1, source_target_pairs={{0,1},{1,0},{2,3},{3,2},{4,5},{5,4},{6,7},{7,6},{8,9},{9,8},{10,11... | collective-permute-start | bytes 491528 | tf_op jit(solution)/shard_map/ppermute | solution.py:224
  60.2 1.7 %collective-permute-start.11 = (bf16[2,2,160,128]{3,2,1,0:T(8,128)(2,1)}, bf16[2,2,160,128]{3,2,1,0:T(8,128)(2,1)S(1)}, u32[]{:S(2)}, u32[]{:S(2)}) collective-permute-start(bf16[2,2,160,128]{3,2,1,0:T(8,128)(2,1)} %get-tuple-element.52), channel_id=1, source_target_pairs={{0,2},{1,3},{2,0},{3,1},{4,6},{5,7},{6,4},{7,5},{8,10},{9,11},{10,... | collective-permute-start | bytes 491528 | tf_op jit(solution)/shard_map/ppermute | solution.py:224
  61.9 0.3 collective-permute-start.12
  62.2 0.6 pad_add_fusion.bits_ref
  62.8 1.5 %collective-permute-done.10.refs_1_ = bf16[2,2,160,128]{3,2,1,0:T(8,128)(2,1)S(1)} collective-permute-done((bf16[2,2,160,128]{3,2,1,0:T(8,128)(2,1)}, bf16[2,2,160,128]{3,2,1,0:T(8,128)(2,1)S(1)}, u32[]{:S(2)}, u32[]{:S(2)}) %collective-permute-start.10) | collective-permute-done | bytes 163872 | tf_op jit(solution)/shard_map/ppermute | solution.py:224
  64.3 1.4 %collective-permute-done.11.refs_3_ = bf16[2,2,160,128]{3,2,1,0:T(8,128)(2,1)S(1)} collective-permute-done((bf16[2,2,160,128]{3,2,1,0:T(8,128)(2,1)}, bf16[2,2,160,128]{3,2,1,0:T(8,128)(2,1)S(1)}, u32[]{:S(2)}, u32[]{:S(2)}) %collective-permute-start.11) | collective-permute-done | bytes 163872 | tf_op jit(solution)/shard_map/ppermute | solution.py:224
  65.7 1.7 %collective-permute-done.12.refs_5_ = bf16[2,2,160,128]{3,2,1,0:T(8,128)(2,1)S(1)} collective-permute-done((bf16[2,2,160,128]{3,2,1,0:T(8,128)(2,1)}, bf16[2,2,160,128]{3,2,1,0:T(8,128)(2,1)S(1)}, u32[]{:S(2)}, u32[]{:S(2)}) %collective-permute-start.12) | collective-permute-done | bytes 163872 | tf_op jit(solution)/shard_map/ppermute | solution.py:224
  67.5 0.7 copy-done.7
  68.1 2.3 %shard_map.72 = (bf16[2,160,128]{2,1,0:T(8,128)(2,1)}, f32[2,160,128]{2,1,0:T(8,128)}, bf16[2,160,128]{2,1,0:T(8,128)(2,1)}, f32[2,160,128]{2,1,0:T(8,128)}, bf1...) custom-call(s32[3]{0:T(128)} %pad_add_fusion.bits_ref, f32[2,2,160,128]{3,2,1,0:T(8,128)} %get-tuple-element.49.refs_0_, ...), custom_call_target="tpu_custom_call" | custom-call | bytes 1474560 | tf_op jit(solution)/shard_map/pallas_call | solution.py:153
  70.5 0.3 collective-permute-start.13
  70.8 0.3 collective-permute-start.14
  71.0 0.6 collective-permute-start.15
  71.7 3.4 %collective-permute-done.13.refs_1_ = bf16[2,160,128]{2,1,0:T(8,128)(2,1)S(1)} collective-permute-done((bf16[2,160,128]{2,1,0:T(8,128)(2,1)}, bf16[2,160,128]{2,1,0:T(8,128)(2,1)S(1)}, u32[]{:S(2)}, u32[]{:S(2)}) %collective-permute-start.13) | collective-permute-done | bytes 81952 | tf_op jit(solution)/shard_map/ppermute | solution.py:224
  75.1 0.3 collective-permute-done.14.refs_3_
  75.4 0.3 collective-permute-done.15.refs_5_
  75.7 0.5 stack.14.bits_ref
  76.3 2.0 %shard_map.73 = (bf16[160,128]{1,0:T(8,128)(2,1)}, f32[160,128]{1,0:T(8,128)}, bf16[160,128]{1,0:T(8,128)(2,1)}, f32[160,128]{1,0:T(8,128)}, bf16[160,128]{1,0:T(8,128)(2,1)}, /*index=5*/f32[160,128]{1,0:T(8,128)}) custom-call(s32[3]{0:T(128)} %stack.14.bits_ref, f32[2,160,128]{2,1,0:T(8,128)} %get-tuple-element.55.refs_0_, bf16[2,160,128]{2,1,0:T(8,128)(2,1)} %copy-done.8, ...), custom_call_target="tpu_custom_call" | custom-call | bytes 737280 | tf_op jit(solution)/shard_map/pallas_call | solution.py:153
  78.3 2.8 %collective-permute-start.16 = (bf16[160,128]{1,0:T(8,128)(2,1)}, bf16[160,128]{1,0:T(8,128)(2,1)S(1)}, u32[]{:S(2)}, u32[]{:S(2)}) collective-permute-start(bf16[160,128]{1,0:T(8,128)(2,1)} %get-tuple-element.62), channel_id=1, source_target_pairs={{0,4},{1,5},{2,6},{3,7},{4,0},{5,1},{6,2},{7,3},{8,12},{9,13},{10,... | collective-permute-start | bytes 122888 | tf_op jit(solution)/shard_map/ppermute | solution.py:224
  81.2 2.8 %collective-permute-start.18 = (bf16[160,128]{1,0:T(8,128)(2,1)}, bf16[160,128]{1,0:T(8,128)(2,1)S(1)}, u32[]{:S(2)}, u32[]{:S(2)}) collective-permute-start(bf16[160,128]{1,0:T(8,128)(2,1)} %get-tuple-element.66), channel_id=1, source_target_pairs={{0,4},{1,5},{2,6},{3,7},{4,0},{5,1},{6,2},{7,3},{8,12},{9,13},{10,... | collective-permute-start | bytes 122888 | tf_op jit(solution)/shard_map/ppermute | solution.py:224
  84.0 5.4 %shard_map.68 = bf16[512,256]{1,0:T(8,128)(2,1)} custom-call(bf16[512,256]{1,0:T(8,128)(2,1)} %bitcast.22, bf16[3,768,256]{2,1,0:T(8,128)(2,1)} %get-tuple-element.36.grad_ref, bf16[9,768,256]{2,1,0:T(8,128)(2,1)} %bitcast.19), custom_call_target="tpu_custom_call" | custom-call | flops 1811939328 | bytes 4980736 | tf_op jit(solution)/shard_map/pallas_call | solution.py:153
  89.4 0.6 copy-done.11
  90.0 1.9 %shard_map.74 = (f32[864,64]{1,0:T(8,128)}, f32[96,64]{1,0:T(8,128)}) custom-call(f32[160,128]{1,0:T(8,128)} %get-tuple-element.61.refs_0_, bf16[160,128]{1,0:T(8,128)(2,1)} %copy-done.11, f32[160,128]{1,0:T(8,128)} %get-tuple-element.63.refs_2_, bf16[160,128]{1,0:T(8,128)(2,1)} %copy-done.12, f32[160,128]{1,0:T(8,128)} %get-tuple-element.65.refs_4_, ...), custom_call_target="tpu_custom_call" | custom-call | bytes 368640 | tf_op jit(solution)/shard_map/pallas_call | solution.py:153
  91.9 1.9 %copy.8 = f32[864,64]{0,1:T(8,128)} copy(f32[864,64]{1,0:T(8,128)} %get-tuple-element.70) | data formatting | bytes 442368
  93.8 1.5 %copy.9 = f32[96,64]{0,1:T(8,128)} copy(f32[96,64]{1,0:T(8,128)} %get-tuple-element.71) | data formatting | bytes 49152
  (42 shorter events, 0.4 us)
Async XLA Ops:
  0.6 10.7 %collective-permute-start.4 = (bf16[256,256]{1,0:T(8,128)(2,1)}, bf16[256,256]{1,0:T(8,128)(2,1)S(1)}, u32[]{:S(2)}, u32[]{:S(2)}) collective-permute-start(bf16[256,256]{1,0:T(8,128)(2,1)} %bitcast.23), channel_id=1, source_target_pairs={{9,0},{10,1},{11,2},{12,3},{13,4},{14,5},{15,6},{17,8},{18,9},{19,... | collective-permute-start | bytes 393224 | tf_op jit(solution)/shard_map/ppermute | solution.py:301
  1.9 9.4 %collective-permute-start.3 = (bf16[256,256]{1,0:T(8,128)(2,1)}, bf16[256,256]{1,0:T(8,128)(2,1)S(1)}, u32[]{:S(2)}, u32[]{:S(2)}) collective-permute-start(bf16[256,256]{1,0:T(8,128)(2,1)} %bitcast.24), channel_id=1, source_target_pairs={{1,0},{2,1},{3,2},{4,3},{5,4},{6,5},{7,6},{9,8},{10,9},{11,10},{12... | collective-permute-start | bytes 393224 | tf_op jit(solution)/shard_map/ppermute | solution.py:301
  3.2 8.1 %collective-permute-start.2 = (bf16[256,256]{1,0:T(8,128)(2,1)}, bf16[256,256]{1,0:T(8,128)(2,1)S(1)}, u32[]{:S(2)}, u32[]{:S(2)}) collective-permute-start(bf16[256,256]{1,0:T(8,128)(2,1)} %bitcast.25), channel_id=1, source_target_pairs={{8,0},{9,1},{10,2},{11,3},{12,4},{13,5},{14,6},{15,7},{16,8},{17,9... | collective-permute-start | bytes 393224 | tf_op jit(solution)/shard_map/ppermute | solution.py:301
  4.5 6.9 %collective-permute-start.1 = (bf16[256,256]{1,0:T(8,128)(2,1)}, bf16[256,256]{1,0:T(8,128)(2,1)S(1)}, u32[]{:S(2)}, u32[]{:S(2)}) collective-permute-start(bf16[256,256]{1,0:T(8,128)(2,1)} %bitcast.26), channel_id=1, source_target_pairs={{8,1},{9,2},{10,3},{11,4},{12,5},{13,6},{14,7},{16,9},{17,10},{18,... | collective-permute-start | bytes 393224 | tf_op jit(solution)/shard_map/ppermute | solution.py:301
  5.2 9.5 %collective-permute-start = (bf16[256,256]{1,0:T(8,128)(2,1)}, bf16[256,256]{1,0:T(8,128)(2,1)S(1)}, u32[]{:S(2)}, u32[]{:S(2)}) collective-permute-start(bf16[256,256]{1,0:T(8,128)(2,1)} %bitcast.27), channel_id=1, source_target_pairs={{0,1},{1,2},{2,3},{3,4},{4,5},{5,6},{6,7},{8,9},{9,10},{10,11},{11... | collective-permute-start | bytes 393224 | tf_op jit(solution)/shard_map/ppermute | solution.py:301
  11.3 3.3 %copy-start.14 = (bf16[256,256]{1,0:T(8,128)(2,1)}, bf16[256,256]{1,0:T(8,128)(2,1)S(1)}, u32[]{:S(2)}) copy-start(bf16[256,256]{1,0:T(8,128)(2,1)S(1)} %collective-permute-done.4.low_next_ref) | copy-start | bytes 393220
  11.4 3.3 %copy-start.15 = (bf16[256,256]{1,0:T(8,128)(2,1)}, bf16[256,256]{1,0:T(8,128)(2,1)S(1)}, u32[]{:S(2)}) copy-start(bf16[256,256]{1,0:T(8,128)(2,1)S(1)} %collective-permute-done.3.low_ref) | copy-start | bytes 393220
  11.4 3.3 %copy-start.16 = (bf16[256,256]{1,0:T(8,128)(2,1)}, bf16[256,256]{1,0:T(8,128)(2,1)S(1)}, u32[]{:S(2)}) copy-start(bf16[256,256]{1,0:T(8,128)(2,1)S(1)} %collective-permute-done.2.next_ref) | copy-start | bytes 393220
  11.4 3.3 %copy-start.17 = (bf16[256,256]{1,0:T(8,128)(2,1)}, bf16[256,256]{1,0:T(8,128)(2,1)S(1)}, u32[]{:S(2)}) copy-start(bf16[256,256]{1,0:T(8,128)(2,1)S(1)} %collective-permute-done.1.up_next_ref) | copy-start | bytes 393220
  14.7 0.7 copy-start.18
  21.4 12.0 %collective-permute-start.5 = (bf16[2,8,432,128]{3,2,1,0:T(8,128)(2,1)}, bf16[2,8,432,128]{3,2,1,0:T(8,128)(2,1)S(1)}, u32[]{:S(2)}, u32[]{:S(2)}) collective-permute-start(bf16[2,8,432,128]{3,2,1,0:T(8,128)(2,1)} %get-tuple-element.38), channel_id=1, source_target_pairs={{0,8},{8,0},{16,24},{24,16},{1,9},{9,1},{17,25},{25,17},{2,10},{10... | collective-permute-start | bytes 5308424 | tf_op jit(solution)/shard_map/ppermute | solution.py:224
  31.7 1.7 %collective-permute-start.6 = (bf16[2,8,48,128]{3,2,1,0:T(8,128)(2,1)}, bf16[2,8,48,128]{3,2,1,0:T(8,128)(2,1)S(1)}, u32[]{:S(2)}, u32[]{:S(2)}) collective-permute-start(bf16[2,8,48,128]{3,2,1,0:T(8,128)(2,1)} %get-tuple-element.42), channel_id=1, source_target_pairs={{0,8},{8,0},{16,24},{24,16},{1,9},{9,1},{17,25},{25,17},{2,10},{10... | collective-permute-start | bytes 589832 | tf_op jit(solution)/shard_map/ppermute | solution.py:224
  33.3 0.7 copy-start.4
  33.3 1.3 %copy-start = (bf16[2,8,432,128]{3,2,1,0:T(8,128)(2,1)}, bf16[2,8,432,128]{3,2,1,0:T(8,128)(2,1)S(1)}, u32[]{:S(2)}) copy-start(bf16[2,8,432,128]{3,2,1,0:T(8,128)(2,1)S(1)} %collective-permute-done.5) | copy-start | bytes 5308420
  38.6 12.8 %collective-permute-start.7 = (bf16[2,2,2,160,128]{4,3,2,1,0:T(8,128)(2,1)}, bf16[2,2,2,160,128]{4,3,2,1,0:T(8,128)(2,1)S(1)}, u32[]{:S(2)}, u32[]{:S(2)}) collective-permute-start(bf16[2,2,2,160,128]{4,3,2,1,0:T(8,128)(2,1)} %get-tuple-element.44), channel_id=1, source_target_pairs={{0,16},{8,24},{16,0},{24,8},{1,17},{9,25},{17,1},{25,9},{2,18},{10... | collective-permute-start | bytes 983048 | tf_op jit(solution)/shard_map/ppermute | solution.py:224
  43.0 10.5 %collective-permute-start.8 = (bf16[2,2,2,160,128]{4,3,2,1,0:T(8,128)(2,1)}, bf16[2,2,2,160,128]{4,3,2,1,0:T(8,128)(2,1)S(1)}, u32[]{:S(2)}, u32[]{:S(2)}) collective-permute-start(bf16[2,2,2,160,128]{4,3,2,1,0:T(8,128)(2,1)} %get-tuple-element.46), channel_id=1, source_target_pairs={{0,1},{1,0},{2,3},{3,2},{4,5},{5,4},{6,7},{7,6},{8,9},{9,8},{10,11... | collective-permute-start | bytes 983048 | tf_op jit(solution)/shard_map/ppermute | solution.py:224
  45.4 9.7 %collective-permute-start.9 = (bf16[2,2,2,160,128]{4,3,2,1,0:T(8,128)(2,1)}, bf16[2,2,2,160,128]{4,3,2,1,0:T(8,128)(2,1)S(1)}, u32[]{:S(2)}, u32[]{:S(2)}) collective-permute-start(bf16[2,2,2,160,128]{4,3,2,1,0:T(8,128)(2,1)} %get-tuple-element.48), channel_id=1, source_target_pairs={{0,2},{1,3},{2,0},{3,1},{4,6},{5,7},{6,4},{7,5},{8,10},{9,11},{10,... | collective-permute-start | bytes 983048 | tf_op jit(solution)/shard_map/ppermute | solution.py:224
  51.4 3.6 %copy-start.1 = (bf16[2,2,2,160,128]{4,3,2,1,0:T(8,128)(2,1)}, bf16[2,2,2,160,128]{4,3,2,1,0:T(8,128)(2,1)S(1)}, u32[]{:S(2)}) copy-start(bf16[2,2,2,160,128]{4,3,2,1,0:T(8,128)(2,1)S(1)} %collective-permute-done.7.refs_1_) | copy-start | bytes 983044
  53.5 1.5 %copy-start.2 = (bf16[2,2,2,160,128]{4,3,2,1,0:T(8,128)(2,1)}, bf16[2,2,2,160,128]{4,3,2,1,0:T(8,128)(2,1)S(1)}, u32[]{:S(2)}) copy-start(bf16[2,2,2,160,128]{4,3,2,1,0:T(8,128)(2,1)S(1)} %collective-permute-done.8.refs_3_) | copy-start | bytes 983044
  55.1 0.7 copy-start.3
  58.8 5.5 %collective-permute-start.10 = (bf16[2,2,160,128]{3,2,1,0:T(8,128)(2,1)}, bf16[2,2,160,128]{3,2,1,0:T(8,128)(2,1)S(1)}, u32[]{:S(2)}, u32[]{:S(2)}) collective-permute-start(bf16[2,2,160,128]{3,2,1,0:T(8,128)(2,1)} %get-tuple-element.50), channel_id=1, source_target_pairs={{0,1},{1,0},{2,3},{3,2},{4,5},{5,4},{6,7},{7,6},{8,9},{9,8},{10,11... | collective-permute-start | bytes 491528 | tf_op jit(solution)/shard_map/ppermute | solution.py:224
  60.2 5.5 %collective-permute-start.11 = (bf16[2,2,160,128]{3,2,1,0:T(8,128)(2,1)}, bf16[2,2,160,128]{3,2,1,0:T(8,128)(2,1)S(1)}, u32[]{:S(2)}, u32[]{:S(2)}) collective-permute-start(bf16[2,2,160,128]{3,2,1,0:T(8,128)(2,1)} %get-tuple-element.52), channel_id=1, source_target_pairs={{0,2},{1,3},{2,0},{3,1},{4,6},{5,7},{6,4},{7,5},{8,10},{9,11},{10,... | collective-permute-start | bytes 491528 | tf_op jit(solution)/shard_map/ppermute | solution.py:224
  61.9 5.5 %collective-permute-start.12 = (bf16[2,2,160,128]{3,2,1,0:T(8,128)(2,1)}, bf16[2,2,160,128]{3,2,1,0:T(8,128)(2,1)S(1)}, u32[]{:S(2)}, u32[]{:S(2)}) collective-permute-start(bf16[2,2,160,128]{3,2,1,0:T(8,128)(2,1)} %get-tuple-element.54), channel_id=1, source_target_pairs={{0,16},{8,24},{16,0},{24,8},{1,17},{9,25},{17,1},{25,9},{2,18},{10... | collective-permute-start | bytes 491528 | tf_op jit(solution)/shard_map/ppermute | solution.py:224
  64.3 3.1 %copy-start.5 = (bf16[2,2,160,128]{3,2,1,0:T(8,128)(2,1)}, bf16[2,2,160,128]{3,2,1,0:T(8,128)(2,1)S(1)}, u32[]{:S(2)}) copy-start(bf16[2,2,160,128]{3,2,1,0:T(8,128)(2,1)S(1)} %collective-permute-done.10.refs_1_) | copy-start | bytes 491524
  65.7 1.8 %copy-start.6 = (bf16[2,2,160,128]{3,2,1,0:T(8,128)(2,1)}, bf16[2,2,160,128]{3,2,1,0:T(8,128)(2,1)S(1)}, u32[]{:S(2)}) copy-start(bf16[2,2,160,128]{3,2,1,0:T(8,128)(2,1)S(1)} %collective-permute-done.11.refs_3_) | copy-start | bytes 491524
  67.5 0.7 copy-start.7
  70.5 4.7 %collective-permute-start.13 = (bf16[2,160,128]{2,1,0:T(8,128)(2,1)}, bf16[2,160,128]{2,1,0:T(8,128)(2,1)S(1)}, u32[]{:S(2)}, u32[]{:S(2)}) collective-permute-start(bf16[2,160,128]{2,1,0:T(8,128)(2,1)} %get-tuple-element.56), channel_id=1, source_target_pairs={{0,2},{1,3},{2,0},{3,1},{4,6},{5,7},{6,4},{7,5},{8,10},{9,11},{10,... | collective-permute-start | bytes 245768 | tf_op jit(solution)/shard_map/ppermute | solution.py:224
  70.8 4.7 %collective-permute-start.14 = (bf16[2,160,128]{2,1,0:T(8,128)(2,1)}, bf16[2,160,128]{2,1,0:T(8,128)(2,1)S(1)}, u32[]{:S(2)}, u32[]{:S(2)}) collective-permute-start(bf16[2,160,128]{2,1,0:T(8,128)(2,1)} %get-tuple-element.58), channel_id=1, source_target_pairs={{0,16},{8,24},{16,0},{24,8},{1,17},{9,25},{17,1},{25,9},{2,18},{10... | collective-permute-start | bytes 245768 | tf_op jit(solution)/shard_map/ppermute | solution.py:224
  71.0 4.7 %collective-permute-start.15 = (bf16[2,160,128]{2,1,0:T(8,128)(2,1)}, bf16[2,160,128]{2,1,0:T(8,128)(2,1)S(1)}, u32[]{:S(2)}, u32[]{:S(2)}) collective-permute-start(bf16[2,160,128]{2,1,0:T(8,128)(2,1)} %get-tuple-element.60), channel_id=1, source_target_pairs={{0,1},{1,0},{2,3},{3,2},{4,5},{5,4},{6,7},{7,6},{8,9},{9,8},{10,11... | collective-permute-start | bytes 245768 | tf_op jit(solution)/shard_map/ppermute | solution.py:224
  75.1 1.1 %copy-start.8 = (bf16[2,160,128]{2,1,0:T(8,128)(2,1)}, bf16[2,160,128]{2,1,0:T(8,128)(2,1)S(1)}, u32[]{:S(2)}) copy-start(bf16[2,160,128]{2,1,0:T(8,128)(2,1)S(1)} %collective-permute-done.13.refs_1_) | copy-start | bytes 245764
  75.4 0.8 copy-start.9
  75.7 0.6 copy-start.10
  78.3 11.0 %collective-permute-start.16 = (bf16[160,128]{1,0:T(8,128)(2,1)}, bf16[160,128]{1,0:T(8,128)(2,1)S(1)}, u32[]{:S(2)}, u32[]{:S(2)}) collective-permute-start(bf16[160,128]{1,0:T(8,128)(2,1)} %get-tuple-element.62), channel_id=1, source_target_pairs={{0,4},{1,5},{2,6},{3,7},{4,0},{5,1},{6,2},{7,3},{8,12},{9,13},{10,... | collective-permute-start | bytes 122888 | tf_op jit(solution)/shard_map/ppermute | solution.py:224
  81.1 8.3 %collective-permute-start.17 = (bf16[160,128]{1,0:T(8,128)(2,1)}, bf16[160,128]{1,0:T(8,128)(2,1)S(1)}, u32[]{:S(2)}, u32[]{:S(2)}) collective-permute-start(bf16[160,128]{1,0:T(8,128)(2,1)} %get-tuple-element.64), channel_id=1, source_target_pairs={{0,4},{1,5},{2,6},{3,7},{4,0},{5,1},{6,2},{7,3},{8,12},{9,13},{10,... | collective-permute-start | bytes 122888 | tf_op jit(solution)/shard_map/ppermute | solution.py:224
  81.2 8.1 %collective-permute-start.18 = (bf16[160,128]{1,0:T(8,128)(2,1)}, bf16[160,128]{1,0:T(8,128)(2,1)S(1)}, u32[]{:S(2)}, u32[]{:S(2)}) collective-permute-start(bf16[160,128]{1,0:T(8,128)(2,1)} %get-tuple-element.66), channel_id=1, source_target_pairs={{0,4},{1,5},{2,6},{3,7},{4,0},{5,1},{6,2},{7,3},{8,12},{9,13},{10,... | collective-permute-start | bytes 122888 | tf_op jit(solution)/shard_map/ppermute | solution.py:224
  89.4 0.6 copy-start.11
  89.4 0.6 copy-start.12
  89.4 0.6 copy-start.13

commit v2 on v0

v2 whole, which is shorter than its diff:
```python
import functools
import math

import jax
import jax.numpy as jnp
from jax import lax
from jax.experimental import pallas as pl
from jax.experimental.pallas import tpu as pltpu
from jax.sharding import PartitionSpec as P

F32 = jnp.float32
BF16 = jnp.bfloat16
MIB = 1024 * 1024


def dot(left, right):
    return jnp.dot(left, right, preferred_element_type=F32)


def dot_nt(left, right):
    return lax.dot_general(left, right, (((1,), (1,)), ((), ())), preferred_element_type=F32)


def shifted_rows(value, step, period):
    if step == 0:
        return value
    rows = value.shape[0]
    moved = pltpu.roll(value, (-step) % rows, 0)
    place = lax.broadcasted_iota(jnp.int32, value.shape, 0) % period + step
    return jnp.where(jnp.logical_and(place >= 0, place < period), moved, 0.0)


def channel_of(place, group, core):
    return (place // group * 2 + core) * group + place % group


def picker(chans, group, core):
    dims = (chans, chans // 2)
    wanted = channel_of(lax.broadcasted_iota(jnp.int32, dims, 1), group, core)
    return (lax.broadcasted_iota(jnp.int32, dims, 0) == wanted).astype(F32).astype(BF16)


def lay_window(window, core, own, other, first, second, frames):
    window[pl.ds(0, frames)] = first[...] + second[...]
    window[pl.ds(pl.multiple_of(frames * (1 + core), frames), frames)] = own[...]
    window[pl.ds(pl.multiple_of(frames * (2 - core), frames), frames)] = other[...]


def silu(value):
    return value / (1.0 + jnp.exp(-value))


def halved(lead, axis, index):
    rest = lead[:axis] + lead[axis + 1 :]
    for flat in range(math.prod(rest)):
        spot, left = [], flat
        for extent in reversed(rest):
            spot.insert(0, left % extent)
            left //= extent
        yield tuple(spot), tuple(spot[:axis]) + (index,) + tuple(spot[axis:])


def bit_of(spot_ref, link):
    return lax.shift_right_logical(spot_ref[link[0]], link[1]) & 1


def split_into(send, keep, lead, axis, mine, read):
    for to, where in halved(lead, axis, 1 - mine):
        send[to] = read(where).astype(send.dtype)
    for to, where in halved(lead, axis, mine):
        keep[to] = read(where)


def terms_kernel(plan, spot_ref, clip_ref, clip_other, first_ref, second_ref, here_ref, here_other, high_ref, high_other,
                 low_ref, low_other, down_ref, window_ref, even_ref, odd_ref, *rest):
    outs, (clips, even_t, odd_t, cross, spread, total) = rest[:-6], rest[-6:]
    cols, chans, group = plan.cols, plan.chans, plan.group
    core = spot_ref[0] & 1
    rows = clip_ref.shape[0]
    span = here_ref.shape[0]
    for k in range(3):
        spread[k * chans : (k + 1) * chans] = down_ref[k].T
    lay_window(clips, core, clip_ref, clip_other, first_ref, second_ref, rows)
    act = silu(clips[...].astype(F32)).astype(BF16)
    act = dot(act, picker(chans, group, core))
    part = chans // 2
    for c in range(3):
        moved = shifted_rows(act, c - 1, cols).astype(BF16)
        for f in range(3 * rows // cols // 2):
            to = slice(f * cols, (f + 1) * cols)
            lanes = slice(c * part, (c + 1) * part)
            for natural, turned, at in ((even_ref, even_t, 2 * f), (odd_ref, odd_t, 2 * f + 1)):
                piece = moved[at * cols : (at + 1) * cols]
                natural[to, lanes] = piece
                turned[lanes, to] = piece.T
    for b, (own, other) in enumerate(((low_ref, low_other), (here_ref, here_other), (high_ref, high_other))):
        window_ref[b, pl.ds(pl.multiple_of(span * core, span), span)] = own[...]
        window_ref[b, pl.ds(pl.multiple_of(span * (1 - core), span), span)] = other[...]
    for b in range(3):
        for s in range(5):
            turned = (even_t, odd_t)[s % 2]
            cells = turned[:, s // 2 * cols : s // 2 * cols + 2 * span]
            cross[b, :, s * chans : (s + 1) * chans] = dot(cells, window_ref[b]).astype(BF16)
    wide = 3 * part
    for a in range(3):
        for b in range(3):
            value = dot(cross[b, :, a * chans : (a + 3) * chans], spread[...])
            begin = (a * 3 + b) * wide
            while begin < (a * 3 + b + 1) * wide:
                h = begin // plan.rows
                end = min((h + 1) * plan.rows, (a * 3 + b + 1) * wide)
                where = plan.spot(h)
                for y in range(2):
                    total[(y,) + where + (slice(begin - h * plan.rows, end - h * plan.rows),)] = value[
                        begin - (a * 3 + b) * wide : end - (a * 3 + b) * wide, y * part : (y + 1) * part
                    ]
                begin = end
    for g in range(3):
        link = plan.orders[g][0]
        begin, end = plan.cuts[g]
        split_into(
            outs[2 * g], outs[2 * g + 1], plan.lead, plan.axis(g, 0), bit_of(spot_ref, link),
            lambda where: total[where + (slice(begin, end),)],
        )


def down_kernel(plan, spot_ref, clip_ref, clip_other, first_ref, second_ref, window_ref, even_ref, odd_ref, weight_ref,
                send_ref, keep_ref, clips, back, picked, total):
    cols, chans, group = plan.cols, plan.chans, plan.group
    core = spot_ref[0] & 1
    rows = clip_ref.shape[0]
    span = window_ref.shape[1]
    part = chans // 2
    wide = 3 * part
    for b in range(3):
        back[b] = window_ref[b].T
    lay_window(clips, core, clip_ref, clip_other, first_ref, second_ref, rows)
    dims = (chans, chans)
    place = lax.broadcasted_iota(jnp.int32, dims, 1)
    wanted = channel_of(place % part, group, place // part)
    order = (lax.broadcasted_iota(jnp.int32, dims, 0) == wanted).astype(F32).astype(BF16)
    mine = (lax.broadcasted_iota(jnp.int32, (1, chans), 1) // part == core).astype(F32).astype(BF16)
    dims = (part, chans)
    wanted = channel_of(lax.broadcasted_iota(jnp.int32, dims, 0), group, core)
    pick = (lax.broadcasted_iota(jnp.int32, dims, 1) == wanted).astype(F32).astype(BF16)
    for b in range(3):
        for a in range(3):
            for c in range(3):
                block = weight_ref[a * 3 + b, c * chans : (c + 1) * chans]
                block = dot(dot(pick, block).astype(BF16), order).astype(BF16)
                picked[b, a * wide + c * part : a * wide + (c + 1) * part] = block
    clip_list = dot(clips[...], order).astype(BF16) * mine
    halves = []
    for parity in range(2):
        halves.append(jnp.concatenate(
            [clip_list[(2 * f + parity) * cols : (2 * f + parity + 1) * cols] for f in range(3 * rows // cols // 2)], axis=0
        ))
    sums = [None] * 3
    for k in range(3):
        begin = (1 + k // 2) * cols
        sums[k] = dot(back[1], halves[k % 2][begin : begin + span])
    for b in range(3):
        cross = []
        for s in range(5):
            cells = (even_ref, odd_ref)[s % 2][s // 2 * cols : s // 2 * cols + span]
            cross.append(dot(back[b], cells).astype(BF16))
        for k in range(3):
            sums[k] = sums[k] + dot(jnp.concatenate(cross[k : k + 3], axis=1), picked[b])
    for k in range(3):
        flipped = sums[k].T
        for parity in range(2):
            for y in range(2):
                total[parity, y, k * part : (k + 1) * part] = flipped[
                    parity * part : (parity + 1) * part, y * part : (y + 1) * part
                ]
    for h in range(math.prod(plan.lead[1:])):
        for y in range(2):
            where = (y,) + plan.spot(h)
            piece = slice(h * plan.down_rows, (h + 1) * plan.down_rows)
            send_ref[where] = total[1 - core, y, piece].astype(BF16)
            keep_ref[where] = total[core, y, piece]


def down_split_kernel(plan, spot_ref, keep_ref, got_ref, send, keep):
    split_into(
        send, keep, plan.lead, plan.axis(0, 0), bit_of(spot_ref, plan.orders[0][0]),
        lambda where: keep_ref[where] + got_ref[where].astype(F32),
    )


def fold_kernel(plan, step, spot_ref, *refs):
    extra = 2 if step == 1 else 0
    ins, outs = refs[: 6 + extra], refs[6 + extra :]
    for g in range(3):
        link = plan.orders[g][step]
        axis = plan.axis(g, step)
        mine = bit_of(spot_ref, link)
        held, got = ins[2 * g], ins[2 * g + 1]

        def read(where):
            value = held[where] + got[where].astype(F32)
            if step == 1 and g == 0:
                value = jnp.concatenate([value, ins[6][where] + ins[7][where].astype(F32)], axis=0)
            return value

        lead = plan.lead[step:]
        if step < 3:
            split_into(outs[2 * g], outs[2 * g + 1], lead, axis, mine, read)
        else:
            third = held.shape[-2]
            for to, where in halved(lead, axis, 1 - mine):
                outs[0][to + (slice(g * third, (g + 1) * third),)] = read(where).astype(BF16)
            for to, where in halved(lead, axis, mine):
                outs[1][to + (slice(g * third, (g + 1) * third),)] = read(where)


def late_kernel(plan, step, spot_ref, held, got, send, keep):
    link = plan.orders[0][step]
    split_into(
        send, keep, plan.lead[step:], plan.axis(0, step), bit_of(spot_ref, link),
        lambda where: held[where] + got[where].astype(F32),
    )


def last_kernel(held, got, out):
    out[...] = held[...] + got[...].astype(F32)


def join_kernel(plan, spot_ref, mine_ref, other_ref, conv_ref, down_ref, turned, down_turned):
    core = spot_ref[0] & 1
    group = plan.group
    rows, down_rows = plan.rows, plan.down_rows
    own, other = mine_ref[...], other_ref[...]
    first, second = jnp.where(core == 0, own, other), jnp.where(core == 0, other, own)

    def merged(begin, end):
        pieces = []
        for at in range(begin, end, group):
            pieces += [first[at : at + group], second[at : at + group]]
        return pieces

    cut = plan.cuts[0][1]
    conv = merged(0, cut) + merged(cut + down_rows, rows + down_rows)
    down = merged(cut, cut + down_rows)
    width = own.shape[1] // 2
    for ref, pieces, space in ((conv_ref, conv, turned), (down_ref, down, down_turned)):
        space[...] = jnp.concatenate(pieces, axis=0).T
        ref[...] = space[pl.ds(pl.multiple_of(core * width, width), width)]


def input_kernel(plan, spot_ref, clip_ref, window_ref, next_low, next_here, next_high, down_ref, weight_ref, out_ref, grads):
    cols, chans = plan.cols, plan.chans
    cells = clip_ref.shape[0]
    span = next_here.shape[0]
    half = span // cols
    core = spot_ref[0] & 1
    for b, later in enumerate((next_low, next_here, next_high)):
        begin = pl.multiple_of(core * span, span)
        own = window_ref[b, pl.ds(begin, span)]
        following = jnp.where(core == 0, window_ref[b, span:], later[...])
        every = jnp.concatenate([own, following], axis=0)
        here = every[: (half + 1) * cols]
        after = every[cols : (half + 2) * cols]
        even = (dot_nt(after, down_ref[0]) + dot_nt(here, down_ref[2])).astype(BF16)
        odd = dot_nt(after, down_ref[1]).astype(BF16)
        for u in range(half + 1):
            grads[b, 2 * u * cols : (2 * u + 1) * cols] = even[u * cols : (u + 1) * cols]
            grads[b, (2 * u + 1) * cols : (2 * u + 2) * cols] = odd[u * cols : (u + 1) * cols]
    acc = [jnp.zeros((cells, chans), F32) for _ in range(3)]
    for a in range(3):
        for b in range(3):
            begin = (2 - a) * cols
            part = grads[b, begin : begin + cells]
            for c in range(3):
                acc[c] = acc[c] + dot_nt(part, weight_ref[a * 3 + b, c * chans : (c + 1) * chans])
    grad_act = acc[1]
    for c in (0, 2):
        grad_act = grad_act + shifted_rows(acc[c], 1 - c, cols)
    value = clip_ref[...].astype(F32)
    sig = 1.0 / (1.0 + jnp.exp(-value))
    own = grads[1, :cells].astype(F32)
    out_ref[...] = (own + grad_act * (sig * (1.0 + value * (1.0 - sig)))).astype(BF16)


def shape(dims, dtype):
    return jax.ShapeDtypeStruct(dims, dtype)


def call(kernel, scalars, args, outs, scratch=(), flops=0, limit=48):
    vmem, smem = pl.BlockSpec(memory_space=pltpu.VMEM), pl.BlockSpec(memory_space=pltpu.SMEM)
    size = sum(a.size * a.dtype.itemsize for a in args)
    return pl.pallas_call(
        kernel,
        out_shape=outs,
        in_specs=[smem] * len(scalars) + [vmem] * len(args),
        out_specs=jax.tree.map(lambda _: vmem, outs),
        scratch_shapes=list(scratch),
        compiler_params=pltpu.CompilerParams(vmem_limit_bytes=limit * MIB),
        cost_estimate=pl.CostEstimate(flops=flops, bytes_accessed=size, transcendentals=0),
    )(*scalars, *args)


class Plan:
    def __init__(self, count, cols, chans):
        nbits = count.bit_length() - 1
        self.cols, self.chans = cols, chans
        self.rows, self.down_rows = 27 * chans // count // 2, 3 * chans // count // 2
        self.group = math.gcd(16, math.gcd(self.rows, self.down_rows))
        self.lead = (2,) * (1 + nbits)
        links = [(0, 1)] + [(1, i) for i in range(nbits)]
        self.place = {link: (0 if link[0] == 0 else nbits - link[1]) for link in links}
        tops, tail = links[:3], links[3:]
        self.orders = [tops[g:] + tops[:g] + tail for g in range(3)]
        total = self.rows + self.down_rows
        self.third = total // 3
        cut = self.third - self.down_rows
        self.cuts = [(0, cut), (cut, cut + self.third), (cut + self.third, self.rows)]

    def spot(self, h):
        nbits = len(self.lead) - 1
        return tuple(h >> (nbits - 1 - i) & 1 for i in range(nbits))

    def axis(self, g, step):
        order = self.orders[g]
        return sum(self.place[link] < self.place[order[step]] for link in order[step + 1 :])


def swapped(value, link):
    axis = ("tm", "height")[link[0]]
    return lax.ppermute(value, axis, [(i, i ^ (1 << link[1])) for i in range(lax.axis_size(axis))])


def body(clip, conv_weight, down_weight, grad_out):
    nframes, nrows, ncols, chans = clip.shape
    half = grad_out.shape[0]
    cells, span = nframes * ncols, half * ncols
    tm_count, count = lax.axis_size("tm"), lax.axis_size("height")
    plan = Plan(count, ncols, chans)
    spot = jnp.stack([lax.axis_index("tm"), lax.axis_index("height")]).astype(jnp.int32)
    mine = grad_out.reshape(span, chans)
    flat = clip.reshape(cells, chans)
    weight = conv_weight.reshape(9, 3 * chans, chans)
    core_link = (0, 0)

    high = lax.ppermute(mine, "height", [(i, i + 1) for i in range(count - 1)])
    low = lax.ppermute(mine, "height", [(i + 1, i) for i in range(count - 1)])
    first = lax.ppermute(flat, "tm", [(i, i + 1) for i in range(1, tm_count - 1, 2)])
    second = lax.ppermute(flat, "tm", [(i, i + 2) for i in range(1, tm_count - 2, 2)])
    clip_other = swapped(flat, core_link)
    mine_other = swapped(mine, core_link)
    high_other, low_other = swapped(high, core_link), swapped(low, core_link)
    back_pairs = [(i + 1, i) for i in range(1, tm_count - 1, 2)]
    next_here, next_low, next_high = (lax.ppermute(v, "tm", back_pairs) for v in (mine, low, high))

    part = chans // 2
    wide = 3 * part
    lead = plan.lead
    outs = [shape((3, 2 * span, chans), BF16), shape((3 * cells // 2, wide), BF16), shape((3 * cells // 2, wide), BF16)]
    for begin, end in plan.cuts:
        outs += [shape(lead[1:] + (end - begin, part), BF16), shape(lead[1:] + (end - begin, part), F32)]
    result = call(
        functools.partial(terms_kernel, plan), [spot],
        [flat, clip_other, first, second, mine, mine_other, high, high_other, low, low_other, down_weight],
        outs,
        [
            pltpu.VMEM((3 * cells, chans), BF16),
            pltpu.VMEM((wide, 3 * cells // 2), BF16),
            pltpu.VMEM((wide, 3 * cells // 2), BF16),
            pltpu.VMEM((3, wide, 5 * chans), BF16),
            pltpu.VMEM((3 * chans, chans), BF16),
            pltpu.VMEM(lead + (plan.rows, part), F32),
        ],
        flops=2 * 9 * wide * 3 * chans * chans,
    )
    window, even, odd = result[:3]
    held = []
    for g in range(3):
        held += [result[4 + 2 * g], swapped(result[3 + 2 * g], plan.orders[g][0])]

    down_dims = lead + (plan.down_rows, part)
    down_send, down_keep = call(
        functools.partial(down_kernel, plan), [spot],
        [flat, clip_other, first, second, window, even, odd, weight],
        [shape(down_dims, BF16), shape(down_dims, F32)],
        [
            pltpu.VMEM((3 * cells, chans), BF16),
            pltpu.VMEM((3, chans, 2 * span), BF16),
            pltpu.VMEM((3, 3 * wide, chans), BF16),
            pltpu.VMEM((2, 2, wide, part), F32),
        ],
        flops=2 * 9 * wide * 3 * chans * chans,
    )
    send, keep = call(
        functools.partial(down_split_kernel, plan), [spot], [down_keep, swapped(down_send, core_link)],
        [shape(down_dims[1:], BF16), shape(down_dims[1:], F32)], limit=8,
    )
    held += [keep, swapped(send, plan.orders[0][0])]
    grad_input = call(
        functools.partial(input_kernel, plan), [spot],
        [flat, window, next_low, next_here, next_high, down_weight, weight],
        shape((cells, chans), BF16),
        [pltpu.VMEM((3, (2 * half + 2) * ncols, chans), BF16)],
        flops=2 * 27 * chans * cells * chans,
    )
    for step in (1, 2):
        dims = lead[step + 1 :] + (plan.third, part)
        result = call(
            functools.partial(fold_kernel, plan, step), [spot], held,
            [shape(dims, BF16), shape(dims, F32)] * 3, limit=16,
        )
        held = []
        for g in range(3):
            held += [result[2 * g + 1], swapped(result[2 * g], plan.orders[g][step])]
    for step in range(3, len(lead)):
        dims = lead[step + 1 :] + (3 * plan.third, part)
        kernel = fold_kernel if step == 3 else late_kernel
        send, keep = call(
            functools.partial(kernel, plan, step), [spot], held, [shape(dims, BF16), shape(dims, F32)], limit=8
        )
        held = [keep, swapped(send, plan.orders[0][step])]
    total = call(last_kernel, [], held, shape((3 * plan.third, part), F32), limit=4)
    grad_conv, grad_down = call(
        functools.partial(join_kernel, plan), [spot], [total, swapped(total, core_link)],
        [shape((part // 2, 2 * plan.rows), F32), shape((part // 2, 2 * plan.down_rows), F32)],
        [pltpu.VMEM((part, 2 * plan.rows), F32), pltpu.VMEM((part, 2 * plan.down_rows), F32)],
        limit=8,
    )
    return (grad_input.reshape(clip.shape), grad_conv.T, grad_down.T)


def solution(mesh):
    placed = (P("tm", "height", None, None), P(), P(), P("tm", "height", None, None))
    return jax.shard_map(
        body,
        mesh=mesh,
        in_specs=placed,
        out_specs=(P("tm", "height", None, None), P("height", "tm"), P("height", "tm")),
        check_vma=False,
    )
```

time: 326 us -> 80 us (0.25)
  the two profiles are of different devices: /device:TPU:0 before, /device:TPU:1 now
where the time goes in v2:
time: 80 us; the launch traced here: 79.6 us
  starting transfers between devices  30.4 us (38%)
  waiting for transfers between devices  23.1 us (29%)
  Pallas kernels  21.2 us (26%)
  local copies, waits for them, and re-layouts  4 us (5%)
  between operations  0.81 us (1%)
    pallas_call x9, Pallas kernels, call(): pl.pallas_call(kernel, out_shape=outs, in_specs=[smem] * len(scalars) + [...  21.2 us
    ppermute x17, starting transfers between devices, swapped(): lax.ppermute(value, axis, [(i, i ^ 1 << link[1]) for i in range(lax.axis_...  16.1 us
    ppermute x17, waiting for transfers between devices, swapped(): lax.ppermute(value, axis, [(i, i ^ 1 << link[1]) for i in range(lax.axis_...  15.3 us
    ppermute x1, starting transfers between devices, body(): lax.ppermute(flat, 'tm', [(i, i + 1) for i in range(1, tm_count - 1, 2)])  4.54 us
    ppermute x3, starting transfers between devices, body(): lax.ppermute(v, 'tm', back_pairs)  4.05 us
    unnamed x16, local copies, waits for them, and re-layouts  4 us
    ppermute x1, waiting for transfers between devices, body(): low = lax.ppermute(mine, 'height', [(i + 1, i) for i in range(count - 1)])  3.69 us
    ppermute x1, starting transfers between devices, body(): high = lax.ppermute(mine, 'height', [(i, i + 1) for i in range(count - 1)])  3.12 us
  transfers between devices with their start and end apart: 24, of which 13 were waited for; matrix products, arithmetic and copies ran while one was open for 0% of the time, Pallas kernels for 15%

profile of v2, /device:TPU:1, one launch (start us, length us, event | category | flops | bytes accessed | tf_op | source)
XLA Modules:
  0.0 79.6 jit_solution(9649203090247451311)
XLA Ops:
  0.6 0.1 collective-permute-start.3
  0.8 0.5 collective-permute-start
  1.2 4.5 %collective-permute-start.1 = (bf16[512,256]{1,0:T(8,128)(2,1)}, bf16[512,256]{1,0:T(8,128)(2,1)S(1)}, u32[]{:S(2)}, u32[]{:S(2)}) collective-permute-start(bf16[512,256]{1,0:T(8,128)(2,1)} %bitcast.13), channel_id=1, source_target_pairs={{8,16},{9,17},{10,18},{11,19},{12,20},{13,21},{14,22},{15,23}} | collective-permute-start | bytes 786440 | tf_op jit(solution)/shard_map/ppermute | solution.py:347
  5.8 1.3 %collective-permute-start.2 = (bf16[512,256]{1,0:T(8,128)(2,1)}, bf16[512,256]{1,0:T(8,128)(2,1)S(1)}, u32[]{:S(2)}, u32[]{:S(2)}) collective-permute-start(bf16[512,256]{1,0:T(8,128)(2,1)} %bitcast.14), channel_id=1, source_target_pairs={{8,24},{9,25},{10,26},{11,27},{12,28},{13,29},{14,30},{15,31}} | collective-permute-start | bytes 786440 | tf_op jit(solution)/shard_map/ppermute | solution.py:348
  7.1 3.1 %collective-permute-start.4 = (bf16[256,256]{1,0:T(8,128)(2,1)}, bf16[256,256]{1,0:T(8,128)(2,1)S(1)}, u32[]{:S(2)}, u32[]{:S(2)}) collective-permute-start(bf16[256,256]{1,0:T(8,128)(2,1)} %bitcast.19), channel_id=1, source_target_pairs={{0,1},{1,2},{2,3},{3,4},{4,5},{5,6},{6,7},{8,9},{9,10},{10,11},{11... | collective-permute-start | bytes 393224 | tf_op jit(solution)/shard_map/ppermute | solution.py:345
  10.2 1.3 %collective-permute-start.6 = (bf16[256,256]{1,0:T(8,128)(2,1)}, bf16[256,256]{1,0:T(8,128)(2,1)S(1)}, u32[]{:S(2)}, u32[]{:S(2)}) collective-permute-start(bf16[256,256]{1,0:T(8,128)(2,1)} %bitcast.20), channel_id=1, source_target_pairs={{1,0},{2,1},{3,2},{4,3},{5,4},{6,5},{7,6},{9,8},{10,9},{11,10},{12... | collective-permute-start | bytes 393224 | tf_op jit(solution)/shard_map/ppermute | solution.py:346
  11.5 0.9 %collective-permute-done.4.high_ref = bf16[256,256]{1,0:T(8,128)(2,1)S(1)} collective-permute-done((bf16[256,256]{1,0:T(8,128)(2,1)}, bf16[256,256]{1,0:T(8,128)(2,1)S(1)}, u32[]{:S(2)}, u32[]{:S(2)}) %collective-permute-start.4) | collective-permute-done | bytes 131104 | tf_op jit(solution)/shard_map/ppermute | solution.py:345
  12.4 3.7 %collective-permute-done.6.low_ref = bf16[256,256]{1,0:T(8,128)(2,1)S(1)} collective-permute-done((bf16[256,256]{1,0:T(8,128)(2,1)}, bf16[256,256]{1,0:T(8,128)(2,1)S(1)}, u32[]{:S(2)}, u32[]{:S(2)}) %collective-permute-start.6) | collective-permute-done | bytes 131104 | tf_op jit(solution)/shard_map/ppermute | solution.py:346
  16.1 0.1 pad_add_fusion.spot_ref
  16.2 1.2 %collective-permute-done.7.low_other = bf16[256,256]{1,0:T(8,128)(2,1)S(1)} collective-permute-done((bf16[256,256]{1,0:T(8,128)(2,1)S(1)}, bf16[256,256]{1,0:T(8,128)(2,1)S(1)}, u32[]{:S(2)}, u32[]{:S(2)}) %collective-permute-start.7) | collective-permute-done | bytes 131104 | tf_op jit(solution)/shard_map/ppermute | solution.py:330
  17.5 0.9 %copy-done.3 = bf16[4,1,128,256]{3,2,1,0:T(8,128)(2,1)S(1)} copy-done((bf16[4,1,128,256]{3,2,1,0:T(8,128)(2,1)S(1)}, bf16[4,1,128,256]{3,2,1,0:T(8,128)(2,1)}, u32[]{:S(2)}) %copy-start.3) | copy-done | bytes 262168
  18.4 1.0 %copy-done.4 = bf16[3,256,256]{2,1,0:T(8,128)(2,1)S(1)} copy-done((bf16[3,256,256]{2,1,0:T(8,128)(2,1)S(1)}, bf16[3,256,256]{2,1,0:T(8,128)(2,1)}, u32[]{:S(2)}) %copy-start.4) | copy-done | bytes 393240
  19.4 0.9 %copy-done.6 = bf16[2,1,128,256]{3,2,1,0:T(8,128)(2,1)S(1)} copy-done((bf16[2,1,128,256]{3,2,1,0:T(8,128)(2,1)S(1)}, bf16[2,1,128,256]{3,2,1,0:T(8,128)(2,1)}, u32[]{:S(2)}) %copy-start.6) | copy-done | bytes 131096
  20.3 5.7 %shard_map.67 = (bf16[3,512,256]{2,1,0:T(8,128)(2,1)}, bf16[768,384]{1,0:T(8,128)(2,1)S(1)}, bf16[768,384]{1,0:T(8,128)(2,1)S(1)}, bf16[2,2,2,112,128]{4,3,2,1,0...) custom-call(s32[2]{0:T(128)S(1)} %pad_add_fusion.spot_ref, ...), custom_call_target="tpu_custom_call" | custom-call | flops 1358954496 | bytes 2228224 | tf_op jit(solution)/shard_map/pallas_call | solution.py:292
  26.0 2.2 %collective-permute-start.12 = (bf16[2,2,2,160,128]{4,3,2,1,0:T(8,128)(2,1)S(1)}, bf16[2,2,2,160,128]{4,3,2,1,0:T(8,128)(2,1)S(1)}, u32[]{:S(2)}, u32[]{:S(2)}) collective-permute-start(bf16[2,2,2,160,128]{4,3,2,1,0:T(8,128)(2,1)S(1)} %get-tuple-element.36), channel_id=1, source_target_pairs={{0,1},{1,0},{2,3},{3,2},{4,5},{5,4},{6,7},{7,6},{8,9},{9,8},{10,11... | collective-permute-start | bytes 983048 | tf_op jit(solution)/shard_map/ppermute | solution.py:330
  28.2 1.3 %collective-permute-start.13 = (bf16[2,2,2,160,128]{4,3,2,1,0:T(8,128)(2,1)S(1)}, bf16[2,2,2,160,128]{4,3,2,1,0:T(8,128)(2,1)S(1)}, u32[]{:S(2)}, u32[]{:S(2)}) collective-permute-start(bf16[2,2,2,160,128]{4,3,2,1,0:T(8,128)(2,1)S(1)} %get-tuple-element.38), channel_id=1, source_target_pairs={{0,2},{1,3},{2,0},{3,1},{4,6},{5,7},{6,4},{7,5},{8,10},{9,11},{10,... | collective-permute-start | bytes 983048 | tf_op jit(solution)/shard_map/ppermute | solution.py:330
  29.5 1.1 %copy-done.1 = bf16[3,512,256]{2,1,0:T(8,128)(2,1)S(1)} copy-done((bf16[3,512,256]{2,1,0:T(8,128)(2,1)S(1)}, bf16[3,512,256]{2,1,0:T(8,128)(2,1)}, u32[]{:S(2)}) %copy-start.1) | copy-done | bytes 786456
  30.6 7.5 %shard_map.69 = (bf16[2,2,2,2,48,128]{5,4,3,2,1,0:T(8,128)(2,1)S(1)}, f32[2,2,2,2,48,128]{5,4,3,2,1,0:T(8,128)S(1)}) custom-call(s32[2]{0:T(128)S(1)} %pad_add_fusion.spot_ref, bf16[512,256]{1,0:T(8,128)(2,1)S(1)} %bitcast.16, bf16[512,256]{1,0:T(8,128)(2,1)S(1)} %collective-permute-done.clip_other, bf16[512,256]{1,0:T(8,128)(2,1)S(1)} %collective-permute-done.1.first_ref, ...), custom_call_target="tpu_custom_call" | custom-call | flops 1358954496 | bytes 6553600 | tf_op jit(solution)/shard_map/pallas_call | solution.py:292
  38.1 0.8 collective-permute-start.14
  38.9 0.4 collective-permute-start.11
  39.3 0.7 collective-permute-done.14.got_ref
  40.0 0.6 shard_map.70
  40.5 0.5 collective-permute-start.15
  41.0 5.0 %collective-permute-done.11.refs_1_ = bf16[2,2,2,112,128]{4,3,2,1,0:T(8,128)(2,1)S(1)} collective-permute-done((bf16[2,2,2,112,128]{4,3,2,1,0:T(8,128)(2,1)S(1)}, bf16[2,2,2,112,128]{4,3,2,1,0:T(8,128)(2,1)S(1)}, u32[]{:S(2)}, u32[]{:S(2)}) %collective-permute-start.11) | collective-permute-done | bytes 229408 | tf_op jit(solution)/shard_map/ppermute | solution.py:330
  46.1 2.1 %collective-permute-done.15.refs_7_ = bf16[2,2,2,48,128]{4,3,2,1,0:T(8,128)(2,1)S(1)} collective-permute-done((bf16[2,2,2,48,128]{4,3,2,1,0:T(8,128)(2,1)S(1)}, bf16[2,2,2,48,128]{4,3,2,1,0:T(8,128)(2,1)S(1)}, u32[]{:S(2)}, u32[]{:S(2)}) %collective-permute-start.15) | collective-permute-done | bytes 98336 | tf_op jit(solution)/shard_map/ppermute | solution.py:330
  48.2 0.7 shard_map.71
  48.9 0.1 collective-permute-start.16
  49.0 0.2 collective-permute-start.17
  49.2 0.4 collective-permute-start.18
  49.6 4.3 %collective-permute-done.16.refs_1_ = bf16[2,2,160,128]{3,2,1,0:T(8,128)(2,1)S(1)} collective-permute-done((bf16[2,2,160,128]{3,2,1,0:T(8,128)(2,1)S(1)}, bf16[2,2,160,128]{3,2,1,0:T(8,128)(2,1)S(1)}, u32[]{:S(2)}, u32[]{:S(2)}) %collective-permute-start.16) | collective-permute-done | bytes 163872 | tf_op jit(solution)/shard_map/ppermute | solution.py:330
  53.9 0.6 shard_map.72
  54.5 1.2 %collective-permute-start.19 = (bf16[2,160,128]{2,1,0:T(8,128)(2,1)S(1)}, bf16[2,160,128]{2,1,0:T(8,128)(2,1)S(1)}, u32[]{:S(2)}, u32[]{:S(2)}) collective-permute-start(bf16[2,160,128]{2,1,0:T(8,128)(2,1)S(1)} %get-tuple-element.52), channel_id=1, source_target_pairs={{0,2},{1,3},{2,0},{3,1},{4,6},{5,7},{6,4},{7,5},{8,10},{9,11},{10,... | collective-permute-start | bytes 245768 | tf_op jit(solution)/shard_map/ppermute | solution.py:330
  55.7 0.3 collective-permute-start.20
  56.1 1.4 %collective-permute-start.21 = (bf16[2,160,128]{2,1,0:T(8,128)(2,1)S(1)}, bf16[2,160,128]{2,1,0:T(8,128)(2,1)S(1)}, u32[]{:S(2)}, u32[]{:S(2)}) collective-permute-start(bf16[2,160,128]{2,1,0:T(8,128)(2,1)S(1)} %get-tuple-element.56), channel_id=1, source_target_pairs={{0,1},{1,0},{2,3},{3,2},{4,5},{5,4},{6,7},{7,6},{8,9},{9,8},{10,11... | collective-permute-start | bytes 245768 | tf_op jit(solution)/shard_map/ppermute | solution.py:330
  57.4 0.4 collective-permute-done.19.refs_1_
  57.9 1.2 %collective-permute-done.20.refs_3_ = bf16[2,160,128]{2,1,0:T(8,128)(2,1)S(1)} collective-permute-done((bf16[2,160,128]{2,1,0:T(8,128)(2,1)S(1)}, bf16[2,160,128]{2,1,0:T(8,128)(2,1)S(1)}, u32[]{:S(2)}, u32[]{:S(2)}) %collective-permute-start.20) | collective-permute-done | bytes 81952 | tf_op jit(solution)/shard_map/ppermute | solution.py:330
  59.0 0.3 collective-permute-done.21.refs_5_
  59.3 0.6 shard_map.73
  59.9 2.1 %collective-permute-start.22 = (bf16[480,128]{1,0:T(8,128)(2,1)S(1)}, bf16[480,128]{1,0:T(8,128)(2,1)S(1)}, u32[]{:S(2)}, u32[]{:S(2)}) collective-permute-start(bf16[480,128]{1,0:T(8,128)(2,1)S(1)} %get-tuple-element.58), channel_id=1, source_target_pairs={{0,4},{1,5},{2,6},{3,7},{4,0},{5,1},{6,2},{7,3},{8,12},{9,13},{10,... | collective-permute-start | bytes 368648 | tf_op jit(solution)/shard_map/ppermute | solution.py:330
  62.1 1.3 %collective-permute-start.9 = (bf16[256,256]{1,0:T(8,128)(2,1)S(1)}, bf16[256,256]{1,0:T(8,128)(2,1)S(1)}, u32[]{:S(2)}, u32[]{:S(2)}) collective-permute-start(bf16[256,256]{1,0:T(8,128)(2,1)S(1)} %bitcast.22), channel_id=1, source_target_pairs={{16,8},{17,9},{18,10},{19,11},{20,12},{21,13},{22,14},{23,15}} | collective-permute-start | bytes 393224 | tf_op jit(solution)/shard_map/ppermute | solution.py:353
  63.4 1.3 %collective-permute-start.8 = (bf16[256,256]{1,0:T(8,128)(2,1)S(1)}, bf16[256,256]{1,0:T(8,128)(2,1)S(1)}, u32[]{:S(2)}, u32[]{:S(2)}) collective-permute-start(bf16[256,256]{1,0:T(8,128)(2,1)S(1)} %collective-permute-done.6.low_ref), channel_id=1, source_target_pairs={{16,8},{17,9},{18,10},{19,11},{20,12},{21,13},{22,14},{23,15}} | collective-permute-start | bytes 393224 | tf_op jit(solution)/shard_map/ppermute | solution.py:353
  64.7 1.5 %collective-permute-start.10 = (bf16[256,256]{1,0:T(8,128)(2,1)S(1)}, bf16[256,256]{1,0:T(8,128)(2,1)S(1)}, u32[]{:S(2)}, u32[]{:S(2)}) collective-permute-start(bf16[256,256]{1,0:T(8,128)(2,1)S(1)} %collective-permute-done.4.high_ref), channel_id=1, source_target_pairs={{16,8},{17,9},{18,10},{19,11},{20,12},{21,13},{22,14},{23,15}} | collective-permute-start | bytes 393224 | tf_op jit(solution)/shard_map/ppermute | solution.py:353
  66.2 4.7 %collective-permute-start.23 = (f32[480,128]{1,0:T(8,128)S(1)}, f32[480,128]{1,0:T(8,128)S(1)}, u32[]{:S(2)}, u32[]{:S(2)}) collective-permute-start(f32[480,128]{1,0:T(8,128)S(1)} %shard_map.74.mine_ref), channel_id=1, source_target_pairs={{0,8},{8,0},{16,24},{24,16},{1,9},{9,1},{17,25},{25,17},{2,10},{10... | collective-permute-start | bytes 737288 | tf_op jit(solution)/shard_map/ppermute | solution.py:330
  70.9 0.3 collective-permute-done.9.next_here
  71.2 1.4 %collective-permute-done.8.next_low = bf16[256,256]{1,0:T(8,128)(2,1)S(1)} collective-permute-done((bf16[256,256]{1,0:T(8,128)(2,1)S(1)}, bf16[256,256]{1,0:T(8,128)(2,1)S(1)}, u32[]{:S(2)}, u32[]{:S(2)}) %collective-permute-start.8) | collective-permute-done | bytes 131104 | tf_op jit(solution)/shard_map/ppermute | solution.py:353
  72.6 1.4 %collective-permute-done.10.next_high = bf16[256,256]{1,0:T(8,128)(2,1)S(1)} collective-permute-done((bf16[256,256]{1,0:T(8,128)(2,1)S(1)}, bf16[256,256]{1,0:T(8,128)(2,1)S(1)}, u32[]{:S(2)}, u32[]{:S(2)}) %collective-permute-start.10) | collective-permute-done | bytes 131104 | tf_op jit(solution)/shard_map/ppermute | solution.py:353
  74.1 4.1 %shard_map.68 = bf16[512,256]{1,0:T(8,128)(2,1)} custom-call(s32[2]{0:T(128)S(1)} %pad_add_fusion.spot_ref, bf16[512,256]{1,0:T(8,128)(2,1)S(1)} %bitcast.17, bf16[3,512,256]{2,1,0:T(8,128)(2,1)S(1)} %copy-done.2, bf16[256,256]{1,0:T(8,128)(2,1)S(1)} %collective-permute-done.8.next_low, bf16[256,256]{1,0:T(8,128)(2,1)S(1)} %collective-permute-done.9.next_here, ...), custom_call_target="tpu_custom_call" | custom-call | flops 1811939328 | bytes 5373952 | tf_op jit(solution)/shard_map/pallas_call | solution.py:292
  78.1 1.5 %shard_map.75 = (f32[64,864]{1,0:T(8,128)}, f32[64,96]{1,0:T(8,128)}) custom-call(s32[2]{0:T(128)S(1)} %pad_add_fusion.spot_ref, f32[480,128]{1,0:T(8,128)S(1)} %shard_map.74.mine_ref, f32[480,128]{1,0:T(8,128)S(1)} %collective-permute-done.23.other_ref), custom_call_target="tpu_custom_call" | custom-call | bytes 491520 | tf_op jit(solution)/shard_map/pallas_call | solution.py:292
  (26 shorter events, 0.1 us)
Async XLA Ops:
  0.6 9.6 %collective-permute-start.3 = (bf16[256,256]{1,0:T(8,128)(2,1)}, bf16[256,256]{1,0:T(8,128)(2,1)S(1)}, u32[]{:S(2)}, u32[]{:S(2)}) collective-permute-start(bf16[256,256]{1,0:T(8,128)(2,1)} %bitcast.18), channel_id=1, source_target_pairs={{0,8},{8,0},{16,24},{24,16},{1,9},{9,1},{17,25},{25,17},{2,10},{10... | collective-permute-start | bytes 393224 | tf_op jit(solution)/shard_map/ppermute | solution.py:330
  0.8 15.5 %collective-permute-start = (bf16[512,256]{1,0:T(8,128)(2,1)}, bf16[512,256]{1,0:T(8,128)(2,1)S(1)}, u32[]{:S(2)}, u32[]{:S(2)}) collective-permute-start(bf16[512,256]{1,0:T(8,128)(2,1)} %bitcast.12), channel_id=1, source_target_pairs={{0,8},{8,0},{16,24},{24,16},{1,9},{9,1},{17,25},{25,17},{2,10},{10... | collective-permute-start | bytes 786440 | tf_op jit(solution)/shard_map/ppermute | solution.py:330
  1.2 15.0 %collective-permute-start.1 = (bf16[512,256]{1,0:T(8,128)(2,1)}, bf16[512,256]{1,0:T(8,128)(2,1)S(1)}, u32[]{:S(2)}, u32[]{:S(2)}) collective-permute-start(bf16[512,256]{1,0:T(8,128)(2,1)} %bitcast.13), channel_id=1, source_target_pairs={{8,16},{9,17},{10,18},{11,19},{12,20},{13,21},{14,22},{15,23}} | collective-permute-start | bytes 786440 | tf_op jit(solution)/shard_map/ppermute | solution.py:347
  5.8 10.5 %collective-permute-start.2 = (bf16[512,256]{1,0:T(8,128)(2,1)}, bf16[512,256]{1,0:T(8,128)(2,1)S(1)}, u32[]{:S(2)}, u32[]{:S(2)}) collective-permute-start(bf16[512,256]{1,0:T(8,128)(2,1)} %bitcast.14), channel_id=1, source_target_pairs={{8,24},{9,25},{10,26},{11,27},{12,28},{13,29},{14,30},{15,31}} | collective-permute-start | bytes 786440 | tf_op jit(solution)/shard_map/ppermute | solution.py:348
  7.1 5.4 %collective-permute-start.4 = (bf16[256,256]{1,0:T(8,128)(2,1)}, bf16[256,256]{1,0:T(8,128)(2,1)S(1)}, u32[]{:S(2)}, u32[]{:S(2)}) collective-permute-start(bf16[256,256]{1,0:T(8,128)(2,1)} %bitcast.19), channel_id=1, source_target_pairs={{0,1},{1,2},{2,3},{3,4},{4,5},{5,6},{6,7},{8,9},{9,10},{10,11},{11... | collective-permute-start | bytes 393224 | tf_op jit(solution)/shard_map/ppermute | solution.py:345
  10.2 5.9 %collective-permute-start.6 = (bf16[256,256]{1,0:T(8,128)(2,1)}, bf16[256,256]{1,0:T(8,128)(2,1)S(1)}, u32[]{:S(2)}, u32[]{:S(2)}) collective-permute-start(bf16[256,256]{1,0:T(8,128)(2,1)} %bitcast.20), channel_id=1, source_target_pairs={{1,0},{2,1},{3,2},{4,3},{5,4},{6,5},{7,6},{9,8},{10,9},{11,10},{12... | collective-permute-start | bytes 393224 | tf_op jit(solution)/shard_map/ppermute | solution.py:346
  12.4 3.8 %collective-permute-start.5 = (bf16[256,256]{1,0:T(8,128)(2,1)S(1)}, bf16[256,256]{1,0:T(8,128)(2,1)S(1)}, u32[]{:S(2)}, u32[]{:S(2)}) collective-permute-start(bf16[256,256]{1,0:T(8,128)(2,1)S(1)} %collective-permute-done.4.high_ref), channel_id=1, source_target_pairs={{0,8},{8,0},{16,24},{24,16},{1,9},{9,1},{17,25},{25,17},{2,10},{10... | collective-permute-start | bytes 393224 | tf_op jit(solution)/shard_map/ppermute | solution.py:330
  16.1 1.3 %collective-permute-start.7 = (bf16[256,256]{1,0:T(8,128)(2,1)S(1)}, bf16[256,256]{1,0:T(8,128)(2,1)S(1)}, u32[]{:S(2)}, u32[]{:S(2)}) collective-permute-start(bf16[256,256]{1,0:T(8,128)(2,1)S(1)} %collective-permute-done.6.low_ref), channel_id=1, source_target_pairs={{0,8},{8,0},{16,24},{24,16},{1,9},{9,1},{17,25},{25,17},{2,10},{10... | collective-permute-start | bytes 393224 | tf_op jit(solution)/shard_map/ppermute | solution.py:330
  17.5 1.0 %copy-start.3 = (bf16[4,1,128,256]{3,2,1,0:T(8,128)(2,1)S(1)}, bf16[4,1,128,256]{3,2,1,0:T(8,128)(2,1)}, u32[]{:S(2)}) copy-start(bf16[4,1,128,256]{3,2,1,0:T(8,128)(2,1)} %param.4) | copy-start | bytes 786436
  18.4 1.0 %copy-start.4 = (bf16[3,256,256]{2,1,0:T(8,128)(2,1)S(1)}, bf16[3,256,256]{2,1,0:T(8,128)(2,1)}, u32[]{:S(2)}) copy-start(bf16[3,256,256]{2,1,0:T(8,128)(2,1)} %down_ref.3) | copy-start | bytes 1179652
  19.4 0.9 %copy-start.6 = (bf16[2,1,128,256]{3,2,1,0:T(8,128)(2,1)S(1)}, bf16[2,1,128,256]{3,2,1,0:T(8,128)(2,1)}, u32[]{:S(2)}) copy-start(bf16[2,1,128,256]{3,2,1,0:T(8,128)(2,1)} %param.7) | copy-start | bytes 393220
  26.0 22.2 %collective-permute-start.12 = (bf16[2,2,2,160,128]{4,3,2,1,0:T(8,128)(2,1)S(1)}, bf16[2,2,2,160,128]{4,3,2,1,0:T(8,128)(2,1)S(1)}, u32[]{:S(2)}, u32[]{:S(2)}) collective-permute-start(bf16[2,2,2,160,128]{4,3,2,1,0:T(8,128)(2,1)S(1)} %get-tuple-element.36), channel_id=1, source_target_pairs={{0,1},{1,0},{2,3},{3,2},{4,5},{5,4},{6,7},{7,6},{8,9},{9,8},{10,11... | collective-permute-start | bytes 983048 | tf_op jit(solution)/shard_map/ppermute | solution.py:330
  28.2 20.0 %collective-permute-start.13 = (bf16[2,2,2,160,128]{4,3,2,1,0:T(8,128)(2,1)S(1)}, bf16[2,2,2,160,128]{4,3,2,1,0:T(8,128)(2,1)S(1)}, u32[]{:S(2)}, u32[]{:S(2)}) collective-permute-start(bf16[2,2,2,160,128]{4,3,2,1,0:T(8,128)(2,1)S(1)} %get-tuple-element.38), channel_id=1, source_target_pairs={{0,2},{1,3},{2,0},{3,1},{4,6},{5,7},{6,4},{7,5},{8,10},{9,11},{10,... | collective-permute-start | bytes 983048 | tf_op jit(solution)/shard_map/ppermute | solution.py:330
  29.5 1.1 %copy-start.1 = (bf16[3,512,256]{2,1,0:T(8,128)(2,1)S(1)}, bf16[3,512,256]{2,1,0:T(8,128)(2,1)}, u32[]{:S(2)}) copy-start(bf16[3,512,256]{2,1,0:T(8,128)(2,1)} %get-tuple-element.32.window_ref) | copy-start | bytes 2359300
  38.1 24.0 %copy-start.7 = (bf16[2,1,128,256]{3,2,1,0:T(8,128)(2,1)S(1)}, bf16[2,1,128,256]{3,2,1,0:T(8,128)(2,1)}, u32[]{:S(2)}) copy-start(bf16[2,1,128,256]{3,2,1,0:T(8,128)(2,1)} %param.7) | copy-start | bytes 393220
  38.1 36.0 %copy-start = (bf16[3,3,3,256,256]{4,3,2,1,0:T(8,128)(2,1)S(1)}, bf16[3,3,3,256,256]{4,3,2,1,0:T(8,128)(2,1)}, u32[]{:S(2)}) copy-start(bf16[3,3,3,256,256]{4,3,2,1,0:T(8,128)(2,1)} %param.5) | copy-start | bytes 10616836
  38.1 36.0 %copy-start.2 = (bf16[3,512,256]{2,1,0:T(8,128)(2,1)S(1)}, bf16[3,512,256]{2,1,0:T(8,128)(2,1)}, u32[]{:S(2)}) copy-start(bf16[3,512,256]{2,1,0:T(8,128)(2,1)} %get-tuple-element.32.window_ref) | copy-start | bytes 2359300
  38.1 36.0 %copy-start.5 = (bf16[3,256,256]{2,1,0:T(8,128)(2,1)S(1)}, bf16[3,256,256]{2,1,0:T(8,128)(2,1)}, u32[]{:S(2)}) copy-start(bf16[3,256,256]{2,1,0:T(8,128)(2,1)} %down_ref.3) | copy-start | bytes 1179652
  38.1 1.9 %collective-permute-start.14 = (bf16[2,2,2,2,48,128]{5,4,3,2,1,0:T(8,128)(2,1)S(1)}, bf16[2,2,2,2,48,128]{5,4,3,2,1,0:T(8,128)(2,1)S(1)}, u32[]{:S(2)}, u32[]{:S(2)}) collective-permute-start(bf16[2,2,2,2,48,128]{5,4,3,2,1,0:T(8,128)(2,1)S(1)} %get-tuple-element.42), channel_id=1, source_target_pairs={{0,8},{8,0},{16,24},{24,16},{1,9},{9,1},{17,25},{25,17},{2,10},{10... | collective-permute-start | bytes 589832 | tf_op jit(solution)/shard_map/ppermute | solution.py:330
  38.9 7.2 %collective-permute-start.11 = (bf16[2,2,2,112,128]{4,3,2,1,0:T(8,128)(2,1)S(1)}, bf16[2,2,2,112,128]{4,3,2,1,0:T(8,128)(2,1)S(1)}, u32[]{:S(2)}, u32[]{:S(2)}) collective-permute-start(bf16[2,2,2,112,128]{4,3,2,1,0:T(8,128)(2,1)S(1)} %get-tuple-element.34), channel_id=1, source_target_pairs={{0,16},{8,24},{16,0},{24,8},{1,17},{9,25},{17,1},{25,9},{2,18},{10... | collective-permute-start | bytes 688136 | tf_op jit(solution)/shard_map/ppermute | solution.py:330
  40.5 7.6 %collective-permute-start.15 = (bf16[2,2,2,48,128]{4,3,2,1,0:T(8,128)(2,1)S(1)}, bf16[2,2,2,48,128]{4,3,2,1,0:T(8,128)(2,1)S(1)}, u32[]{:S(2)}, u32[]{:S(2)}) collective-permute-start(bf16[2,2,2,48,128]{4,3,2,1,0:T(8,128)(2,1)S(1)} %get-tuple-element.44), channel_id=1, source_target_pairs={{0,16},{8,24},{16,0},{24,8},{1,17},{9,25},{17,1},{25,9},{2,18},{10... | collective-permute-start | bytes 294920 | tf_op jit(solution)/shard_map/ppermute | solution.py:330
  48.9 4.9 %collective-permute-start.16 = (bf16[2,2,160,128]{3,2,1,0:T(8,128)(2,1)S(1)}, bf16[2,2,160,128]{3,2,1,0:T(8,128)(2,1)S(1)}, u32[]{:S(2)}, u32[]{:S(2)}) collective-permute-start(bf16[2,2,160,128]{3,2,1,0:T(8,128)(2,1)S(1)} %get-tuple-element.46), channel_id=1, source_target_pairs={{0,1},{1,0},{2,3},{3,2},{4,5},{5,4},{6,7},{7,6},{8,9},{9,8},{10,11... | collective-permute-start | bytes 491528 | tf_op jit(solution)/shard_map/ppermute | solution.py:330
  49.0 4.9 %collective-permute-start.17 = (bf16[2,2,160,128]{3,2,1,0:T(8,128)(2,1)S(1)}, bf16[2,2,160,128]{3,2,1,0:T(8,128)(2,1)S(1)}, u32[]{:S(2)}, u32[]{:S(2)}) collective-permute-start(bf16[2,2,160,128]{3,2,1,0:T(8,128)(2,1)S(1)} %get-tuple-element.48), channel_id=1, source_target_pairs={{0,2},{1,3},{2,0},{3,1},{4,6},{5,7},{6,4},{7,5},{8,10},{9,11},{10,... | collective-permute-start | bytes 491528 | tf_op jit(solution)/shard_map/ppermute | solution.py:330
  49.2 4.6 %collective-permute-start.18 = (bf16[2,2,160,128]{3,2,1,0:T(8,128)(2,1)S(1)}, bf16[2,2,160,128]{3,2,1,0:T(8,128)(2,1)S(1)}, u32[]{:S(2)}, u32[]{:S(2)}) collective-permute-start(bf16[2,2,160,128]{3,2,1,0:T(8,128)(2,1)S(1)} %get-tuple-element.50), channel_id=1, source_target_pairs={{0,16},{8,24},{16,0},{24,8},{1,17},{9,25},{17,1},{25,9},{2,18},{10... | collective-permute-start | bytes 491528 | tf_op jit(solution)/shard_map/ppermute | solution.py:330
  54.5 3.4 %collective-permute-start.19 = (bf16[2,160,128]{2,1,0:T(8,128)(2,1)S(1)}, bf16[2,160,128]{2,1,0:T(8,128)(2,1)S(1)}, u32[]{:S(2)}, u32[]{:S(2)}) collective-permute-start(bf16[2,160,128]{2,1,0:T(8,128)(2,1)S(1)} %get-tuple-element.52), channel_id=1, source_target_pairs={{0,2},{1,3},{2,0},{3,1},{4,6},{5,7},{6,4},{7,5},{8,10},{9,11},{10,... | collective-permute-start | bytes 245768 | tf_op jit(solution)/shard_map/ppermute | solution.py:330
  55.7 3.3 %collective-permute-start.20 = (bf16[2,160,128]{2,1,0:T(8,128)(2,1)S(1)}, bf16[2,160,128]{2,1,0:T(8,128)(2,1)S(1)}, u32[]{:S(2)}, u32[]{:S(2)}) collective-permute-start(bf16[2,160,128]{2,1,0:T(8,128)(2,1)S(1)} %get-tuple-element.54), channel_id=1, source_target_pairs={{0,16},{8,24},{16,0},{24,8},{1,17},{9,25},{17,1},{25,9},{2,18},{10... | collective-permute-start | bytes 245768 | tf_op jit(solution)/shard_map/ppermute | solution.py:330
  56.1 3.3 %collective-permute-start.21 = (bf16[2,160,128]{2,1,0:T(8,128)(2,1)S(1)}, bf16[2,160,128]{2,1,0:T(8,128)(2,1)S(1)}, u32[]{:S(2)}, u32[]{:S(2)}) collective-permute-start(bf16[2,160,128]{2,1,0:T(8,128)(2,1)S(1)} %get-tuple-element.56), channel_id=1, source_target_pairs={{0,1},{1,0},{2,3},{3,2},{4,5},{5,4},{6,7},{7,6},{8,9},{9,8},{10,11... | collective-permute-start | bytes 245768 | tf_op jit(solution)/shard_map/ppermute | solution.py:330
  59.9 6.2 %collective-permute-start.22 = (bf16[480,128]{1,0:T(8,128)(2,1)S(1)}, bf16[480,128]{1,0:T(8,128)(2,1)S(1)}, u32[]{:S(2)}, u32[]{:S(2)}) collective-permute-start(bf16[480,128]{1,0:T(8,128)(2,1)S(1)} %get-tuple-element.58), channel_id=1, source_target_pairs={{0,4},{1,5},{2,6},{3,7},{4,0},{5,1},{6,2},{7,3},{8,12},{9,13},{10,... | collective-permute-start | bytes 368648 | tf_op jit(solution)/shard_map/ppermute | solution.py:330
  62.1 9.1 %collective-permute-start.9 = (bf16[256,256]{1,0:T(8,128)(2,1)S(1)}, bf16[256,256]{1,0:T(8,128)(2,1)S(1)}, u32[]{:S(2)}, u32[]{:S(2)}) collective-permute-start(bf16[256,256]{1,0:T(8,128)(2,1)S(1)} %bitcast.22), channel_id=1, source_target_pairs={{16,8},{17,9},{18,10},{19,11},{20,12},{21,13},{22,14},{23,15}} | collective-permute-start | bytes 393224 | tf_op jit(solution)/shard_map/ppermute | solution.py:353
  63.4 9.3 %collective-permute-start.8 = (bf16[256,256]{1,0:T(8,128)(2,1)S(1)}, bf16[256,256]{1,0:T(8,128)(2,1)S(1)}, u32[]{:S(2)}, u32[]{:S(2)}) collective-permute-start(bf16[256,256]{1,0:T(8,128)(2,1)S(1)} %collective-permute-done.6.low_ref), channel_id=1, source_target_pairs={{16,8},{17,9},{18,10},{19,11},{20,12},{21,13},{22,14},{23,15}} | collective-permute-start | bytes 393224 | tf_op jit(solution)/shard_map/ppermute | solution.py:353
  64.7 9.4 %collective-permute-start.10 = (bf16[256,256]{1,0:T(8,128)(2,1)S(1)}, bf16[256,256]{1,0:T(8,128)(2,1)S(1)}, u32[]{:S(2)}, u32[]{:S(2)}) collective-permute-start(bf16[256,256]{1,0:T(8,128)(2,1)S(1)} %collective-permute-done.4.high_ref), channel_id=1, source_target_pairs={{16,8},{17,9},{18,10},{19,11},{20,12},{21,13},{22,14},{23,15}} | collective-permute-start | bytes 393224 | tf_op jit(solution)/shard_map/ppermute | solution.py:353
  66.2 11.9 %collective-permute-start.23 = (f32[480,128]{1,0:T(8,128)S(1)}, f32[480,128]{1,0:T(8,128)S(1)}, u32[]{:S(2)}, u32[]{:S(2)}) collective-permute-start(f32[480,128]{1,0:T(8,128)S(1)} %shard_map.74.mine_ref), channel_id=1, source_target_pairs={{0,8},{8,0},{16,24},{24,16},{1,9},{9,1},{17,25},{25,17},{2,10},{10... | collective-permute-start | bytes 737288 | tf_op jit(solution)/shard_map/ppermute | solution.py:330

commit v3 on v2

v3 whole, which is shorter than its diff:
```python
import functools
import math

import jax
import jax.numpy as jnp
from jax import lax
from jax.experimental import pallas as pl
from jax.experimental.pallas import tpu as pltpu
from jax.sharding import PartitionSpec as P

F32 = jnp.float32
BF16 = jnp.bfloat16
MIB = 1024 * 1024


def dot(left, right):
    return jnp.dot(left, right, preferred_element_type=F32)


def dot_nt(left, right):
    return lax.dot_general(left, right, (((1,), (1,)), ((), ())), preferred_element_type=F32)


def shifted_rows(value, step, period):
    if step == 0:
        return value
    rows = value.shape[0]
    moved = pltpu.roll(value, (-step) % rows, 0)
    place = lax.broadcasted_iota(jnp.int32, value.shape, 0) % period + step
    return jnp.where(jnp.logical_and(place >= 0, place < period), moved, 0.0)


def channel_of(place, group, core):
    return (place // group * 2 + core) * group + place % group


def one_hot(wanted, chans):
    dims = (wanted.shape[0], chans)
    return (lax.broadcasted_iota(jnp.int32, dims, 1) == wanted).astype(F32).astype(BF16)


def picker(chans, group, core):
    place = lax.broadcasted_iota(jnp.int32, (chans // 2, chans), 0)
    return one_hot(channel_of(place, group, core), chans)


def lay_pair(window, core, own, other, begin=0):
    size = own.shape[0]
    window[pl.ds(pl.multiple_of(begin + size * core, size), size)] = own[...]
    window[pl.ds(pl.multiple_of(begin + size * (1 - core), size), size)] = other[...]


def silu(value):
    return value / (1.0 + jnp.exp(-value))


def halved(lead, axis, index):
    rest = lead[:axis] + lead[axis + 1 :]
    for flat in range(math.prod(rest)):
        spot, left = [], flat
        for extent in reversed(rest):
            spot.insert(0, left % extent)
            left //= extent
        yield tuple(spot), tuple(spot[:axis]) + (index,) + tuple(spot[axis:])


def bit_of(spot_ref, link):
    return lax.shift_right_logical(spot_ref[link[0]], link[1]) & 1


def split_into(send, keep, lead, axis, mine, read):
    for to, where in halved(lead, axis, 1 - mine):
        send[to] = read(where).astype(send.dtype)
    for to, where in halved(lead, axis, mine):
        keep[to] = read(where)


def weights_kernel(plan, spot_ref, weight_ref, down_ref, turned_ref, spread_ref):
    chans, group = plan.chans, plan.group
    part = chans // 2
    core = spot_ref[0] & 1
    place = lax.broadcasted_iota(jnp.int32, (chans, chans), 0)
    order = one_hot(channel_of(place % part, group, place // part), chans)
    pick = picker(chans, group, core)
    for ab in range(9):
        picked = [dot(pick, weight_ref[ab, c * chans : (c + 1) * chans]).astype(BF16) for c in range(3)]
        turned_ref[ab] = dot_nt(order, jnp.concatenate(picked, axis=0)).astype(BF16)
    for k in range(3):
        spread_ref[k * chans : (k + 1) * chans] = down_ref[k].T


def row_terms(plan, even, odd, cells, spread_ref, turned_ref, b):
    chans = plan.chans
    span = cells.shape[0]
    cross = []
    for s in range(5):
        begin = s // 2 * plan.cols
        cross.append(dot((even, odd)[s % 2][:, begin : begin + span], cells).astype(BF16))
    conv, down = [], None
    for a in range(3):
        three = jnp.concatenate(cross[a : a + 3], axis=1)
        conv.append(dot(three, spread_ref[...]))
        term = dot(turned_ref[a * 3 + b], three)
        down = term if down is None else down + term
    return conv, down


def near_kernel(plan, spot_ref, clip_ref, clip_other, first_ref, second_ref, here_ref, here_other, side_ref, side_other,
                spread_ref, turned_ref, even_ref, odd_ref, conv_ref, down_ref, clips, cells, more_cells):
    cols, chans, group = plan.cols, plan.chans, plan.group
    part = chans // 2
    core = spot_ref[0] & 1
    rows = clip_ref.shape[0]
    span = here_ref.shape[0]
    clips[:rows] = first_ref[...] + second_ref[...]
    lay_pair(clips, core, clip_ref, clip_other, rows)
    pick = picker(chans, group, core)
    value = clips[...]
    chosen = dot_nt(pick, silu(value.astype(F32)).astype(BF16))
    steps = lax.broadcasted_iota(jnp.int32, chosen.shape, 1) % cols
    count = 3 * rows // cols // 2
    for c in range(3):
        moved = chosen
        if c != 1:
            moved = pltpu.roll(chosen, (1 - c) % chosen.shape[1], 1)
            moved = jnp.where(steps == (0 if c == 0 else cols - 1), 0.0, moved)
        moved = moved.astype(BF16)
        lanes = slice(c * part, (c + 1) * part)
        for f in range(count):
            to = slice(f * cols, (f + 1) * cols)
            even_ref[lanes, to] = moved[:, 2 * f * cols : (2 * f + 1) * cols]
            odd_ref[lanes, to] = moved[:, (2 * f + 1) * cols : (2 * f + 2) * cols]
    plain = dot_nt(pick, value).astype(BF16)
    halves = [
        jnp.concatenate([plain[:, (2 * f + p) * cols : (2 * f + p + 1) * cols] for f in range(count)], axis=1)
        for p in range(2)
    ]
    lay_pair(cells, core, here_ref, here_other)
    lay_pair(more_cells, core, side_ref, side_other)
    here = cells[...]
    conv, down = row_terms(plan, even_ref, odd_ref, here, spread_ref, turned_ref, 1)
    for a in range(3):
        conv_ref[0, a] = conv[a]
    b = 2 * (spot_ref[1] & 1)
    conv, more = row_terms(plan, even_ref, odd_ref, more_cells[...], spread_ref, turned_ref, b)
    for a in range(3):
        conv_ref[1, a] = conv[a]
    down_ref[...] = down + more
    own = pl.ds(pl.multiple_of(core * part, part), part)
    for k in range(3):
        begin = (1 + k // 2) * cols
        lanes = slice(k * chans, (k + 1) * chans)
        down_ref[own, lanes] = down_ref[own, lanes] + dot(halves[k % 2][:, begin : begin + 2 * span], here)


def far_kernel(plan, spot_ref, here_ref, side_ref, far_ref, far_other, even_ref, odd_ref, conv_ref, down_ref, spread_ref,
               turned_ref, head_ref, *rest):
    outs, (cells, total) = rest[:-2], rest[-2:]
    chans = plan.chans
    part = chans // 2
    core = spot_ref[0] & 1
    odd_row = spot_ref[1] & 1
    lay_pair(cells, core, far_ref, far_other)
    conv, down = row_terms(plan, even_ref, odd_ref, cells[...], spread_ref, turned_ref, 2 - 2 * odd_row)
    down = down_ref[...] + down
    for slot, ref in enumerate((here_ref, side_ref, far_ref)):
        head_ref[slot] = ref[...]
    wide = 3 * part

    def place(a, b, value):
        first = (a * 3 + b) * wide
        begin = first
        while begin < first + wide:
            h = begin // plan.rows
            end = min((h + 1) * plan.rows, first + wide)
            for y in range(2):
                total[(y,) + plan.spot(h) + (slice(begin - h * plan.rows, end - h * plan.rows),)] = value[
                    begin - first : end - first, y * part : (y + 1) * part
                ]
            begin = end

    for a in range(3):
        place(a, 1, conv_ref[0, a])
    for parity in range(2):
        @pl.when(odd_row == parity)
        def _():
            for a in range(3):
                place(a, 2 * parity, conv_ref[1, a])
                place(a, 2 - 2 * parity, conv[a])
    for g in range(3):
        link = plan.orders[g][0]
        begin, end = plan.cuts[g]
        split_into(
            outs[2 * g], outs[2 * g + 1], plan.lead, plan.axis(g, 0), bit_of(spot_ref, link),
            lambda where: total[where + (slice(begin, end),)],
        )
    mine = core == 0
    low, high = down[:part], down[part:]
    for ref, value in ((outs[6], jnp.where(mine, high, low)), (outs[7], jnp.where(mine, low, high))):
        for h in range(math.prod(plan.lead[1:])):
            begin = h * plan.down_rows
            while begin < (h + 1) * plan.down_rows:
                k = begin // part
                end = min((k + 1) * part, (h + 1) * plan.down_rows)
                for y in range(2):
                    ref[(y,) + plan.spot(h) + (slice(begin - h * plan.down_rows, end - h * plan.down_rows),)] = value[
                        begin - k * part : end - k * part, k * chans + y * part : k * chans + (y + 1) * part
                    ].astype(ref.dtype)
                begin = end


def down_split_kernel(plan, spot_ref, keep_ref, got_ref, send, keep):
    split_into(
        send, keep, plan.lead, plan.axis(0, 0), bit_of(spot_ref, plan.orders[0][0]),
        lambda where: keep_ref[where] + got_ref[where].astype(F32),
    )


def fold_kernel(plan, step, spot_ref, *refs):
    extra = 2 if step == 1 else 0
    ins, outs = refs[: 6 + extra], refs[6 + extra :]
    for g in range(3):
        link = plan.orders[g][step]
        axis = plan.axis(g, step)
        mine = bit_of(spot_ref, link)
        held, got = ins[2 * g], ins[2 * g + 1]

        def read(where):
            value = held[where] + got[where].astype(F32)
            if step == 1 and g == 0:
                value = jnp.concatenate([value, ins[6][where] + ins[7][where].astype(F32)], axis=0)
            return value

        lead = plan.lead[step:]
        if step < 3:
            split_into(outs[2 * g], outs[2 * g + 1], lead, axis, mine, read)
        else:
            third = held.shape[-2]
            for to, where in halved(lead, axis, 1 - mine):
                outs[0][to + (slice(g * third, (g + 1) * third),)] = read(where).astype(BF16)
            for to, where in halved(lead, axis, mine):
                outs[1][to + (slice(g * third, (g + 1) * third),)] = read(where)


def late_kernel(plan, step, spot_ref, held, got, send, keep):
    link = plan.orders[0][step]
    split_into(
        send, keep, plan.lead[step:], plan.axis(0, step), bit_of(spot_ref, link),
        lambda where: held[where] + got[where].astype(F32),
    )


def last_kernel(held, got, out):
    out[...] = held[...] + got[...].astype(F32)


def join_kernel(plan, spot_ref, mine_ref, other_ref, conv_ref, down_ref, turned, down_turned):
    core = spot_ref[0] & 1
    group = plan.group
    rows, down_rows = plan.rows, plan.down_rows
    own, other = mine_ref[...], other_ref[...]
    first, second = jnp.where(core == 0, own, other), jnp.where(core == 0, other, own)

    def merged(begin, end):
        pieces = []
        for at in range(begin, end, group):
            pieces += [first[at : at + group], second[at : at + group]]
        return pieces

    cut = plan.cuts[0][1]
    conv = merged(0, cut) + merged(cut + down_rows, rows + down_rows)
    down = merged(cut, cut + down_rows)
    width = own.shape[1] // 2
    for ref, pieces, space in ((conv_ref, conv, turned), (down_ref, down, down_turned)):
        space[...] = jnp.concatenate(pieces, axis=0).T
        ref[...] = space[pl.ds(pl.multiple_of(core * width, width), width)]


def input_kernel(plan, spot_ref, clip_ref, here_ref, here_other, side_ref, side_other, far_ref, far_other, next_ref,
                 down_ref, weight_ref, out_ref, grads):
    cols, chans = plan.cols, plan.chans
    cells = clip_ref.shape[0]
    half = here_ref.shape[0] // cols
    core = spot_ref[0] & 1
    side = 2 * (spot_ref[1] & 1)
    rows = ((here_ref, here_other), (side_ref, side_other), (far_ref, far_other))
    for slot, (own, other) in enumerate(rows):
        following = jnp.where(core == 0, other[...], next_ref[slot])
        every = jnp.concatenate([own[...], following], axis=0)
        here = every[: (half + 1) * cols]
        after = every[cols : (half + 2) * cols]
        even = (dot_nt(after, down_ref[0]) + dot_nt(here, down_ref[2])).astype(BF16)
        odd = dot_nt(after, down_ref[1]).astype(BF16)
        for u in range(half + 1):
            grads[slot, 2 * u * cols : (2 * u + 1) * cols] = even[u * cols : (u + 1) * cols]
            grads[slot, (2 * u + 1) * cols : (2 * u + 2) * cols] = odd[u * cols : (u + 1) * cols]
    acc = [jnp.zeros((cells, chans), F32) for _ in range(3)]
    for a in range(3):
        for slot, b in enumerate((1, side, 2 - side)):
            begin = (2 - a) * cols
            part = grads[slot, begin : begin + cells]
            for c in range(3):
                acc[c] = acc[c] + dot_nt(part, weight_ref[a * 3 + b, c * chans : (c + 1) * chans])
    grad_act = acc[1]
    for c in (0, 2):
        grad_act = grad_act + shifted_rows(acc[c], 1 - c, cols)
    value = clip_ref[...].astype(F32)
    sig = 1.0 / (1.0 + jnp.exp(-value))
    own = grads[0, :cells].astype(F32)
    out_ref[...] = (own + grad_act * (sig * (1.0 + value * (1.0 - sig)))).astype(BF16)


def shape(dims, dtype):
    return jax.ShapeDtypeStruct(dims, dtype)


def call(kernel, scalars, args, outs, scratch=(), us=1, limit=48, after=()):
    vmem, smem = pl.BlockSpec(memory_space=pltpu.VMEM), pl.BlockSpec(memory_space=pltpu.SMEM)
    size = sum(a.size * a.dtype.itemsize for a in args)
    given = len(scalars) + len(args)

    def run(*refs):
        kernel(*refs[:given], *refs[given + len(after) :])

    return pl.pallas_call(
        run,
        out_shape=outs,
        in_specs=[smem] * len(scalars) + [vmem] * len(args) + [pl.BlockSpec(memory_space=pl.ANY)] * len(after),
        out_specs=jax.tree.map(lambda _: vmem, outs),
        scratch_shapes=list(scratch),
        compiler_params=pltpu.CompilerParams(vmem_limit_bytes=limit * MIB),
        cost_estimate=pl.CostEstimate(flops=int(us * 1.15e9), bytes_accessed=size, transcendentals=0),
    )(*scalars, *args, *after)


class Plan:
    def __init__(self, count, cols, chans):
        nbits = count.bit_length() - 1
        self.cols, self.chans = cols, chans
        self.rows, self.down_rows = 27 * chans // count // 2, 3 * chans // count // 2
        self.group = math.gcd(16, math.gcd(self.rows, self.down_rows))
        self.lead = (2,) * (1 + nbits)
        links = [(0, 1)] + [(1, i) for i in range(nbits)]
        self.place = {link: (0 if link[0] == 0 else nbits - link[1]) for link in links}
        tops, tail = links[:3], links[3:]
        self.orders = [tops[g:] + tops[:g] + tail for g in range(3)]
        total = self.rows + self.down_rows
        self.third = total // 3
        cut = self.third - self.down_rows
        self.cuts = [(0, cut), (cut, cut + self.third), (cut + self.third, self.rows)]

    def spot(self, h):
        nbits = len(self.lead) - 1
        return tuple(h >> (nbits - 1 - i) & 1 for i in range(nbits))

    def axis(self, g, step):
        order = self.orders[g]
        return sum(self.place[link] < self.place[order[step]] for link in order[step + 1 :])


def swapped(value, link):
    axis = ("tm", "height")[link[0]]
    return lax.ppermute(value, axis, [(i, i ^ (1 << link[1])) for i in range(lax.axis_size(axis))])


def body(clip, conv_weight, down_weight, grad_out):
    nframes, nrows, ncols, chans = clip.shape
    half = grad_out.shape[0]
    cells, span = nframes * ncols, half * ncols
    tm_count, count = lax.axis_size("tm"), lax.axis_size("height")
    plan = Plan(count, ncols, chans)
    spot = jnp.stack([lax.axis_index("tm"), lax.axis_index("height")]).astype(jnp.int32)
    mine = grad_out.reshape(span, chans)
    flat = clip.reshape(cells, chans)
    weight = conv_weight.reshape(9, 3 * chans, chans)
    core_link = (0, 0)
    part = chans // 2
    wide = 3 * part
    lead = plan.lead
    pair = 2 * span

    side = swapped(mine, (1, 0))
    here_other = swapped(mine, core_link)
    clip_other = swapped(flat, core_link)
    first = lax.ppermute(flat, "tm", [(i, i + 1) for i in range(1, tm_count - 1, 2)])
    second = lax.ppermute(flat, "tm", [(i, i + 2) for i in range(1, tm_count - 2, 2)])
    far = lax.ppermute(
        side, "height", [(i, i + (2 if i % 2 == 0 else -2)) for i in range(count) if 0 <= i + (2 if i % 2 == 0 else -2) < count]
    )
    side_other, far_other = swapped(side, core_link), swapped(far, core_link)

    turned, spread = call(
        functools.partial(weights_kernel, plan), [spot], [weight, down_weight],
        [shape((9, chans, wide), BF16), shape((wide * 2, chans), BF16)], us=2, limit=16,
    )
    even, odd, conv_near, down_near = call(
        functools.partial(near_kernel, plan), [spot],
        [flat, clip_other, first, second, mine, here_other, side, side_other, spread, turned],
        [
            shape((wide, 3 * cells // 2), BF16), shape((wide, 3 * cells // 2), BF16),
            shape((2, 3, wide, chans), F32), shape((chans, 3 * chans), F32),
        ],
        [pltpu.VMEM((3 * cells, chans), BF16), pltpu.VMEM((pair, chans), BF16), pltpu.VMEM((pair, chans), BF16)],
        us=5, limit=24,
    )
    outs = [shape((3, span, chans), BF16)]
    for begin, end in plan.cuts:
        outs += [shape(lead[1:] + (end - begin, part), BF16), shape(lead[1:] + (end - begin, part), F32)]
    down_dims = lead + (plan.down_rows, part)
    outs += [shape(down_dims, BF16), shape(down_dims, F32)]
    result = call(
        functools.partial(far_kernel, plan), [spot],
        [mine, side, far, far_other, even, odd, conv_near, down_near, spread, turned],
        outs,
        [pltpu.VMEM((pair, chans), BF16), pltpu.VMEM(lead + (plan.rows, part), F32)],
        us=4, limit=24,
    )
    head, down_send, down_keep = result[0], result[7], result[8]
    held = []
    for g in range(3):
        held += [result[2 + 2 * g], swapped(result[1 + 2 * g], plan.orders[g][0])]
    send, keep = call(
        functools.partial(down_split_kernel, plan), [spot], [down_keep, swapped(down_send, core_link)],
        [shape(down_dims[1:], BF16), shape(down_dims[1:], F32)], limit=8,
    )
    held += [keep, swapped(send, plan.orders[0][0])]
    following = lax.ppermute(head, "tm", [(i + 1, i) for i in range(1, tm_count - 1, 2)])
    grad_input = call(
        functools.partial(input_kernel, plan), [spot],
        [flat, mine, here_other, side, side_other, far, far_other, following, down_weight, weight],
        shape((cells, chans), BF16),
        [pltpu.VMEM((3, (2 * half + 2) * ncols, chans), BF16)],
        us=4, limit=24,
    )
    for step in (1, 2):
        dims = lead[step + 1 :] + (plan.third, part)
        result = call(
            functools.partial(fold_kernel, plan, step), [spot], held,
            [shape(dims, BF16), shape(dims, F32)] * 3, limit=16,
        )
        held = []
        for g in range(3):
            held += [result[2 * g + 1], swapped(result[2 * g], plan.orders[g][step])]
    for step in range(3, len(lead)):
        dims = lead[step + 1 :] + (3 * plan.third, part)
        kernel = fold_kernel if step == 3 else late_kernel
        send, keep = call(
            functools.partial(kernel, plan, step), [spot], held, [shape(dims, BF16), shape(dims, F32)], limit=8,
            after=[grad_input] if step == 3 else (),
        )
        held = [keep, swapped(send, plan.orders[0][step])]
    total = call(last_kernel, [], held, shape((3 * plan.third, part), F32), limit=4)
    grad_conv, grad_down = call(
        functools.partial(join_kernel, plan), [spot], [total, swapped(total, core_link)],
        [shape((part // 2, 2 * plan.rows), F32), shape((part // 2, 2 * plan.down_rows), F32)],
        [pltpu.VMEM((part, 2 * plan.rows), F32), pltpu.VMEM((part, 2 * plan.down_rows), F32)],
        limit=8,
    )
    return (grad_input.reshape(clip.shape), grad_conv.T, grad_down.T)


def solution(mesh):
    placed = (P("tm", "height", None, None), P(), P(), P("tm", "height", None, None))
    return jax.shard_map(
        body,
        mesh=mesh,
        in_specs=placed,
        out_specs=(P("tm", "height", None, None), P("height", "tm"), P("height", "tm")),
        check_vma=False,
    )
```

time: 80 us -> 65.7 us (0.82)
  the two profiles are of different devices: /device:TPU:1 before, /device:TPU:0 now
where the time goes in v3:
time: 65.7 us; the launch traced here: 65.4 us
  starting transfers between devices  24.6 us (37%)
  Pallas kernels  18.8 us (29%)
  waiting for transfers between devices  17.2 us (26%)
  local copies, waits for them, and re-layouts  3.96 us (6%)
  between operations  0.84 us (1%)
    ppermute x18, starting transfers between devices, swapped(): lax.ppermute(value, axis, [(i, i ^ 1 << link[1]) for i in range(lax.axis_...  18.9 us
    pallas_call x10, Pallas kernels, call(): pl.pallas_call(run, out_shape=outs, in_specs=[smem] * len(scalars) + [vme...  18.8 us
    ppermute x18, waiting for transfers between devices, swapped(): lax.ppermute(value, axis, [(i, i ^ 1 << link[1]) for i in range(lax.axis_...  17.2 us
    unnamed x14, local copies, waits for them, and re-layouts  3.96 us
    ppermute x1, starting transfers between devices, body(): lax.ppermute(side, 'height', [(i, i + (2 if i % 2 == 0 else -2)) for i in...  3.48 us
  transfers between devices with their start and end apart: 22, of which 7 were waited for; matrix products, arithmetic and copies ran while one was open for 0% of the time, Pallas kernels for 21%

profile of v3, /device:TPU:0, one launch (start us, length us, event | category | flops | bytes accessed | tf_op | source)
XLA Modules:
  0.0 65.4 jit_solution(17902135740318525679)
XLA Ops:
  0.6 3.0 %collective-permute-start.1 = (bf16[256,256]{1,0:T(8,128)(2,1)}, bf16[256,256]{1,0:T(8,128)(2,1)S(1)}, u32[]{:S(2)}, u32[]{:S(2)}) collective-permute-start(bf16[256,256]{1,0:T(8,128)(2,1)} %bitcast.17), channel_id=1, source_target_pairs={{0,1},{1,0},{2,3},{3,2},{4,5},{5,4},{6,7},{7,6},{8,9},{9,8},{10,11... | collective-permute-start | bytes 393224 | tf_op jit(solution)/shard_map/ppermute | solution.py:363
  3.6 0.0 collective-permute-start
  3.6 0.7 %collective-permute-start.7 = (bf16[512,256]{1,0:T(8,128)(2,1)}, bf16[512,256]{1,0:T(8,128)(2,1)S(1)}, u32[]{:S(2)}, u32[]{:S(2)}) collective-permute-start(bf16[512,256]{1,0:T(8,128)(2,1)} %bitcast.12), channel_id=1, source_target_pairs={{8,24},{9,25},{10,26},{11,27},{12,28},{13,29},{14,30},{15,31}} | collective-permute-start | bytes 786440 | tf_op jit(solution)/shard_map/ppermute | solution.py:386
  4.3 0.7 %collective-permute-start.6 = (bf16[512,256]{1,0:T(8,128)(2,1)}, bf16[512,256]{1,0:T(8,128)(2,1)S(1)}, u32[]{:S(2)}, u32[]{:S(2)}) collective-permute-start(bf16[512,256]{1,0:T(8,128)(2,1)} %bitcast.13), channel_id=1, source_target_pairs={{8,16},{9,17},{10,18},{11,19},{12,20},{13,21},{14,22},{15,23}} | collective-permute-start | bytes 786440 | tf_op jit(solution)/shard_map/ppermute | solution.py:385
  5.0 3.7 %collective-permute-start.5 = (bf16[512,256]{1,0:T(8,128)(2,1)}, bf16[512,256]{1,0:T(8,128)(2,1)S(1)}, u32[]{:S(2)}, u32[]{:S(2)}) collective-permute-start(bf16[512,256]{1,0:T(8,128)(2,1)} %bitcast.14), channel_id=1, source_target_pairs={{0,8},{8,0},{16,24},{24,16},{1,9},{9,1},{17,25},{25,17},{2,10},{10... | collective-permute-start | bytes 786440 | tf_op jit(solution)/shard_map/ppermute | solution.py:363
  8.7 0.1 pad_add_fusion.refs_0_
  8.8 0.0 collective-permute-done.1.refs_7_.refs_2_.refs_4_
  8.8 3.5 %collective-permute-start.3 = (bf16[256,256]{1,0:T(8,128)(2,1)S(1)}, bf16[256,256]{1,0:T(8,128)(2,1)S(1)}, u32[]{:S(2)}, u32[]{:S(2)}) collective-permute-start(bf16[256,256]{1,0:T(8,128)(2,1)S(1)} %collective-permute-done.1.refs_7_.refs_2_.refs_4_), channel_id=1, source_target_pairs={{0,2},{2,4},{3,1},{4,6},{5,3},{7,5},{8,10},{10,12},{11,9},{12,14},... | collective-permute-start | bytes 393224 | tf_op jit(solution)/shard_map/ppermute | solution.py:387
  12.2 0.0 collective-permute-done.refs_6_.refs_3_
  12.3 0.1 collective-permute-start.2
  12.3 0.0 copy-start
  12.3 2.0 %copy-done = bf16[3,3,3,256,256]{4,3,2,1,0:T(8,128)(2,1)S(1)} copy-done((bf16[3,3,3,256,256]{4,3,2,1,0:T(8,128)(2,1)S(1)}, bf16[3,3,3,256,256]{4,3,2,1,0:T(8,128)(2,1)}, u32[]{:S(2)}) %copy-start) | copy-done | bytes 3538968
  14.3 1.0 %copy-done.2 = bf16[3,256,256]{2,1,0:T(8,128)(2,1)S(1)} copy-done((bf16[3,256,256]{2,1,0:T(8,128)(2,1)S(1)}, bf16[3,256,256]{2,1,0:T(8,128)(2,1)}, u32[]{:S(2)}) %copy-start.2) | copy-done | bytes 393240
  15.3 3.1 %shard_map.67 = (bf16[9,256,384]{2,1,0:T(8,128)(2,1)S(1)}, bf16[768,256]{1,0:T(8,128)(2,1)S(1)}) custom-call(s32[2]{0:T(128)S(1)} %pad_add_fusion.refs_0_, bf16[9,768,256]{2,1,0:T(8,128)(2,1)S(1)} %bitcast.10, bf16[3,256,256]{2,1,0:T(8,128)(2,1)S(1)} %copy-done.2), custom_call_target="tpu_custom_call" | custom-call | flops 2300000000 | bytes 3932160 | tf_op jit(solution)/shard_map/pallas_call | solution.py:325
  18.4 0.6 collective-permute-start.4
  19.0 4.8 %shard_map.68 = (bf16[384,768]{1,0:T(8,128)(2,1)S(1)}, bf16[384,768]{1,0:T(8,128)(2,1)S(1)}, f32[2,3,384,256]{3,2,1,0:T(8,128)S(1)}, f32[256,768]{1,0:T(8,128)S(1)}) custom-call(s32[2]{0:T(128)S(1)} %pad_add_fusion.refs_0_, bf16[512,256]{1,0:T(8,128)(2,1)S(1)} %bitcast.15, bf16[512,256]{1,0:T(8,128)(2,1)S(1)} %collective-permute-done.5.refs_2_, ...), custom_call_target="tpu_custom_call" | custom-call | flops 5750000128 | bytes 3735552 | tf_op jit(solution)/shard_map/pallas_call | solution.py:325
  23.9 2.8 %shard_map.69 = (bf16[3,256,256]{2,1,0:T(8,128)(2,1)S(1)}, bf16[2,2,2,112,128]{4,3,2,1,0:T(8,128)(2,1)S(1)}, f32[2,2,2,112,128]{4,3,2,1,0:T(8,128)S(1)}, bf16[2,...) custom-call(s32[2]{0:T(128)S(1)} %pad_add_fusion.refs_0_, ...), custom_call_target="tpu_custom_call" | custom-call | flops 4600000000 | bytes 7012352 | tf_op jit(solution)/shard_map/pallas_call | solution.py:325
  26.7 0.1 collective-permute-start.12
  26.8 0.0 collective-permute-start.10
  26.9 1.6 %collective-permute-start.11 = (bf16[2,2,2,160,128]{4,3,2,1,0:T(8,128)(2,1)S(1)}, bf16[2,2,2,160,128]{4,3,2,1,0:T(8,128)(2,1)S(1)}, u32[]{:S(2)}, u32[]{:S(2)}) collective-permute-start(bf16[2,2,2,160,128]{4,3,2,1,0:T(8,128)(2,1)S(1)} %get-tuple-element.48), channel_id=1, source_target_pairs={{0,2},{1,3},{2,0},{3,1},{4,6},{5,7},{6,4},{7,5},{8,10},{9,11},{10,... | collective-permute-start | bytes 983048 | tf_op jit(solution)/shard_map/ppermute | solution.py:363
  28.5 0.6 collective-permute-start.9
  29.1 0.6 shard_map.71
  29.7 1.5 %collective-permute-start.13 = (bf16[2,2,2,48,128]{4,3,2,1,0:T(8,128)(2,1)S(1)}, bf16[2,2,2,48,128]{4,3,2,1,0:T(8,128)(2,1)S(1)}, u32[]{:S(2)}, u32[]{:S(2)}) collective-permute-start(bf16[2,2,2,48,128]{4,3,2,1,0:T(8,128)(2,1)S(1)} %get-tuple-element.52), channel_id=1, source_target_pairs={{0,16},{8,24},{16,0},{24,8},{1,17},{9,25},{17,1},{25,9},{2,18},{10... | collective-permute-start | bytes 294920 | tf_op jit(solution)/shard_map/ppermute | solution.py:363
  31.2 0.9 %collective-permute-start.8 = (bf16[3,256,256]{2,1,0:T(8,128)(2,1)S(1)}, bf16[3,256,256]{2,1,0:T(8,128)(2,1)S(1)}, u32[]{:S(2)}, u32[]{:S(2)}) collective-permute-start(bf16[3,256,256]{2,1,0:T(8,128)(2,1)S(1)} %get-tuple-element.42), channel_id=1, source_target_pairs={{16,8},{17,9},{18,10},{19,11},{20,12},{21,13},{22,14},{23,15}} | collective-permute-start | bytes 1179656 | tf_op jit(solution)/shard_map/ppermute | solution.py:427
  32.0 4.9 %collective-permute-done.9.refs_2_ = bf16[2,2,2,112,128]{4,3,2,1,0:T(8,128)(2,1)S(1)} collective-permute-done((bf16[2,2,2,112,128]{4,3,2,1,0:T(8,128)(2,1)S(1)}, bf16[2,2,2,112,128]{4,3,2,1,0:T(8,128)(2,1)S(1)}, u32[]{:S(2)}, u32[]{:S(2)}) %collective-permute-start.9) | collective-permute-done | bytes 229408 | tf_op jit(solution)/shard_map/ppermute | solution.py:363
  37.0 1.2 %collective-permute-done.13.refs_8_ = bf16[2,2,2,48,128]{4,3,2,1,0:T(8,128)(2,1)S(1)} collective-permute-done((bf16[2,2,2,48,128]{4,3,2,1,0:T(8,128)(2,1)S(1)}, bf16[2,2,2,48,128]{4,3,2,1,0:T(8,128)(2,1)S(1)}, u32[]{:S(2)}, u32[]{:S(2)}) %collective-permute-start.13) | collective-permute-done | bytes 98336 | tf_op jit(solution)/shard_map/ppermute | solution.py:363
  38.2 0.7 %shard_map.72 = (bf16[2,2,160,128]{3,2,1,0:T(8,128)(2,1)S(1)}, f32[2,2,160,128]{3,2,1,0:T(8,128)S(1)}, bf16[2,2,160,128]{3,2,1,0:T(8,128)(2,1)S(1)}, f32[2,2,160...) custom-call(s32[2]{0:T(128)S(1)} %pad_add_fusion.refs_0_, ...), custom_call_target="tpu_custom_call" | custom-call | flops 1150000000 | bytes 2949120 | tf_op jit(solution)/shard_map/pallas_call | solution.py:325
  38.9 0.0 copy-start.1
  38.9 0.0 copy-start.3
  39.0 1.8 %collective-permute-start.14 = (bf16[2,2,160,128]{3,2,1,0:T(8,128)(2,1)S(1)}, bf16[2,2,160,128]{3,2,1,0:T(8,128)(2,1)S(1)}, u32[]{:S(2)}, u32[]{:S(2)}) collective-permute-start(bf16[2,2,160,128]{3,2,1,0:T(8,128)(2,1)S(1)} %get-tuple-element.54), channel_id=1, source_target_pairs={{0,1},{1,0},{2,3},{3,2},{4,5},{5,4},{6,7},{7,6},{8,9},{9,8},{10,11... | collective-permute-start | bytes 491528 | tf_op jit(solution)/shard_map/ppermute | solution.py:363
  40.8 0.5 collective-permute-start.15
  41.2 0.3 collective-permute-start.16
  41.6 2.8 %collective-permute-done.14.refs_2_ = bf16[2,2,160,128]{3,2,1,0:T(8,128)(2,1)S(1)} collective-permute-done((bf16[2,2,160,128]{3,2,1,0:T(8,128)(2,1)S(1)}, bf16[2,2,160,128]{3,2,1,0:T(8,128)(2,1)S(1)}, u32[]{:S(2)}, u32[]{:S(2)}) %collective-permute-start.14) | collective-permute-done | bytes 163872 | tf_op jit(solution)/shard_map/ppermute | solution.py:363
  44.4 1.7 %collective-permute-done.15.refs_4_ = bf16[2,2,160,128]{3,2,1,0:T(8,128)(2,1)S(1)} collective-permute-done((bf16[2,2,160,128]{3,2,1,0:T(8,128)(2,1)S(1)}, bf16[2,2,160,128]{3,2,1,0:T(8,128)(2,1)S(1)}, u32[]{:S(2)}, u32[]{:S(2)}) %collective-permute-start.15) | collective-permute-done | bytes 163872 | tf_op jit(solution)/shard_map/ppermute | solution.py:363
  46.1 0.5 collective-permute-done.16.refs_6_
  46.5 0.6 shard_map.73
  47.2 1.6 %collective-permute-start.17 = (bf16[2,160,128]{2,1,0:T(8,128)(2,1)S(1)}, bf16[2,160,128]{2,1,0:T(8,128)(2,1)S(1)}, u32[]{:S(2)}, u32[]{:S(2)}) collective-permute-start(bf16[2,160,128]{2,1,0:T(8,128)(2,1)S(1)} %get-tuple-element.60), channel_id=1, source_target_pairs={{0,2},{1,3},{2,0},{3,1},{4,6},{5,7},{6,4},{7,5},{8,10},{9,11},{10,... | collective-permute-start | bytes 245768 | tf_op jit(solution)/shard_map/ppermute | solution.py:363
  48.8 0.3 collective-permute-start.18
  49.2 0.4 collective-permute-start.19
  49.5 4.1 %shard_map.70.refs_7_ = bf16[512,256]{1,0:T(8,128)(2,1)} custom-call(s32[2]{0:T(128)S(1)} %pad_add_fusion.refs_0_, bf16[512,256]{1,0:T(8,128)(2,1)S(1)} %bitcast.16, bf16[256,256]{1,0:T(8,128)(2,1)S(1)} %bitcast.21, bf16[256,256]{1,0:T(8,128)(2,1)S(1)} %collective-permute-done.refs_6_.refs_3_, ...), custom_call_target="tpu_custom_call" | custom-call | flops 4600000000 | bytes 5373952 | tf_op jit(solution)/shard_map/pallas_call | solution.py:325
  53.6 0.0 copy-start.6
  53.6 0.9 %copy-done.6 = bf16[512,256]{1,0:T(8,128)(2,1)S(1)} copy-done((bf16[512,256]{1,0:T(8,128)(2,1)S(1)}, bf16[512,256]{1,0:T(8,128)(2,1)}, u32[]{:S(2)}) %copy-start.6) | copy-done | bytes 262168
  54.6 0.6 shard_map.74
  55.2 2.7 %collective-permute-start.20 = (bf16[480,128]{1,0:T(8,128)(2,1)S(1)}, bf16[480,128]{1,0:T(8,128)(2,1)S(1)}, u32[]{:S(2)}, u32[]{:S(2)}) collective-permute-start(bf16[480,128]{1,0:T(8,128)(2,1)S(1)} %get-tuple-element.66), channel_id=1, source_target_pairs={{0,4},{1,5},{2,6},{3,7},{4,0},{5,1},{6,2},{7,3},{8,12},{9,13},{10,... | collective-permute-start | bytes 368648 | tf_op jit(solution)/shard_map/ppermute | solution.py:363
  57.8 4.5 %collective-permute-done.20.refs_1_ = bf16[480,128]{1,0:T(8,128)(2,1)S(1)} collective-permute-done((bf16[480,128]{1,0:T(8,128)(2,1)S(1)}, bf16[480,128]{1,0:T(8,128)(2,1)S(1)}, u32[]{:S(2)}, u32[]{:S(2)}) %collective-permute-start.20) | collective-permute-done | bytes 122912 | tf_op jit(solution)/shard_map/ppermute | solution.py:363
  62.4 0.1 collective-permute-start.21
  62.4 1.5 %collective-permute-done.21.refs_2_ = f32[480,128]{1,0:T(8,128)S(1)} collective-permute-done((f32[480,128]{1,0:T(8,128)S(1)}, f32[480,128]{1,0:T(8,128)S(1)}, u32[]{:S(2)}, u32[]{:S(2)}) %collective-permute-start.21) | collective-permute-done | bytes 245792 | tf_op jit(solution)/shard_map/ppermute | solution.py:363
  63.9 1.5 %shard_map.76 = (f32[64,864]{1,0:T(8,128)}, f32[64,96]{1,0:T(8,128)}) custom-call(s32[2]{0:T(128)S(1)} %pad_add_fusion.refs_0_, f32[480,128]{1,0:T(8,128)S(1)} %shard_map.75.refs_1_, f32[480,128]{1,0:T(8,128)S(1)} %collective-permute-done.21.refs_2_), custom_call_target="tpu_custom_call" | custom-call | flops 1150000000 | bytes 491520 | tf_op jit(solution)/shard_map/pallas_call | solution.py:325
  (21 shorter events, 0.1 us)
Async XLA Ops:
  0.6 8.1 %collective-permute-start.1 = (bf16[256,256]{1,0:T(8,128)(2,1)}, bf16[256,256]{1,0:T(8,128)(2,1)S(1)}, u32[]{:S(2)}, u32[]{:S(2)}) collective-permute-start(bf16[256,256]{1,0:T(8,128)(2,1)} %bitcast.17), channel_id=1, source_target_pairs={{0,1},{1,0},{2,3},{3,2},{4,5},{5,4},{6,7},{7,6},{8,9},{9,8},{10,11... | collective-permute-start | bytes 393224 | tf_op jit(solution)/shard_map/ppermute | solution.py:363
  3.6 8.6 %collective-permute-start = (bf16[256,256]{1,0:T(8,128)(2,1)}, bf16[256,256]{1,0:T(8,128)(2,1)S(1)}, u32[]{:S(2)}, u32[]{:S(2)}) collective-permute-start(bf16[256,256]{1,0:T(8,128)(2,1)} %bitcast.18), channel_id=1, source_target_pairs={{0,8},{8,0},{16,24},{24,16},{1,9},{9,1},{17,25},{25,17},{2,10},{10... | collective-permute-start | bytes 393224 | tf_op jit(solution)/shard_map/ppermute | solution.py:363
  3.6 15.3 %collective-permute-start.7 = (bf16[512,256]{1,0:T(8,128)(2,1)}, bf16[512,256]{1,0:T(8,128)(2,1)S(1)}, u32[]{:S(2)}, u32[]{:S(2)}) collective-permute-start(bf16[512,256]{1,0:T(8,128)(2,1)} %bitcast.12), channel_id=1, source_target_pairs={{8,24},{9,25},{10,26},{11,27},{12,28},{13,29},{14,30},{15,31}} | collective-permute-start | bytes 786440 | tf_op jit(solution)/shard_map/ppermute | solution.py:386
  4.3 14.7 %collective-permute-start.6 = (bf16[512,256]{1,0:T(8,128)(2,1)}, bf16[512,256]{1,0:T(8,128)(2,1)S(1)}, u32[]{:S(2)}, u32[]{:S(2)}) collective-permute-start(bf16[512,256]{1,0:T(8,128)(2,1)} %bitcast.13), channel_id=1, source_target_pairs={{8,16},{9,17},{10,18},{11,19},{12,20},{13,21},{14,22},{15,23}} | collective-permute-start | bytes 786440 | tf_op jit(solution)/shard_map/ppermute | solution.py:385
  5.0 14.0 %collective-permute-start.5 = (bf16[512,256]{1,0:T(8,128)(2,1)}, bf16[512,256]{1,0:T(8,128)(2,1)S(1)}, u32[]{:S(2)}, u32[]{:S(2)}) collective-permute-start(bf16[512,256]{1,0:T(8,128)(2,1)} %bitcast.14), channel_id=1, source_target_pairs={{0,8},{8,0},{16,24},{24,16},{1,9},{9,1},{17,25},{25,17},{2,10},{10... | collective-permute-start | bytes 786440 | tf_op jit(solution)/shard_map/ppermute | solution.py:363
  8.8 9.6 %collective-permute-start.3 = (bf16[256,256]{1,0:T(8,128)(2,1)S(1)}, bf16[256,256]{1,0:T(8,128)(2,1)S(1)}, u32[]{:S(2)}, u32[]{:S(2)}) collective-permute-start(bf16[256,256]{1,0:T(8,128)(2,1)S(1)} %collective-permute-done.1.refs_7_.refs_2_.refs_4_), channel_id=1, source_target_pairs={{0,2},{2,4},{3,1},{4,6},{5,3},{7,5},{8,10},{10,12},{11,9},{12,14},... | collective-permute-start | bytes 393224 | tf_op jit(solution)/shard_map/ppermute | solution.py:387
  12.3 6.7 %collective-permute-start.2 = (bf16[256,256]{1,0:T(8,128)(2,1)S(1)}, bf16[256,256]{1,0:T(8,128)(2,1)S(1)}, u32[]{:S(2)}, u32[]{:S(2)}) collective-permute-start(bf16[256,256]{1,0:T(8,128)(2,1)S(1)} %collective-permute-done.1.refs_7_.refs_2_.refs_4_), channel_id=1, source_target_pairs={{0,8},{8,0},{16,24},{24,16},{1,9},{9,1},{17,25},{25,17},{2,10},{10... | collective-permute-start | bytes 393224 | tf_op jit(solution)/shard_map/ppermute | solution.py:363
  12.3 2.0 %copy-start = (bf16[3,3,3,256,256]{4,3,2,1,0:T(8,128)(2,1)S(1)}, bf16[3,3,3,256,256]{4,3,2,1,0:T(8,128)(2,1)}, u32[]{:S(2)}) copy-start(bf16[3,3,3,256,256]{4,3,2,1,0:T(8,128)(2,1)} %param.5) | copy-start | bytes 10616836
  14.3 1.0 %copy-start.2 = (bf16[3,256,256]{2,1,0:T(8,128)(2,1)S(1)}, bf16[3,256,256]{2,1,0:T(8,128)(2,1)}, u32[]{:S(2)}) copy-start(bf16[3,256,256]{2,1,0:T(8,128)(2,1)} %refs_9_.1) | copy-start | bytes 1179652
  15.3 3.7 %copy-start.4 = (bf16[4,1,128,256]{3,2,1,0:T(8,128)(2,1)S(1)}, bf16[4,1,128,256]{3,2,1,0:T(8,128)(2,1)}, u32[]{:S(2)}) copy-start(bf16[4,1,128,256]{3,2,1,0:T(8,128)(2,1)} %param.4) | copy-start | bytes 786436
  15.3 3.7 %copy-start.5 = (bf16[2,1,128,256]{3,2,1,0:T(8,128)(2,1)S(1)}, bf16[2,1,128,256]{3,2,1,0:T(8,128)(2,1)}, u32[]{:S(2)}) copy-start(bf16[2,1,128,256]{3,2,1,0:T(8,128)(2,1)} %param.7) | copy-start | bytes 393220
  18.4 5.4 %collective-permute-start.4 = (bf16[256,256]{1,0:T(8,128)(2,1)S(1)}, bf16[256,256]{1,0:T(8,128)(2,1)S(1)}, u32[]{:S(2)}, u32[]{:S(2)}) collective-permute-start(bf16[256,256]{1,0:T(8,128)(2,1)S(1)} %collective-permute-done.3.refs_3_.refs_6_), channel_id=1, source_target_pairs={{0,8},{8,0},{16,24},{24,16},{1,9},{9,1},{17,25},{25,17},{2,10},{10... | collective-permute-start | bytes 393224 | tf_op jit(solution)/shard_map/ppermute | solution.py:363
  26.7 2.4 %collective-permute-start.12 = (bf16[2,2,2,2,48,128]{5,4,3,2,1,0:T(8,128)(2,1)S(1)}, bf16[2,2,2,2,48,128]{5,4,3,2,1,0:T(8,128)(2,1)S(1)}, u32[]{:S(2)}, u32[]{:S(2)}) collective-permute-start(bf16[2,2,2,2,48,128]{5,4,3,2,1,0:T(8,128)(2,1)S(1)} %get-tuple-element.50), channel_id=1, source_target_pairs={{0,8},{8,0},{16,24},{24,16},{1,9},{9,1},{17,25},{25,17},{2,10},{10... | collective-permute-start | bytes 589832 | tf_op jit(solution)/shard_map/ppermute | solution.py:363
  26.8 11.4 %collective-permute-start.10 = (bf16[2,2,2,160,128]{4,3,2,1,0:T(8,128)(2,1)S(1)}, bf16[2,2,2,160,128]{4,3,2,1,0:T(8,128)(2,1)S(1)}, u32[]{:S(2)}, u32[]{:S(2)}) collective-permute-start(bf16[2,2,2,160,128]{4,3,2,1,0:T(8,128)(2,1)S(1)} %get-tuple-element.46), channel_id=1, source_target_pairs={{0,1},{1,0},{2,3},{3,2},{4,5},{5,4},{6,7},{7,6},{8,9},{9,8},{10,11... | collective-permute-start | bytes 983048 | tf_op jit(solution)/shard_map/ppermute | solution.py:363
  26.9 11.3 %collective-permute-start.11 = (bf16[2,2,2,160,128]{4,3,2,1,0:T(8,128)(2,1)S(1)}, bf16[2,2,2,160,128]{4,3,2,1,0:T(8,128)(2,1)S(1)}, u32[]{:S(2)}, u32[]{:S(2)}) collective-permute-start(bf16[2,2,2,160,128]{4,3,2,1,0:T(8,128)(2,1)S(1)} %get-tuple-element.48), channel_id=1, source_target_pairs={{0,2},{1,3},{2,0},{3,1},{4,6},{5,7},{6,4},{7,5},{8,10},{9,11},{10,... | collective-permute-start | bytes 983048 | tf_op jit(solution)/shard_map/ppermute | solution.py:363
  28.5 8.5 %collective-permute-start.9 = (bf16[2,2,2,112,128]{4,3,2,1,0:T(8,128)(2,1)S(1)}, bf16[2,2,2,112,128]{4,3,2,1,0:T(8,128)(2,1)S(1)}, u32[]{:S(2)}, u32[]{:S(2)}) collective-permute-start(bf16[2,2,2,112,128]{4,3,2,1,0:T(8,128)(2,1)S(1)} %get-tuple-element.44), channel_id=1, source_target_pairs={{0,16},{8,24},{16,0},{24,8},{1,17},{9,25},{17,1},{25,9},{2,18},{10... | collective-permute-start | bytes 688136 | tf_op jit(solution)/shard_map/ppermute | solution.py:363
  29.7 8.5 %collective-permute-start.13 = (bf16[2,2,2,48,128]{4,3,2,1,0:T(8,128)(2,1)S(1)}, bf16[2,2,2,48,128]{4,3,2,1,0:T(8,128)(2,1)S(1)}, u32[]{:S(2)}, u32[]{:S(2)}) collective-permute-start(bf16[2,2,2,48,128]{4,3,2,1,0:T(8,128)(2,1)S(1)} %get-tuple-element.52), channel_id=1, source_target_pairs={{0,16},{8,24},{16,0},{24,8},{1,17},{9,25},{17,1},{25,9},{2,18},{10... | collective-permute-start | bytes 294920 | tf_op jit(solution)/shard_map/ppermute | solution.py:363
  31.2 18.4 %collective-permute-start.8 = (bf16[3,256,256]{2,1,0:T(8,128)(2,1)S(1)}, bf16[3,256,256]{2,1,0:T(8,128)(2,1)S(1)}, u32[]{:S(2)}, u32[]{:S(2)}) collective-permute-start(bf16[3,256,256]{2,1,0:T(8,128)(2,1)S(1)} %get-tuple-element.42), channel_id=1, source_target_pairs={{16,8},{17,9},{18,10},{19,11},{20,12},{21,13},{22,14},{23,15}} | collective-permute-start | bytes 1179656 | tf_op jit(solution)/shard_map/ppermute | solution.py:427
  38.9 10.6 %copy-start.1 = (bf16[3,3,3,256,256]{4,3,2,1,0:T(8,128)(2,1)S(1)}, bf16[3,3,3,256,256]{4,3,2,1,0:T(8,128)(2,1)}, u32[]{:S(2)}) copy-start(bf16[3,3,3,256,256]{4,3,2,1,0:T(8,128)(2,1)} %param.5) | copy-start | bytes 10616836
  38.9 10.6 %copy-start.3 = (bf16[3,256,256]{2,1,0:T(8,128)(2,1)S(1)}, bf16[3,256,256]{2,1,0:T(8,128)(2,1)}, u32[]{:S(2)}) copy-start(bf16[3,256,256]{2,1,0:T(8,128)(2,1)} %refs_9_.1) | copy-start | bytes 1179652
  39.0 5.4 %collective-permute-start.14 = (bf16[2,2,160,128]{3,2,1,0:T(8,128)(2,1)S(1)}, bf16[2,2,160,128]{3,2,1,0:T(8,128)(2,1)S(1)}, u32[]{:S(2)}, u32[]{:S(2)}) collective-permute-start(bf16[2,2,160,128]{3,2,1,0:T(8,128)(2,1)S(1)} %get-tuple-element.54), channel_id=1, source_target_pairs={{0,1},{1,0},{2,3},{3,2},{4,5},{5,4},{6,7},{7,6},{8,9},{9,8},{10,11... | collective-permute-start | bytes 491528 | tf_op jit(solution)/shard_map/ppermute | solution.py:363
  40.8 5.3 %collective-permute-start.15 = (bf16[2,2,160,128]{3,2,1,0:T(8,128)(2,1)S(1)}, bf16[2,2,160,128]{3,2,1,0:T(8,128)(2,1)S(1)}, u32[]{:S(2)}, u32[]{:S(2)}) collective-permute-start(bf16[2,2,160,128]{3,2,1,0:T(8,128)(2,1)S(1)} %get-tuple-element.56), channel_id=1, source_target_pairs={{0,2},{1,3},{2,0},{3,1},{4,6},{5,7},{6,4},{7,5},{8,10},{9,11},{10,... | collective-permute-start | bytes 491528 | tf_op jit(solution)/shard_map/ppermute | solution.py:363
  41.2 5.3 %collective-permute-start.16 = (bf16[2,2,160,128]{3,2,1,0:T(8,128)(2,1)S(1)}, bf16[2,2,160,128]{3,2,1,0:T(8,128)(2,1)S(1)}, u32[]{:S(2)}, u32[]{:S(2)}) collective-permute-start(bf16[2,2,160,128]{3,2,1,0:T(8,128)(2,1)S(1)} %get-tuple-element.58), channel_id=1, source_target_pairs={{0,16},{8,24},{16,0},{24,8},{1,17},{9,25},{17,1},{25,9},{2,18},{10... | collective-permute-start | bytes 491528 | tf_op jit(solution)/shard_map/ppermute | solution.py:363
  47.2 6.4 %collective-permute-start.17 = (bf16[2,160,128]{2,1,0:T(8,128)(2,1)S(1)}, bf16[2,160,128]{2,1,0:T(8,128)(2,1)S(1)}, u32[]{:S(2)}, u32[]{:S(2)}) collective-permute-start(bf16[2,160,128]{2,1,0:T(8,128)(2,1)S(1)} %get-tuple-element.60), channel_id=1, source_target_pairs={{0,2},{1,3},{2,0},{3,1},{4,6},{5,7},{6,4},{7,5},{8,10},{9,11},{10,... | collective-permute-start | bytes 245768 | tf_op jit(solution)/shard_map/ppermute | solution.py:363
  48.8 4.8 %collective-permute-start.18 = (bf16[2,160,128]{2,1,0:T(8,128)(2,1)S(1)}, bf16[2,160,128]{2,1,0:T(8,128)(2,1)S(1)}, u32[]{:S(2)}, u32[]{:S(2)}) collective-permute-start(bf16[2,160,128]{2,1,0:T(8,128)(2,1)S(1)} %get-tuple-element.62), channel_id=1, source_target_pairs={{0,16},{8,24},{16,0},{24,8},{1,17},{9,25},{17,1},{25,9},{2,18},{10... | collective-permute-start | bytes 245768 | tf_op jit(solution)/shard_map/ppermute | solution.py:363
  49.2 4.4 %collective-permute-start.19 = (bf16[2,160,128]{2,1,0:T(8,128)(2,1)S(1)}, bf16[2,160,128]{2,1,0:T(8,128)(2,1)S(1)}, u32[]{:S(2)}, u32[]{:S(2)}) collective-permute-start(bf16[2,160,128]{2,1,0:T(8,128)(2,1)S(1)} %get-tuple-element.64), channel_id=1, source_target_pairs={{0,1},{1,0},{2,3},{3,2},{4,5},{5,4},{6,7},{7,6},{8,9},{9,8},{10,11... | collective-permute-start | bytes 245768 | tf_op jit(solution)/shard_map/ppermute | solution.py:363
  53.6 1.0 %copy-start.6 = (bf16[512,256]{1,0:T(8,128)(2,1)S(1)}, bf16[512,256]{1,0:T(8,128)(2,1)}, u32[]{:S(2)}) copy-start(bf16[512,256]{1,0:T(8,128)(2,1)} %shard_map.70.refs_7_) | copy-start | bytes 786436
  55.2 7.2 %collective-permute-start.20 = (bf16[480,128]{1,0:T(8,128)(2,1)S(1)}, bf16[480,128]{1,0:T(8,128)(2,1)S(1)}, u32[]{:S(2)}, u32[]{:S(2)}) collective-permute-start(bf16[480,128]{1,0:T(8,128)(2,1)S(1)} %get-tuple-element.66), channel_id=1, source_target_pairs={{0,4},{1,5},{2,6},{3,7},{4,0},{5,1},{6,2},{7,3},{8,12},{9,13},{10,... | collective-permute-start | bytes 368648 | tf_op jit(solution)/shard_map/ppermute | solution.py:363
  62.4 1.6 %collective-permute-start.21 = (f32[480,128]{1,0:T(8,128)S(1)}, f32[480,128]{1,0:T(8,128)S(1)}, u32[]{:S(2)}, u32[]{:S(2)}) collective-permute-start(f32[480,128]{1,0:T(8,128)S(1)} %shard_map.75.refs_1_), channel_id=1, source_target_pairs={{0,8},{8,0},{16,24},{24,16},{1,9},{9,1},{17,25},{25,17},{2,10},{10... | collective-permute-start | bytes 737288 | tf_op jit(solution)/shard_map/ppermute | solution.py:363

commit v4 on v3

--- a/solution.py
+++ b/solution.py
@@ -75,48 +75,51 @@
         keep[to] = read(where)
 
 
-def weights_kernel(plan, spot_ref, weight_ref, down_ref, turned_ref, spread_ref):
-    chans, group = plan.chans, plan.group
-    part = chans // 2
+def weights_kernel(plan, spot_ref, weight_ref, down_ref, turned_ref, spread_ref, weights, downs, sems):
+    chans = plan.chans
     core = spot_ref[0] & 1
-    place = lax.broadcasted_iota(jnp.int32, (chans, chans), 0)
-    order = one_hot(channel_of(place % part, group, place // part), chans)
-    pick = picker(chans, group, core)
+    copies = [pltpu.make_async_copy(down_ref, downs, sems.at[9])]
+    copies += [pltpu.make_async_copy(weight_ref.at[ab, :, :, core], weights.at[ab], sems.at[ab]) for ab in range(9)]
+    for copy in copies:
+        copy.start()
+    same = one_hot(lax.broadcasted_iota(jnp.int32, (chans, chans), 0), chans)
+    copies[0].wait()
+    for k in range(3):
+        spread_ref[k * chans : (k + 1) * chans] = dot_nt(same, downs[k]).astype(BF16)
     for ab in range(9):
-        picked = [dot(pick, weight_ref[ab, c * chans : (c + 1) * chans]).astype(BF16) for c in range(3)]
-        turned_ref[ab] = dot_nt(order, jnp.concatenate(picked, axis=0)).astype(BF16)
-    for k in range(3):
-        spread_ref[k * chans : (k + 1) * chans] = down_ref[k].T
-
-
-def row_terms(plan, even, odd, cells, spread_ref, turned_ref, b):
+        copies[ab + 1].wait()
+        turned_ref[ab] = dot_nt(same, weights[ab].reshape(3 * chans // 2, chans)).astype(BF16)
+
+
+def row_terms(plan, even, odd, cells, spread_ref, turned_ref, b, conv_ref):
     chans = plan.chans
     span = cells.shape[0]
     cross = []
     for s in range(5):
         begin = s // 2 * plan.cols
         cross.append(dot((even, odd)[s % 2][:, begin : begin + span], cells).astype(BF16))
-    conv, down = [], None
+    down = None
     for a in range(3):
         three = jnp.concatenate(cross[a : a + 3], axis=1)
-        conv.append(dot(three, spread_ref[...]))
+        conv_ref[a] = dot(three, spread_ref[...])
         term = dot(turned_ref[a * 3 + b], three)
         down = term if down is None else down + term
-    return conv, down
-
-
-def near_kernel(plan, spot_ref, clip_ref, clip_other, first_ref, second_ref, here_ref, here_other, side_ref, side_other,
-                spread_ref, turned_ref, even_ref, odd_ref, conv_ref, down_ref, clips, cells, more_cells):
-    cols, chans, group = plan.cols, plan.chans, plan.group
+    return down
+
+
+def own_kernel(plan, spot_ref, clip_ref, clip_other, first_ref, second_ref, here_ref, here_other, spread_ref, turned_ref,
+               even_ref, odd_ref, conv_ref, sum_ref, plus_ref, clips, cells):
+    cols, chans = plan.cols, plan.chans
     part = chans // 2
     core = spot_ref[0] & 1
     rows = clip_ref.shape[0]
-    span = here_ref.shape[0]
     clips[:rows] = first_ref[...] + second_ref[...]
     lay_pair(clips, core, clip_ref, clip_other, rows)
-    pick = picker(chans, group, core)
-    value = clips[...]
-    chosen = dot_nt(pick, silu(value.astype(F32)).astype(BF16))
+    lay_pair(cells, core, here_ref, here_other)
+    pick = picker(chans, plan.group, core)
+    plain = dot_nt(pick, clips[...])
+    chosen = silu(plain).astype(BF16).astype(F32)
+    plain = plain.astype(BF16)
     steps = lax.broadcasted_iota(jnp.int32, chosen.shape, 1) % cols
     count = 3 * rows // cols // 2
     for c in range(3):
@@ -130,39 +133,31 @@
             to = slice(f * cols, (f + 1) * cols)
             even_ref[lanes, to] = moved[:, 2 * f * cols : (2 * f + 1) * cols]
             odd_ref[lanes, to] = moved[:, (2 * f + 1) * cols : (2 * f + 2) * cols]
-    plain = dot_nt(pick, value).astype(BF16)
-    halves = [
-        jnp.concatenate([plain[:, (2 * f + p) * cols : (2 * f + p + 1) * cols] for f in range(count)], axis=1)
-        for p in range(2)
-    ]
-    lay_pair(cells, core, here_ref, here_other)
-    lay_pair(more_cells, core, side_ref, side_other)
     here = cells[...]
-    conv, down = row_terms(plan, even_ref, odd_ref, here, spread_ref, turned_ref, 1)
-    for a in range(3):
-        conv_ref[0, a] = conv[a]
+    for k in range(3):
+        halves = [plain[:, (2 * f + k % 2) * cols : (2 * f + k % 2 + 1) * cols] for f in range(count)]
+        begin = 1 + k // 2
+        frames = jnp.concatenate(halves[begin : begin + here.shape[0] // cols], axis=1)
+        plus_ref[:, k * chans : (k + 1) * chans] = dot(frames, here)
+    sum_ref[...] = row_terms(plan, even_ref, odd_ref, here, spread_ref, turned_ref, 1, conv_ref)
+
+
+def side_kernel(plan, spot_ref, side_ref, side_other, even_ref, odd_ref, spread_ref, turned_ref, conv_ref, sum_ref, cells):
+    lay_pair(cells, spot_ref[0] & 1, side_ref, side_other)
     b = 2 * (spot_ref[1] & 1)
-    conv, more = row_terms(plan, even_ref, odd_ref, more_cells[...], spread_ref, turned_ref, b)
-    for a in range(3):
-        conv_ref[1, a] = conv[a]
-    down_ref[...] = down + more
-    own = pl.ds(pl.multiple_of(core * part, part), part)
-    for k in range(3):
-        begin = (1 + k // 2) * cols
-        lanes = slice(k * chans, (k + 1) * chans)
-        down_ref[own, lanes] = down_ref[own, lanes] + dot(halves[k % 2][:, begin : begin + 2 * span], here)
-
-
-def far_kernel(plan, spot_ref, here_ref, side_ref, far_ref, far_other, even_ref, odd_ref, conv_ref, down_ref, spread_ref,
-               turned_ref, head_ref, *rest):
-    outs, (cells, total) = rest[:-2], rest[-2:]
+    sum_ref[...] = row_terms(plan, even_ref, odd_ref, cells[...], spread_ref, turned_ref, b, conv_ref)
+
+
+def far_kernel(plan, spot_ref, here_ref, side_ref, far_ref, far_other, even_ref, odd_ref, own_conv, own_sum, plus_ref, side_conv,
+               side_sum, spread_ref, turned_ref, head_ref, *rest):
+    outs, (cells, conv, total) = rest[:-3], rest[-3:]
     chans = plan.chans
     part = chans // 2
     core = spot_ref[0] & 1
     odd_row = spot_ref[1] & 1
     lay_pair(cells, core, far_ref, far_other)
-    conv, down = row_terms(plan, even_ref, odd_ref, cells[...], spread_ref, turned_ref, 2 - 2 * odd_row)
-    down = down_ref[...] + down
+    down = row_terms(plan, even_ref, odd_ref, cells[...], spread_ref, turned_ref, 2 - 2 * odd_row, conv)
+    down = own_sum[...] + side_sum[...] + down
     for slot, ref in enumerate((here_ref, side_ref, far_ref)):
         head_ref[slot] = ref[...]
     wide = 3 * part
@@ -180,12 +175,12 @@
             begin = end
 
     for a in range(3):
-        place(a, 1, conv_ref[0, a])
+        place(a, 1, own_conv[a])
     for parity in range(2):
         @pl.when(odd_row == parity)
         def _():
             for a in range(3):
-                place(a, 2 * parity, conv_ref[1, a])
+                place(a, 2 * parity, side_conv[a])
                 place(a, 2 - 2 * parity, conv[a])
     for g in range(3):
         link = plan.orders[g][0]
@@ -195,8 +190,11 @@
             lambda where: total[where + (slice(begin, end),)],
         )
     mine = core == 0
-    low, high = down[:part], down[part:]
-    for ref, value in ((outs[6], jnp.where(mine, high, low)), (outs[7], jnp.where(mine, low, high))):
+    pairs = range(0, chans, 2 * plan.group)
+    low = jnp.concatenate([down[i : i + plan.group] for i in pairs], axis=0)
+    high = jnp.concatenate([down[i + plan.group : i + 2 * plan.group] for i in pairs], axis=0)
+    keep = jnp.where(mine, low, high) + plus_ref[...]
+    for ref, value in ((outs[6], jnp.where(mine, high, low)), (outs[7], keep)):
         for h in range(math.prod(plan.lead[1:])):
             begin = h * plan.down_rows
             while begin < (h + 1) * plan.down_rows:
@@ -209,16 +207,10 @@
                 begin = end
 
 
-def down_split_kernel(plan, spot_ref, keep_ref, got_ref, send, keep):
-    split_into(
-        send, keep, plan.lead, plan.axis(0, 0), bit_of(spot_ref, plan.orders[0][0]),
-        lambda where: keep_ref[where] + got_ref[where].astype(F32),
-    )
-
-
 def fold_kernel(plan, step, spot_ref, *refs):
     extra = 2 if step == 1 else 0
     ins, outs = refs[: 6 + extra], refs[6 + extra :]
+    at = 0
     for g in range(3):
         link = plan.orders[g][step]
         axis = plan.axis(g, step)
@@ -227,7 +219,7 @@
 
         def read(where):
             value = held[where] + got[where].astype(F32)
-            if step == 1 and g == 0:
+            if extra and g == 0:
                 value = jnp.concatenate([value, ins[6][where] + ins[7][where].astype(F32)], axis=0)
             return value
 
@@ -235,30 +227,27 @@
         if step < 3:
             split_into(outs[2 * g], outs[2 * g + 1], lead, axis, mine, read)
         else:
-            third = held.shape[-2]
+            rows = slice(at, at + held.shape[-2])
+            at = at + held.shape[-2]
             for to, where in halved(lead, axis, 1 - mine):
-                outs[0][to + (slice(g * third, (g + 1) * third),)] = read(where).astype(BF16)
+                outs[0][to + (rows,)] = read(where).astype(BF16)
             for to, where in halved(lead, axis, mine):
-                outs[1][to + (slice(g * third, (g + 1) * third),)] = read(where)
-
-
-def late_kernel(plan, step, spot_ref, held, got, send, keep):
-    link = plan.orders[0][step]
+                outs[1][to + (rows,)] = read(where)
+
+
+def single_kernel(plan, step, spot_ref, held, got, send, keep):
     split_into(
-        send, keep, plan.lead[step:], plan.axis(0, step), bit_of(spot_ref, link),
+        send, keep, plan.lead[step:], plan.axis(0, step), bit_of(spot_ref, plan.orders[0][step]),
         lambda where: held[where] + got[where].astype(F32),
     )
 
 
-def last_kernel(held, got, out):
-    out[...] = held[...] + got[...].astype(F32)
-
-
-def join_kernel(plan, spot_ref, mine_ref, other_ref, conv_ref, down_ref, turned, down_turned):
+def join_kernel(plan, spot_ref, held, got, held_other, got_other, conv_ref, down_ref, turned, down_turned):
     core = spot_ref[0] & 1
     group = plan.group
     rows, down_rows = plan.rows, plan.down_rows
-    own, other = mine_ref[...], other_ref[...]
+    own = held[...] + got[...].astype(F32)
+    other = held_other[...] + got_other[...].astype(F32)
     first, second = jnp.where(core == 0, own, other), jnp.where(core == 0, other, own)
 
     def merged(begin, end):
@@ -277,10 +266,11 @@
 
 
 def input_kernel(plan, spot_ref, clip_ref, here_ref, here_other, side_ref, side_other, far_ref, far_other, next_ref,
-                 down_ref, weight_ref, out_ref, grads):
+                 down_ref, weight_ref, out_ref, done_ref, grads):
     cols, chans = plan.cols, plan.chans
     cells = clip_ref.shape[0]
-    half = here_ref.shape[0] // cols
+    span = side_ref.shape[0]
+    half = span // cols
     core = spot_ref[0] & 1
     side = 2 * (spot_ref[1] & 1)
     rows = ((here_ref, here_other), (side_ref, side_other), (far_ref, far_other))
@@ -308,14 +298,18 @@
     sig = 1.0 / (1.0 + jnp.exp(-value))
     own = grads[0, :cells].astype(F32)
     out_ref[...] = (own + grad_act * (sig * (1.0 + value * (1.0 - sig)))).astype(BF16)
+    done_ref[...] = jnp.zeros_like(done_ref)
 
 
 def shape(dims, dtype):
     return jax.ShapeDtypeStruct(dims, dtype)
 
 
-def call(kernel, scalars, args, outs, scratch=(), us=1, limit=48, after=()):
+def call(kernel, scalars, args, outs, scratch=(), us=1, limit=48, after=(), left=0):
     vmem, smem = pl.BlockSpec(memory_space=pltpu.VMEM), pl.BlockSpec(memory_space=pltpu.SMEM)
+    hbm = pl.BlockSpec(memory_space=pltpu.HBM)
+    args = [pltpu.with_memory_space_constraint(a, pltpu.HBM) for a in args[:left]] + list(args[left:])
+    after = list(after)
     size = sum(a.size * a.dtype.itemsize for a in args)
     given = len(scalars) + len(args)
 
@@ -325,7 +319,7 @@
     return pl.pallas_call(
         run,
         out_shape=outs,
-        in_specs=[smem] * len(scalars) + [vmem] * len(args) + [pl.BlockSpec(memory_space=pl.ANY)] * len(after),
+        in_specs=[smem] * len(scalars) + [hbm] * left + [vmem] * (len(args) - left) + [vmem] * len(after),
         out_specs=jax.tree.map(lambda _: vmem, outs),
         scratch_shapes=list(scratch),
         compiler_params=pltpu.CompilerParams(vmem_limit_bytes=limit * MIB),
@@ -344,10 +338,9 @@
         self.place = {link: (0 if link[0] == 0 else nbits - link[1]) for link in links}
         tops, tail = links[:3], links[3:]
         self.orders = [tops[g:] + tops[:g] + tail for g in range(3)]
-        total = self.rows + self.down_rows
-        self.third = total // 3
-        cut = self.third - self.down_rows
-        self.cuts = [(0, cut), (cut, cut + self.third), (cut + self.third, self.rows)]
+        third = (self.rows + self.down_rows) // 3
+        cut = third - self.down_rows
+        self.cuts = [(0, cut), (cut, cut + third), (cut + third, self.rows)]
 
     def spot(self, h):
         nbits = len(self.lead) - 1
@@ -384,24 +377,30 @@
     clip_other = swapped(flat, core_link)
     first = lax.ppermute(flat, "tm", [(i, i + 1) for i in range(1, tm_count - 1, 2)])
     second = lax.ppermute(flat, "tm", [(i, i + 2) for i in range(1, tm_count - 2, 2)])
+    listed = (9, 3, part // plan.group, 2, plan.group, chans)
+    turned, spread = call(
+        functools.partial(weights_kernel, plan), [spot], [weight.reshape(listed), down_weight],
+        [shape((9, chans, wide), BF16), shape((2 * wide, chans), BF16)],
+        [pltpu.VMEM(listed[:3] + listed[4:], BF16), pltpu.VMEM(down_weight.shape, BF16), pltpu.SemaphoreType.DMA((10,))],
+        us=3, limit=16, left=2,
+    )
     far = lax.ppermute(
         side, "height", [(i, i + (2 if i % 2 == 0 else -2)) for i in range(count) if 0 <= i + (2 if i % 2 == 0 else -2) < count]
     )
-    side_other, far_other = swapped(side, core_link), swapped(far, core_link)
-
-    turned, spread = call(
-        functools.partial(weights_kernel, plan), [spot], [weight, down_weight],
-        [shape((9, chans, wide), BF16), shape((wide * 2, chans), BF16)], us=2, limit=16,
-    )
-    even, odd, conv_near, down_near = call(
-        functools.partial(near_kernel, plan), [spot],
-        [flat, clip_other, first, second, mine, here_other, side, side_other, spread, turned],
-        [
-            shape((wide, 3 * cells // 2), BF16), shape((wide, 3 * cells // 2), BF16),
-            shape((2, 3, wide, chans), F32), shape((chans, 3 * chans), F32),
-        ],
-        [pltpu.VMEM((3 * cells, chans), BF16), pltpu.VMEM((pair, chans), BF16), pltpu.VMEM((pair, chans), BF16)],
-        us=5, limit=24,
+    side_other = swapped(side, core_link)
+
+    terms = [shape((3, wide, chans), F32), shape((chans, 3 * chans), F32)]
+    even, odd, own_conv, own_sum, plus = call(
+        functools.partial(own_kernel, plan), [spot],
+        [flat, clip_other, first, second, mine, here_other, spread, turned],
+        [shape((wide, 3 * cells // 2), BF16), shape((wide, 3 * cells // 2), BF16), *terms, shape((part, 3 * chans), F32)],
+        [pltpu.VMEM((3 * cells, chans), BF16), pltpu.VMEM((pair, chans), BF16)], us=3, limit=20,
+    )
+    far, plus = lax.optimization_barrier((far, plus))
+    far_other = swapped(far, core_link)
+    side_conv, side_sum = call(
+        functools.partial(side_kernel, plan), [spot], [side, side_other, even, odd, spread, turned], terms,
+        [pltpu.VMEM((pair, chans), BF16)], us=2, limit=20,
     )
     outs = [shape((3, span, chans), BF16)]
     for begin, end in plan.cuts:
@@ -410,48 +409,47 @@
     outs += [shape(down_dims, BF16), shape(down_dims, F32)]
     result = call(
         functools.partial(far_kernel, plan), [spot],
-        [mine, side, far, far_other, even, odd, conv_near, down_near, spread, turned],
-        outs,
-        [pltpu.VMEM((pair, chans), BF16), pltpu.VMEM(lead + (plan.rows, part), F32)],
-        us=4, limit=24,
-    )
-    head, down_send, down_keep = result[0], result[7], result[8]
+        [mine, side, far, far_other, even, odd, own_conv, own_sum, plus, side_conv, side_sum, spread, turned], outs,
+        [pltpu.VMEM((pair, chans), BF16), pltpu.VMEM((3, wide, chans), F32), pltpu.VMEM(lead + (plan.rows, part), F32)],
+        us=3, limit=20,
+    )
+    head = result[0]
     held = []
     for g in range(3):
         held += [result[2 + 2 * g], swapped(result[1 + 2 * g], plan.orders[g][0])]
     send, keep = call(
-        functools.partial(down_split_kernel, plan), [spot], [down_keep, swapped(down_send, core_link)],
+        functools.partial(single_kernel, plan, 0), [spot], [result[8], swapped(result[7], core_link)],
         [shape(down_dims[1:], BF16), shape(down_dims[1:], F32)], limit=8,
     )
-    held += [keep, swapped(send, plan.orders[0][0])]
+    down_held = [keep, swapped(send, plan.orders[0][0])]
     following = lax.ppermute(head, "tm", [(i + 1, i) for i in range(1, tm_count - 1, 2)])
-    grad_input = call(
+    grad_input, done = call(
         functools.partial(input_kernel, plan), [spot],
         [flat, mine, here_other, side, side_other, far, far_other, following, down_weight, weight],
-        shape((cells, chans), BF16),
+        [shape((cells, chans), BF16), shape((8, part), F32)],
         [pltpu.VMEM((3, (2 * half + 2) * ncols, chans), BF16)],
         us=4, limit=24,
     )
     for step in (1, 2):
-        dims = lead[step + 1 :] + (plan.third, part)
-        result = call(
-            functools.partial(fold_kernel, plan, step), [spot], held,
-            [shape(dims, BF16), shape(dims, F32)] * 3, limit=16,
-        )
+        outs = []
+        for g in range(3):
+            rows = plan.cuts[g][1] - plan.cuts[g][0] + (plan.down_rows if g == 0 else 0)
+            outs += [shape(lead[step + 1 :] + (rows, part), BF16), shape(lead[step + 1 :] + (rows, part), F32)]
+        extra = down_held if step == 1 else []
+        result = call(functools.partial(fold_kernel, plan, step), [spot], held + extra, outs, limit=12)
         held = []
         for g in range(3):
             held += [result[2 * g + 1], swapped(result[2 * g], plan.orders[g][step])]
     for step in range(3, len(lead)):
-        dims = lead[step + 1 :] + (3 * plan.third, part)
-        kernel = fold_kernel if step == 3 else late_kernel
+        dims = lead[step + 1 :] + (plan.rows + plan.down_rows, part)
+        kernel = fold_kernel if step == 3 else single_kernel
         send, keep = call(
             functools.partial(kernel, plan, step), [spot], held, [shape(dims, BF16), shape(dims, F32)], limit=8,
-            after=[grad_input] if step == 3 else (),
+            after=[done] if step == 3 else (),
         )
         held = [keep, swapped(send, plan.orders[0][step])]
-    total = call(last_kernel, [], held, shape((3 * plan.third, part), F32), limit=4)
     grad_conv, grad_down = call(
-        functools.partial(join_kernel, plan), [spot], [total, swapped(total, core_link)],
+        functools.partial(join_kernel, plan), [spot], held + [swapped(v, core_link) for v in held],
         [shape((part // 2, 2 * plan.rows), F32), shape((part // 2, 2 * plan.down_rows), F32)],
         [pltpu.VMEM((part, 2 * plan.rows), F32), pltpu.VMEM((part, 2 * plan.down_rows), F32)],
         limit=8,

time: 65.7 us -> 63.5 us (0.967)
  local copies, waits for them, and re-layouts: 3.96 us -> 0.01 us
  Pallas kernels: 18.8 us -> 20.5 us
    unnamed x14 -> x8, local copies, waits for them, and re-layouts: 3.96 us -> 0.01 us
    pallas_call x10, Pallas kernels: 18.8 us -> 20.5 us  [call(): pl.pallas_call(run, out_shape=outs, in_specs=[smem] * len(scalars) + [hbm...]
    ppermute x18 -> x19, starting transfers between devices: 18.9 us -> 19.5 us  [swapped(): lax.ppermute(value, axis, [(i, i ^ 1 << link[1]) for i in range(lax.axis_...]
    ppermute x18 -> x19, waiting for transfers between devices: 17.2 us -> 16.8 us  [swapped(): lax.ppermute(value, axis, [(i, i ^ 1 << link[1]) for i in range(lax.axis_...]
  transfers between devices with their start and end apart: 22 -> 23, of which waited for: 7 -> 7; matrix products, arithmetic and copies ran while one was open for 0% -> 0% of each run, Pallas kernels for 21% -> 25%
where the time goes in v4:
time: 63.5 us; the launch traced here: 63.3 us
  starting transfers between devices  25 us (39%)
  Pallas kernels  20.5 us (32%)
  waiting for transfers between devices  16.9 us (27%)
  between operations  0.8 us (1%)
    pallas_call x10, Pallas kernels, call(): pl.pallas_call(run, out_shape=outs, in_specs=[smem] * len(scalars) + [hbm...  20.5 us
    ppermute x19, starting transfers between devices, swapped(): lax.ppermute(value, axis, [(i, i ^ 1 << link[1]) for i in range(lax.axis_...  19.5 us
    ppermute x19, waiting for transfers between devices, swapped(): lax.ppermute(value, axis, [(i, i ^ 1 << link[1]) for i in range(lax.axis_...  16.8 us
    ppermute x1, starting transfers between devices, body(): lax.ppermute(side, 'height', [(i, i + (2 if i % 2 == 0 else -2)) for i in...  3.48 us
  transfers between devices with their start and end apart: 23, of which 7 were waited for; matrix products, arithmetic and copies ran while one was open for 0% of the time, Pallas kernels for 25%

profile of v4, /device:TPU:0, one launch (start us, length us, event | category | flops | bytes accessed | tf_op | source)
XLA Modules:
  0.0 63.3 jit_solution(8202249190403578511)
XLA Ops:
  0.6 3.0 %collective-permute-start.1 = (bf16[256,256]{1,0:T(8,128)(2,1)}, bf16[256,256]{1,0:T(8,128)(2,1)S(1)}, u32[]{:S(2)}, u32[]{:S(2)}) collective-permute-start(bf16[256,256]{1,0:T(8,128)(2,1)} %bitcast.18), channel_id=1, source_target_pairs={{0,1},{1,0},{2,3},{3,2},{4,5},{5,4},{6,7},{7,6},{8,9},{9,8},{10,11... | collective-permute-start | bytes 393224 | tf_op jit(solution)/shard_map/ppermute | solution.py:356
  3.6 0.7 %collective-permute-start.6 = (bf16[512,256]{1,0:T(8,128)(2,1)}, bf16[512,256]{1,0:T(8,128)(2,1)S(1)}, u32[]{:S(2)}, u32[]{:S(2)}) collective-permute-start(bf16[512,256]{1,0:T(8,128)(2,1)} %bitcast.13), channel_id=1, source_target_pairs={{8,24},{9,25},{10,26},{11,27},{12,28},{13,29},{14,30},{15,31}} | collective-permute-start | bytes 786440 | tf_op jit(solution)/shard_map/ppermute | solution.py:379
  4.3 0.7 %collective-permute-start.5 = (bf16[512,256]{1,0:T(8,128)(2,1)}, bf16[512,256]{1,0:T(8,128)(2,1)S(1)}, u32[]{:S(2)}, u32[]{:S(2)}) collective-permute-start(bf16[512,256]{1,0:T(8,128)(2,1)} %bitcast.14), channel_id=1, source_target_pairs={{8,16},{9,17},{10,18},{11,19},{12,20},{13,21},{14,22},{15,23}} | collective-permute-start | bytes 786440 | tf_op jit(solution)/shard_map/ppermute | solution.py:378
  5.0 3.7 %collective-permute-start.4 = (bf16[512,256]{1,0:T(8,128)(2,1)}, bf16[512,256]{1,0:T(8,128)(2,1)S(1)}, u32[]{:S(2)}, u32[]{:S(2)}) collective-permute-start(bf16[512,256]{1,0:T(8,128)(2,1)} %bitcast.15), channel_id=1, source_target_pairs={{0,8},{8,0},{16,24},{24,16},{1,9},{9,1},{17,25},{25,17},{2,10},{10... | collective-permute-start | bytes 786440 | tf_op jit(solution)/shard_map/ppermute | solution.py:356
  8.7 0.1 pad_add_fusion.refs_0_
  8.8 4.3 %shard_map.67 = (bf16[9,256,384]{2,1,0:T(8,128)(2,1)S(1)}, bf16[768,256]{1,0:T(8,128)(2,1)S(1)}) custom-call(s32[2]{0:T(128)S(1)} %pad_add_fusion.refs_0_, bf16[9,3,8,2,16,256]{5,4,3,2,1,0:T(8,128)(2,1)} %bitcast.11, bf16[3,256,256]{2,1,0:T(8,128)(2,1)} %refs_9_.1), custom_call_target="tpu_custom_call" | custom-call | flops 3449999872 | bytes 3932160 | tf_op jit(solution)/shard_map/pallas_call | solution.py:319
  13.1 0.0 collective-permute-done.1.refs_1_.refs_2_.refs_4_
  13.1 3.5 %collective-permute-start.3 = (bf16[256,256]{1,0:T(8,128)(2,1)S(1)}, bf16[256,256]{1,0:T(8,128)(2,1)S(1)}, u32[]{:S(2)}, u32[]{:S(2)}) collective-permute-start(bf16[256,256]{1,0:T(8,128)(2,1)S(1)} %collective-permute-done.1.refs_1_.refs_2_.refs_4_), channel_id=1, source_target_pairs={{0,2},{2,4},{3,1},{4,6},{5,3},{7,5},{8,10},{10,12},{11,9},{12,14},... | collective-permute-start | bytes 393224 | tf_op jit(solution)/shard_map/ppermute | solution.py:387
  16.6 0.0 collective-permute-done.refs_6_.refs_3_
  16.6 0.1 collective-permute-start.2
  16.6 0.0 collective-permute-done.6.refs_4_
  16.7 0.0 collective-permute-done.5.refs_3_
  16.7 2.9 %shard_map.68 = (bf16[384,768]{1,0:T(8,128)(2,1)S(1)}, bf16[384,768]{1,0:T(8,128)(2,1)S(1)}, f32[3,384,256]{2,1,0:T(8,128)S(1)}, f32[256,768]{1,0:T(8,128)S(1)}, f32[128,768]{1,0:T(8,128)S(1)}) custom-call(s32[2]{0:T(128)S(1)} %pad_add_fusion.refs_0_, bf16[512,256]{1,0:T(8,128)(2,1)S(1)} %bitcast.16, bf16[512,256]{1,0:T(8,128)(2,1)S(1)} %collective-permute-done.4.refs_2_, ...), custom_call_target="tpu_custom_call" | custom-call | flops 3449999872 | bytes 3473408 | tf_op jit(solution)/shard_map/pallas_call | solution.py:319
  19.6 0.0 collective-permute-done.3.refs_3_.refs_6_
  19.6 0.5 collective-permute-start.7
  20.2 0.0 collective-permute-done.2.refs_2_.refs_5_
  20.2 2.3 %shard_map.69 = (f32[3,384,256]{2,1,0:T(8,128)S(1)}, f32[256,768]{1,0:T(8,128)S(1)}) custom-call(s32[2]{0:T(128)S(1)} %pad_add_fusion.refs_0_, bf16[256,256]{1,0:T(8,128)(2,1)S(1)} %collective-permute-done.1.refs_1_.refs_2_.refs_4_, bf16[256,256]{1,0:T(8,128)(2,1)S(1)} %collective-permute-done.2.refs_2_.refs_5_, ...), custom_call_target="tpu_custom_call" | custom-call | flops 2300000000 | bytes 3604480 | tf_op jit(solution)/shard_map/pallas_call | solution.py:319
  22.5 0.0 collective-permute-done.7.refs_4_.refs_7_
  22.5 2.9 %shard_map.70 = (bf16[3,256,256]{2,1,0:T(8,128)(2,1)S(1)}, bf16[2,2,2,112,128]{4,3,2,1,0:T(8,128)(2,1)S(1)}, f32[2,2,2,112,128]{4,3,2,1,0:T(8,128)S(1)}, bf16[2,...) custom-call(s32[2]{0:T(128)S(1)} %pad_add_fusion.refs_0_, ...), custom_call_target="tpu_custom_call" | custom-call | flops 3449999872 | bytes 8192000 | tf_op jit(solution)/shard_map/pallas_call | solution.py:319
  25.4 0.1 collective-permute-start.12
  25.5 1.2 %collective-permute-start.10 = (bf16[2,2,2,160,128]{4,3,2,1,0:T(8,128)(2,1)S(1)}, bf16[2,2,2,160,128]{4,3,2,1,0:T(8,128)(2,1)S(1)}, u32[]{:S(2)}, u32[]{:S(2)}) collective-permute-start(bf16[2,2,2,160,128]{4,3,2,1,0:T(8,128)(2,1)S(1)} %get-tuple-element.59), channel_id=1, source_target_pairs={{0,1},{1,0},{2,3},{3,2},{4,5},{5,4},{6,7},{7,6},{8,9},{9,8},{10,11... | collective-permute-start | bytes 983048 | tf_op jit(solution)/shard_map/ppermute | solution.py:356
  26.8 1.6 %collective-permute-start.11 = (bf16[2,2,2,160,128]{4,3,2,1,0:T(8,128)(2,1)S(1)}, bf16[2,2,2,160,128]{4,3,2,1,0:T(8,128)(2,1)S(1)}, u32[]{:S(2)}, u32[]{:S(2)}) collective-permute-start(bf16[2,2,2,160,128]{4,3,2,1,0:T(8,128)(2,1)S(1)} %get-tuple-element.61), channel_id=1, source_target_pairs={{0,2},{1,3},{2,0},{3,1},{4,6},{5,7},{6,4},{7,5},{8,10},{9,11},{10,... | collective-permute-start | bytes 983048 | tf_op jit(solution)/shard_map/ppermute | solution.py:356
  28.3 0.0 collective-permute-start.9
  28.3 0.0 collective-permute-done.12.refs_2_
  28.3 0.6 shard_map.72
  28.9 2.1 %collective-permute-start.13 = (bf16[2,2,2,48,128]{4,3,2,1,0:T(8,128)(2,1)S(1)}, bf16[2,2,2,48,128]{4,3,2,1,0:T(8,128)(2,1)S(1)}, u32[]{:S(2)}, u32[]{:S(2)}) collective-permute-start(bf16[2,2,2,48,128]{4,3,2,1,0:T(8,128)(2,1)S(1)} %get-tuple-element.65), channel_id=1, source_target_pairs={{0,16},{8,24},{16,0},{24,8},{1,17},{9,25},{17,1},{25,9},{2,18},{10... | collective-permute-start | bytes 294920 | tf_op jit(solution)/shard_map/ppermute | solution.py:356
  31.0 0.7 %collective-permute-start.8 = (bf16[3,256,256]{2,1,0:T(8,128)(2,1)S(1)}, bf16[3,256,256]{2,1,0:T(8,128)(2,1)S(1)}, u32[]{:S(2)}, u32[]{:S(2)}) collective-permute-start(bf16[3,256,256]{2,1,0:T(8,128)(2,1)S(1)} %get-tuple-element.54), channel_id=1, source_target_pairs={{16,8},{17,9},{18,10},{19,11},{20,12},{21,13},{22,14},{23,15}} | collective-permute-start | bytes 1179656 | tf_op jit(solution)/shard_map/ppermute | solution.py:425
  31.7 4.7 %collective-permute-done.9.refs_2_ = bf16[2,2,2,112,128]{4,3,2,1,0:T(8,128)(2,1)S(1)} collective-permute-done((bf16[2,2,2,112,128]{4,3,2,1,0:T(8,128)(2,1)S(1)}, bf16[2,2,2,112,128]{4,3,2,1,0:T(8,128)(2,1)S(1)}, u32[]{:S(2)}, u32[]{:S(2)}) %collective-permute-start.9) | collective-permute-done | bytes 229408 | tf_op jit(solution)/shard_map/ppermute | solution.py:356
  36.4 1.1 %collective-permute-done.13.refs_8_ = bf16[2,2,2,48,128]{4,3,2,1,0:T(8,128)(2,1)S(1)} collective-permute-done((bf16[2,2,2,48,128]{4,3,2,1,0:T(8,128)(2,1)S(1)}, bf16[2,2,2,48,128]{4,3,2,1,0:T(8,128)(2,1)S(1)}, u32[]{:S(2)}, u32[]{:S(2)}) %collective-permute-start.13) | collective-permute-done | bytes 98336 | tf_op jit(solution)/shard_map/ppermute | solution.py:356
  37.5 0.0 collective-permute-done.10.refs_4_
  37.5 0.0 collective-permute-done.11.refs_6_
  37.5 0.7 %shard_map.73 = (bf16[2,2,160,128]{3,2,1,0:T(8,128)(2,1)S(1)}, f32[2,2,160,128]{3,2,1,0:T(8,128)S(1)}, bf16[2,2,160,128]{3,2,1,0:T(8,128)(2,1)S(1)}, f32[2,2,160...) custom-call(s32[2]{0:T(128)S(1)} %pad_add_fusion.refs_0_, ...), custom_call_target="tpu_custom_call" | custom-call | flops 1150000000 | bytes 2949120 | tf_op jit(solution)/shard_map/pallas_call | solution.py:319
  38.2 1.6 %collective-permute-start.14 = (bf16[2,2,160,128]{3,2,1,0:T(8,128)(2,1)S(1)}, bf16[2,2,160,128]{3,2,1,0:T(8,128)(2,1)S(1)}, u32[]{:S(2)}, u32[]{:S(2)}) collective-permute-start(bf16[2,2,160,128]{3,2,1,0:T(8,128)(2,1)S(1)} %get-tuple-element.67), channel_id=1, source_target_pairs={{0,1},{1,0},{2,3},{3,2},{4,5},{5,4},{6,7},{7,6},{8,9},{9,8},{10,11... | collective-permute-start | bytes 491528 | tf_op jit(solution)/shard_map/ppermute | solution.py:356
  39.8 0.3 collective-permute-start.15
  40.0 0.3 collective-permute-start.16
  40.3 3.3 %collective-permute-done.14.refs_2_ = bf16[2,2,160,128]{3,2,1,0:T(8,128)(2,1)S(1)} collective-permute-done((bf16[2,2,160,128]{3,2,1,0:T(8,128)(2,1)S(1)}, bf16[2,2,160,128]{3,2,1,0:T(8,128)(2,1)S(1)}, u32[]{:S(2)}, u32[]{:S(2)}) %collective-permute-start.14) | collective-permute-done | bytes 163872 | tf_op jit(solution)/shard_map/ppermute | solution.py:356
  43.6 1.5 %collective-permute-done.15.refs_4_ = bf16[2,2,160,128]{3,2,1,0:T(8,128)(2,1)S(1)} collective-permute-done((bf16[2,2,160,128]{3,2,1,0:T(8,128)(2,1)S(1)}, bf16[2,2,160,128]{3,2,1,0:T(8,128)(2,1)S(1)}, u32[]{:S(2)}, u32[]{:S(2)}) %collective-permute-start.15) | collective-permute-done | bytes 163872 | tf_op jit(solution)/shard_map/ppermute | solution.py:356
  45.1 0.3 collective-permute-done.16.refs_6_
  45.4 0.6 %shard_map.74 = (bf16[2,160,128]{2,1,0:T(8,128)(2,1)S(1)}, f32[2,160,128]{2,1,0:T(8,128)S(1)}, bf16[2,160,128]{2,1,0:T(8,128)(2,1)S(1)}, f32[2,160,128]{2,1,0:T(...) custom-call(s32[2]{0:T(128)S(1)} %pad_add_fusion.refs_0_, ...), custom_call_target="tpu_custom_call" | custom-call | flops 1150000000 | bytes 1474560 | tf_op jit(solution)/shard_map/pallas_call | solution.py:319
  46.0 1.8 %collective-permute-start.17 = (bf16[2,160,128]{2,1,0:T(8,128)(2,1)S(1)}, bf16[2,160,128]{2,1,0:T(8,128)(2,1)S(1)}, u32[]{:S(2)}, u32[]{:S(2)}) collective-permute-start(bf16[2,160,128]{2,1,0:T(8,128)(2,1)S(1)} %get-tuple-element.73), channel_id=1, source_target_pairs={{0,2},{1,3},{2,0},{3,1},{4,6},{5,7},{6,4},{7,5},{8,10},{9,11},{10,... | collective-permute-start | bytes 245768 | tf_op jit(solution)/shard_map/ppermute | solution.py:356
  47.8 0.3 collective-permute-start.18
  48.1 0.5 collective-permute-start.19
  48.6 4.1 %shard_map.71 = (bf16[512,256]{1,0:T(8,128)(2,1)}, f32[8,128]{1,0:T(8,128)S(1)}) custom-call(s32[2]{0:T(128)S(1)} %pad_add_fusion.refs_0_, bf16[512,256]{1,0:T(8,128)(2,1)S(1)} %bitcast.17, bf16[256,256]{1,0:T(8,128)(2,1)S(1)} %bitcast.22, bf16[256,256]{1,0:T(8,128)(2,1)S(1)} %collective-permute-done.refs_6_.refs_3_, ...), custom_call_target="tpu_custom_call" | custom-call | flops 4600000000 | bytes 5373952 | tf_op jit(solution)/shard_map/pallas_call | solution.py:319
  52.7 0.6 shard_map.75
  53.3 2.5 %collective-permute-start.20 = (bf16[480,128]{1,0:T(8,128)(2,1)S(1)}, bf16[480,128]{1,0:T(8,128)(2,1)S(1)}, u32[]{:S(2)}, u32[]{:S(2)}) collective-permute-start(bf16[480,128]{1,0:T(8,128)(2,1)S(1)} %get-tuple-element.80), channel_id=1, source_target_pairs={{0,4},{1,5},{2,6},{3,7},{4,0},{5,1},{6,2},{7,3},{8,12},{9,13},{10,... | collective-permute-start | bytes 368648 | tf_op jit(solution)/shard_map/ppermute | solution.py:356
  55.8 4.7 %collective-permute-done.20.refs_2_ = bf16[480,128]{1,0:T(8,128)(2,1)S(1)} collective-permute-done((bf16[480,128]{1,0:T(8,128)(2,1)S(1)}, bf16[480,128]{1,0:T(8,128)(2,1)S(1)}, u32[]{:S(2)}, u32[]{:S(2)}) %collective-permute-start.20) | collective-permute-done | bytes 122912 | tf_op jit(solution)/shard_map/ppermute | solution.py:356
  60.5 1.3 %collective-permute-done.22.refs_4_ = bf16[480,128]{1,0:T(8,128)(2,1)S(1)} collective-permute-done((bf16[480,128]{1,0:T(8,128)(2,1)S(1)}, bf16[480,128]{1,0:T(8,128)(2,1)S(1)}, u32[]{:S(2)}, u32[]{:S(2)}) %collective-permute-start.22) | collective-permute-done | bytes 122912 | tf_op jit(solution)/shard_map/ppermute | solution.py:356
  61.8 1.5 %shard_map.76 = (f32[64,864]{1,0:T(8,128)}, f32[64,96]{1,0:T(8,128)}) custom-call(s32[2]{0:T(128)S(1)} %pad_add_fusion.refs_0_, f32[480,128]{1,0:T(8,128)S(1)} %get-tuple-element.79.refs_1_, bf16[480,128]{1,0:T(8,128)(2,1)S(1)} %collective-permute-done.20.refs_2_, f32[480,128]{1,0:T(8,128)S(1)} %collective-permute-done.21.refs_3_, ...), custom_call_target="tpu_custom_call" | custom-call | flops 1150000000 | bytes 737280 | tf_op jit(solution)/shard_map/pallas_call | solution.py:319
  (17 shorter events, 0.0 us)
Async XLA Ops:
  0.6 12.4 %collective-permute-start.1 = (bf16[256,256]{1,0:T(8,128)(2,1)}, bf16[256,256]{1,0:T(8,128)(2,1)S(1)}, u32[]{:S(2)}, u32[]{:S(2)}) collective-permute-start(bf16[256,256]{1,0:T(8,128)(2,1)} %bitcast.18), channel_id=1, source_target_pairs={{0,1},{1,0},{2,3},{3,2},{4,5},{5,4},{6,7},{7,6},{8,9},{9,8},{10,11... | collective-permute-start | bytes 393224 | tf_op jit(solution)/shard_map/ppermute | solution.py:356
  3.6 12.9 %collective-permute-start = (bf16[256,256]{1,0:T(8,128)(2,1)}, bf16[256,256]{1,0:T(8,128)(2,1)S(1)}, u32[]{:S(2)}, u32[]{:S(2)}) collective-permute-start(bf16[256,256]{1,0:T(8,128)(2,1)} %bitcast.19), channel_id=1, source_target_pairs={{0,8},{8,0},{16,24},{24,16},{1,9},{9,1},{17,25},{25,17},{2,10},{10... | collective-permute-start | bytes 393224 | tf_op jit(solution)/shard_map/ppermute | solution.py:356
  3.6 13.0 %collective-permute-start.6 = (bf16[512,256]{1,0:T(8,128)(2,1)}, bf16[512,256]{1,0:T(8,128)(2,1)S(1)}, u32[]{:S(2)}, u32[]{:S(2)}) collective-permute-start(bf16[512,256]{1,0:T(8,128)(2,1)} %bitcast.13), channel_id=1, source_target_pairs={{8,24},{9,25},{10,26},{11,27},{12,28},{13,29},{14,30},{15,31}} | collective-permute-start | bytes 786440 | tf_op jit(solution)/shard_map/ppermute | solution.py:379
  4.3 12.3 %collective-permute-start.5 = (bf16[512,256]{1,0:T(8,128)(2,1)}, bf16[512,256]{1,0:T(8,128)(2,1)S(1)}, u32[]{:S(2)}, u32[]{:S(2)}) collective-permute-start(bf16[512,256]{1,0:T(8,128)(2,1)} %bitcast.14), channel_id=1, source_target_pairs={{8,16},{9,17},{10,18},{11,19},{12,20},{13,21},{14,22},{15,23}} | collective-permute-start | bytes 786440 | tf_op jit(solution)/shard_map/ppermute | solution.py:378
  5.0 11.7 %collective-permute-start.4 = (bf16[512,256]{1,0:T(8,128)(2,1)}, bf16[512,256]{1,0:T(8,128)(2,1)S(1)}, u32[]{:S(2)}, u32[]{:S(2)}) collective-permute-start(bf16[512,256]{1,0:T(8,128)(2,1)} %bitcast.15), channel_id=1, source_target_pairs={{0,8},{8,0},{16,24},{24,16},{1,9},{9,1},{17,25},{25,17},{2,10},{10... | collective-permute-start | bytes 786440 | tf_op jit(solution)/shard_map/ppermute | solution.py:356
  8.8 7.9 %copy-start.2 = (bf16[4,1,128,256]{3,2,1,0:T(8,128)(2,1)S(1)}, bf16[4,1,128,256]{3,2,1,0:T(8,128)(2,1)}, u32[]{:S(2)}) copy-start(bf16[4,1,128,256]{3,2,1,0:T(8,128)(2,1)} %param.4) | copy-start | bytes 786436
  8.8 7.9 %copy-start.3 = (bf16[2,1,128,256]{3,2,1,0:T(8,128)(2,1)S(1)}, bf16[2,1,128,256]{3,2,1,0:T(8,128)(2,1)}, u32[]{:S(2)}) copy-start(bf16[2,1,128,256]{3,2,1,0:T(8,128)(2,1)} %param.7) | copy-start | bytes 393220
  13.1 6.6 %collective-permute-start.3 = (bf16[256,256]{1,0:T(8,128)(2,1)S(1)}, bf16[256,256]{1,0:T(8,128)(2,1)S(1)}, u32[]{:S(2)}, u32[]{:S(2)}) collective-permute-start(bf16[256,256]{1,0:T(8,128)(2,1)S(1)} %collective-permute-done.1.refs_1_.refs_2_.refs_4_), channel_id=1, source_target_pairs={{0,2},{2,4},{3,1},{4,6},{5,3},{7,5},{8,10},{10,12},{11,9},{12,14},... | collective-permute-start | bytes 393224 | tf_op jit(solution)/shard_map/ppermute | solution.py:387
  16.6 3.6 %collective-permute-start.2 = (bf16[256,256]{1,0:T(8,128)(2,1)S(1)}, bf16[256,256]{1,0:T(8,128)(2,1)S(1)}, u32[]{:S(2)}, u32[]{:S(2)}) collective-permute-start(bf16[256,256]{1,0:T(8,128)(2,1)S(1)} %collective-permute-done.1.refs_1_.refs_2_.refs_4_), channel_id=1, source_target_pairs={{0,8},{8,0},{16,24},{24,16},{1,9},{9,1},{17,25},{25,17},{2,10},{10... | collective-permute-start | bytes 393224 | tf_op jit(solution)/shard_map/ppermute | solution.py:356
  19.6 2.9 %collective-permute-start.7 = (bf16[256,256]{1,0:T(8,128)(2,1)S(1)}, bf16[256,256]{1,0:T(8,128)(2,1)S(1)}, u32[]{:S(2)}, u32[]{:S(2)}) collective-permute-start(bf16[256,256]{1,0:T(8,128)(2,1)S(1)} %collective-permute-done.3.refs_3_.refs_6_), channel_id=1, source_target_pairs={{0,8},{8,0},{16,24},{24,16},{1,9},{9,1},{17,25},{25,17},{2,10},{10... | collective-permute-start | bytes 393224 | tf_op jit(solution)/shard_map/ppermute | solution.py:356
  25.4 2.9 %collective-permute-start.12 = (bf16[2,2,2,2,48,128]{5,4,3,2,1,0:T(8,128)(2,1)S(1)}, bf16[2,2,2,2,48,128]{5,4,3,2,1,0:T(8,128)(2,1)S(1)}, u32[]{:S(2)}, u32[]{:S(2)}) collective-permute-start(bf16[2,2,2,2,48,128]{5,4,3,2,1,0:T(8,128)(2,1)S(1)} %get-tuple-element.63), channel_id=1, source_target_pairs={{0,8},{8,0},{16,24},{24,16},{1,9},{9,1},{17,25},{25,17},{2,10},{10... | collective-permute-start | bytes 589832 | tf_op jit(solution)/shard_map/ppermute | solution.py:356
  25.5 11.9 %collective-permute-start.10 = (bf16[2,2,2,160,128]{4,3,2,1,0:T(8,128)(2,1)S(1)}, bf16[2,2,2,160,128]{4,3,2,1,0:T(8,128)(2,1)S(1)}, u32[]{:S(2)}, u32[]{:S(2)}) collective-permute-start(bf16[2,2,2,160,128]{4,3,2,1,0:T(8,128)(2,1)S(1)} %get-tuple-element.59), channel_id=1, source_target_pairs={{0,1},{1,0},{2,3},{3,2},{4,5},{5,4},{6,7},{7,6},{8,9},{9,8},{10,11... | collective-permute-start | bytes 983048 | tf_op jit(solution)/shard_map/ppermute | solution.py:356
  26.8 10.7 %collective-permute-start.11 = (bf16[2,2,2,160,128]{4,3,2,1,0:T(8,128)(2,1)S(1)}, bf16[2,2,2,160,128]{4,3,2,1,0:T(8,128)(2,1)S(1)}, u32[]{:S(2)}, u32[]{:S(2)}) collective-permute-start(bf16[2,2,2,160,128]{4,3,2,1,0:T(8,128)(2,1)S(1)} %get-tuple-element.61), channel_id=1, source_target_pairs={{0,2},{1,3},{2,0},{3,1},{4,6},{5,7},{6,4},{7,5},{8,10},{9,11},{10,... | collective-permute-start | bytes 983048 | tf_op jit(solution)/shard_map/ppermute | solution.py:356
  28.3 8.1 %collective-permute-start.9 = (bf16[2,2,2,112,128]{4,3,2,1,0:T(8,128)(2,1)S(1)}, bf16[2,2,2,112,128]{4,3,2,1,0:T(8,128)(2,1)S(1)}, u32[]{:S(2)}, u32[]{:S(2)}) collective-permute-start(bf16[2,2,2,112,128]{4,3,2,1,0:T(8,128)(2,1)S(1)} %get-tuple-element.57), channel_id=1, source_target_pairs={{0,16},{8,24},{16,0},{24,8},{1,17},{9,25},{17,1},{25,9},{2,18},{10... | collective-permute-start | bytes 688136 | tf_op jit(solution)/shard_map/ppermute | solution.py:356
  28.9 8.5 %collective-permute-start.13 = (bf16[2,2,2,48,128]{4,3,2,1,0:T(8,128)(2,1)S(1)}, bf16[2,2,2,48,128]{4,3,2,1,0:T(8,128)(2,1)S(1)}, u32[]{:S(2)}, u32[]{:S(2)}) collective-permute-start(bf16[2,2,2,48,128]{4,3,2,1,0:T(8,128)(2,1)S(1)} %get-tuple-element.65), channel_id=1, source_target_pairs={{0,16},{8,24},{16,0},{24,8},{1,17},{9,25},{17,1},{25,9},{2,18},{10... | collective-permute-start | bytes 294920 | tf_op jit(solution)/shard_map/ppermute | solution.py:356
  31.0 17.6 %collective-permute-start.8 = (bf16[3,256,256]{2,1,0:T(8,128)(2,1)S(1)}, bf16[3,256,256]{2,1,0:T(8,128)(2,1)S(1)}, u32[]{:S(2)}, u32[]{:S(2)}) collective-permute-start(bf16[3,256,256]{2,1,0:T(8,128)(2,1)S(1)} %get-tuple-element.54), channel_id=1, source_target_pairs={{16,8},{17,9},{18,10},{19,11},{20,12},{21,13},{22,14},{23,15}} | collective-permute-start | bytes 1179656 | tf_op jit(solution)/shard_map/ppermute | solution.py:425
  38.2 5.4 %collective-permute-start.14 = (bf16[2,2,160,128]{3,2,1,0:T(8,128)(2,1)S(1)}, bf16[2,2,160,128]{3,2,1,0:T(8,128)(2,1)S(1)}, u32[]{:S(2)}, u32[]{:S(2)}) collective-permute-start(bf16[2,2,160,128]{3,2,1,0:T(8,128)(2,1)S(1)} %get-tuple-element.67), channel_id=1, source_target_pairs={{0,1},{1,0},{2,3},{3,2},{4,5},{5,4},{6,7},{7,6},{8,9},{9,8},{10,11... | collective-permute-start | bytes 491528 | tf_op jit(solution)/shard_map/ppermute | solution.py:356
  39.8 5.3 %collective-permute-start.15 = (bf16[2,2,160,128]{3,2,1,0:T(8,128)(2,1)S(1)}, bf16[2,2,160,128]{3,2,1,0:T(8,128)(2,1)S(1)}, u32[]{:S(2)}, u32[]{:S(2)}) collective-permute-start(bf16[2,2,160,128]{3,2,1,0:T(8,128)(2,1)S(1)} %get-tuple-element.69), channel_id=1, source_target_pairs={{0,2},{1,3},{2,0},{3,1},{4,6},{5,7},{6,4},{7,5},{8,10},{9,11},{10,... | collective-permute-start | bytes 491528 | tf_op jit(solution)/shard_map/ppermute | solution.py:356
  40.0 5.3 %collective-permute-start.16 = (bf16[2,2,160,128]{3,2,1,0:T(8,128)(2,1)S(1)}, bf16[2,2,160,128]{3,2,1,0:T(8,128)(2,1)S(1)}, u32[]{:S(2)}, u32[]{:S(2)}) collective-permute-start(bf16[2,2,160,128]{3,2,1,0:T(8,128)(2,1)S(1)} %get-tuple-element.71), channel_id=1, source_target_pairs={{0,16},{8,24},{16,0},{24,8},{1,17},{9,25},{17,1},{25,9},{2,18},{10... | collective-permute-start | bytes 491528 | tf_op jit(solution)/shard_map/ppermute | solution.py:356
  45.4 3.3 %copy-start = (bf16[3,3,3,256,256]{4,3,2,1,0:T(8,128)(2,1)S(1)}, bf16[3,3,3,256,256]{4,3,2,1,0:T(8,128)(2,1)}, u32[]{:S(2)}) copy-start(bf16[3,3,3,256,256]{4,3,2,1,0:T(8,128)(2,1)} %param.5) | copy-start | bytes 10616836
  45.4 3.3 %copy-start.1 = (bf16[3,256,256]{2,1,0:T(8,128)(2,1)S(1)}, bf16[3,256,256]{2,1,0:T(8,128)(2,1)}, u32[]{:S(2)}) copy-start(bf16[3,256,256]{2,1,0:T(8,128)(2,1)} %refs_9_.1) | copy-start | bytes 1179652
  46.0 6.7 %collective-permute-start.17 = (bf16[2,160,128]{2,1,0:T(8,128)(2,1)S(1)}, bf16[2,160,128]{2,1,0:T(8,128)(2,1)S(1)}, u32[]{:S(2)}, u32[]{:S(2)}) collective-permute-start(bf16[2,160,128]{2,1,0:T(8,128)(2,1)S(1)} %get-tuple-element.73), channel_id=1, source_target_pairs={{0,2},{1,3},{2,0},{3,1},{4,6},{5,7},{6,4},{7,5},{8,10},{9,11},{10,... | collective-permute-start | bytes 245768 | tf_op jit(solution)/shard_map/ppermute | solution.py:356
  47.8 4.9 %collective-permute-start.18 = (bf16[2,160,128]{2,1,0:T(8,128)(2,1)S(1)}, bf16[2,160,128]{2,1,0:T(8,128)(2,1)S(1)}, u32[]{:S(2)}, u32[]{:S(2)}) collective-permute-start(bf16[2,160,128]{2,1,0:T(8,128)(2,1)S(1)} %get-tuple-element.75), channel_id=1, source_target_pairs={{0,16},{8,24},{16,0},{24,8},{1,17},{9,25},{17,1},{25,9},{2,18},{10... | collective-permute-start | bytes 245768 | tf_op jit(solution)/shard_map/ppermute | solution.py:356
  48.1 4.6 %collective-permute-start.19 = (bf16[2,160,128]{2,1,0:T(8,128)(2,1)S(1)}, bf16[2,160,128]{2,1,0:T(8,128)(2,1)S(1)}, u32[]{:S(2)}, u32[]{:S(2)}) collective-permute-start(bf16[2,160,128]{2,1,0:T(8,128)(2,1)S(1)} %get-tuple-element.77), channel_id=1, source_target_pairs={{0,1},{1,0},{2,3},{3,2},{4,5},{5,4},{6,7},{7,6},{8,9},{9,8},{10,11... | collective-permute-start | bytes 245768 | tf_op jit(solution)/shard_map/ppermute | solution.py:356
  53.3 7.2 %collective-permute-start.20 = (bf16[480,128]{1,0:T(8,128)(2,1)S(1)}, bf16[480,128]{1,0:T(8,128)(2,1)S(1)}, u32[]{:S(2)}, u32[]{:S(2)}) collective-permute-start(bf16[480,128]{1,0:T(8,128)(2,1)S(1)} %get-tuple-element.80), channel_id=1, source_target_pairs={{0,4},{1,5},{2,6},{3,7},{4,0},{5,1},{6,2},{7,3},{8,12},{9,13},{10,... | collective-permute-start | bytes 368648 | tf_op jit(solution)/shard_map/ppermute | solution.py:356
  55.8 6.0 %collective-permute-start.21 = (f32[480,128]{1,0:T(8,128)S(1)}, f32[480,128]{1,0:T(8,128)S(1)}, u32[]{:S(2)}, u32[]{:S(2)}) collective-permute-start(f32[480,128]{1,0:T(8,128)S(1)} %get-tuple-element.79.refs_1_), channel_id=1, source_target_pairs={{0,8},{8,0},{16,24},{24,16},{1,9},{9,1},{17,25},{25,17},{2,10},{10... | collective-permute-start | bytes 737288 | tf_op jit(solution)/shard_map/ppermute | solution.py:356
  60.5 1.3 %collective-permute-start.22 = (bf16[480,128]{1,0:T(8,128)(2,1)S(1)}, bf16[480,128]{1,0:T(8,128)(2,1)S(1)}, u32[]{:S(2)}, u32[]{:S(2)}) collective-permute-start(bf16[480,128]{1,0:T(8,128)(2,1)S(1)} %collective-permute-done.20.refs_2_), channel_id=1, source_target_pairs={{0,8},{8,0},{16,24},{24,16},{1,9},{9,1},{17,25},{25,17},{2,10},{10... | collective-permute-start | bytes 368648 | tf_op jit(solution)/shard_map/ppermute | solution.py:356

commit v5 on v4

--- a/solution.py
+++ b/solution.py
@@ -88,7 +88,8 @@
         spread_ref[k * chans : (k + 1) * chans] = dot_nt(same, downs[k]).astype(BF16)
     for ab in range(9):
         copies[ab + 1].wait()
-        turned_ref[ab] = dot_nt(same, weights[ab].reshape(3 * chans // 2, chans)).astype(BF16)
+        block = weights[ab].reshape(3 * chans // 2, chans)
+        turned_ref[ab] = block.T if ab % 2 else dot_nt(same, block).astype(BF16)
 
 
 def row_terms(plan, even, odd, cells, spread_ref, turned_ref, b, conv_ref):
@@ -376,7 +377,7 @@
     here_other = swapped(mine, core_link)
     clip_other = swapped(flat, core_link)
     first = lax.ppermute(flat, "tm", [(i, i + 1) for i in range(1, tm_count - 1, 2)])
-    second = lax.ppermute(flat, "tm", [(i, i + 2) for i in range(1, tm_count - 2, 2)])
+    second = lax.ppermute(clip_other, "tm", [(i, i + 3) for i in range(0, tm_count - 3, 2)])
     listed = (9, 3, part // plan.group, 2, plan.group, chans)
     turned, spread = call(
         functools.partial(weights_kernel, plan), [spot], [weight.reshape(listed), down_weight],

time: 63.5 us -> 62.3 us (0.981)
    ppermute x19, starting transfers between devices: 19.5 us -> 16.2 us  [swapped(): lax.ppermute(value, axis, [(i, i ^ 1 << link[1]) for i in range(lax.axis_...]
    ppermute x1, starting transfers between devices: 0.67 us -> 3.38 us  [body(): lax.ppermute(clip_other, 'tm', [(i, i + 3) for i in range(0, tm_count - 3...]
  transfers between devices with their start and end apart: 23 -> 23, of which waited for: 7 -> 7; matrix products, arithmetic and copies ran while one was open for 0% -> 0% of each run, Pallas kernels for 25% -> 24%
where the time goes in v5:
time: 62.3 us; the launch traced here: 62.1 us
  starting transfers between devices  24.4 us (39%)
  Pallas kernels  19.9 us (32%)
  waiting for transfers between devices  16.9 us (27%)
  between operations  0.81 us (1%)
    pallas_call x10, Pallas kernels, call(): pl.pallas_call(run, out_shape=outs, in_specs=[smem] * len(scalars) + [hbm...  19.9 us
    ppermute x19, waiting for transfers between devices, swapped(): lax.ppermute(value, axis, [(i, i ^ 1 << link[1]) for i in range(lax.axis_...  16.8 us
    ppermute x19, starting transfers between devices, swapped(): lax.ppermute(value, axis, [(i, i ^ 1 << link[1]) for i in range(lax.axis_...  16.2 us
    ppermute x1, starting transfers between devices, body(): lax.ppermute(side, 'height', [(i, i + (2 if i % 2 == 0 else -2)) for i in...  3.49 us
    ppermute x1, starting transfers between devices, body(): lax.ppermute(clip_other, 'tm', [(i, i + 3) for i in range(0, tm_count - 3...  3.38 us
  transfers between devices with their start and end apart: 23, of which 7 were waited for; matrix products, arithmetic and copies ran while one was open for 0% of the time, Pallas kernels for 24%

profile of v5, /device:TPU:0, one launch (start us, length us, event | category | flops | bytes accessed | tf_op | source)
XLA Modules:
  0.0 62.1 jit_solution(3967961497975592437)
XLA Ops:
  0.6 0.5 collective-permute-start.4
  1.1 2.6 %collective-permute-start.1 = (bf16[256,256]{1,0:T(8,128)(2,1)}, bf16[256,256]{1,0:T(8,128)(2,1)S(1)}, u32[]{:S(2)}, u32[]{:S(2)}) collective-permute-start(bf16[256,256]{1,0:T(8,128)(2,1)} %bitcast.17), channel_id=1, source_target_pairs={{0,1},{1,0},{2,3},{3,2},{4,5},{5,4},{6,7},{7,6},{8,9},{9,8},{10,11... | collective-permute-start | bytes 393224 | tf_op jit(solution)/shard_map/ppermute | solution.py:357
  3.7 0.2 collective-permute-start
  3.9 0.7 %collective-permute-start.5 = (bf16[512,256]{1,0:T(8,128)(2,1)}, bf16[512,256]{1,0:T(8,128)(2,1)S(1)}, u32[]{:S(2)}, u32[]{:S(2)}) collective-permute-start(bf16[512,256]{1,0:T(8,128)(2,1)} %bitcast.14), channel_id=1, source_target_pairs={{8,16},{9,17},{10,18},{11,19},{12,20},{13,21},{14,22},{15,23}} | collective-permute-start | bytes 786440 | tf_op jit(solution)/shard_map/ppermute | solution.py:379
  4.6 0.1 pad_add_fusion.refs_0_
  4.6 0.0 collective-permute-done.4.refs_2_
  4.6 3.4 %collective-permute-start.6 = (bf16[512,256]{1,0:T(8,128)(2,1)S(1)}, bf16[512,256]{1,0:T(8,128)(2,1)S(1)}, u32[]{:S(2)}, u32[]{:S(2)}) collective-permute-start(bf16[512,256]{1,0:T(8,128)(2,1)S(1)} %collective-permute-done.4.refs_2_), channel_id=1, source_target_pairs={{0,24},{1,25},{2,26},{3,27},{4,28},{5,29},{6,30},{7,31}} | collective-permute-start | bytes 786440 | tf_op jit(solution)/shard_map/ppermute | solution.py:380
  8.0 0.0 copy-start.2
  8.0 0.0 copy-start.3
  8.0 3.7 %shard_map.67 = (bf16[9,256,384]{2,1,0:T(8,128)(2,1)S(1)}, bf16[768,256]{1,0:T(8,128)(2,1)S(1)}) custom-call(s32[2]{0:T(128)S(1)} %pad_add_fusion.refs_0_, bf16[9,3,8,2,16,256]{5,4,3,2,1,0:T(8,128)(2,1)} %bitcast.11, bf16[3,256,256]{2,1,0:T(8,128)(2,1)} %refs_9_.1), custom_call_target="tpu_custom_call" | custom-call | flops 3449999872 | bytes 3932160 | tf_op jit(solution)/shard_map/pallas_call | solution.py:320
  11.7 0.0 collective-permute-done.1.refs_1_.refs_2_.refs_4_
  11.8 3.5 %collective-permute-start.3 = (bf16[256,256]{1,0:T(8,128)(2,1)S(1)}, bf16[256,256]{1,0:T(8,128)(2,1)S(1)}, u32[]{:S(2)}, u32[]{:S(2)}) collective-permute-start(bf16[256,256]{1,0:T(8,128)(2,1)S(1)} %collective-permute-done.1.refs_1_.refs_2_.refs_4_), channel_id=1, source_target_pairs={{0,2},{2,4},{3,1},{4,6},{5,3},{7,5},{8,10},{10,12},{11,9},{12,14},... | collective-permute-start | bytes 393224 | tf_op jit(solution)/shard_map/ppermute | solution.py:388
  15.3 0.1 collective-permute-start.2
  15.3 0.0 collective-permute-done.refs_6_.refs_3_
  15.4 0.0 collective-permute-done.6.refs_4_
  15.4 2.9 %shard_map.68 = (bf16[384,768]{1,0:T(8,128)(2,1)S(1)}, bf16[384,768]{1,0:T(8,128)(2,1)S(1)}, f32[3,384,256]{2,1,0:T(8,128)S(1)}, f32[256,768]{1,0:T(8,128)S(1)}, f32[128,768]{1,0:T(8,128)S(1)}) custom-call(s32[2]{0:T(128)S(1)} %pad_add_fusion.refs_0_, bf16[512,256]{1,0:T(8,128)(2,1)S(1)} %bitcast.15, bf16[512,256]{1,0:T(8,128)(2,1)S(1)} %collective-permute-done.4.refs_2_, ...), custom_call_target="tpu_custom_call" | custom-call | flops 3449999872 | bytes 3473408 | tf_op jit(solution)/shard_map/pallas_call | solution.py:320
  18.3 0.5 collective-permute-start.7
  18.9 2.3 %shard_map.69 = (f32[3,384,256]{2,1,0:T(8,128)S(1)}, f32[256,768]{1,0:T(8,128)S(1)}) custom-call(s32[2]{0:T(128)S(1)} %pad_add_fusion.refs_0_, bf16[256,256]{1,0:T(8,128)(2,1)S(1)} %collective-permute-done.1.refs_1_.refs_2_.refs_4_, bf16[256,256]{1,0:T(8,128)(2,1)S(1)} %collective-permute-done.2.refs_2_.refs_5_, ...), custom_call_target="tpu_custom_call" | custom-call | flops 2300000000 | bytes 3604480 | tf_op jit(solution)/shard_map/pallas_call | solution.py:320
  21.2 0.0 collective-permute-done.7.refs_4_.refs_7_
  21.2 2.9 %shard_map.70 = (bf16[3,256,256]{2,1,0:T(8,128)(2,1)S(1)}, bf16[2,2,2,112,128]{4,3,2,1,0:T(8,128)(2,1)S(1)}, f32[2,2,2,112,128]{4,3,2,1,0:T(8,128)S(1)}, bf16[2,...) custom-call(s32[2]{0:T(128)S(1)} %pad_add_fusion.refs_0_, ...), custom_call_target="tpu_custom_call" | custom-call | flops 3449999872 | bytes 8192000 | tf_op jit(solution)/shard_map/pallas_call | solution.py:320
  24.1 0.1 collective-permute-start.12
  24.2 1.4 %collective-permute-start.10 = (bf16[2,2,2,160,128]{4,3,2,1,0:T(8,128)(2,1)S(1)}, bf16[2,2,2,160,128]{4,3,2,1,0:T(8,128)(2,1)S(1)}, u32[]{:S(2)}, u32[]{:S(2)}) collective-permute-start(bf16[2,2,2,160,128]{4,3,2,1,0:T(8,128)(2,1)S(1)} %get-tuple-element.59), channel_id=1, source_target_pairs={{0,1},{1,0},{2,3},{3,2},{4,5},{5,4},{6,7},{7,6},{8,9},{9,8},{10,11... | collective-permute-start | bytes 983048 | tf_op jit(solution)/shard_map/ppermute | solution.py:357
  25.6 1.6 %collective-permute-start.11 = (bf16[2,2,2,160,128]{4,3,2,1,0:T(8,128)(2,1)S(1)}, bf16[2,2,2,160,128]{4,3,2,1,0:T(8,128)(2,1)S(1)}, u32[]{:S(2)}, u32[]{:S(2)}) collective-permute-start(bf16[2,2,2,160,128]{4,3,2,1,0:T(8,128)(2,1)S(1)} %get-tuple-element.61), channel_id=1, source_target_pairs={{0,2},{1,3},{2,0},{3,1},{4,6},{5,7},{6,4},{7,5},{8,10},{9,11},{10,... | collective-permute-start | bytes 983048 | tf_op jit(solution)/shard_map/ppermute | solution.py:357
  27.2 0.6 shard_map.72
  27.8 2.1 %collective-permute-start.13 = (bf16[2,2,2,48,128]{4,3,2,1,0:T(8,128)(2,1)S(1)}, bf16[2,2,2,48,128]{4,3,2,1,0:T(8,128)(2,1)S(1)}, u32[]{:S(2)}, u32[]{:S(2)}) collective-permute-start(bf16[2,2,2,48,128]{4,3,2,1,0:T(8,128)(2,1)S(1)} %get-tuple-element.65), channel_id=1, source_target_pairs={{0,16},{8,24},{16,0},{24,8},{1,17},{9,25},{17,1},{25,9},{2,18},{10... | collective-permute-start | bytes 294920 | tf_op jit(solution)/shard_map/ppermute | solution.py:357
  29.9 0.7 %collective-permute-start.8 = (bf16[3,256,256]{2,1,0:T(8,128)(2,1)S(1)}, bf16[3,256,256]{2,1,0:T(8,128)(2,1)S(1)}, u32[]{:S(2)}, u32[]{:S(2)}) collective-permute-start(bf16[3,256,256]{2,1,0:T(8,128)(2,1)S(1)} %get-tuple-element.54), channel_id=1, source_target_pairs={{16,8},{17,9},{18,10},{19,11},{20,12},{21,13},{22,14},{23,15}} | collective-permute-start | bytes 1179656 | tf_op jit(solution)/shard_map/ppermute | solution.py:426
  30.5 4.7 %collective-permute-done.9.refs_2_ = bf16[2,2,2,112,128]{4,3,2,1,0:T(8,128)(2,1)S(1)} collective-permute-done((bf16[2,2,2,112,128]{4,3,2,1,0:T(8,128)(2,1)S(1)}, bf16[2,2,2,112,128]{4,3,2,1,0:T(8,128)(2,1)S(1)}, u32[]{:S(2)}, u32[]{:S(2)}) %collective-permute-start.9) | collective-permute-done | bytes 229408 | tf_op jit(solution)/shard_map/ppermute | solution.py:357
  35.3 1.1 %collective-permute-done.13.refs_8_ = bf16[2,2,2,48,128]{4,3,2,1,0:T(8,128)(2,1)S(1)} collective-permute-done((bf16[2,2,2,48,128]{4,3,2,1,0:T(8,128)(2,1)S(1)}, bf16[2,2,2,48,128]{4,3,2,1,0:T(8,128)(2,1)S(1)}, u32[]{:S(2)}, u32[]{:S(2)}) %collective-permute-start.13) | collective-permute-done | bytes 98336 | tf_op jit(solution)/shard_map/ppermute | solution.py:357
  36.3 0.0 collective-permute-done.10.refs_4_
  36.3 0.0 collective-permute-done.11.refs_6_
  36.3 0.7 %shard_map.73 = (bf16[2,2,160,128]{3,2,1,0:T(8,128)(2,1)S(1)}, f32[2,2,160,128]{3,2,1,0:T(8,128)S(1)}, bf16[2,2,160,128]{3,2,1,0:T(8,128)(2,1)S(1)}, f32[2,2,160...) custom-call(s32[2]{0:T(128)S(1)} %pad_add_fusion.refs_0_, ...), custom_call_target="tpu_custom_call" | custom-call | flops 1150000000 | bytes 2949120 | tf_op jit(solution)/shard_map/pallas_call | solution.py:320
  37.0 1.6 %collective-permute-start.14 = (bf16[2,2,160,128]{3,2,1,0:T(8,128)(2,1)S(1)}, bf16[2,2,160,128]{3,2,1,0:T(8,128)(2,1)S(1)}, u32[]{:S(2)}, u32[]{:S(2)}) collective-permute-start(bf16[2,2,160,128]{3,2,1,0:T(8,128)(2,1)S(1)} %get-tuple-element.67), channel_id=1, source_target_pairs={{0,1},{1,0},{2,3},{3,2},{4,5},{5,4},{6,7},{7,6},{8,9},{9,8},{10,11... | collective-permute-start | bytes 491528 | tf_op jit(solution)/shard_map/ppermute | solution.py:357
  38.6 0.3 collective-permute-start.15
  38.9 0.3 collective-permute-start.16
  39.2 3.3 %collective-permute-done.14.refs_2_ = bf16[2,2,160,128]{3,2,1,0:T(8,128)(2,1)S(1)} collective-permute-done((bf16[2,2,160,128]{3,2,1,0:T(8,128)(2,1)S(1)}, bf16[2,2,160,128]{3,2,1,0:T(8,128)(2,1)S(1)}, u32[]{:S(2)}, u32[]{:S(2)}) %collective-permute-start.14) | collective-permute-done | bytes 163872 | tf_op jit(solution)/shard_map/ppermute | solution.py:357
  42.4 1.5 %collective-permute-done.15.refs_4_ = bf16[2,2,160,128]{3,2,1,0:T(8,128)(2,1)S(1)} collective-permute-done((bf16[2,2,160,128]{3,2,1,0:T(8,128)(2,1)S(1)}, bf16[2,2,160,128]{3,2,1,0:T(8,128)(2,1)S(1)}, u32[]{:S(2)}, u32[]{:S(2)}) %collective-permute-start.15) | collective-permute-done | bytes 163872 | tf_op jit(solution)/shard_map/ppermute | solution.py:357
  43.9 0.3 collective-permute-done.16.refs_6_
  44.2 0.6 %shard_map.74 = (bf16[2,160,128]{2,1,0:T(8,128)(2,1)S(1)}, f32[2,160,128]{2,1,0:T(8,128)S(1)}, bf16[2,160,128]{2,1,0:T(8,128)(2,1)S(1)}, f32[2,160,128]{2,1,0:T(...) custom-call(s32[2]{0:T(128)S(1)} %pad_add_fusion.refs_0_, ...), custom_call_target="tpu_custom_call" | custom-call | flops 1150000000 | bytes 1474560 | tf_op jit(solution)/shard_map/pallas_call | solution.py:320
  44.8 1.8 %collective-permute-start.17 = (bf16[2,160,128]{2,1,0:T(8,128)(2,1)S(1)}, bf16[2,160,128]{2,1,0:T(8,128)(2,1)S(1)}, u32[]{:S(2)}, u32[]{:S(2)}) collective-permute-start(bf16[2,160,128]{2,1,0:T(8,128)(2,1)S(1)} %get-tuple-element.73), channel_id=1, source_target_pairs={{0,2},{1,3},{2,0},{3,1},{4,6},{5,7},{6,4},{7,5},{8,10},{9,11},{10,... | collective-permute-start | bytes 245768 | tf_op jit(solution)/shard_map/ppermute | solution.py:357
  46.7 0.3 collective-permute-start.18
  46.9 0.5 collective-permute-start.19
  47.5 0.0 collective-permute-done.8.refs_8_
  47.5 4.1 %shard_map.71 = (bf16[512,256]{1,0:T(8,128)(2,1)}, f32[8,128]{1,0:T(8,128)S(1)}) custom-call(s32[2]{0:T(128)S(1)} %pad_add_fusion.refs_0_, bf16[512,256]{1,0:T(8,128)(2,1)S(1)} %bitcast.16, bf16[256,256]{1,0:T(8,128)(2,1)S(1)} %bitcast.21, bf16[256,256]{1,0:T(8,128)(2,1)S(1)} %collective-permute-done.refs_6_.refs_3_, ...), custom_call_target="tpu_custom_call" | custom-call | flops 4600000000 | bytes 5373952 | tf_op jit(solution)/shard_map/pallas_call | solution.py:320
  51.6 0.6 shard_map.75
  52.2 2.5 %collective-permute-start.20 = (bf16[480,128]{1,0:T(8,128)(2,1)S(1)}, bf16[480,128]{1,0:T(8,128)(2,1)S(1)}, u32[]{:S(2)}, u32[]{:S(2)}) collective-permute-start(bf16[480,128]{1,0:T(8,128)(2,1)S(1)} %get-tuple-element.80), channel_id=1, source_target_pairs={{0,4},{1,5},{2,6},{3,7},{4,0},{5,1},{6,2},{7,3},{8,12},{9,13},{10,... | collective-permute-start | bytes 368648 | tf_op jit(solution)/shard_map/ppermute | solution.py:357
  54.6 4.7 %collective-permute-done.20.refs_2_ = bf16[480,128]{1,0:T(8,128)(2,1)S(1)} collective-permute-done((bf16[480,128]{1,0:T(8,128)(2,1)S(1)}, bf16[480,128]{1,0:T(8,128)(2,1)S(1)}, u32[]{:S(2)}, u32[]{:S(2)}) %collective-permute-start.20) | collective-permute-done | bytes 122912 | tf_op jit(solution)/shard_map/ppermute | solution.py:357
  59.3 1.3 %collective-permute-done.22.refs_4_ = bf16[480,128]{1,0:T(8,128)(2,1)S(1)} collective-permute-done((bf16[480,128]{1,0:T(8,128)(2,1)S(1)}, bf16[480,128]{1,0:T(8,128)(2,1)S(1)}, u32[]{:S(2)}, u32[]{:S(2)}) %collective-permute-start.22) | collective-permute-done | bytes 122912 | tf_op jit(solution)/shard_map/ppermute | solution.py:357
  60.7 1.5 %shard_map.76 = (f32[64,864]{1,0:T(8,128)}, f32[64,96]{1,0:T(8,128)}) custom-call(s32[2]{0:T(128)S(1)} %pad_add_fusion.refs_0_, f32[480,128]{1,0:T(8,128)S(1)} %get-tuple-element.79.refs_1_, bf16[480,128]{1,0:T(8,128)(2,1)S(1)} %collective-permute-done.20.refs_2_, f32[480,128]{1,0:T(8,128)S(1)} %collective-permute-done.21.refs_3_, ...), custom_call_target="tpu_custom_call" | custom-call | flops 1150000000 | bytes 737280 | tf_op jit(solution)/shard_map/pallas_call | solution.py:320
  (17 shorter events, 0.0 us)
Async XLA Ops:
  0.6 4.0 %collective-permute-start.4 = (bf16[512,256]{1,0:T(8,128)(2,1)}, bf16[512,256]{1,0:T(8,128)(2,1)S(1)}, u32[]{:S(2)}, u32[]{:S(2)}) collective-permute-start(bf16[512,256]{1,0:T(8,128)(2,1)} %bitcast.13), channel_id=1, source_target_pairs={{0,8},{8,0},{16,24},{24,16},{1,9},{9,1},{17,25},{25,17},{2,10},{10... | collective-permute-start | bytes 786440 | tf_op jit(solution)/shard_map/ppermute | solution.py:357
  1.1 10.6 %collective-permute-start.1 = (bf16[256,256]{1,0:T(8,128)(2,1)}, bf16[256,256]{1,0:T(8,128)(2,1)S(1)}, u32[]{:S(2)}, u32[]{:S(2)}) collective-permute-start(bf16[256,256]{1,0:T(8,128)(2,1)} %bitcast.17), channel_id=1, source_target_pairs={{0,1},{1,0},{2,3},{3,2},{4,5},{5,4},{6,7},{7,6},{8,9},{9,8},{10,11... | collective-permute-start | bytes 393224 | tf_op jit(solution)/shard_map/ppermute | solution.py:357
  3.7 11.6 %collective-permute-start = (bf16[256,256]{1,0:T(8,128)(2,1)}, bf16[256,256]{1,0:T(8,128)(2,1)S(1)}, u32[]{:S(2)}, u32[]{:S(2)}) collective-permute-start(bf16[256,256]{1,0:T(8,128)(2,1)} %bitcast.18), channel_id=1, source_target_pairs={{0,8},{8,0},{16,24},{24,16},{1,9},{9,1},{17,25},{25,17},{2,10},{10... | collective-permute-start | bytes 393224 | tf_op jit(solution)/shard_map/ppermute | solution.py:357
  3.9 11.5 %collective-permute-start.5 = (bf16[512,256]{1,0:T(8,128)(2,1)}, bf16[512,256]{1,0:T(8,128)(2,1)S(1)}, u32[]{:S(2)}, u32[]{:S(2)}) collective-permute-start(bf16[512,256]{1,0:T(8,128)(2,1)} %bitcast.14), channel_id=1, source_target_pairs={{8,16},{9,17},{10,18},{11,19},{12,20},{13,21},{14,22},{15,23}} | collective-permute-start | bytes 786440 | tf_op jit(solution)/shard_map/ppermute | solution.py:379
  4.6 10.7 %collective-permute-start.6 = (bf16[512,256]{1,0:T(8,128)(2,1)S(1)}, bf16[512,256]{1,0:T(8,128)(2,1)S(1)}, u32[]{:S(2)}, u32[]{:S(2)}) collective-permute-start(bf16[512,256]{1,0:T(8,128)(2,1)S(1)} %collective-permute-done.4.refs_2_), channel_id=1, source_target_pairs={{0,24},{1,25},{2,26},{3,27},{4,28},{5,29},{6,30},{7,31}} | collective-permute-start | bytes 786440 | tf_op jit(solution)/shard_map/ppermute | solution.py:380
  8.0 7.3 %copy-start.2 = (bf16[4,1,128,256]{3,2,1,0:T(8,128)(2,1)S(1)}, bf16[4,1,128,256]{3,2,1,0:T(8,128)(2,1)}, u32[]{:S(2)}) copy-start(bf16[4,1,128,256]{3,2,1,0:T(8,128)(2,1)} %param.4) | copy-start | bytes 786436
  8.0 7.3 %copy-start.3 = (bf16[2,1,128,256]{3,2,1,0:T(8,128)(2,1)S(1)}, bf16[2,1,128,256]{3,2,1,0:T(8,128)(2,1)}, u32[]{:S(2)}) copy-start(bf16[2,1,128,256]{3,2,1,0:T(8,128)(2,1)} %param.7) | copy-start | bytes 393220
  11.8 6.6 %collective-permute-start.3 = (bf16[256,256]{1,0:T(8,128)(2,1)S(1)}, bf16[256,256]{1,0:T(8,128)(2,1)S(1)}, u32[]{:S(2)}, u32[]{:S(2)}) collective-permute-start(bf16[256,256]{1,0:T(8,128)(2,1)S(1)} %collective-permute-done.1.refs_1_.refs_2_.refs_4_), channel_id=1, source_target_pairs={{0,2},{2,4},{3,1},{4,6},{5,3},{7,5},{8,10},{10,12},{11,9},{12,14},... | collective-permute-start | bytes 393224 | tf_op jit(solution)/shard_map/ppermute | solution.py:388
  15.3 3.6 %collective-permute-start.2 = (bf16[256,256]{1,0:T(8,128)(2,1)S(1)}, bf16[256,256]{1,0:T(8,128)(2,1)S(1)}, u32[]{:S(2)}, u32[]{:S(2)}) collective-permute-start(bf16[256,256]{1,0:T(8,128)(2,1)S(1)} %collective-permute-done.1.refs_1_.refs_2_.refs_4_), channel_id=1, source_target_pairs={{0,8},{8,0},{16,24},{24,16},{1,9},{9,1},{17,25},{25,17},{2,10},{10... | collective-permute-start | bytes 393224 | tf_op jit(solution)/shard_map/ppermute | solution.py:357
  18.3 2.9 %collective-permute-start.7 = (bf16[256,256]{1,0:T(8,128)(2,1)S(1)}, bf16[256,256]{1,0:T(8,128)(2,1)S(1)}, u32[]{:S(2)}, u32[]{:S(2)}) collective-permute-start(bf16[256,256]{1,0:T(8,128)(2,1)S(1)} %collective-permute-done.3.refs_3_.refs_6_), channel_id=1, source_target_pairs={{0,8},{8,0},{16,24},{24,16},{1,9},{9,1},{17,25},{25,17},{2,10},{10... | collective-permute-start | bytes 393224 | tf_op jit(solution)/shard_map/ppermute | solution.py:357
  24.1 3.0 %collective-permute-start.12 = (bf16[2,2,2,2,48,128]{5,4,3,2,1,0:T(8,128)(2,1)S(1)}, bf16[2,2,2,2,48,128]{5,4,3,2,1,0:T(8,128)(2,1)S(1)}, u32[]{:S(2)}, u32[]{:S(2)}) collective-permute-start(bf16[2,2,2,2,48,128]{5,4,3,2,1,0:T(8,128)(2,1)S(1)} %get-tuple-element.63), channel_id=1, source_target_pairs={{0,8},{8,0},{16,24},{24,16},{1,9},{9,1},{17,25},{25,17},{2,10},{10... | collective-permute-start | bytes 589832 | tf_op jit(solution)/shard_map/ppermute | solution.py:357
  24.2 12.1 %collective-permute-start.10 = (bf16[2,2,2,160,128]{4,3,2,1,0:T(8,128)(2,1)S(1)}, bf16[2,2,2,160,128]{4,3,2,1,0:T(8,128)(2,1)S(1)}, u32[]{:S(2)}, u32[]{:S(2)}) collective-permute-start(bf16[2,2,2,160,128]{4,3,2,1,0:T(8,128)(2,1)S(1)} %get-tuple-element.59), channel_id=1, source_target_pairs={{0,1},{1,0},{2,3},{3,2},{4,5},{5,4},{6,7},{7,6},{8,9},{9,8},{10,11... | collective-permute-start | bytes 983048 | tf_op jit(solution)/shard_map/ppermute | solution.py:357
  25.6 10.7 %collective-permute-start.11 = (bf16[2,2,2,160,128]{4,3,2,1,0:T(8,128)(2,1)S(1)}, bf16[2,2,2,160,128]{4,3,2,1,0:T(8,128)(2,1)S(1)}, u32[]{:S(2)}, u32[]{:S(2)}) collective-permute-start(bf16[2,2,2,160,128]{4,3,2,1,0:T(8,128)(2,1)S(1)} %get-tuple-element.61), channel_id=1, source_target_pairs={{0,2},{1,3},{2,0},{3,1},{4,6},{5,7},{6,4},{7,5},{8,10},{9,11},{10,... | collective-permute-start | bytes 983048 | tf_op jit(solution)/shard_map/ppermute | solution.py:357
  27.2 8.1 %collective-permute-start.9 = (bf16[2,2,2,112,128]{4,3,2,1,0:T(8,128)(2,1)S(1)}, bf16[2,2,2,112,128]{4,3,2,1,0:T(8,128)(2,1)S(1)}, u32[]{:S(2)}, u32[]{:S(2)}) collective-permute-start(bf16[2,2,2,112,128]{4,3,2,1,0:T(8,128)(2,1)S(1)} %get-tuple-element.57), channel_id=1, source_target_pairs={{0,16},{8,24},{16,0},{24,8},{1,17},{9,25},{17,1},{25,9},{2,18},{10... | collective-permute-start | bytes 688136 | tf_op jit(solution)/shard_map/ppermute | solution.py:357
  27.8 8.5 %collective-permute-start.13 = (bf16[2,2,2,48,128]{4,3,2,1,0:T(8,128)(2,1)S(1)}, bf16[2,2,2,48,128]{4,3,2,1,0:T(8,128)(2,1)S(1)}, u32[]{:S(2)}, u32[]{:S(2)}) collective-permute-start(bf16[2,2,2,48,128]{4,3,2,1,0:T(8,128)(2,1)S(1)} %get-tuple-element.65), channel_id=1, source_target_pairs={{0,16},{8,24},{16,0},{24,8},{1,17},{9,25},{17,1},{25,9},{2,18},{10... | collective-permute-start | bytes 294920 | tf_op jit(solution)/shard_map/ppermute | solution.py:357
  29.9 17.6 %collective-permute-start.8 = (bf16[3,256,256]{2,1,0:T(8,128)(2,1)S(1)}, bf16[3,256,256]{2,1,0:T(8,128)(2,1)S(1)}, u32[]{:S(2)}, u32[]{:S(2)}) collective-permute-start(bf16[3,256,256]{2,1,0:T(8,128)(2,1)S(1)} %get-tuple-element.54), channel_id=1, source_target_pairs={{16,8},{17,9},{18,10},{19,11},{20,12},{21,13},{22,14},{23,15}} | collective-permute-start | bytes 1179656 | tf_op jit(solution)/shard_map/ppermute | solution.py:426
  37.0 5.4 %collective-permute-start.14 = (bf16[2,2,160,128]{3,2,1,0:T(8,128)(2,1)S(1)}, bf16[2,2,160,128]{3,2,1,0:T(8,128)(2,1)S(1)}, u32[]{:S(2)}, u32[]{:S(2)}) collective-permute-start(bf16[2,2,160,128]{3,2,1,0:T(8,128)(2,1)S(1)} %get-tuple-element.67), channel_id=1, source_target_pairs={{0,1},{1,0},{2,3},{3,2},{4,5},{5,4},{6,7},{7,6},{8,9},{9,8},{10,11... | collective-permute-start | bytes 491528 | tf_op jit(solution)/shard_map/ppermute | solution.py:357
  38.6 5.3 %collective-permute-start.15 = (bf16[2,2,160,128]{3,2,1,0:T(8,128)(2,1)S(1)}, bf16[2,2,160,128]{3,2,1,0:T(8,128)(2,1)S(1)}, u32[]{:S(2)}, u32[]{:S(2)}) collective-permute-start(bf16[2,2,160,128]{3,2,1,0:T(8,128)(2,1)S(1)} %get-tuple-element.69), channel_id=1, source_target_pairs={{0,2},{1,3},{2,0},{3,1},{4,6},{5,7},{6,4},{7,5},{8,10},{9,11},{10,... | collective-permute-start | bytes 491528 | tf_op jit(solution)/shard_map/ppermute | solution.py:357
  38.9 5.3 %collective-permute-start.16 = (bf16[2,2,160,128]{3,2,1,0:T(8,128)(2,1)S(1)}, bf16[2,2,160,128]{3,2,1,0:T(8,128)(2,1)S(1)}, u32[]{:S(2)}, u32[]{:S(2)}) collective-permute-start(bf16[2,2,160,128]{3,2,1,0:T(8,128)(2,1)S(1)} %get-tuple-element.71), channel_id=1, source_target_pairs={{0,16},{8,24},{16,0},{24,8},{1,17},{9,25},{17,1},{25,9},{2,18},{10... | collective-permute-start | bytes 491528 | tf_op jit(solution)/shard_map/ppermute | solution.py:357
  44.2 3.3 %copy-start = (bf16[3,3,3,256,256]{4,3,2,1,0:T(8,128)(2,1)S(1)}, bf16[3,3,3,256,256]{4,3,2,1,0:T(8,128)(2,1)}, u32[]{:S(2)}) copy-start(bf16[3,3,3,256,256]{4,3,2,1,0:T(8,128)(2,1)} %param.5) | copy-start | bytes 10616836
  44.2 3.3 %copy-start.1 = (bf16[3,256,256]{2,1,0:T(8,128)(2,1)S(1)}, bf16[3,256,256]{2,1,0:T(8,128)(2,1)}, u32[]{:S(2)}) copy-start(bf16[3,256,256]{2,1,0:T(8,128)(2,1)} %refs_9_.1) | copy-start | bytes 1179652
  44.8 6.7 %collective-permute-start.17 = (bf16[2,160,128]{2,1,0:T(8,128)(2,1)S(1)}, bf16[2,160,128]{2,1,0:T(8,128)(2,1)S(1)}, u32[]{:S(2)}, u32[]{:S(2)}) collective-permute-start(bf16[2,160,128]{2,1,0:T(8,128)(2,1)S(1)} %get-tuple-element.73), channel_id=1, source_target_pairs={{0,2},{1,3},{2,0},{3,1},{4,6},{5,7},{6,4},{7,5},{8,10},{9,11},{10,... | collective-permute-start | bytes 245768 | tf_op jit(solution)/shard_map/ppermute | solution.py:357
  46.7 4.9 %collective-permute-start.18 = (bf16[2,160,128]{2,1,0:T(8,128)(2,1)S(1)}, bf16[2,160,128]{2,1,0:T(8,128)(2,1)S(1)}, u32[]{:S(2)}, u32[]{:S(2)}) collective-permute-start(bf16[2,160,128]{2,1,0:T(8,128)(2,1)S(1)} %get-tuple-element.75), channel_id=1, source_target_pairs={{0,16},{8,24},{16,0},{24,8},{1,17},{9,25},{17,1},{25,9},{2,18},{10... | collective-permute-start | bytes 245768 | tf_op jit(solution)/shard_map/ppermute | solution.py:357
  46.9 4.6 %collective-permute-start.19 = (bf16[2,160,128]{2,1,0:T(8,128)(2,1)S(1)}, bf16[2,160,128]{2,1,0:T(8,128)(2,1)S(1)}, u32[]{:S(2)}, u32[]{:S(2)}) collective-permute-start(bf16[2,160,128]{2,1,0:T(8,128)(2,1)S(1)} %get-tuple-element.77), channel_id=1, source_target_pairs={{0,1},{1,0},{2,3},{3,2},{4,5},{5,4},{6,7},{7,6},{8,9},{9,8},{10,11... | collective-permute-start | bytes 245768 | tf_op jit(solution)/shard_map/ppermute | solution.py:357
  52.2 7.2 %collective-permute-start.20 = (bf16[480,128]{1,0:T(8,128)(2,1)S(1)}, bf16[480,128]{1,0:T(8,128)(2,1)S(1)}, u32[]{:S(2)}, u32[]{:S(2)}) collective-permute-start(bf16[480,128]{1,0:T(8,128)(2,1)S(1)} %get-tuple-element.80), channel_id=1, source_target_pairs={{0,4},{1,5},{2,6},{3,7},{4,0},{5,1},{6,2},{7,3},{8,12},{9,13},{10,... | collective-permute-start | bytes 368648 | tf_op jit(solution)/shard_map/ppermute | solution.py:357
  54.6 6.0 %collective-permute-start.21 = (f32[480,128]{1,0:T(8,128)S(1)}, f32[480,128]{1,0:T(8,128)S(1)}, u32[]{:S(2)}, u32[]{:S(2)}) collective-permute-start(f32[480,128]{1,0:T(8,128)S(1)} %get-tuple-element.79.refs_1_), channel_id=1, source_target_pairs={{0,8},{8,0},{16,24},{24,16},{1,9},{9,1},{17,25},{25,17},{2,10},{10... | collective-permute-start | bytes 737288 | tf_op jit(solution)/shard_map/ppermute | solution.py:357
  59.3 1.3 %collective-permute-start.22 = (bf16[480,128]{1,0:T(8,128)(2,1)S(1)}, bf16[480,128]{1,0:T(8,128)(2,1)S(1)}, u32[]{:S(2)}, u32[]{:S(2)}) collective-permute-start(bf16[480,128]{1,0:T(8,128)(2,1)S(1)} %collective-permute-done.20.refs_2_), channel_id=1, source_target_pairs={{0,8},{8,0},{16,24},{24,16},{1,9},{9,1},{17,25},{25,17},{2,10},{10... | collective-permute-start | bytes 368648 | tf_op jit(solution)/shard_map/ppermute | solution.py:357

commit v6 on v5

--- a/solution.py
+++ b/solution.py
@@ -82,14 +82,13 @@
     copies += [pltpu.make_async_copy(weight_ref.at[ab, :, :, core], weights.at[ab], sems.at[ab]) for ab in range(9)]
     for copy in copies:
         copy.start()
-    same = one_hot(lax.broadcasted_iota(jnp.int32, (chans, chans), 0), chans)
     copies[0].wait()
     for k in range(3):
-        spread_ref[k * chans : (k + 1) * chans] = dot_nt(same, downs[k]).astype(BF16)
+        spread_ref[k * chans : (k + 1) * chans] = downs[k].T
     for ab in range(9):
         copies[ab + 1].wait()
         block = weights[ab].reshape(3 * chans // 2, chans)
-        turned_ref[ab] = block.T if ab % 2 else dot_nt(same, block).astype(BF16)
+        turned_ref[ab] = block.T
 
 
 def row_terms(plan, even, odd, cells, spread_ref, turned_ref, b, conv_ref):
@@ -99,12 +98,11 @@
     for s in range(5):
         begin = s // 2 * plan.cols
         cross.append(dot((even, odd)[s % 2][:, begin : begin + span], cells).astype(BF16))
-    down = None
+    threes = [jnp.concatenate(cross[a : a + 3], axis=1) for a in range(3)]
     for a in range(3):
-        three = jnp.concatenate(cross[a : a + 3], axis=1)
-        conv_ref[a] = dot(three, spread_ref[...])
-        term = dot(turned_ref[a * 3 + b], three)
-        down = term if down is None else down + term
+        conv_ref[a] = dot(threes[a], spread_ref[...])
+    turned = jnp.concatenate([turned_ref[a * 3 + b] for a in range(3)], axis=1)
+    down = dot(turned, jnp.concatenate(threes, axis=0))
     return down
 
 
@@ -208,39 +206,23 @@
                 begin = end
 
 
-def fold_kernel(plan, step, spot_ref, *refs):
-    extra = 2 if step == 1 else 0
-    ins, outs = refs[: 6 + extra], refs[6 + extra :]
-    at = 0
-    for g in range(3):
-        link = plan.orders[g][step]
-        axis = plan.axis(g, step)
-        mine = bit_of(spot_ref, link)
-        held, got = ins[2 * g], ins[2 * g + 1]
-
-        def read(where):
-            value = held[where] + got[where].astype(F32)
-            if extra and g == 0:
-                value = jnp.concatenate([value, ins[6][where] + ins[7][where].astype(F32)], axis=0)
-            return value
-
-        lead = plan.lead[step:]
-        if step < 3:
-            split_into(outs[2 * g], outs[2 * g + 1], lead, axis, mine, read)
-        else:
-            rows = slice(at, at + held.shape[-2])
-            at = at + held.shape[-2]
-            for to, where in halved(lead, axis, 1 - mine):
-                outs[0][to + (rows,)] = read(where).astype(BF16)
-            for to, where in halved(lead, axis, mine):
-                outs[1][to + (rows,)] = read(where)
-
-
-def single_kernel(plan, step, spot_ref, held, got, send, keep):
-    split_into(
-        send, keep, plan.lead[step:], plan.axis(0, step), bit_of(spot_ref, plan.orders[0][step]),
-        lambda where: held[where] + got[where].astype(F32),
-    )
+def merge_kernel(plan, step, spot_ref, *refs):
+    ins, (send, keep) = refs[:-2], refs[-2:]
+
+    def read(where):
+        return jnp.concatenate([ins[i][where] + ins[i + 1][where].astype(F32) for i in range(0, len(ins), 2)], axis=0)
+
+    split_into(send, keep, plan.lead[step:], plan.axis(0, step), bit_of(spot_ref, plan.orders[0][step]), read)
+
+
+def single_kernel(plan, g, step, spot_ref, *refs):
+    ins, (send, keep) = refs[:-2], refs[-2:]
+
+    def read(where):
+        pieces = [ins[i][where] + ins[i + 1][where].astype(F32) for i in range(0, len(ins), 2)]
+        return pieces[0] if len(pieces) == 1 else jnp.concatenate(pieces, axis=0)
+
+    split_into(send, keep, plan.lead[step:], plan.axis(g, step), bit_of(spot_ref, plan.orders[g][step]), read)
 
 
 def join_kernel(plan, spot_ref, held, got, held_other, got_other, conv_ref, down_ref, turned, down_turned):
@@ -285,13 +267,12 @@
         for u in range(half + 1):
             grads[slot, 2 * u * cols : (2 * u + 1) * cols] = even[u * cols : (u + 1) * cols]
             grads[slot, (2 * u + 1) * cols : (2 * u + 2) * cols] = odd[u * cols : (u + 1) * cols]
-    acc = [jnp.zeros((cells, chans), F32) for _ in range(3)]
-    for a in range(3):
-        for slot, b in enumerate((1, side, 2 - side)):
-            begin = (2 - a) * cols
-            part = grads[slot, begin : begin + cells]
-            for c in range(3):
-                acc[c] = acc[c] + dot_nt(part, weight_ref[a * 3 + b, c * chans : (c + 1) * chans])
+    taps = [(a, slot, b) for a in range(3) for slot, b in enumerate((1, side, 2 - side))]
+    left = jnp.concatenate([grads[slot, (2 - a) * cols : (2 - a) * cols + cells] for a, slot, _ in taps], axis=1)
+    acc = []
+    for c in range(3):
+        right = jnp.concatenate([weight_ref[a * 3 + b, c * chans : (c + 1) * chans] for a, _, b in taps], axis=1)
+        acc.append(dot_nt(left, right))
     grad_act = acc[1]
     for c in (0, 2):
         grad_act = grad_act + shifted_rows(acc[c], 1 - c, cols)
@@ -419,7 +400,7 @@
     for g in range(3):
         held += [result[2 + 2 * g], swapped(result[1 + 2 * g], plan.orders[g][0])]
     send, keep = call(
-        functools.partial(single_kernel, plan, 0), [spot], [result[8], swapped(result[7], core_link)],
+        functools.partial(single_kernel, plan, 0, 0), [spot], [result[8], swapped(result[7], core_link)],
         [shape(down_dims[1:], BF16), shape(down_dims[1:], F32)], limit=8,
     )
     down_held = [keep, swapped(send, plan.orders[0][0])]
@@ -431,21 +412,21 @@
         [pltpu.VMEM((3, (2 * half + 2) * ncols, chans), BF16)],
         us=4, limit=24,
     )
+    held = [held[:2] + down_held, held[2:4], held[4:6]]
     for step in (1, 2):
-        outs = []
         for g in range(3):
             rows = plan.cuts[g][1] - plan.cuts[g][0] + (plan.down_rows if g == 0 else 0)
-            outs += [shape(lead[step + 1 :] + (rows, part), BF16), shape(lead[step + 1 :] + (rows, part), F32)]
-        extra = down_held if step == 1 else []
-        result = call(functools.partial(fold_kernel, plan, step), [spot], held + extra, outs, limit=12)
-        held = []
-        for g in range(3):
-            held += [result[2 * g + 1], swapped(result[2 * g], plan.orders[g][step])]
+            dims = lead[step + 1 :] + (rows, part)
+            send, keep = call(
+                functools.partial(single_kernel, plan, g, step), [spot], held[g], [shape(dims, BF16), shape(dims, F32)],
+                us=0.5, limit=8,
+            )
+            held[g] = [keep, swapped(send, plan.orders[g][step])]
+    held = sum(held, [])
     for step in range(3, len(lead)):
         dims = lead[step + 1 :] + (plan.rows + plan.down_rows, part)
-        kernel = fold_kernel if step == 3 else single_kernel
         send, keep = call(
-            functools.partial(kernel, plan, step), [spot], held, [shape(dims, BF16), shape(dims, F32)], limit=8,
+            functools.partial(merge_kernel, plan, step), [spot], held, [shape(dims, BF16), shape(dims, F32)], limit=8,
             after=[done] if step == 3 else (),
         )
         held = [keep, swapped(send, plan.orders[0][step])]

time: 62.3 us -> 61 us (0.979)
  waiting for transfers between devices: 16.9 us -> 12.5 us
  starting transfers between devices: 24.4 us -> 26.6 us
  Pallas kernels: 19.9 us -> 20.7 us
    ppermute x19, waiting for transfers between devices: 16.8 us -> 12.4 us  [swapped(): lax.ppermute(value, axis, [(i, i ^ 1 << link[1]) for i in range(lax.axis_...]
    ppermute x19, starting transfers between devices: 16.2 us -> 18.4 us  [swapped(): lax.ppermute(value, axis, [(i, i ^ 1 << link[1]) for i in range(lax.axis_...]
    pallas_call x10 -> x14, Pallas kernels: 19.9 us -> 20.7 us  [call(): pl.pallas_call(run, out_shape=outs, in_specs=[smem] * len(scalars) + [hbm...]
  transfers between devices with their start and end apart: 23 -> 23, of which waited for: 7 -> 6; matrix products, arithmetic and copies ran while one was open for 0% -> 0% of each run, Pallas kernels for 24% -> 26%
where the time goes in v6:
time: 61 us; the launch traced here: 60.8 us
  starting transfers between devices  26.6 us (44%)
  Pallas kernels  20.7 us (34%)
  waiting for transfers between devices  12.5 us (20%)
  between operations  0.83 us (1%)
    pallas_call x14, Pallas kernels, call(): pl.pallas_call(run, out_shape=outs, in_specs=[smem] * len(scalars) + [hbm...  20.7 us
    ppermute x19, starting transfers between devices, swapped(): lax.ppermute(value, axis, [(i, i ^ 1 << link[1]) for i in range(lax.axis_...  18.4 us
    ppermute x19, waiting for transfers between devices, swapped(): lax.ppermute(value, axis, [(i, i ^ 1 << link[1]) for i in range(lax.axis_...  12.4 us
    ppermute x1, starting transfers between devices, body(): lax.ppermute(side, 'height', [(i, i + (2 if i % 2 == 0 else -2)) for i in...  3.49 us
    ppermute x1, starting transfers between devices, body(): lax.ppermute(clip_other, 'tm', [(i, i + 3) for i in range(0, tm_count - 3...  3.38 us
  transfers between devices with their start and end apart: 23, of which 6 were waited for; matrix products, arithmetic and copies ran while one was open for 0% of the time, Pallas kernels for 26%

profile of v6, /device:TPU:0, one launch (start us, length us, event | category | flops | bytes accessed | tf_op | source)
XLA Modules:
  0.0 60.8 jit_solution(12184462369079234235)
XLA Ops:
  0.6 0.5 collective-permute-start.4
  1.1 2.6 %collective-permute-start.1 = (bf16[256,256]{1,0:T(8,128)(2,1)}, bf16[256,256]{1,0:T(8,128)(2,1)S(1)}, u32[]{:S(2)}, u32[]{:S(2)}) collective-permute-start(bf16[256,256]{1,0:T(8,128)(2,1)} %bitcast.17), channel_id=1, source_target_pairs={{0,1},{1,0},{2,3},{3,2},{4,5},{5,4},{6,7},{7,6},{8,9},{9,8},{10,11... | collective-permute-start | bytes 393224 | tf_op jit(solution)/shard_map/ppermute | solution.py:338
  3.7 0.2 collective-permute-start
  3.9 0.7 %collective-permute-start.5 = (bf16[512,256]{1,0:T(8,128)(2,1)}, bf16[512,256]{1,0:T(8,128)(2,1)S(1)}, u32[]{:S(2)}, u32[]{:S(2)}) collective-permute-start(bf16[512,256]{1,0:T(8,128)(2,1)} %bitcast.14), channel_id=1, source_target_pairs={{8,16},{9,17},{10,18},{11,19},{12,20},{13,21},{14,22},{15,23}} | collective-permute-start | bytes 786440 | tf_op jit(solution)/shard_map/ppermute | solution.py:360
  4.6 0.1 pad_add_fusion.refs_0_
  4.6 0.0 collective-permute-done.4.refs_2_
  4.6 3.4 %collective-permute-start.6 = (bf16[512,256]{1,0:T(8,128)(2,1)S(1)}, bf16[512,256]{1,0:T(8,128)(2,1)S(1)}, u32[]{:S(2)}, u32[]{:S(2)}) collective-permute-start(bf16[512,256]{1,0:T(8,128)(2,1)S(1)} %collective-permute-done.4.refs_2_), channel_id=1, source_target_pairs={{0,24},{1,25},{2,26},{3,27},{4,28},{5,29},{6,30},{7,31}} | collective-permute-start | bytes 786440 | tf_op jit(solution)/shard_map/ppermute | solution.py:361
  8.0 0.0 copy-start.2
  8.0 0.0 copy-start.3
  8.0 2.7 %shard_map.67 = (bf16[9,256,384]{2,1,0:T(8,128)(2,1)S(1)}, bf16[768,256]{1,0:T(8,128)(2,1)S(1)}) custom-call(s32[2]{0:T(128)S(1)} %pad_add_fusion.refs_0_, bf16[9,3,8,2,16,256]{5,4,3,2,1,0:T(8,128)(2,1)} %bitcast.11, bf16[3,256,256]{2,1,0:T(8,128)(2,1)} %refs_9_.1), custom_call_target="tpu_custom_call" | custom-call | flops 3449999872 | bytes 3932160 | tf_op jit(solution)/shard_map/pallas_call | solution.py:301
  10.8 0.0 collective-permute-done.1.refs_1_.refs_2_.refs_4_
  10.8 3.5 %collective-permute-start.3 = (bf16[256,256]{1,0:T(8,128)(2,1)S(1)}, bf16[256,256]{1,0:T(8,128)(2,1)S(1)}, u32[]{:S(2)}, u32[]{:S(2)}) collective-permute-start(bf16[256,256]{1,0:T(8,128)(2,1)S(1)} %collective-permute-done.1.refs_1_.refs_2_.refs_4_), channel_id=1, source_target_pairs={{0,2},{2,4},{3,1},{4,6},{5,3},{7,5},{8,10},{10,12},{11,9},{12,14},... | collective-permute-start | bytes 393224 | tf_op jit(solution)/shard_map/ppermute | solution.py:369
  14.3 0.1 collective-permute-start.2
  14.4 2.9 %shard_map.68 = (bf16[384,768]{1,0:T(8,128)(2,1)S(1)}, bf16[384,768]{1,0:T(8,128)(2,1)S(1)}, f32[3,384,256]{2,1,0:T(8,128)S(1)}, f32[256,768]{1,0:T(8,128)S(1)}, f32[128,768]{1,0:T(8,128)S(1)}) custom-call(s32[2]{0:T(128)S(1)} %pad_add_fusion.refs_0_, bf16[512,256]{1,0:T(8,128)(2,1)S(1)} %bitcast.15, bf16[512,256]{1,0:T(8,128)(2,1)S(1)} %collective-permute-done.4.refs_2_, ...), custom_call_target="tpu_custom_call" | custom-call | flops 3449999872 | bytes 3473408 | tf_op jit(solution)/shard_map/pallas_call | solution.py:301
  17.3 0.0 collective-permute-done.3.refs_3_.refs_6_
  17.4 0.5 collective-permute-start.7
  17.9 2.2 %shard_map.69 = (f32[3,384,256]{2,1,0:T(8,128)S(1)}, f32[256,768]{1,0:T(8,128)S(1)}) custom-call(s32[2]{0:T(128)S(1)} %pad_add_fusion.refs_0_, bf16[256,256]{1,0:T(8,128)(2,1)S(1)} %collective-permute-done.1.refs_1_.refs_2_.refs_4_, bf16[256,256]{1,0:T(8,128)(2,1)S(1)} %collective-permute-done.2.refs_2_.refs_5_, ...), custom_call_target="tpu_custom_call" | custom-call | flops 2300000000 | bytes 3604480 | tf_op jit(solution)/shard_map/pallas_call | solution.py:301
  20.1 2.8 %shard_map.70 = (bf16[3,256,256]{2,1,0:T(8,128)(2,1)S(1)}, bf16[2,2,2,112,128]{4,3,2,1,0:T(8,128)(2,1)S(1)}, f32[2,2,2,112,128]{4,3,2,1,0:T(8,128)S(1)}, bf16[2,...) custom-call(s32[2]{0:T(128)S(1)} %pad_add_fusion.refs_0_, ...), custom_call_target="tpu_custom_call" | custom-call | flops 3449999872 | bytes 8192000 | tf_op jit(solution)/shard_map/pallas_call | solution.py:301
  22.9 0.1 collective-permute-start.10
  23.0 1.4 %collective-permute-start.14 = (bf16[2,2,2,160,128]{4,3,2,1,0:T(8,128)(2,1)S(1)}, bf16[2,2,2,160,128]{4,3,2,1,0:T(8,128)(2,1)S(1)}, u32[]{:S(2)}, u32[]{:S(2)}) collective-permute-start(bf16[2,2,2,160,128]{4,3,2,1,0:T(8,128)(2,1)S(1)} %get-tuple-element.67), channel_id=1, source_target_pairs={{0,1},{1,0},{2,3},{3,2},{4,5},{5,4},{6,7},{7,6},{8,9},{9,8},{10,11... | collective-permute-start | bytes 983048 | tf_op jit(solution)/shard_map/ppermute | solution.py:338
  24.4 0.2 collective-permute-start.9
  24.6 1.6 %collective-permute-start.17 = (bf16[2,2,2,160,128]{4,3,2,1,0:T(8,128)(2,1)S(1)}, bf16[2,2,2,160,128]{4,3,2,1,0:T(8,128)(2,1)S(1)}, u32[]{:S(2)}, u32[]{:S(2)}) collective-permute-start(bf16[2,2,2,160,128]{4,3,2,1,0:T(8,128)(2,1)S(1)} %get-tuple-element.73), channel_id=1, source_target_pairs={{0,2},{1,3},{2,0},{3,1},{4,6},{5,7},{6,4},{7,5},{8,10},{9,11},{10,... | collective-permute-start | bytes 983048 | tf_op jit(solution)/shard_map/ppermute | solution.py:338
  26.2 0.6 shard_map.72
  26.8 1.9 %collective-permute-start.11 = (bf16[2,2,2,48,128]{4,3,2,1,0:T(8,128)(2,1)S(1)}, bf16[2,2,2,48,128]{4,3,2,1,0:T(8,128)(2,1)S(1)}, u32[]{:S(2)}, u32[]{:S(2)}) collective-permute-start(bf16[2,2,2,48,128]{4,3,2,1,0:T(8,128)(2,1)S(1)} %get-tuple-element.61), channel_id=1, source_target_pairs={{0,16},{8,24},{16,0},{24,8},{1,17},{9,25},{17,1},{25,9},{2,18},{10... | collective-permute-start | bytes 294920 | tf_op jit(solution)/shard_map/ppermute | solution.py:338
  28.7 0.7 %collective-permute-start.8 = (bf16[3,256,256]{2,1,0:T(8,128)(2,1)S(1)}, bf16[3,256,256]{2,1,0:T(8,128)(2,1)S(1)}, u32[]{:S(2)}, u32[]{:S(2)}) collective-permute-start(bf16[3,256,256]{2,1,0:T(8,128)(2,1)S(1)} %get-tuple-element.54), channel_id=1, source_target_pairs={{16,8},{17,9},{18,10},{19,11},{20,12},{21,13},{22,14},{23,15}} | collective-permute-start | bytes 1179656 | tf_op jit(solution)/shard_map/ppermute | solution.py:407
  29.4 3.4 %collective-permute-done.9.refs_2_ = bf16[2,2,2,112,128]{4,3,2,1,0:T(8,128)(2,1)S(1)} collective-permute-done((bf16[2,2,2,112,128]{4,3,2,1,0:T(8,128)(2,1)S(1)}, bf16[2,2,2,112,128]{4,3,2,1,0:T(8,128)(2,1)S(1)}, u32[]{:S(2)}, u32[]{:S(2)}) %collective-permute-start.9) | collective-permute-done | bytes 229408 | tf_op jit(solution)/shard_map/ppermute | solution.py:338
  32.8 1.1 %collective-permute-done.11.refs_4_ = bf16[2,2,2,48,128]{4,3,2,1,0:T(8,128)(2,1)S(1)} collective-permute-done((bf16[2,2,2,48,128]{4,3,2,1,0:T(8,128)(2,1)S(1)}, bf16[2,2,2,48,128]{4,3,2,1,0:T(8,128)(2,1)S(1)}, u32[]{:S(2)}, u32[]{:S(2)}) %collective-permute-start.11) | collective-permute-done | bytes 98336 | tf_op jit(solution)/shard_map/ppermute | solution.py:338
  33.9 0.6 %shard_map.73 = (bf16[2,2,160,128]{3,2,1,0:T(8,128)(2,1)S(1)}, f32[2,2,160,128]{3,2,1,0:T(8,128)S(1)}) custom-call(s32[2]{0:T(128)S(1)} %pad_add_fusion.refs_0_, f32[2,2,2,112,128]{4,3,2,1,0:T(8,128)S(1)} %get-tuple-element.56.refs_1_, bf16[2,2,2,112,128]{4,3,2,1,0:T(8,128)(2,1)S(1)} %collective-permute-done.9.refs_2_, ...), custom_call_target="tpu_custom_call" | custom-call | flops 575000000 | bytes 983040 | tf_op jit(solution)/shard_map/pallas_call | solution.py:301
  34.5 1.1 %collective-permute-start.12 = (bf16[2,2,160,128]{3,2,1,0:T(8,128)(2,1)S(1)}, bf16[2,2,160,128]{3,2,1,0:T(8,128)(2,1)S(1)}, u32[]{:S(2)}, u32[]{:S(2)}) collective-permute-start(bf16[2,2,160,128]{3,2,1,0:T(8,128)(2,1)S(1)} %get-tuple-element.63), channel_id=1, source_target_pairs={{0,1},{1,0},{2,3},{3,2},{4,5},{5,4},{6,7},{7,6},{8,9},{9,8},{10,11... | collective-permute-start | bytes 491528 | tf_op jit(solution)/shard_map/ppermute | solution.py:338
  35.6 0.6 %shard_map.75 = (bf16[2,2,160,128]{3,2,1,0:T(8,128)(2,1)S(1)}, f32[2,2,160,128]{3,2,1,0:T(8,128)S(1)}) custom-call(s32[2]{0:T(128)S(1)} %pad_add_fusion.refs_0_, f32[2,2,2,160,128]{4,3,2,1,0:T(8,128)S(1)} %get-tuple-element.66.refs_1_, bf16[2,2,2,160,128]{4,3,2,1,0:T(8,128)(2,1)S(1)} %collective-permute-done.14.refs_2_), custom_call_target="tpu_custom_call" | custom-call | flops 575000000 | bytes 983040 | tf_op jit(solution)/shard_map/pallas_call | solution.py:301
  36.2 2.1 %collective-permute-start.15 = (bf16[2,2,160,128]{3,2,1,0:T(8,128)(2,1)S(1)}, bf16[2,2,160,128]{3,2,1,0:T(8,128)(2,1)S(1)}, u32[]{:S(2)}, u32[]{:S(2)}) collective-permute-start(bf16[2,2,160,128]{3,2,1,0:T(8,128)(2,1)S(1)} %get-tuple-element.69), channel_id=1, source_target_pairs={{0,2},{1,3},{2,0},{3,1},{4,6},{5,7},{6,4},{7,5},{8,10},{9,11},{10,... | collective-permute-start | bytes 491528 | tf_op jit(solution)/shard_map/ppermute | solution.py:338
  38.3 0.6 shard_map.77
  38.9 0.9 %collective-permute-start.18 = (bf16[2,2,160,128]{3,2,1,0:T(8,128)(2,1)S(1)}, bf16[2,2,160,128]{3,2,1,0:T(8,128)(2,1)S(1)}, u32[]{:S(2)}, u32[]{:S(2)}) collective-permute-start(bf16[2,2,160,128]{3,2,1,0:T(8,128)(2,1)S(1)} %get-tuple-element.75), channel_id=1, source_target_pairs={{0,16},{8,24},{16,0},{24,8},{1,17},{9,25},{17,1},{25,9},{2,18},{10... | collective-permute-start | bytes 491528 | tf_op jit(solution)/shard_map/ppermute | solution.py:338
  39.8 0.0 collective-permute-done.12.refs_2_
  39.9 0.6 shard_map.74
  40.4 1.6 %collective-permute-start.13 = (bf16[2,160,128]{2,1,0:T(8,128)(2,1)S(1)}, bf16[2,160,128]{2,1,0:T(8,128)(2,1)S(1)}, u32[]{:S(2)}, u32[]{:S(2)}) collective-permute-start(bf16[2,160,128]{2,1,0:T(8,128)(2,1)S(1)} %get-tuple-element.65), channel_id=1, source_target_pairs={{0,2},{1,3},{2,0},{3,1},{4,6},{5,7},{6,4},{7,5},{8,10},{9,11},{10,... | collective-permute-start | bytes 245768 | tf_op jit(solution)/shard_map/ppermute | solution.py:338
  42.1 0.6 shard_map.76
  42.7 0.8 %collective-permute-start.16 = (bf16[2,160,128]{2,1,0:T(8,128)(2,1)S(1)}, bf16[2,160,128]{2,1,0:T(8,128)(2,1)S(1)}, u32[]{:S(2)}, u32[]{:S(2)}) collective-permute-start(bf16[2,160,128]{2,1,0:T(8,128)(2,1)S(1)} %get-tuple-element.71), channel_id=1, source_target_pairs={{0,16},{8,24},{16,0},{24,8},{1,17},{9,25},{17,1},{25,9},{2,18},{10... | collective-permute-start | bytes 245768 | tf_op jit(solution)/shard_map/ppermute | solution.py:338
  43.5 1.7 %collective-permute-done.18.refs_2_ = bf16[2,2,160,128]{3,2,1,0:T(8,128)(2,1)S(1)} collective-permute-done((bf16[2,2,160,128]{3,2,1,0:T(8,128)(2,1)S(1)}, bf16[2,2,160,128]{3,2,1,0:T(8,128)(2,1)S(1)}, u32[]{:S(2)}, u32[]{:S(2)}) %collective-permute-start.18) | collective-permute-done | bytes 163872 | tf_op jit(solution)/shard_map/ppermute | solution.py:338
  45.2 0.6 shard_map.78
  45.7 0.2 collective-permute-start.19
  45.9 3.9 %shard_map.71 = (bf16[512,256]{1,0:T(8,128)(2,1)}, f32[8,128]{1,0:T(8,128)S(1)}) custom-call(s32[2]{0:T(128)S(1)} %pad_add_fusion.refs_0_, bf16[512,256]{1,0:T(8,128)(2,1)S(1)} %bitcast.16, bf16[256,256]{1,0:T(8,128)(2,1)S(1)} %bitcast.21, bf16[256,256]{1,0:T(8,128)(2,1)S(1)} %collective-permute-done.refs_6_.refs_3_, ...), custom_call_target="tpu_custom_call" | custom-call | flops 4600000000 | bytes 5373952 | tf_op jit(solution)/shard_map/pallas_call | solution.py:301
  49.8 0.4 collective-permute-done.19.refs_6_
  50.2 0.6 shard_map.79
  50.8 2.6 %collective-permute-start.20 = (bf16[480,128]{1,0:T(8,128)(2,1)S(1)}, bf16[480,128]{1,0:T(8,128)(2,1)S(1)}, u32[]{:S(2)}, u32[]{:S(2)}) collective-permute-start(bf16[480,128]{1,0:T(8,128)(2,1)S(1)} %get-tuple-element.80), channel_id=1, source_target_pairs={{0,4},{1,5},{2,6},{3,7},{4,0},{5,1},{6,2},{7,3},{8,12},{9,13},{10,... | collective-permute-start | bytes 368648 | tf_op jit(solution)/shard_map/ppermute | solution.py:338
  53.5 4.5 %collective-permute-done.20.refs_2_ = bf16[480,128]{1,0:T(8,128)(2,1)S(1)} collective-permute-done((bf16[480,128]{1,0:T(8,128)(2,1)S(1)}, bf16[480,128]{1,0:T(8,128)(2,1)S(1)}, u32[]{:S(2)}, u32[]{:S(2)}) %collective-permute-start.20) | collective-permute-done | bytes 122912 | tf_op jit(solution)/shard_map/ppermute | solution.py:338
  58.0 1.3 %collective-permute-done.22.refs_4_ = bf16[480,128]{1,0:T(8,128)(2,1)S(1)} collective-permute-done((bf16[480,128]{1,0:T(8,128)(2,1)S(1)}, bf16[480,128]{1,0:T(8,128)(2,1)S(1)}, u32[]{:S(2)}, u32[]{:S(2)}) %collective-permute-start.22) | collective-permute-done | bytes 122912 | tf_op jit(solution)/shard_map/ppermute | solution.py:338
  59.3 1.5 %shard_map.80 = (f32[64,864]{1,0:T(8,128)}, f32[64,96]{1,0:T(8,128)}) custom-call(s32[2]{0:T(128)S(1)} %pad_add_fusion.refs_0_, f32[480,128]{1,0:T(8,128)S(1)} %get-tuple-element.79.refs_1_, bf16[480,128]{1,0:T(8,128)(2,1)S(1)} %collective-permute-done.20.refs_2_, f32[480,128]{1,0:T(8,128)S(1)} %collective-permute-done.21.refs_3_, ...), custom_call_target="tpu_custom_call" | custom-call | flops 1150000000 | bytes 737280 | tf_op jit(solution)/shard_map/pallas_call | solution.py:301
  (21 shorter events, 0.1 us)
Async XLA Ops:
  0.6 4.0 %collective-permute-start.4 = (bf16[512,256]{1,0:T(8,128)(2,1)}, bf16[512,256]{1,0:T(8,128)(2,1)S(1)}, u32[]{:S(2)}, u32[]{:S(2)}) collective-permute-start(bf16[512,256]{1,0:T(8,128)(2,1)} %bitcast.13), channel_id=1, source_target_pairs={{0,8},{8,0},{16,24},{24,16},{1,9},{9,1},{17,25},{25,17},{2,10},{10... | collective-permute-start | bytes 786440 | tf_op jit(solution)/shard_map/ppermute | solution.py:338
  1.1 9.6 %collective-permute-start.1 = (bf16[256,256]{1,0:T(8,128)(2,1)}, bf16[256,256]{1,0:T(8,128)(2,1)S(1)}, u32[]{:S(2)}, u32[]{:S(2)}) collective-permute-start(bf16[256,256]{1,0:T(8,128)(2,1)} %bitcast.17), channel_id=1, source_target_pairs={{0,1},{1,0},{2,3},{3,2},{4,5},{5,4},{6,7},{7,6},{8,9},{9,8},{10,11... | collective-permute-start | bytes 393224 | tf_op jit(solution)/shard_map/ppermute | solution.py:338
  3.7 10.7 %collective-permute-start = (bf16[256,256]{1,0:T(8,128)(2,1)}, bf16[256,256]{1,0:T(8,128)(2,1)S(1)}, u32[]{:S(2)}, u32[]{:S(2)}) collective-permute-start(bf16[256,256]{1,0:T(8,128)(2,1)} %bitcast.18), channel_id=1, source_target_pairs={{0,8},{8,0},{16,24},{24,16},{1,9},{9,1},{17,25},{25,17},{2,10},{10... | collective-permute-start | bytes 393224 | tf_op jit(solution)/shard_map/ppermute | solution.py:338
  3.9 10.5 %collective-permute-start.5 = (bf16[512,256]{1,0:T(8,128)(2,1)}, bf16[512,256]{1,0:T(8,128)(2,1)S(1)}, u32[]{:S(2)}, u32[]{:S(2)}) collective-permute-start(bf16[512,256]{1,0:T(8,128)(2,1)} %bitcast.14), channel_id=1, source_target_pairs={{8,16},{9,17},{10,18},{11,19},{12,20},{13,21},{14,22},{15,23}} | collective-permute-start | bytes 786440 | tf_op jit(solution)/shard_map/ppermute | solution.py:360
  4.6 9.8 %collective-permute-start.6 = (bf16[512,256]{1,0:T(8,128)(2,1)S(1)}, bf16[512,256]{1,0:T(8,128)(2,1)S(1)}, u32[]{:S(2)}, u32[]{:S(2)}) collective-permute-start(bf16[512,256]{1,0:T(8,128)(2,1)S(1)} %collective-permute-done.4.refs_2_), channel_id=1, source_target_pairs={{0,24},{1,25},{2,26},{3,27},{4,28},{5,29},{6,30},{7,31}} | collective-permute-start | bytes 786440 | tf_op jit(solution)/shard_map/ppermute | solution.py:361
  8.0 6.4 %copy-start.2 = (bf16[4,1,128,256]{3,2,1,0:T(8,128)(2,1)S(1)}, bf16[4,1,128,256]{3,2,1,0:T(8,128)(2,1)}, u32[]{:S(2)}) copy-start(bf16[4,1,128,256]{3,2,1,0:T(8,128)(2,1)} %param.4) | copy-start | bytes 786436
  8.0 6.4 %copy-start.3 = (bf16[2,1,128,256]{3,2,1,0:T(8,128)(2,1)S(1)}, bf16[2,1,128,256]{3,2,1,0:T(8,128)(2,1)}, u32[]{:S(2)}) copy-start(bf16[2,1,128,256]{3,2,1,0:T(8,128)(2,1)} %param.7) | copy-start | bytes 393220
  10.8 6.6 %collective-permute-start.3 = (bf16[256,256]{1,0:T(8,128)(2,1)S(1)}, bf16[256,256]{1,0:T(8,128)(2,1)S(1)}, u32[]{:S(2)}, u32[]{:S(2)}) collective-permute-start(bf16[256,256]{1,0:T(8,128)(2,1)S(1)} %collective-permute-done.1.refs_1_.refs_2_.refs_4_), channel_id=1, source_target_pairs={{0,2},{2,4},{3,1},{4,6},{5,3},{7,5},{8,10},{10,12},{11,9},{12,14},... | collective-permute-start | bytes 393224 | tf_op jit(solution)/shard_map/ppermute | solution.py:369
  14.3 3.6 %collective-permute-start.2 = (bf16[256,256]{1,0:T(8,128)(2,1)S(1)}, bf16[256,256]{1,0:T(8,128)(2,1)S(1)}, u32[]{:S(2)}, u32[]{:S(2)}) collective-permute-start(bf16[256,256]{1,0:T(8,128)(2,1)S(1)} %collective-permute-done.1.refs_1_.refs_2_.refs_4_), channel_id=1, source_target_pairs={{0,8},{8,0},{16,24},{24,16},{1,9},{9,1},{17,25},{25,17},{2,10},{10... | collective-permute-start | bytes 393224 | tf_op jit(solution)/shard_map/ppermute | solution.py:338
  17.4 2.8 %collective-permute-start.7 = (bf16[256,256]{1,0:T(8,128)(2,1)S(1)}, bf16[256,256]{1,0:T(8,128)(2,1)S(1)}, u32[]{:S(2)}, u32[]{:S(2)}) collective-permute-start(bf16[256,256]{1,0:T(8,128)(2,1)S(1)} %collective-permute-done.3.refs_3_.refs_6_), channel_id=1, source_target_pairs={{0,8},{8,0},{16,24},{24,16},{1,9},{9,1},{17,25},{25,17},{2,10},{10... | collective-permute-start | bytes 393224 | tf_op jit(solution)/shard_map/ppermute | solution.py:338
  22.9 3.3 %collective-permute-start.10 = (bf16[2,2,2,2,48,128]{5,4,3,2,1,0:T(8,128)(2,1)S(1)}, bf16[2,2,2,2,48,128]{5,4,3,2,1,0:T(8,128)(2,1)S(1)}, u32[]{:S(2)}, u32[]{:S(2)}) collective-permute-start(bf16[2,2,2,2,48,128]{5,4,3,2,1,0:T(8,128)(2,1)S(1)} %get-tuple-element.59), channel_id=1, source_target_pairs={{0,8},{8,0},{16,24},{24,16},{1,9},{9,1},{17,25},{25,17},{2,10},{10... | collective-permute-start | bytes 589832 | tf_op jit(solution)/shard_map/ppermute | solution.py:338
  23.0 12.5 %collective-permute-start.14 = (bf16[2,2,2,160,128]{4,3,2,1,0:T(8,128)(2,1)S(1)}, bf16[2,2,2,160,128]{4,3,2,1,0:T(8,128)(2,1)S(1)}, u32[]{:S(2)}, u32[]{:S(2)}) collective-permute-start(bf16[2,2,2,160,128]{4,3,2,1,0:T(8,128)(2,1)S(1)} %get-tuple-element.67), channel_id=1, source_target_pairs={{0,1},{1,0},{2,3},{3,2},{4,5},{5,4},{6,7},{7,6},{8,9},{9,8},{10,11... | collective-permute-start | bytes 983048 | tf_op jit(solution)/shard_map/ppermute | solution.py:338
  24.4 8.4 %collective-permute-start.9 = (bf16[2,2,2,112,128]{4,3,2,1,0:T(8,128)(2,1)S(1)}, bf16[2,2,2,112,128]{4,3,2,1,0:T(8,128)(2,1)S(1)}, u32[]{:S(2)}, u32[]{:S(2)}) collective-permute-start(bf16[2,2,2,112,128]{4,3,2,1,0:T(8,128)(2,1)S(1)} %get-tuple-element.57), channel_id=1, source_target_pairs={{0,16},{8,24},{16,0},{24,8},{1,17},{9,25},{17,1},{25,9},{2,18},{10... | collective-permute-start | bytes 688136 | tf_op jit(solution)/shard_map/ppermute | solution.py:338
  24.6 13.7 %collective-permute-start.17 = (bf16[2,2,2,160,128]{4,3,2,1,0:T(8,128)(2,1)S(1)}, bf16[2,2,2,160,128]{4,3,2,1,0:T(8,128)(2,1)S(1)}, u32[]{:S(2)}, u32[]{:S(2)}) collective-permute-start(bf16[2,2,2,160,128]{4,3,2,1,0:T(8,128)(2,1)S(1)} %get-tuple-element.73), channel_id=1, source_target_pairs={{0,2},{1,3},{2,0},{3,1},{4,6},{5,7},{6,4},{7,5},{8,10},{9,11},{10,... | collective-permute-start | bytes 983048 | tf_op jit(solution)/shard_map/ppermute | solution.py:338
  26.8 7.1 %collective-permute-start.11 = (bf16[2,2,2,48,128]{4,3,2,1,0:T(8,128)(2,1)S(1)}, bf16[2,2,2,48,128]{4,3,2,1,0:T(8,128)(2,1)S(1)}, u32[]{:S(2)}, u32[]{:S(2)}) collective-permute-start(bf16[2,2,2,48,128]{4,3,2,1,0:T(8,128)(2,1)S(1)} %get-tuple-element.61), channel_id=1, source_target_pairs={{0,16},{8,24},{16,0},{24,8},{1,17},{9,25},{17,1},{25,9},{2,18},{10... | collective-permute-start | bytes 294920 | tf_op jit(solution)/shard_map/ppermute | solution.py:338
  28.7 17.2 %collective-permute-start.8 = (bf16[3,256,256]{2,1,0:T(8,128)(2,1)S(1)}, bf16[3,256,256]{2,1,0:T(8,128)(2,1)S(1)}, u32[]{:S(2)}, u32[]{:S(2)}) collective-permute-start(bf16[3,256,256]{2,1,0:T(8,128)(2,1)S(1)} %get-tuple-element.54), channel_id=1, source_target_pairs={{16,8},{17,9},{18,10},{19,11},{20,12},{21,13},{22,14},{23,15}} | collective-permute-start | bytes 1179656 | tf_op jit(solution)/shard_map/ppermute | solution.py:407
  34.5 5.4 %collective-permute-start.12 = (bf16[2,2,160,128]{3,2,1,0:T(8,128)(2,1)S(1)}, bf16[2,2,160,128]{3,2,1,0:T(8,128)(2,1)S(1)}, u32[]{:S(2)}, u32[]{:S(2)}) collective-permute-start(bf16[2,2,160,128]{3,2,1,0:T(8,128)(2,1)S(1)} %get-tuple-element.63), channel_id=1, source_target_pairs={{0,1},{1,0},{2,3},{3,2},{4,5},{5,4},{6,7},{7,6},{8,9},{9,8},{10,11... | collective-permute-start | bytes 491528 | tf_op jit(solution)/shard_map/ppermute | solution.py:338
  36.2 5.9 %collective-permute-start.15 = (bf16[2,2,160,128]{3,2,1,0:T(8,128)(2,1)S(1)}, bf16[2,2,160,128]{3,2,1,0:T(8,128)(2,1)S(1)}, u32[]{:S(2)}, u32[]{:S(2)}) collective-permute-start(bf16[2,2,160,128]{3,2,1,0:T(8,128)(2,1)S(1)} %get-tuple-element.69), channel_id=1, source_target_pairs={{0,2},{1,3},{2,0},{3,1},{4,6},{5,7},{6,4},{7,5},{8,10},{9,11},{10,... | collective-permute-start | bytes 491528 | tf_op jit(solution)/shard_map/ppermute | solution.py:338
  38.9 6.3 %collective-permute-start.18 = (bf16[2,2,160,128]{3,2,1,0:T(8,128)(2,1)S(1)}, bf16[2,2,160,128]{3,2,1,0:T(8,128)(2,1)S(1)}, u32[]{:S(2)}, u32[]{:S(2)}) collective-permute-start(bf16[2,2,160,128]{3,2,1,0:T(8,128)(2,1)S(1)} %get-tuple-element.75), channel_id=1, source_target_pairs={{0,16},{8,24},{16,0},{24,8},{1,17},{9,25},{17,1},{25,9},{2,18},{10... | collective-permute-start | bytes 491528 | tf_op jit(solution)/shard_map/ppermute | solution.py:338
  40.4 9.4 %collective-permute-start.13 = (bf16[2,160,128]{2,1,0:T(8,128)(2,1)S(1)}, bf16[2,160,128]{2,1,0:T(8,128)(2,1)S(1)}, u32[]{:S(2)}, u32[]{:S(2)}) collective-permute-start(bf16[2,160,128]{2,1,0:T(8,128)(2,1)S(1)} %get-tuple-element.65), channel_id=1, source_target_pairs={{0,2},{1,3},{2,0},{3,1},{4,6},{5,7},{6,4},{7,5},{8,10},{9,11},{10,... | collective-permute-start | bytes 245768 | tf_op jit(solution)/shard_map/ppermute | solution.py:338
  42.1 3.8 %copy-start = (bf16[3,3,3,256,256]{4,3,2,1,0:T(8,128)(2,1)S(1)}, bf16[3,3,3,256,256]{4,3,2,1,0:T(8,128)(2,1)}, u32[]{:S(2)}) copy-start(bf16[3,3,3,256,256]{4,3,2,1,0:T(8,128)(2,1)} %param.5) | copy-start | bytes 10616836
  42.1 3.8 %copy-start.1 = (bf16[3,256,256]{2,1,0:T(8,128)(2,1)S(1)}, bf16[3,256,256]{2,1,0:T(8,128)(2,1)}, u32[]{:S(2)}) copy-start(bf16[3,256,256]{2,1,0:T(8,128)(2,1)} %refs_9_.1) | copy-start | bytes 1179652
  42.7 7.1 %collective-permute-start.16 = (bf16[2,160,128]{2,1,0:T(8,128)(2,1)S(1)}, bf16[2,160,128]{2,1,0:T(8,128)(2,1)S(1)}, u32[]{:S(2)}, u32[]{:S(2)}) collective-permute-start(bf16[2,160,128]{2,1,0:T(8,128)(2,1)S(1)} %get-tuple-element.71), channel_id=1, source_target_pairs={{0,16},{8,24},{16,0},{24,8},{1,17},{9,25},{17,1},{25,9},{2,18},{10... | collective-permute-start | bytes 245768 | tf_op jit(solution)/shard_map/ppermute | solution.py:338
  45.7 4.5 %collective-permute-start.19 = (bf16[2,160,128]{2,1,0:T(8,128)(2,1)S(1)}, bf16[2,160,128]{2,1,0:T(8,128)(2,1)S(1)}, u32[]{:S(2)}, u32[]{:S(2)}) collective-permute-start(bf16[2,160,128]{2,1,0:T(8,128)(2,1)S(1)} %get-tuple-element.77), channel_id=1, source_target_pairs={{0,1},{1,0},{2,3},{3,2},{4,5},{5,4},{6,7},{7,6},{8,9},{9,8},{10,11... | collective-permute-start | bytes 245768 | tf_op jit(solution)/shard_map/ppermute | solution.py:338
  50.8 7.1 %collective-permute-start.20 = (bf16[480,128]{1,0:T(8,128)(2,1)S(1)}, bf16[480,128]{1,0:T(8,128)(2,1)S(1)}, u32[]{:S(2)}, u32[]{:S(2)}) collective-permute-start(bf16[480,128]{1,0:T(8,128)(2,1)S(1)} %get-tuple-element.80), channel_id=1, source_target_pairs={{0,4},{1,5},{2,6},{3,7},{4,0},{5,1},{6,2},{7,3},{8,12},{9,13},{10,... | collective-permute-start | bytes 368648 | tf_op jit(solution)/shard_map/ppermute | solution.py:338
  53.5 5.8 %collective-permute-start.21 = (f32[480,128]{1,0:T(8,128)S(1)}, f32[480,128]{1,0:T(8,128)S(1)}, u32[]{:S(2)}, u32[]{:S(2)}) collective-permute-start(f32[480,128]{1,0:T(8,128)S(1)} %get-tuple-element.79.refs_1_), channel_id=1, source_target_pairs={{0,8},{8,0},{16,24},{24,16},{1,9},{9,1},{17,25},{25,17},{2,10},{10... | collective-permute-start | bytes 737288 | tf_op jit(solution)/shard_map/ppermute | solution.py:338
  58.0 1.3 %collective-permute-start.22 = (bf16[480,128]{1,0:T(8,128)(2,1)S(1)}, bf16[480,128]{1,0:T(8,128)(2,1)S(1)}, u32[]{:S(2)}, u32[]{:S(2)}) collective-permute-start(bf16[480,128]{1,0:T(8,128)(2,1)S(1)} %collective-permute-done.20.refs_2_), channel_id=1, source_target_pairs={{0,8},{8,0},{16,24},{24,16},{1,9},{9,1},{17,25},{25,17},{2,10},{10... | collective-permute-start | bytes 368648 | tf_op jit(solution)/shard_map/ppermute | solution.py:338

commit v7 on v6

--- a/solution.py
+++ b/solution.py
@@ -248,25 +248,28 @@
         ref[...] = space[pl.ds(pl.multiple_of(core * width, width), width)]
 
 
-def input_kernel(plan, spot_ref, clip_ref, here_ref, here_other, side_ref, side_other, far_ref, far_other, next_ref,
-                 down_ref, weight_ref, out_ref, done_ref, grads):
+def grads_kernel(plan, spot_ref, here_ref, here_other, side_ref, side_other, far_ref, far_other, next_ref, spread_ref, grads, done_ref):
     cols, chans = plan.cols, plan.chans
-    cells = clip_ref.shape[0]
-    span = side_ref.shape[0]
-    half = span // cols
+    half = side_ref.shape[0] // cols
     core = spot_ref[0] & 1
-    side = 2 * (spot_ref[1] & 1)
     rows = ((here_ref, here_other), (side_ref, side_other), (far_ref, far_other))
     for slot, (own, other) in enumerate(rows):
         following = jnp.where(core == 0, other[...], next_ref[slot])
         every = jnp.concatenate([own[...], following], axis=0)
         here = every[: (half + 1) * cols]
         after = every[cols : (half + 2) * cols]
-        even = (dot_nt(after, down_ref[0]) + dot_nt(here, down_ref[2])).astype(BF16)
-        odd = dot_nt(after, down_ref[1]).astype(BF16)
+        even = (dot(after, spread_ref[:chans]) + dot(here, spread_ref[2 * chans :])).astype(BF16)
+        odd = dot(after, spread_ref[chans : 2 * chans]).astype(BF16)
         for u in range(half + 1):
             grads[slot, 2 * u * cols : (2 * u + 1) * cols] = even[u * cols : (u + 1) * cols]
             grads[slot, (2 * u + 1) * cols : (2 * u + 2) * cols] = odd[u * cols : (u + 1) * cols]
+    done_ref[...] = jnp.zeros_like(done_ref)
+
+
+def input_kernel(plan, spot_ref, clip_ref, grads, weight_ref, out_ref, done_ref):
+    cols, chans = plan.cols, plan.chans
+    cells = clip_ref.shape[0]
+    side = 2 * (spot_ref[1] & 1)
     taps = [(a, slot, b) for a in range(3) for slot, b in enumerate((1, side, 2 - side))]
     left = jnp.concatenate([grads[slot, (2 - a) * cols : (2 - a) * cols + cells] for a, slot, _ in taps], axis=1)
     acc = []
@@ -376,7 +379,7 @@
         functools.partial(own_kernel, plan), [spot],
         [flat, clip_other, first, second, mine, here_other, spread, turned],
         [shape((wide, 3 * cells // 2), BF16), shape((wide, 3 * cells // 2), BF16), *terms, shape((part, 3 * chans), F32)],
-        [pltpu.VMEM((3 * cells, chans), BF16), pltpu.VMEM((pair, chans), BF16)], us=3, limit=20,
+        [pltpu.VMEM((3 * cells, chans), BF16), pltpu.VMEM((pair, chans), BF16)], us=6, limit=20,
     )
     far, plus = lax.optimization_barrier((far, plus))
     far_other = swapped(far, core_link)
@@ -405,12 +408,14 @@
     )
     down_held = [keep, swapped(send, plan.orders[0][0])]
     following = lax.ppermute(head, "tm", [(i + 1, i) for i in range(1, tm_count - 1, 2)])
+    grads, ready = call(
+        functools.partial(grads_kernel, plan), [spot],
+        [mine, here_other, side, side_other, far, far_other, following, spread],
+        [shape((3, (2 * half + 2) * ncols, chans), BF16), shape((8, part), F32)], us=1, limit=16,
+    )
     grad_input, done = call(
-        functools.partial(input_kernel, plan), [spot],
-        [flat, mine, here_other, side, side_other, far, far_other, following, down_weight, weight],
-        [shape((cells, chans), BF16), shape((8, part), F32)],
-        [pltpu.VMEM((3, (2 * half + 2) * ncols, chans), BF16)],
-        us=4, limit=24,
+        functools.partial(input_kernel, plan), [spot], [flat, grads, weight],
+        [shape((cells, chans), BF16), shape((8, part), F32)], us=2, limit=24,
     )
     held = [held[:2] + down_held, held[2:4], held[4:6]]
     for step in (1, 2):
@@ -419,7 +424,7 @@
             dims = lead[step + 1 :] + (rows, part)
             send, keep = call(
                 functools.partial(single_kernel, plan, g, step), [spot], held[g], [shape(dims, BF16), shape(dims, F32)],
-                us=0.5, limit=8,
+                us=1, limit=8, after=[ready] if (g, step) == (2, 2) else (),
             )
             held[g] = [keep, swapped(send, plan.orders[g][step])]
     held = sum(held, [])

time: 61 us -> 60 us (0.984)
  waiting for transfers between devices: 12.5 us -> 9.77 us
  Pallas kernels: 20.7 us -> 21.4 us
    ppermute x19, waiting for transfers between devices: 12.4 us -> 9.72 us  [swapped(): lax.ppermute(value, axis, [(i, i ^ 1 << link[1]) for i in range(lax.axis_...]
    pallas_call x14 -> x15, Pallas kernels: 20.7 us -> 21.4 us  [call(): pl.pallas_call(run, out_shape=outs, in_specs=[smem] * len(scalars) + [hbm...]
  transfers between devices with their start and end apart: 23 -> 23, of which waited for: 6 -> 5; matrix products, arithmetic and copies ran while one was open for 0% -> 0% of each run, Pallas kernels for 26% -> 28%
where the time goes in v7:
time: 60 us; the launch traced here: 59.7 us
  starting transfers between devices  27 us (45%)
  Pallas kernels  21.4 us (36%)
  waiting for transfers between devices  9.77 us (16%)
  between operations  0.83 us (1%)
    pallas_call x15, Pallas kernels, call(): pl.pallas_call(run, out_shape=outs, in_specs=[smem] * len(scalars) + [hbm...  21.4 us
    ppermute x19, starting transfers between devices, swapped(): lax.ppermute(value, axis, [(i, i ^ 1 << link[1]) for i in range(lax.axis_...  18.8 us
    ppermute x19, waiting for transfers between devices, swapped(): lax.ppermute(value, axis, [(i, i ^ 1 << link[1]) for i in range(lax.axis_...  9.72 us
    ppermute x1, starting transfers between devices, body(): lax.ppermute(side, 'height', [(i, i + (2 if i % 2 == 0 else -2)) for i in...  3.49 us
    ppermute x1, starting transfers between devices, body(): lax.ppermute(clip_other, 'tm', [(i, i + 3) for i in range(0, tm_count - 3...  3.38 us
  transfers between devices with their start and end apart: 23, of which 5 were waited for; matrix products, arithmetic and copies ran while one was open for 0% of the time, Pallas kernels for 28%

profile of v7, /device:TPU:0, one launch (start us, length us, event | category | flops | bytes accessed | tf_op | source)
XLA Modules:
  0.0 59.7 jit_solution(8959796991489110561)
XLA Ops:
  0.6 0.5 collective-permute-start.4
  1.1 2.6 %collective-permute-start.1 = (bf16[256,256]{1,0:T(8,128)(2,1)}, bf16[256,256]{1,0:T(8,128)(2,1)S(1)}, u32[]{:S(2)}, u32[]{:S(2)}) collective-permute-start(bf16[256,256]{1,0:T(8,128)(2,1)} %bitcast.17), channel_id=1, source_target_pairs={{0,1},{1,0},{2,3},{3,2},{4,5},{5,4},{6,7},{7,6},{8,9},{9,8},{10,11... | collective-permute-start | bytes 393224 | tf_op jit(solution)/shard_map/ppermute | solution.py:341
  3.7 0.2 collective-permute-start
  3.9 0.7 %collective-permute-start.5 = (bf16[512,256]{1,0:T(8,128)(2,1)}, bf16[512,256]{1,0:T(8,128)(2,1)S(1)}, u32[]{:S(2)}, u32[]{:S(2)}) collective-permute-start(bf16[512,256]{1,0:T(8,128)(2,1)} %bitcast.14), channel_id=1, source_target_pairs={{8,16},{9,17},{10,18},{11,19},{12,20},{13,21},{14,22},{15,23}} | collective-permute-start | bytes 786440 | tf_op jit(solution)/shard_map/ppermute | solution.py:363
  4.6 0.1 pad_add_fusion.refs_0_
  4.6 3.4 %collective-permute-start.6 = (bf16[512,256]{1,0:T(8,128)(2,1)S(1)}, bf16[512,256]{1,0:T(8,128)(2,1)S(1)}, u32[]{:S(2)}, u32[]{:S(2)}) collective-permute-start(bf16[512,256]{1,0:T(8,128)(2,1)S(1)} %collective-permute-done.4.refs_2_), channel_id=1, source_target_pairs={{0,24},{1,25},{2,26},{3,27},{4,28},{5,29},{6,30},{7,31}} | collective-permute-start | bytes 786440 | tf_op jit(solution)/shard_map/ppermute | solution.py:364
  8.0 0.0 copy-start.1
  8.0 0.0 copy-start.2
  8.0 2.7 %shard_map.67 = (bf16[9,256,384]{2,1,0:T(8,128)(2,1)S(1)}, bf16[768,256]{1,0:T(8,128)(2,1)S(1)}) custom-call(s32[2]{0:T(128)S(1)} %pad_add_fusion.refs_0_, bf16[9,3,8,2,16,256]{5,4,3,2,1,0:T(8,128)(2,1)} %bitcast.11, bf16[3,256,256]{2,1,0:T(8,128)(2,1)} %refs_2_.1), custom_call_target="tpu_custom_call" | custom-call | flops 3449999872 | bytes 3932160 | tf_op jit(solution)/shard_map/pallas_call | solution.py:304
  10.8 3.5 %collective-permute-start.3 = (bf16[256,256]{1,0:T(8,128)(2,1)S(1)}, bf16[256,256]{1,0:T(8,128)(2,1)S(1)}, u32[]{:S(2)}, u32[]{:S(2)}) collective-permute-start(bf16[256,256]{1,0:T(8,128)(2,1)S(1)} %collective-permute-done.1.refs_1_.refs_2_.refs_3_), channel_id=1, source_target_pairs={{0,2},{2,4},{3,1},{4,6},{5,3},{7,5},{8,10},{10,12},{11,9},{12,14},... | collective-permute-start | bytes 393224 | tf_op jit(solution)/shard_map/ppermute | solution.py:372
  14.3 0.1 collective-permute-start.2
  14.4 0.0 collective-permute-done.5.refs_3_
  14.4 0.0 collective-permute-done.6.refs_4_
  14.4 2.9 %shard_map.68 = (bf16[384,768]{1,0:T(8,128)(2,1)S(1)}, bf16[384,768]{1,0:T(8,128)(2,1)S(1)}, f32[3,384,256]{2,1,0:T(8,128)S(1)}, f32[256,768]{1,0:T(8,128)S(1)}, f32[128,768]{1,0:T(8,128)S(1)}) custom-call(s32[2]{0:T(128)S(1)} %pad_add_fusion.refs_0_, bf16[512,256]{1,0:T(8,128)(2,1)S(1)} %bitcast.15, bf16[512,256]{1,0:T(8,128)(2,1)S(1)} %collective-permute-done.4.refs_2_, ...), custom_call_target="tpu_custom_call" | custom-call | flops 6899999744 | bytes 3473408 | tf_op jit(solution)/shard_map/pallas_call | solution.py:304
  17.3 0.1 collective-permute-done.3.refs_3_.refs_5_
  17.4 0.5 collective-permute-start.7
  17.9 2.2 %shard_map.69 = (f32[3,384,256]{2,1,0:T(8,128)S(1)}, f32[256,768]{1,0:T(8,128)S(1)}) custom-call(s32[2]{0:T(128)S(1)} %pad_add_fusion.refs_0_, bf16[256,256]{1,0:T(8,128)(2,1)S(1)} %collective-permute-done.1.refs_1_.refs_2_.refs_3_, bf16[256,256]{1,0:T(8,128)(2,1)S(1)} %collective-permute-done.2.refs_2_.refs_4_, ...), custom_call_target="tpu_custom_call" | custom-call | flops 2300000000 | bytes 3604480 | tf_op jit(solution)/shard_map/pallas_call | solution.py:304
  20.1 2.8 %shard_map.70 = (bf16[3,256,256]{2,1,0:T(8,128)(2,1)S(1)}, bf16[2,2,2,112,128]{4,3,2,1,0:T(8,128)(2,1)S(1)}, f32[2,2,2,112,128]{4,3,2,1,0:T(8,128)S(1)}, bf16[2,...) custom-call(s32[2]{0:T(128)S(1)} %pad_add_fusion.refs_0_, ...), custom_call_target="tpu_custom_call" | custom-call | flops 3449999872 | bytes 8192000 | tf_op jit(solution)/shard_map/pallas_call | solution.py:304
  22.9 0.1 collective-permute-start.10
  23.0 1.1 %collective-permute-start.9 = (bf16[2,2,2,112,128]{4,3,2,1,0:T(8,128)(2,1)S(1)}, bf16[2,2,2,112,128]{4,3,2,1,0:T(8,128)(2,1)S(1)}, u32[]{:S(2)}, u32[]{:S(2)}) collective-permute-start(bf16[2,2,2,112,128]{4,3,2,1,0:T(8,128)(2,1)S(1)} %get-tuple-element.60), channel_id=1, source_target_pairs={{0,16},{8,24},{16,0},{24,8},{1,17},{9,25},{17,1},{25,9},{2,18},{10... | collective-permute-start | bytes 688136 | tf_op jit(solution)/shard_map/ppermute | solution.py:341
  24.1 0.5 collective-permute-start.14
  24.6 1.6 %collective-permute-start.17 = (bf16[2,2,2,160,128]{4,3,2,1,0:T(8,128)(2,1)S(1)}, bf16[2,2,2,160,128]{4,3,2,1,0:T(8,128)(2,1)S(1)}, u32[]{:S(2)}, u32[]{:S(2)}) collective-permute-start(bf16[2,2,2,160,128]{4,3,2,1,0:T(8,128)(2,1)S(1)} %get-tuple-element.76), channel_id=1, source_target_pairs={{0,2},{1,3},{2,0},{3,1},{4,6},{5,7},{6,4},{7,5},{8,10},{9,11},{10,... | collective-permute-start | bytes 983048 | tf_op jit(solution)/shard_map/ppermute | solution.py:341
  26.2 0.6 shard_map.73
  26.8 1.9 %collective-permute-start.11 = (bf16[2,2,2,48,128]{4,3,2,1,0:T(8,128)(2,1)S(1)}, bf16[2,2,2,48,128]{4,3,2,1,0:T(8,128)(2,1)S(1)}, u32[]{:S(2)}, u32[]{:S(2)}) collective-permute-start(bf16[2,2,2,48,128]{4,3,2,1,0:T(8,128)(2,1)S(1)} %get-tuple-element.64), channel_id=1, source_target_pairs={{0,16},{8,24},{16,0},{24,8},{1,17},{9,25},{17,1},{25,9},{2,18},{10... | collective-permute-start | bytes 294920 | tf_op jit(solution)/shard_map/ppermute | solution.py:341
  28.7 0.7 %collective-permute-start.8 = (bf16[3,256,256]{2,1,0:T(8,128)(2,1)S(1)}, bf16[3,256,256]{2,1,0:T(8,128)(2,1)S(1)}, u32[]{:S(2)}, u32[]{:S(2)}) collective-permute-start(bf16[3,256,256]{2,1,0:T(8,128)(2,1)S(1)} %get-tuple-element.56), channel_id=1, source_target_pairs={{16,8},{17,9},{18,10},{19,11},{20,12},{21,13},{22,14},{23,15}} | collective-permute-start | bytes 1179656 | tf_op jit(solution)/shard_map/ppermute | solution.py:410
  29.3 2.1 %collective-permute-done.9.refs_2_ = bf16[2,2,2,112,128]{4,3,2,1,0:T(8,128)(2,1)S(1)} collective-permute-done((bf16[2,2,2,112,128]{4,3,2,1,0:T(8,128)(2,1)S(1)}, bf16[2,2,2,112,128]{4,3,2,1,0:T(8,128)(2,1)S(1)}, u32[]{:S(2)}, u32[]{:S(2)}) %collective-permute-start.9) | collective-permute-done | bytes 229408 | tf_op jit(solution)/shard_map/ppermute | solution.py:341
  31.4 1.7 %collective-permute-done.11.refs_4_ = bf16[2,2,2,48,128]{4,3,2,1,0:T(8,128)(2,1)S(1)} collective-permute-done((bf16[2,2,2,48,128]{4,3,2,1,0:T(8,128)(2,1)S(1)}, bf16[2,2,2,48,128]{4,3,2,1,0:T(8,128)(2,1)S(1)}, u32[]{:S(2)}, u32[]{:S(2)}) %collective-permute-start.11) | collective-permute-done | bytes 98336 | tf_op jit(solution)/shard_map/ppermute | solution.py:341
  33.1 0.6 %shard_map.74 = (bf16[2,2,160,128]{3,2,1,0:T(8,128)(2,1)S(1)}, f32[2,2,160,128]{3,2,1,0:T(8,128)S(1)}) custom-call(s32[2]{0:T(128)S(1)} %pad_add_fusion.refs_0_, f32[2,2,2,112,128]{4,3,2,1,0:T(8,128)S(1)} %get-tuple-element.59.refs_1_, bf16[2,2,2,112,128]{4,3,2,1,0:T(8,128)(2,1)S(1)} %collective-permute-done.9.refs_2_, ...), custom_call_target="tpu_custom_call" | custom-call | flops 1150000000 | bytes 983040 | tf_op jit(solution)/shard_map/pallas_call | solution.py:304
  33.7 1.1 %collective-permute-start.12 = (bf16[2,2,160,128]{3,2,1,0:T(8,128)(2,1)S(1)}, bf16[2,2,160,128]{3,2,1,0:T(8,128)(2,1)S(1)}, u32[]{:S(2)}, u32[]{:S(2)}) collective-permute-start(bf16[2,2,160,128]{3,2,1,0:T(8,128)(2,1)S(1)} %get-tuple-element.66), channel_id=1, source_target_pairs={{0,1},{1,0},{2,3},{3,2},{4,5},{5,4},{6,7},{7,6},{8,9},{9,8},{10,11... | collective-permute-start | bytes 491528 | tf_op jit(solution)/shard_map/ppermute | solution.py:341
  34.8 0.6 %shard_map.76 = (bf16[2,2,160,128]{3,2,1,0:T(8,128)(2,1)S(1)}, f32[2,2,160,128]{3,2,1,0:T(8,128)S(1)}) custom-call(s32[2]{0:T(128)S(1)} %pad_add_fusion.refs_0_, f32[2,2,2,160,128]{4,3,2,1,0:T(8,128)S(1)} %get-tuple-element.69.refs_1_, bf16[2,2,2,160,128]{4,3,2,1,0:T(8,128)(2,1)S(1)} %collective-permute-done.14.refs_2_), custom_call_target="tpu_custom_call" | custom-call | flops 1150000000 | bytes 983040 | tf_op jit(solution)/shard_map/pallas_call | solution.py:304
  35.4 1.6 %collective-permute-start.15 = (bf16[2,2,160,128]{3,2,1,0:T(8,128)(2,1)S(1)}, bf16[2,2,160,128]{3,2,1,0:T(8,128)(2,1)S(1)}, u32[]{:S(2)}, u32[]{:S(2)}) collective-permute-start(bf16[2,2,160,128]{3,2,1,0:T(8,128)(2,1)S(1)} %get-tuple-element.72), channel_id=1, source_target_pairs={{0,2},{1,3},{2,0},{3,1},{4,6},{5,7},{6,4},{7,5},{8,10},{9,11},{10,... | collective-permute-start | bytes 491528 | tf_op jit(solution)/shard_map/ppermute | solution.py:341
  37.0 0.6 %shard_map.78 = (bf16[2,2,160,128]{3,2,1,0:T(8,128)(2,1)S(1)}, f32[2,2,160,128]{3,2,1,0:T(8,128)S(1)}) custom-call(s32[2]{0:T(128)S(1)} %pad_add_fusion.refs_0_, f32[2,2,2,160,128]{4,3,2,1,0:T(8,128)S(1)} %get-tuple-element.75.refs_1_, bf16[2,2,2,160,128]{4,3,2,1,0:T(8,128)(2,1)S(1)} %collective-permute-done.17.refs_2_), custom_call_target="tpu_custom_call" | custom-call | flops 1150000000 | bytes 983040 | tf_op jit(solution)/shard_map/pallas_call | solution.py:304
  37.6 0.6 %collective-permute-start.18 = (bf16[2,2,160,128]{3,2,1,0:T(8,128)(2,1)S(1)}, bf16[2,2,160,128]{3,2,1,0:T(8,128)(2,1)S(1)}, u32[]{:S(2)}, u32[]{:S(2)}) collective-permute-start(bf16[2,2,160,128]{3,2,1,0:T(8,128)(2,1)S(1)} %get-tuple-element.78), channel_id=1, source_target_pairs={{0,16},{8,24},{16,0},{24,8},{1,17},{9,25},{17,1},{25,9},{2,18},{10... | collective-permute-start | bytes 491528 | tf_op jit(solution)/shard_map/ppermute | solution.py:341
  38.3 1.2 %shard_map.71 = (bf16[3,768,256]{2,1,0:T(8,128)(2,1)S(1)}, f32[8,128]{1,0:T(8,128)S(1)}) custom-call(s32[2]{0:T(128)S(1)} %pad_add_fusion.refs_0_, bf16[256,256]{1,0:T(8,128)(2,1)S(1)} %bitcast.21, bf16[256,256]{1,0:T(8,128)(2,1)S(1)} %collective-permute-done.refs_6_.refs_2_, bf16[256,256]{1,0:T(8,128)(2,1)S(1)} %collective-permute-done.1.refs_1_.refs_2_.refs_3_, ...), custom_call_target="tpu_custom_call" | custom-call | flops 1150000000 | bytes 1572864 | tf_op jit(solution)/shard_map/pallas_call | solution.py:304
  39.5 0.1 collective-permute-done.12.refs_2_
  39.5 0.6 shard_map.75
  40.1 1.7 %collective-permute-start.13 = (bf16[2,160,128]{2,1,0:T(8,128)(2,1)S(1)}, bf16[2,160,128]{2,1,0:T(8,128)(2,1)S(1)}, u32[]{:S(2)}, u32[]{:S(2)}) collective-permute-start(bf16[2,160,128]{2,1,0:T(8,128)(2,1)S(1)} %get-tuple-element.68), channel_id=1, source_target_pairs={{0,2},{1,3},{2,0},{3,1},{4,6},{5,7},{6,4},{7,5},{8,10},{9,11},{10,... | collective-permute-start | bytes 245768 | tf_op jit(solution)/shard_map/ppermute | solution.py:341
  41.8 0.6 shard_map.77
  42.4 1.3 %collective-permute-start.16 = (bf16[2,160,128]{2,1,0:T(8,128)(2,1)S(1)}, bf16[2,160,128]{2,1,0:T(8,128)(2,1)S(1)}, u32[]{:S(2)}, u32[]{:S(2)}) collective-permute-start(bf16[2,160,128]{2,1,0:T(8,128)(2,1)S(1)} %get-tuple-element.74), channel_id=1, source_target_pairs={{0,16},{8,24},{16,0},{24,8},{1,17},{9,25},{17,1},{25,9},{2,18},{10... | collective-permute-start | bytes 245768 | tf_op jit(solution)/shard_map/ppermute | solution.py:341
  43.7 0.6 shard_map.79
  44.3 0.9 %collective-permute-start.19 = (bf16[2,160,128]{2,1,0:T(8,128)(2,1)S(1)}, bf16[2,160,128]{2,1,0:T(8,128)(2,1)S(1)}, u32[]{:S(2)}, u32[]{:S(2)}) collective-permute-start(bf16[2,160,128]{2,1,0:T(8,128)(2,1)S(1)} %get-tuple-element.81), channel_id=1, source_target_pairs={{0,1},{1,0},{2,3},{3,2},{4,5},{5,4},{6,7},{7,6},{8,9},{9,8},{10,11... | collective-permute-start | bytes 245768 | tf_op jit(solution)/shard_map/ppermute | solution.py:341
  45.2 0.6 copy-done
  45.7 3.4 %shard_map.72 = (bf16[512,256]{1,0:T(8,128)(2,1)}, f32[8,128]{1,0:T(8,128)S(1)}) custom-call(s32[2]{0:T(128)S(1)} %pad_add_fusion.refs_0_, bf16[512,256]{1,0:T(8,128)(2,1)S(1)} %bitcast.16, bf16[3,768,256]{2,1,0:T(8,128)(2,1)S(1)} %get-tuple-element.57.refs_2_, bf16[9,768,256]{2,1,0:T(8,128)(2,1)S(1)} %bitcast.12), custom_call_target="tpu_custom_call" | custom-call | flops 2300000000 | bytes 4980736 | tf_op jit(solution)/shard_map/pallas_call | solution.py:304
  49.2 0.6 %shard_map.80 = (bf16[480,128]{1,0:T(8,128)(2,1)S(1)}, f32[480,128]{1,0:T(8,128)S(1)}) custom-call(s32[2]{0:T(128)S(1)} %pad_add_fusion.refs_0_, f32[2,160,128]{2,1,0:T(8,128)S(1)} %get-tuple-element.67.refs_1_, bf16[2,160,128]{2,1,0:T(8,128)(2,1)S(1)} %collective-permute-done.13.refs_2_, f32[2,160,128]{2,1,0:T(8,128)S(1)} %get-tuple-element.73.refs_3_, ...), custom_call_target="tpu_custom_call" | custom-call | flops 1150000000 | bytes 737280 | tf_op jit(solution)/shard_map/pallas_call | solution.py:304
  49.8 2.6 %collective-permute-start.20 = (bf16[480,128]{1,0:T(8,128)(2,1)S(1)}, bf16[480,128]{1,0:T(8,128)(2,1)S(1)}, u32[]{:S(2)}, u32[]{:S(2)}) collective-permute-start(bf16[480,128]{1,0:T(8,128)(2,1)S(1)} %get-tuple-element.84), channel_id=1, source_target_pairs={{0,4},{1,5},{2,6},{3,7},{4,0},{5,1},{6,2},{7,3},{8,12},{9,13},{10,... | collective-permute-start | bytes 368648 | tf_op jit(solution)/shard_map/ppermute | solution.py:341
  52.4 4.5 %collective-permute-done.20.refs_2_ = bf16[480,128]{1,0:T(8,128)(2,1)S(1)} collective-permute-done((bf16[480,128]{1,0:T(8,128)(2,1)S(1)}, bf16[480,128]{1,0:T(8,128)(2,1)S(1)}, u32[]{:S(2)}, u32[]{:S(2)}) %collective-permute-start.20) | collective-permute-done | bytes 122912 | tf_op jit(solution)/shard_map/ppermute | solution.py:341
  56.9 1.3 %collective-permute-done.22.refs_4_ = bf16[480,128]{1,0:T(8,128)(2,1)S(1)} collective-permute-done((bf16[480,128]{1,0:T(8,128)(2,1)S(1)}, bf16[480,128]{1,0:T(8,128)(2,1)S(1)}, u32[]{:S(2)}, u32[]{:S(2)}) %collective-permute-start.22) | collective-permute-done | bytes 122912 | tf_op jit(solution)/shard_map/ppermute | solution.py:341
  58.3 1.5 %shard_map.81 = (f32[64,864]{1,0:T(8,128)}, f32[64,96]{1,0:T(8,128)}) custom-call(s32[2]{0:T(128)S(1)} %pad_add_fusion.refs_0_, f32[480,128]{1,0:T(8,128)S(1)} %get-tuple-element.83.refs_1_, bf16[480,128]{1,0:T(8,128)(2,1)S(1)} %collective-permute-done.20.refs_2_, f32[480,128]{1,0:T(8,128)S(1)} %collective-permute-done.21.refs_3_, ...), custom_call_target="tpu_custom_call" | custom-call | flops 1150000000 | bytes 737280 | tf_op jit(solution)/shard_map/pallas_call | solution.py:304
  (20 shorter events, 0.1 us)
Async XLA Ops:
  0.6 4.0 %collective-permute-start.4 = (bf16[512,256]{1,0:T(8,128)(2,1)}, bf16[512,256]{1,0:T(8,128)(2,1)S(1)}, u32[]{:S(2)}, u32[]{:S(2)}) collective-permute-start(bf16[512,256]{1,0:T(8,128)(2,1)} %bitcast.13), channel_id=1, source_target_pairs={{0,8},{8,0},{16,24},{24,16},{1,9},{9,1},{17,25},{25,17},{2,10},{10... | collective-permute-start | bytes 786440 | tf_op jit(solution)/shard_map/ppermute | solution.py:341
  1.1 9.6 %collective-permute-start.1 = (bf16[256,256]{1,0:T(8,128)(2,1)}, bf16[256,256]{1,0:T(8,128)(2,1)S(1)}, u32[]{:S(2)}, u32[]{:S(2)}) collective-permute-start(bf16[256,256]{1,0:T(8,128)(2,1)} %bitcast.17), channel_id=1, source_target_pairs={{0,1},{1,0},{2,3},{3,2},{4,5},{5,4},{6,7},{7,6},{8,9},{9,8},{10,11... | collective-permute-start | bytes 393224 | tf_op jit(solution)/shard_map/ppermute | solution.py:341
  3.7 10.7 %collective-permute-start = (bf16[256,256]{1,0:T(8,128)(2,1)}, bf16[256,256]{1,0:T(8,128)(2,1)S(1)}, u32[]{:S(2)}, u32[]{:S(2)}) collective-permute-start(bf16[256,256]{1,0:T(8,128)(2,1)} %bitcast.18), channel_id=1, source_target_pairs={{0,8},{8,0},{16,24},{24,16},{1,9},{9,1},{17,25},{25,17},{2,10},{10... | collective-permute-start | bytes 393224 | tf_op jit(solution)/shard_map/ppermute | solution.py:341
  3.9 10.5 %collective-permute-start.5 = (bf16[512,256]{1,0:T(8,128)(2,1)}, bf16[512,256]{1,0:T(8,128)(2,1)S(1)}, u32[]{:S(2)}, u32[]{:S(2)}) collective-permute-start(bf16[512,256]{1,0:T(8,128)(2,1)} %bitcast.14), channel_id=1, source_target_pairs={{8,16},{9,17},{10,18},{11,19},{12,20},{13,21},{14,22},{15,23}} | collective-permute-start | bytes 786440 | tf_op jit(solution)/shard_map/ppermute | solution.py:363
  4.6 9.8 %collective-permute-start.6 = (bf16[512,256]{1,0:T(8,128)(2,1)S(1)}, bf16[512,256]{1,0:T(8,128)(2,1)S(1)}, u32[]{:S(2)}, u32[]{:S(2)}) collective-permute-start(bf16[512,256]{1,0:T(8,128)(2,1)S(1)} %collective-permute-done.4.refs_2_), channel_id=1, source_target_pairs={{0,24},{1,25},{2,26},{3,27},{4,28},{5,29},{6,30},{7,31}} | collective-permute-start | bytes 786440 | tf_op jit(solution)/shard_map/ppermute | solution.py:364
  8.0 6.4 %copy-start.1 = (bf16[4,1,128,256]{3,2,1,0:T(8,128)(2,1)S(1)}, bf16[4,1,128,256]{3,2,1,0:T(8,128)(2,1)}, u32[]{:S(2)}) copy-start(bf16[4,1,128,256]{3,2,1,0:T(8,128)(2,1)} %param.4) | copy-start | bytes 786436
  8.0 6.4 %copy-start.2 = (bf16[2,1,128,256]{3,2,1,0:T(8,128)(2,1)S(1)}, bf16[2,1,128,256]{3,2,1,0:T(8,128)(2,1)}, u32[]{:S(2)}) copy-start(bf16[2,1,128,256]{3,2,1,0:T(8,128)(2,1)} %param.7) | copy-start | bytes 393220
  10.8 6.6 %collective-permute-start.3 = (bf16[256,256]{1,0:T(8,128)(2,1)S(1)}, bf16[256,256]{1,0:T(8,128)(2,1)S(1)}, u32[]{:S(2)}, u32[]{:S(2)}) collective-permute-start(bf16[256,256]{1,0:T(8,128)(2,1)S(1)} %collective-permute-done.1.refs_1_.refs_2_.refs_3_), channel_id=1, source_target_pairs={{0,2},{2,4},{3,1},{4,6},{5,3},{7,5},{8,10},{10,12},{11,9},{12,14},... | collective-permute-start | bytes 393224 | tf_op jit(solution)/shard_map/ppermute | solution.py:372
  14.3 3.6 %collective-permute-start.2 = (bf16[256,256]{1,0:T(8,128)(2,1)S(1)}, bf16[256,256]{1,0:T(8,128)(2,1)S(1)}, u32[]{:S(2)}, u32[]{:S(2)}) collective-permute-start(bf16[256,256]{1,0:T(8,128)(2,1)S(1)} %collective-permute-done.1.refs_1_.refs_2_.refs_3_), channel_id=1, source_target_pairs={{0,8},{8,0},{16,24},{24,16},{1,9},{9,1},{17,25},{25,17},{2,10},{10... | collective-permute-start | bytes 393224 | tf_op jit(solution)/shard_map/ppermute | solution.py:341
  17.4 2.7 %collective-permute-start.7 = (bf16[256,256]{1,0:T(8,128)(2,1)S(1)}, bf16[256,256]{1,0:T(8,128)(2,1)S(1)}, u32[]{:S(2)}, u32[]{:S(2)}) collective-permute-start(bf16[256,256]{1,0:T(8,128)(2,1)S(1)} %collective-permute-done.3.refs_3_.refs_5_), channel_id=1, source_target_pairs={{0,8},{8,0},{16,24},{24,16},{1,9},{9,1},{17,25},{25,17},{2,10},{10... | collective-permute-start | bytes 393224 | tf_op jit(solution)/shard_map/ppermute | solution.py:341
  22.9 3.3 %collective-permute-start.10 = (bf16[2,2,2,2,48,128]{5,4,3,2,1,0:T(8,128)(2,1)S(1)}, bf16[2,2,2,2,48,128]{5,4,3,2,1,0:T(8,128)(2,1)S(1)}, u32[]{:S(2)}, u32[]{:S(2)}) collective-permute-start(bf16[2,2,2,2,48,128]{5,4,3,2,1,0:T(8,128)(2,1)S(1)} %get-tuple-element.62), channel_id=1, source_target_pairs={{0,8},{8,0},{16,24},{24,16},{1,9},{9,1},{17,25},{25,17},{2,10},{10... | collective-permute-start | bytes 589832 | tf_op jit(solution)/shard_map/ppermute | solution.py:341
  23.0 8.5 %collective-permute-start.9 = (bf16[2,2,2,112,128]{4,3,2,1,0:T(8,128)(2,1)S(1)}, bf16[2,2,2,112,128]{4,3,2,1,0:T(8,128)(2,1)S(1)}, u32[]{:S(2)}, u32[]{:S(2)}) collective-permute-start(bf16[2,2,2,112,128]{4,3,2,1,0:T(8,128)(2,1)S(1)} %get-tuple-element.60), channel_id=1, source_target_pairs={{0,16},{8,24},{16,0},{24,8},{1,17},{9,25},{17,1},{25,9},{2,18},{10... | collective-permute-start | bytes 688136 | tf_op jit(solution)/shard_map/ppermute | solution.py:341
  24.1 10.7 %collective-permute-start.14 = (bf16[2,2,2,160,128]{4,3,2,1,0:T(8,128)(2,1)S(1)}, bf16[2,2,2,160,128]{4,3,2,1,0:T(8,128)(2,1)S(1)}, u32[]{:S(2)}, u32[]{:S(2)}) collective-permute-start(bf16[2,2,2,160,128]{4,3,2,1,0:T(8,128)(2,1)S(1)} %get-tuple-element.70), channel_id=1, source_target_pairs={{0,1},{1,0},{2,3},{3,2},{4,5},{5,4},{6,7},{7,6},{8,9},{9,8},{10,11... | collective-permute-start | bytes 983048 | tf_op jit(solution)/shard_map/ppermute | solution.py:341
  24.6 12.4 %collective-permute-start.17 = (bf16[2,2,2,160,128]{4,3,2,1,0:T(8,128)(2,1)S(1)}, bf16[2,2,2,160,128]{4,3,2,1,0:T(8,128)(2,1)S(1)}, u32[]{:S(2)}, u32[]{:S(2)}) collective-permute-start(bf16[2,2,2,160,128]{4,3,2,1,0:T(8,128)(2,1)S(1)} %get-tuple-element.76), channel_id=1, source_target_pairs={{0,2},{1,3},{2,0},{3,1},{4,6},{5,7},{6,4},{7,5},{8,10},{9,11},{10,... | collective-permute-start | bytes 983048 | tf_op jit(solution)/shard_map/ppermute | solution.py:341
  26.8 6.3 %collective-permute-start.11 = (bf16[2,2,2,48,128]{4,3,2,1,0:T(8,128)(2,1)S(1)}, bf16[2,2,2,48,128]{4,3,2,1,0:T(8,128)(2,1)S(1)}, u32[]{:S(2)}, u32[]{:S(2)}) collective-permute-start(bf16[2,2,2,48,128]{4,3,2,1,0:T(8,128)(2,1)S(1)} %get-tuple-element.64), channel_id=1, source_target_pairs={{0,16},{8,24},{16,0},{24,8},{1,17},{9,25},{17,1},{25,9},{2,18},{10... | collective-permute-start | bytes 294920 | tf_op jit(solution)/shard_map/ppermute | solution.py:341
  28.7 9.6 %collective-permute-start.8 = (bf16[3,256,256]{2,1,0:T(8,128)(2,1)S(1)}, bf16[3,256,256]{2,1,0:T(8,128)(2,1)S(1)}, u32[]{:S(2)}, u32[]{:S(2)}) collective-permute-start(bf16[3,256,256]{2,1,0:T(8,128)(2,1)S(1)} %get-tuple-element.56), channel_id=1, source_target_pairs={{16,8},{17,9},{18,10},{19,11},{20,12},{21,13},{22,14},{23,15}} | collective-permute-start | bytes 1179656 | tf_op jit(solution)/shard_map/ppermute | solution.py:410
  33.7 5.8 %collective-permute-start.12 = (bf16[2,2,160,128]{3,2,1,0:T(8,128)(2,1)S(1)}, bf16[2,2,160,128]{3,2,1,0:T(8,128)(2,1)S(1)}, u32[]{:S(2)}, u32[]{:S(2)}) collective-permute-start(bf16[2,2,160,128]{3,2,1,0:T(8,128)(2,1)S(1)} %get-tuple-element.66), channel_id=1, source_target_pairs={{0,1},{1,0},{2,3},{3,2},{4,5},{5,4},{6,7},{7,6},{8,9},{9,8},{10,11... | collective-permute-start | bytes 491528 | tf_op jit(solution)/shard_map/ppermute | solution.py:341
  35.4 6.4 %collective-permute-start.15 = (bf16[2,2,160,128]{3,2,1,0:T(8,128)(2,1)S(1)}, bf16[2,2,160,128]{3,2,1,0:T(8,128)(2,1)S(1)}, u32[]{:S(2)}, u32[]{:S(2)}) collective-permute-start(bf16[2,2,160,128]{3,2,1,0:T(8,128)(2,1)S(1)} %get-tuple-element.72), channel_id=1, source_target_pairs={{0,2},{1,3},{2,0},{3,1},{4,6},{5,7},{6,4},{7,5},{8,10},{9,11},{10,... | collective-permute-start | bytes 491528 | tf_op jit(solution)/shard_map/ppermute | solution.py:341
  37.6 6.1 %collective-permute-start.18 = (bf16[2,2,160,128]{3,2,1,0:T(8,128)(2,1)S(1)}, bf16[2,2,160,128]{3,2,1,0:T(8,128)(2,1)S(1)}, u32[]{:S(2)}, u32[]{:S(2)}) collective-permute-start(bf16[2,2,160,128]{3,2,1,0:T(8,128)(2,1)S(1)} %get-tuple-element.78), channel_id=1, source_target_pairs={{0,16},{8,24},{16,0},{24,8},{1,17},{9,25},{17,1},{25,9},{2,18},{10... | collective-permute-start | bytes 491528 | tf_op jit(solution)/shard_map/ppermute | solution.py:341
  40.1 9.0 %collective-permute-start.13 = (bf16[2,160,128]{2,1,0:T(8,128)(2,1)S(1)}, bf16[2,160,128]{2,1,0:T(8,128)(2,1)S(1)}, u32[]{:S(2)}, u32[]{:S(2)}) collective-permute-start(bf16[2,160,128]{2,1,0:T(8,128)(2,1)S(1)} %get-tuple-element.68), channel_id=1, source_target_pairs={{0,2},{1,3},{2,0},{3,1},{4,6},{5,7},{6,4},{7,5},{8,10},{9,11},{10,... | collective-permute-start | bytes 245768 | tf_op jit(solution)/shard_map/ppermute | solution.py:341
  42.4 6.8 %collective-permute-start.16 = (bf16[2,160,128]{2,1,0:T(8,128)(2,1)S(1)}, bf16[2,160,128]{2,1,0:T(8,128)(2,1)S(1)}, u32[]{:S(2)}, u32[]{:S(2)}) collective-permute-start(bf16[2,160,128]{2,1,0:T(8,128)(2,1)S(1)} %get-tuple-element.74), channel_id=1, source_target_pairs={{0,16},{8,24},{16,0},{24,8},{1,17},{9,25},{17,1},{25,9},{2,18},{10... | collective-permute-start | bytes 245768 | tf_op jit(solution)/shard_map/ppermute | solution.py:341
  43.7 2.0 %copy-start = (bf16[3,3,3,256,256]{4,3,2,1,0:T(8,128)(2,1)S(1)}, bf16[3,3,3,256,256]{4,3,2,1,0:T(8,128)(2,1)}, u32[]{:S(2)}) copy-start(bf16[3,3,3,256,256]{4,3,2,1,0:T(8,128)(2,1)} %param.5) | copy-start | bytes 10616836
  44.3 4.8 %collective-permute-start.19 = (bf16[2,160,128]{2,1,0:T(8,128)(2,1)S(1)}, bf16[2,160,128]{2,1,0:T(8,128)(2,1)S(1)}, u32[]{:S(2)}, u32[]{:S(2)}) collective-permute-start(bf16[2,160,128]{2,1,0:T(8,128)(2,1)S(1)} %get-tuple-element.81), channel_id=1, source_target_pairs={{0,1},{1,0},{2,3},{3,2},{4,5},{5,4},{6,7},{7,6},{8,9},{9,8},{10,11... | collective-permute-start | bytes 245768 | tf_op jit(solution)/shard_map/ppermute | solution.py:341
  49.8 7.2 %collective-permute-start.20 = (bf16[480,128]{1,0:T(8,128)(2,1)S(1)}, bf16[480,128]{1,0:T(8,128)(2,1)S(1)}, u32[]{:S(2)}, u32[]{:S(2)}) collective-permute-start(bf16[480,128]{1,0:T(8,128)(2,1)S(1)} %get-tuple-element.84), channel_id=1, source_target_pairs={{0,4},{1,5},{2,6},{3,7},{4,0},{5,1},{6,2},{7,3},{8,12},{9,13},{10,... | collective-permute-start | bytes 368648 | tf_op jit(solution)/shard_map/ppermute | solution.py:341
  52.4 5.9 %collective-permute-start.21 = (f32[480,128]{1,0:T(8,128)S(1)}, f32[480,128]{1,0:T(8,128)S(1)}, u32[]{:S(2)}, u32[]{:S(2)}) collective-permute-start(f32[480,128]{1,0:T(8,128)S(1)} %get-tuple-element.83.refs_1_), channel_id=1, source_target_pairs={{0,8},{8,0},{16,24},{24,16},{1,9},{9,1},{17,25},{25,17},{2,10},{10... | collective-permute-start | bytes 737288 | tf_op jit(solution)/shard_map/ppermute | solution.py:341
  56.9 1.3 %collective-permute-start.22 = (bf16[480,128]{1,0:T(8,128)(2,1)S(1)}, bf16[480,128]{1,0:T(8,128)(2,1)S(1)}, u32[]{:S(2)}, u32[]{:S(2)}) collective-permute-start(bf16[480,128]{1,0:T(8,128)(2,1)S(1)} %collective-permute-done.20.refs_2_), channel_id=1, source_target_pairs={{0,8},{8,0},{16,24},{24,16},{1,9},{9,1},{17,25},{25,17},{2,10},{10... | collective-permute-start | bytes 368648 | tf_op jit(solution)/shard_map/ppermute | solution.py:341

commit v8 on v7

--- a/solution.py
+++ b/solution.py
@@ -432,14 +432,14 @@
         dims = lead[step + 1 :] + (plan.rows + plan.down_rows, part)
         send, keep = call(
             functools.partial(merge_kernel, plan, step), [spot], held, [shape(dims, BF16), shape(dims, F32)], limit=8,
-            after=[done] if step == 3 else (),
         )
         held = [keep, swapped(send, plan.orders[0][step])]
+    arrived, done = lax.optimization_barrier((held[1], done))
     grad_conv, grad_down = call(
-        functools.partial(join_kernel, plan), [spot], held + [swapped(v, core_link) for v in held],
+        functools.partial(join_kernel, plan), [spot], held + [swapped(held[0], core_link), swapped(arrived, core_link)],
         [shape((part // 2, 2 * plan.rows), F32), shape((part // 2, 2 * plan.down_rows), F32)],
         [pltpu.VMEM((part, 2 * plan.rows), F32), pltpu.VMEM((part, 2 * plan.down_rows), F32)],
-        limit=8,
+        limit=8, after=[done],
     )
     return (grad_input.reshape(clip.shape), grad_conv.T, grad_down.T)
 

time: 60 us -> 59.6 us (level)
  transfers between devices with their start and end apart: 23 -> 23, of which waited for: 5 -> 7; matrix products, arithmetic and copies ran while one was open for 0% -> 0% of each run, Pallas kernels for 28% -> 28%
where the time goes in v8:
time: 59.6 us; the launch traced here: 59.4 us
  starting transfers between devices  27 us (45%)
  Pallas kernels  21.4 us (36%)
  waiting for transfers between devices  9.98 us (17%)
  between operations  0.83 us (1%)
    pallas_call x15, Pallas kernels, call(): pl.pallas_call(run, out_shape=outs, in_specs=[smem] * len(scalars) + [hbm...  21.4 us
    ppermute x19, starting transfers between devices, swapped(): lax.ppermute(value, axis, [(i, i ^ 1 << link[1]) for i in range(lax.axis_...  18.8 us
    ppermute x19, waiting for transfers between devices, swapped(): lax.ppermute(value, axis, [(i, i ^ 1 << link[1]) for i in range(lax.axis_...  9.92 us
    ppermute x1, starting transfers between devices, body(): lax.ppermute(side, 'height', [(i, i + (2 if i % 2 == 0 else -2)) for i in...  3.49 us
    ppermute x1, starting transfers between devices, body(): lax.ppermute(clip_other, 'tm', [(i, i + 3) for i in range(0, tm_count - 3...  3.38 us
  transfers between devices with their start and end apart: 23, of which 7 were waited for; matrix products, arithmetic and copies ran while one was open for 0% of the time, Pallas kernels for 28%

profile of v8, /device:TPU:0, one launch (start us, length us, event | category | flops | bytes accessed | tf_op | source)
XLA Modules:
  0.0 59.4 jit_solution(8532862083622649217)
XLA Ops:
  0.6 0.5 collective-permute-start.4
  1.1 2.6 %collective-permute-start.1 = (bf16[256,256]{1,0:T(8,128)(2,1)}, bf16[256,256]{1,0:T(8,128)(2,1)S(1)}, u32[]{:S(2)}, u32[]{:S(2)}) collective-permute-start(bf16[256,256]{1,0:T(8,128)(2,1)} %bitcast.17), channel_id=1, source_target_pairs={{0,1},{1,0},{2,3},{3,2},{4,5},{5,4},{6,7},{7,6},{8,9},{9,8},{10,11... | collective-permute-start | bytes 393224 | tf_op jit(solution)/shard_map/ppermute | solution.py:341
  3.7 0.2 collective-permute-start
  3.9 0.7 %collective-permute-start.5 = (bf16[512,256]{1,0:T(8,128)(2,1)}, bf16[512,256]{1,0:T(8,128)(2,1)S(1)}, u32[]{:S(2)}, u32[]{:S(2)}) collective-permute-start(bf16[512,256]{1,0:T(8,128)(2,1)} %bitcast.14), channel_id=1, source_target_pairs={{8,16},{9,17},{10,18},{11,19},{12,20},{13,21},{14,22},{15,23}} | collective-permute-start | bytes 786440 | tf_op jit(solution)/shard_map/ppermute | solution.py:363
  4.6 0.1 pad_add_fusion.refs_0_
  4.6 3.4 %collective-permute-start.6 = (bf16[512,256]{1,0:T(8,128)(2,1)S(1)}, bf16[512,256]{1,0:T(8,128)(2,1)S(1)}, u32[]{:S(2)}, u32[]{:S(2)}) collective-permute-start(bf16[512,256]{1,0:T(8,128)(2,1)S(1)} %collective-permute-done.4.refs_2_), channel_id=1, source_target_pairs={{0,24},{1,25},{2,26},{3,27},{4,28},{5,29},{6,30},{7,31}} | collective-permute-start | bytes 786440 | tf_op jit(solution)/shard_map/ppermute | solution.py:364
  8.0 0.0 copy-start.1
  8.0 0.0 copy-start.2
  8.0 2.7 %shard_map.67 = (bf16[9,256,384]{2,1,0:T(8,128)(2,1)S(1)}, bf16[768,256]{1,0:T(8,128)(2,1)S(1)}) custom-call(s32[2]{0:T(128)S(1)} %pad_add_fusion.refs_0_, bf16[9,3,8,2,16,256]{5,4,3,2,1,0:T(8,128)(2,1)} %bitcast.11, bf16[3,256,256]{2,1,0:T(8,128)(2,1)} %refs_2_.1), custom_call_target="tpu_custom_call" | custom-call | flops 3449999872 | bytes 3932160 | tf_op jit(solution)/shard_map/pallas_call | solution.py:304
  10.8 0.0 collective-permute-done.1.refs_1_.refs_2_.refs_3_
  10.8 3.5 %collective-permute-start.3 = (bf16[256,256]{1,0:T(8,128)(2,1)S(1)}, bf16[256,256]{1,0:T(8,128)(2,1)S(1)}, u32[]{:S(2)}, u32[]{:S(2)}) collective-permute-start(bf16[256,256]{1,0:T(8,128)(2,1)S(1)} %collective-permute-done.1.refs_1_.refs_2_.refs_3_), channel_id=1, source_target_pairs={{0,2},{2,4},{3,1},{4,6},{5,3},{7,5},{8,10},{10,12},{11,9},{12,14},... | collective-permute-start | bytes 393224 | tf_op jit(solution)/shard_map/ppermute | solution.py:372
  14.3 0.1 collective-permute-start.2
  14.4 2.9 %shard_map.68 = (bf16[384,768]{1,0:T(8,128)(2,1)S(1)}, bf16[384,768]{1,0:T(8,128)(2,1)S(1)}, f32[3,384,256]{2,1,0:T(8,128)S(1)}, f32[256,768]{1,0:T(8,128)S(1)}, f32[128,768]{1,0:T(8,128)S(1)}) custom-call(s32[2]{0:T(128)S(1)} %pad_add_fusion.refs_0_, bf16[512,256]{1,0:T(8,128)(2,1)S(1)} %bitcast.15, bf16[512,256]{1,0:T(8,128)(2,1)S(1)} %collective-permute-done.4.refs_2_, ...), custom_call_target="tpu_custom_call" | custom-call | flops 6899999744 | bytes 3473408 | tf_op jit(solution)/shard_map/pallas_call | solution.py:304
  17.3 0.1 collective-permute-done.3.refs_3_.refs_5_
  17.4 0.5 collective-permute-start.7
  17.9 2.2 %shard_map.69 = (f32[3,384,256]{2,1,0:T(8,128)S(1)}, f32[256,768]{1,0:T(8,128)S(1)}) custom-call(s32[2]{0:T(128)S(1)} %pad_add_fusion.refs_0_, bf16[256,256]{1,0:T(8,128)(2,1)S(1)} %collective-permute-done.1.refs_1_.refs_2_.refs_3_, bf16[256,256]{1,0:T(8,128)(2,1)S(1)} %collective-permute-done.2.refs_2_.refs_4_, ...), custom_call_target="tpu_custom_call" | custom-call | flops 2300000000 | bytes 3604480 | tf_op jit(solution)/shard_map/pallas_call | solution.py:304
  20.1 2.8 %shard_map.70 = (bf16[3,256,256]{2,1,0:T(8,128)(2,1)S(1)}, bf16[2,2,2,112,128]{4,3,2,1,0:T(8,128)(2,1)S(1)}, f32[2,2,2,112,128]{4,3,2,1,0:T(8,128)S(1)}, bf16[2,...) custom-call(s32[2]{0:T(128)S(1)} %pad_add_fusion.refs_0_, ...), custom_call_target="tpu_custom_call" | custom-call | flops 3449999872 | bytes 8192000 | tf_op jit(solution)/shard_map/pallas_call | solution.py:304
  22.9 0.1 collective-permute-start.10
  23.0 1.1 %collective-permute-start.9 = (bf16[2,2,2,112,128]{4,3,2,1,0:T(8,128)(2,1)S(1)}, bf16[2,2,2,112,128]{4,3,2,1,0:T(8,128)(2,1)S(1)}, u32[]{:S(2)}, u32[]{:S(2)}) collective-permute-start(bf16[2,2,2,112,128]{4,3,2,1,0:T(8,128)(2,1)S(1)} %get-tuple-element.62), channel_id=1, source_target_pairs={{0,16},{8,24},{16,0},{24,8},{1,17},{9,25},{17,1},{25,9},{2,18},{10... | collective-permute-start | bytes 688136 | tf_op jit(solution)/shard_map/ppermute | solution.py:341
  24.1 0.5 collective-permute-start.14
  24.6 1.6 %collective-permute-start.17 = (bf16[2,2,2,160,128]{4,3,2,1,0:T(8,128)(2,1)S(1)}, bf16[2,2,2,160,128]{4,3,2,1,0:T(8,128)(2,1)S(1)}, u32[]{:S(2)}, u32[]{:S(2)}) collective-permute-start(bf16[2,2,2,160,128]{4,3,2,1,0:T(8,128)(2,1)S(1)} %get-tuple-element.78), channel_id=1, source_target_pairs={{0,2},{1,3},{2,0},{3,1},{4,6},{5,7},{6,4},{7,5},{8,10},{9,11},{10,... | collective-permute-start | bytes 983048 | tf_op jit(solution)/shard_map/ppermute | solution.py:341
  26.2 0.6 shard_map.73
  26.8 1.9 %collective-permute-start.11 = (bf16[2,2,2,48,128]{4,3,2,1,0:T(8,128)(2,1)S(1)}, bf16[2,2,2,48,128]{4,3,2,1,0:T(8,128)(2,1)S(1)}, u32[]{:S(2)}, u32[]{:S(2)}) collective-permute-start(bf16[2,2,2,48,128]{4,3,2,1,0:T(8,128)(2,1)S(1)} %get-tuple-element.66), channel_id=1, source_target_pairs={{0,16},{8,24},{16,0},{24,8},{1,17},{9,25},{17,1},{25,9},{2,18},{10... | collective-permute-start | bytes 294920 | tf_op jit(solution)/shard_map/ppermute | solution.py:341
  28.7 0.7 %collective-permute-start.8 = (bf16[3,256,256]{2,1,0:T(8,128)(2,1)S(1)}, bf16[3,256,256]{2,1,0:T(8,128)(2,1)S(1)}, u32[]{:S(2)}, u32[]{:S(2)}) collective-permute-start(bf16[3,256,256]{2,1,0:T(8,128)(2,1)S(1)} %get-tuple-element.58), channel_id=1, source_target_pairs={{16,8},{17,9},{18,10},{19,11},{20,12},{21,13},{22,14},{23,15}} | collective-permute-start | bytes 1179656 | tf_op jit(solution)/shard_map/ppermute | solution.py:410
  29.3 2.1 %collective-permute-done.9.refs_2_ = bf16[2,2,2,112,128]{4,3,2,1,0:T(8,128)(2,1)S(1)} collective-permute-done((bf16[2,2,2,112,128]{4,3,2,1,0:T(8,128)(2,1)S(1)}, bf16[2,2,2,112,128]{4,3,2,1,0:T(8,128)(2,1)S(1)}, u32[]{:S(2)}, u32[]{:S(2)}) %collective-permute-start.9) | collective-permute-done | bytes 229408 | tf_op jit(solution)/shard_map/ppermute | solution.py:341
  31.4 1.7 %collective-permute-done.11.refs_4_ = bf16[2,2,2,48,128]{4,3,2,1,0:T(8,128)(2,1)S(1)} collective-permute-done((bf16[2,2,2,48,128]{4,3,2,1,0:T(8,128)(2,1)S(1)}, bf16[2,2,2,48,128]{4,3,2,1,0:T(8,128)(2,1)S(1)}, u32[]{:S(2)}, u32[]{:S(2)}) %collective-permute-start.11) | collective-permute-done | bytes 98336 | tf_op jit(solution)/shard_map/ppermute | solution.py:341
  33.1 0.6 %shard_map.74 = (bf16[2,2,160,128]{3,2,1,0:T(8,128)(2,1)S(1)}, f32[2,2,160,128]{3,2,1,0:T(8,128)S(1)}) custom-call(s32[2]{0:T(128)S(1)} %pad_add_fusion.refs_0_, f32[2,2,2,112,128]{4,3,2,1,0:T(8,128)S(1)} %get-tuple-element.61.refs_1_, bf16[2,2,2,112,128]{4,3,2,1,0:T(8,128)(2,1)S(1)} %collective-permute-done.9.refs_2_, ...), custom_call_target="tpu_custom_call" | custom-call | flops 1150000000 | bytes 983040 | tf_op jit(solution)/shard_map/pallas_call | solution.py:304
  33.7 1.1 %collective-permute-start.12 = (bf16[2,2,160,128]{3,2,1,0:T(8,128)(2,1)S(1)}, bf16[2,2,160,128]{3,2,1,0:T(8,128)(2,1)S(1)}, u32[]{:S(2)}, u32[]{:S(2)}) collective-permute-start(bf16[2,2,160,128]{3,2,1,0:T(8,128)(2,1)S(1)} %get-tuple-element.68), channel_id=1, source_target_pairs={{0,1},{1,0},{2,3},{3,2},{4,5},{5,4},{6,7},{7,6},{8,9},{9,8},{10,11... | collective-permute-start | bytes 491528 | tf_op jit(solution)/shard_map/ppermute | solution.py:341
  34.8 0.6 %shard_map.76 = (bf16[2,2,160,128]{3,2,1,0:T(8,128)(2,1)S(1)}, f32[2,2,160,128]{3,2,1,0:T(8,128)S(1)}) custom-call(s32[2]{0:T(128)S(1)} %pad_add_fusion.refs_0_, f32[2,2,2,160,128]{4,3,2,1,0:T(8,128)S(1)} %get-tuple-element.71.refs_1_, bf16[2,2,2,160,128]{4,3,2,1,0:T(8,128)(2,1)S(1)} %collective-permute-done.14.refs_2_), custom_call_target="tpu_custom_call" | custom-call | flops 1150000000 | bytes 983040 | tf_op jit(solution)/shard_map/pallas_call | solution.py:304
  35.4 1.6 %collective-permute-start.15 = (bf16[2,2,160,128]{3,2,1,0:T(8,128)(2,1)S(1)}, bf16[2,2,160,128]{3,2,1,0:T(8,128)(2,1)S(1)}, u32[]{:S(2)}, u32[]{:S(2)}) collective-permute-start(bf16[2,2,160,128]{3,2,1,0:T(8,128)(2,1)S(1)} %get-tuple-element.74), channel_id=1, source_target_pairs={{0,2},{1,3},{2,0},{3,1},{4,6},{5,7},{6,4},{7,5},{8,10},{9,11},{10,... | collective-permute-start | bytes 491528 | tf_op jit(solution)/shard_map/ppermute | solution.py:341
  37.0 0.6 %shard_map.78 = (bf16[2,2,160,128]{3,2,1,0:T(8,128)(2,1)S(1)}, f32[2,2,160,128]{3,2,1,0:T(8,128)S(1)}) custom-call(s32[2]{0:T(128)S(1)} %pad_add_fusion.refs_0_, f32[2,2,2,160,128]{4,3,2,1,0:T(8,128)S(1)} %get-tuple-element.77.refs_1_, bf16[2,2,2,160,128]{4,3,2,1,0:T(8,128)(2,1)S(1)} %collective-permute-done.17.refs_2_), custom_call_target="tpu_custom_call" | custom-call | flops 1150000000 | bytes 983040 | tf_op jit(solution)/shard_map/pallas_call | solution.py:304
  37.6 0.6 %collective-permute-start.18 = (bf16[2,2,160,128]{3,2,1,0:T(8,128)(2,1)S(1)}, bf16[2,2,160,128]{3,2,1,0:T(8,128)(2,1)S(1)}, u32[]{:S(2)}, u32[]{:S(2)}) collective-permute-start(bf16[2,2,160,128]{3,2,1,0:T(8,128)(2,1)S(1)} %get-tuple-element.80), channel_id=1, source_target_pairs={{0,16},{8,24},{16,0},{24,8},{1,17},{9,25},{17,1},{25,9},{2,18},{10... | collective-permute-start | bytes 491528 | tf_op jit(solution)/shard_map/ppermute | solution.py:341
  38.3 1.2 %shard_map.71 = (bf16[3,768,256]{2,1,0:T(8,128)(2,1)S(1)}, f32[8,128]{1,0:T(8,128)S(1)}) custom-call(s32[2]{0:T(128)S(1)} %pad_add_fusion.refs_0_, bf16[256,256]{1,0:T(8,128)(2,1)S(1)} %bitcast.21, bf16[256,256]{1,0:T(8,128)(2,1)S(1)} %collective-permute-done.refs_6_.refs_2_, bf16[256,256]{1,0:T(8,128)(2,1)S(1)} %collective-permute-done.1.refs_1_.refs_2_.refs_3_, ...), custom_call_target="tpu_custom_call" | custom-call | flops 1150000000 | bytes 1572864 | tf_op jit(solution)/shard_map/pallas_call | solution.py:304
  39.5 0.1 collective-permute-done.12.refs_2_
  39.5 0.6 shard_map.75
  40.1 1.7 %collective-permute-start.13 = (bf16[2,160,128]{2,1,0:T(8,128)(2,1)S(1)}, bf16[2,160,128]{2,1,0:T(8,128)(2,1)S(1)}, u32[]{:S(2)}, u32[]{:S(2)}) collective-permute-start(bf16[2,160,128]{2,1,0:T(8,128)(2,1)S(1)} %get-tuple-element.70), channel_id=1, source_target_pairs={{0,2},{1,3},{2,0},{3,1},{4,6},{5,7},{6,4},{7,5},{8,10},{9,11},{10,... | collective-permute-start | bytes 245768 | tf_op jit(solution)/shard_map/ppermute | solution.py:341
  41.8 0.6 shard_map.77
  42.4 1.3 %collective-permute-start.16 = (bf16[2,160,128]{2,1,0:T(8,128)(2,1)S(1)}, bf16[2,160,128]{2,1,0:T(8,128)(2,1)S(1)}, u32[]{:S(2)}, u32[]{:S(2)}) collective-permute-start(bf16[2,160,128]{2,1,0:T(8,128)(2,1)S(1)} %get-tuple-element.76), channel_id=1, source_target_pairs={{0,16},{8,24},{16,0},{24,8},{1,17},{9,25},{17,1},{25,9},{2,18},{10... | collective-permute-start | bytes 245768 | tf_op jit(solution)/shard_map/ppermute | solution.py:341
  43.7 0.6 shard_map.79
  44.3 0.9 %collective-permute-start.19 = (bf16[2,160,128]{2,1,0:T(8,128)(2,1)S(1)}, bf16[2,160,128]{2,1,0:T(8,128)(2,1)S(1)}, u32[]{:S(2)}, u32[]{:S(2)}) collective-permute-start(bf16[2,160,128]{2,1,0:T(8,128)(2,1)S(1)} %get-tuple-element.83), channel_id=1, source_target_pairs={{0,1},{1,0},{2,3},{3,2},{4,5},{5,4},{6,7},{7,6},{8,9},{9,8},{10,11... | collective-permute-start | bytes 245768 | tf_op jit(solution)/shard_map/ppermute | solution.py:341
  45.2 1.7 %collective-permute-done.16.refs_4_ = bf16[2,160,128]{2,1,0:T(8,128)(2,1)S(1)} collective-permute-done((bf16[2,160,128]{2,1,0:T(8,128)(2,1)S(1)}, bf16[2,160,128]{2,1,0:T(8,128)(2,1)S(1)}, u32[]{:S(2)}, u32[]{:S(2)}) %collective-permute-start.16) | collective-permute-done | bytes 81952 | tf_op jit(solution)/shard_map/ppermute | solution.py:341
  46.9 1.9 %collective-permute-done.19.refs_6_ = bf16[2,160,128]{2,1,0:T(8,128)(2,1)S(1)} collective-permute-done((bf16[2,160,128]{2,1,0:T(8,128)(2,1)S(1)}, bf16[2,160,128]{2,1,0:T(8,128)(2,1)S(1)}, u32[]{:S(2)}, u32[]{:S(2)}) %collective-permute-start.19) | collective-permute-done | bytes 81952 | tf_op jit(solution)/shard_map/ppermute | solution.py:341
  48.8 0.6 %shard_map.80 = (bf16[480,128]{1,0:T(8,128)(2,1)S(1)}, f32[480,128]{1,0:T(8,128)S(1)}) custom-call(s32[2]{0:T(128)S(1)} %pad_add_fusion.refs_0_, f32[2,160,128]{2,1,0:T(8,128)S(1)} %get-tuple-element.69.refs_1_, bf16[2,160,128]{2,1,0:T(8,128)(2,1)S(1)} %collective-permute-done.13.refs_2_, f32[2,160,128]{2,1,0:T(8,128)S(1)} %get-tuple-element.75.refs_3_, ...), custom_call_target="tpu_custom_call" | custom-call | flops 1150000000 | bytes 737280 | tf_op jit(solution)/shard_map/pallas_call | solution.py:304
  49.4 2.6 %collective-permute-start.20 = (bf16[480,128]{1,0:T(8,128)(2,1)S(1)}, bf16[480,128]{1,0:T(8,128)(2,1)S(1)}, u32[]{:S(2)}, u32[]{:S(2)}) collective-permute-start(bf16[480,128]{1,0:T(8,128)(2,1)S(1)} %get-tuple-element.85), channel_id=1, source_target_pairs={{0,4},{1,5},{2,6},{3,7},{4,0},{5,1},{6,2},{7,3},{8,12},{9,13},{10,... | collective-permute-start | bytes 368648 | tf_op jit(solution)/shard_map/ppermute | solution.py:341
  52.1 3.4 %shard_map.72 = (bf16[512,256]{1,0:T(8,128)(2,1)}, f32[8,128]{1,0:T(8,128)S(1)}) custom-call(s32[2]{0:T(128)S(1)} %pad_add_fusion.refs_0_, bf16[512,256]{1,0:T(8,128)(2,1)S(1)} %bitcast.16, bf16[3,768,256]{2,1,0:T(8,128)(2,1)S(1)} %get-tuple-element.59.refs_2_, bf16[9,768,256]{2,1,0:T(8,128)(2,1)S(1)} %bitcast.12), custom_call_target="tpu_custom_call" | custom-call | flops 2300000000 | bytes 4980736 | tf_op jit(solution)/shard_map/pallas_call | solution.py:304
  55.5 1.1 %collective-permute-done.20.refs_2_ = bf16[480,128]{1,0:T(8,128)(2,1)S(1)} collective-permute-done((bf16[480,128]{1,0:T(8,128)(2,1)S(1)}, bf16[480,128]{1,0:T(8,128)(2,1)S(1)}, u32[]{:S(2)}, u32[]{:S(2)}) %collective-permute-start.20) | collective-permute-done | bytes 122912 | tf_op jit(solution)/shard_map/ppermute | solution.py:341
  56.6 1.3 %collective-permute-done.22.refs_4_ = bf16[480,128]{1,0:T(8,128)(2,1)S(1)} collective-permute-done((bf16[480,128]{1,0:T(8,128)(2,1)S(1)}, bf16[480,128]{1,0:T(8,128)(2,1)S(1)}, u32[]{:S(2)}, u32[]{:S(2)}) %collective-permute-start.22) | collective-permute-done | bytes 122912 | tf_op jit(solution)/shard_map/ppermute | solution.py:341
  57.9 1.5 %shard_map.81 = (f32[64,864]{1,0:T(8,128)}, f32[64,96]{1,0:T(8,128)}) custom-call(s32[2]{0:T(128)S(1)} %pad_add_fusion.refs_0_, f32[480,128]{1,0:T(8,128)S(1)} %get-tuple-element.84.refs_1_, bf16[480,128]{1,0:T(8,128)(2,1)S(1)} %collective-permute-done.20.refs_2_, f32[480,128]{1,0:T(8,128)S(1)} %collective-permute-done.21.refs_3_, ...), custom_call_target="tpu_custom_call" | custom-call | flops 1150000000 | bytes 737280 | tf_op jit(solution)/shard_map/pallas_call | solution.py:304
  (20 shorter events, 0.0 us)
Async XLA Ops:
  0.6 4.0 %collective-permute-start.4 = (bf16[512,256]{1,0:T(8,128)(2,1)}, bf16[512,256]{1,0:T(8,128)(2,1)S(1)}, u32[]{:S(2)}, u32[]{:S(2)}) collective-permute-start(bf16[512,256]{1,0:T(8,128)(2,1)} %bitcast.13), channel_id=1, source_target_pairs={{0,8},{8,0},{16,24},{24,16},{1,9},{9,1},{17,25},{25,17},{2,10},{10... | collective-permute-start | bytes 786440 | tf_op jit(solution)/shard_map/ppermute | solution.py:341
  1.1 9.6 %collective-permute-start.1 = (bf16[256,256]{1,0:T(8,128)(2,1)}, bf16[256,256]{1,0:T(8,128)(2,1)S(1)}, u32[]{:S(2)}, u32[]{:S(2)}) collective-permute-start(bf16[256,256]{1,0:T(8,128)(2,1)} %bitcast.17), channel_id=1, source_target_pairs={{0,1},{1,0},{2,3},{3,2},{4,5},{5,4},{6,7},{7,6},{8,9},{9,8},{10,11... | collective-permute-start | bytes 393224 | tf_op jit(solution)/shard_map/ppermute | solution.py:341
  3.7 10.7 %collective-permute-start = (bf16[256,256]{1,0:T(8,128)(2,1)}, bf16[256,256]{1,0:T(8,128)(2,1)S(1)}, u32[]{:S(2)}, u32[]{:S(2)}) collective-permute-start(bf16[256,256]{1,0:T(8,128)(2,1)} %bitcast.18), channel_id=1, source_target_pairs={{0,8},{8,0},{16,24},{24,16},{1,9},{9,1},{17,25},{25,17},{2,10},{10... | collective-permute-start | bytes 393224 | tf_op jit(solution)/shard_map/ppermute | solution.py:341
  3.9 10.5 %collective-permute-start.5 = (bf16[512,256]{1,0:T(8,128)(2,1)}, bf16[512,256]{1,0:T(8,128)(2,1)S(1)}, u32[]{:S(2)}, u32[]{:S(2)}) collective-permute-start(bf16[512,256]{1,0:T(8,128)(2,1)} %bitcast.14), channel_id=1, source_target_pairs={{8,16},{9,17},{10,18},{11,19},{12,20},{13,21},{14,22},{15,23}} | collective-permute-start | bytes 786440 | tf_op jit(solution)/shard_map/ppermute | solution.py:363
  4.6 9.8 %collective-permute-start.6 = (bf16[512,256]{1,0:T(8,128)(2,1)S(1)}, bf16[512,256]{1,0:T(8,128)(2,1)S(1)}, u32[]{:S(2)}, u32[]{:S(2)}) collective-permute-start(bf16[512,256]{1,0:T(8,128)(2,1)S(1)} %collective-permute-done.4.refs_2_), channel_id=1, source_target_pairs={{0,24},{1,25},{2,26},{3,27},{4,28},{5,29},{6,30},{7,31}} | collective-permute-start | bytes 786440 | tf_op jit(solution)/shard_map/ppermute | solution.py:364
  8.0 6.4 %copy-start.1 = (bf16[4,1,128,256]{3,2,1,0:T(8,128)(2,1)S(1)}, bf16[4,1,128,256]{3,2,1,0:T(8,128)(2,1)}, u32[]{:S(2)}) copy-start(bf16[4,1,128,256]{3,2,1,0:T(8,128)(2,1)} %param.4) | copy-start | bytes 786436
  8.0 6.4 %copy-start.2 = (bf16[2,1,128,256]{3,2,1,0:T(8,128)(2,1)S(1)}, bf16[2,1,128,256]{3,2,1,0:T(8,128)(2,1)}, u32[]{:S(2)}) copy-start(bf16[2,1,128,256]{3,2,1,0:T(8,128)(2,1)} %param.7) | copy-start | bytes 393220
  10.8 6.6 %collective-permute-start.3 = (bf16[256,256]{1,0:T(8,128)(2,1)S(1)}, bf16[256,256]{1,0:T(8,128)(2,1)S(1)}, u32[]{:S(2)}, u32[]{:S(2)}) collective-permute-start(bf16[256,256]{1,0:T(8,128)(2,1)S(1)} %collective-permute-done.1.refs_1_.refs_2_.refs_3_), channel_id=1, source_target_pairs={{0,2},{2,4},{3,1},{4,6},{5,3},{7,5},{8,10},{10,12},{11,9},{12,14},... | collective-permute-start | bytes 393224 | tf_op jit(solution)/shard_map/ppermute | solution.py:372
  14.3 3.6 %collective-permute-start.2 = (bf16[256,256]{1,0:T(8,128)(2,1)S(1)}, bf16[256,256]{1,0:T(8,128)(2,1)S(1)}, u32[]{:S(2)}, u32[]{:S(2)}) collective-permute-start(bf16[256,256]{1,0:T(8,128)(2,1)S(1)} %collective-permute-done.1.refs_1_.refs_2_.refs_3_), channel_id=1, source_target_pairs={{0,8},{8,0},{16,24},{24,16},{1,9},{9,1},{17,25},{25,17},{2,10},{10... | collective-permute-start | bytes 393224 | tf_op jit(solution)/shard_map/ppermute | solution.py:341
  17.4 2.7 %collective-permute-start.7 = (bf16[256,256]{1,0:T(8,128)(2,1)S(1)}, bf16[256,256]{1,0:T(8,128)(2,1)S(1)}, u32[]{:S(2)}, u32[]{:S(2)}) collective-permute-start(bf16[256,256]{1,0:T(8,128)(2,1)S(1)} %collective-permute-done.3.refs_3_.refs_5_), channel_id=1, source_target_pairs={{0,8},{8,0},{16,24},{24,16},{1,9},{9,1},{17,25},{25,17},{2,10},{10... | collective-permute-start | bytes 393224 | tf_op jit(solution)/shard_map/ppermute | solution.py:341
  22.9 3.3 %collective-permute-start.10 = (bf16[2,2,2,2,48,128]{5,4,3,2,1,0:T(8,128)(2,1)S(1)}, bf16[2,2,2,2,48,128]{5,4,3,2,1,0:T(8,128)(2,1)S(1)}, u32[]{:S(2)}, u32[]{:S(2)}) collective-permute-start(bf16[2,2,2,2,48,128]{5,4,3,2,1,0:T(8,128)(2,1)S(1)} %get-tuple-element.64), channel_id=1, source_target_pairs={{0,8},{8,0},{16,24},{24,16},{1,9},{9,1},{17,25},{25,17},{2,10},{10... | collective-permute-start | bytes 589832 | tf_op jit(solution)/shard_map/ppermute | solution.py:341
  23.0 8.5 %collective-permute-start.9 = (bf16[2,2,2,112,128]{4,3,2,1,0:T(8,128)(2,1)S(1)}, bf16[2,2,2,112,128]{4,3,2,1,0:T(8,128)(2,1)S(1)}, u32[]{:S(2)}, u32[]{:S(2)}) collective-permute-start(bf16[2,2,2,112,128]{4,3,2,1,0:T(8,128)(2,1)S(1)} %get-tuple-element.62), channel_id=1, source_target_pairs={{0,16},{8,24},{16,0},{24,8},{1,17},{9,25},{17,1},{25,9},{2,18},{10... | collective-permute-start | bytes 688136 | tf_op jit(solution)/shard_map/ppermute | solution.py:341
  24.1 10.7 %collective-permute-start.14 = (bf16[2,2,2,160,128]{4,3,2,1,0:T(8,128)(2,1)S(1)}, bf16[2,2,2,160,128]{4,3,2,1,0:T(8,128)(2,1)S(1)}, u32[]{:S(2)}, u32[]{:S(2)}) collective-permute-start(bf16[2,2,2,160,128]{4,3,2,1,0:T(8,128)(2,1)S(1)} %get-tuple-element.72), channel_id=1, source_target_pairs={{0,1},{1,0},{2,3},{3,2},{4,5},{5,4},{6,7},{7,6},{8,9},{9,8},{10,11... | collective-permute-start | bytes 983048 | tf_op jit(solution)/shard_map/ppermute | solution.py:341
  24.6 12.4 %collective-permute-start.17 = (bf16[2,2,2,160,128]{4,3,2,1,0:T(8,128)(2,1)S(1)}, bf16[2,2,2,160,128]{4,3,2,1,0:T(8,128)(2,1)S(1)}, u32[]{:S(2)}, u32[]{:S(2)}) collective-permute-start(bf16[2,2,2,160,128]{4,3,2,1,0:T(8,128)(2,1)S(1)} %get-tuple-element.78), channel_id=1, source_target_pairs={{0,2},{1,3},{2,0},{3,1},{4,6},{5,7},{6,4},{7,5},{8,10},{9,11},{10,... | collective-permute-start | bytes 983048 | tf_op jit(solution)/shard_map/ppermute | solution.py:341
  26.8 6.3 %collective-permute-start.11 = (bf16[2,2,2,48,128]{4,3,2,1,0:T(8,128)(2,1)S(1)}, bf16[2,2,2,48,128]{4,3,2,1,0:T(8,128)(2,1)S(1)}, u32[]{:S(2)}, u32[]{:S(2)}) collective-permute-start(bf16[2,2,2,48,128]{4,3,2,1,0:T(8,128)(2,1)S(1)} %get-tuple-element.66), channel_id=1, source_target_pairs={{0,16},{8,24},{16,0},{24,8},{1,17},{9,25},{17,1},{25,9},{2,18},{10... | collective-permute-start | bytes 294920 | tf_op jit(solution)/shard_map/ppermute | solution.py:341
  28.7 9.6 %collective-permute-start.8 = (bf16[3,256,256]{2,1,0:T(8,128)(2,1)S(1)}, bf16[3,256,256]{2,1,0:T(8,128)(2,1)S(1)}, u32[]{:S(2)}, u32[]{:S(2)}) collective-permute-start(bf16[3,256,256]{2,1,0:T(8,128)(2,1)S(1)} %get-tuple-element.58), channel_id=1, source_target_pairs={{16,8},{17,9},{18,10},{19,11},{20,12},{21,13},{22,14},{23,15}} | collective-permute-start | bytes 1179656 | tf_op jit(solution)/shard_map/ppermute | solution.py:410
  33.7 5.8 %collective-permute-start.12 = (bf16[2,2,160,128]{3,2,1,0:T(8,128)(2,1)S(1)}, bf16[2,2,160,128]{3,2,1,0:T(8,128)(2,1)S(1)}, u32[]{:S(2)}, u32[]{:S(2)}) collective-permute-start(bf16[2,2,160,128]{3,2,1,0:T(8,128)(2,1)S(1)} %get-tuple-element.68), channel_id=1, source_target_pairs={{0,1},{1,0},{2,3},{3,2},{4,5},{5,4},{6,7},{7,6},{8,9},{9,8},{10,11... | collective-permute-start | bytes 491528 | tf_op jit(solution)/shard_map/ppermute | solution.py:341
  35.4 6.4 %collective-permute-start.15 = (bf16[2,2,160,128]{3,2,1,0:T(8,128)(2,1)S(1)}, bf16[2,2,160,128]{3,2,1,0:T(8,128)(2,1)S(1)}, u32[]{:S(2)}, u32[]{:S(2)}) collective-permute-start(bf16[2,2,160,128]{3,2,1,0:T(8,128)(2,1)S(1)} %get-tuple-element.74), channel_id=1, source_target_pairs={{0,2},{1,3},{2,0},{3,1},{4,6},{5,7},{6,4},{7,5},{8,10},{9,11},{10,... | collective-permute-start | bytes 491528 | tf_op jit(solution)/shard_map/ppermute | solution.py:341
  37.6 6.1 %collective-permute-start.18 = (bf16[2,2,160,128]{3,2,1,0:T(8,128)(2,1)S(1)}, bf16[2,2,160,128]{3,2,1,0:T(8,128)(2,1)S(1)}, u32[]{:S(2)}, u32[]{:S(2)}) collective-permute-start(bf16[2,2,160,128]{3,2,1,0:T(8,128)(2,1)S(1)} %get-tuple-element.80), channel_id=1, source_target_pairs={{0,16},{8,24},{16,0},{24,8},{1,17},{9,25},{17,1},{25,9},{2,18},{10... | collective-permute-start | bytes 491528 | tf_op jit(solution)/shard_map/ppermute | solution.py:341
  40.1 5.0 %collective-permute-start.13 = (bf16[2,160,128]{2,1,0:T(8,128)(2,1)S(1)}, bf16[2,160,128]{2,1,0:T(8,128)(2,1)S(1)}, u32[]{:S(2)}, u32[]{:S(2)}) collective-permute-start(bf16[2,160,128]{2,1,0:T(8,128)(2,1)S(1)} %get-tuple-element.70), channel_id=1, source_target_pairs={{0,2},{1,3},{2,0},{3,1},{4,6},{5,7},{6,4},{7,5},{8,10},{9,11},{10,... | collective-permute-start | bytes 245768 | tf_op jit(solution)/shard_map/ppermute | solution.py:341
  42.4 4.5 %collective-permute-start.16 = (bf16[2,160,128]{2,1,0:T(8,128)(2,1)S(1)}, bf16[2,160,128]{2,1,0:T(8,128)(2,1)S(1)}, u32[]{:S(2)}, u32[]{:S(2)}) collective-permute-start(bf16[2,160,128]{2,1,0:T(8,128)(2,1)S(1)} %get-tuple-element.76), channel_id=1, source_target_pairs={{0,16},{8,24},{16,0},{24,8},{1,17},{9,25},{17,1},{25,9},{2,18},{10... | collective-permute-start | bytes 245768 | tf_op jit(solution)/shard_map/ppermute | solution.py:341
  44.3 4.5 %collective-permute-start.19 = (bf16[2,160,128]{2,1,0:T(8,128)(2,1)S(1)}, bf16[2,160,128]{2,1,0:T(8,128)(2,1)S(1)}, u32[]{:S(2)}, u32[]{:S(2)}) collective-permute-start(bf16[2,160,128]{2,1,0:T(8,128)(2,1)S(1)} %get-tuple-element.83), channel_id=1, source_target_pairs={{0,1},{1,0},{2,3},{3,2},{4,5},{5,4},{6,7},{7,6},{8,9},{9,8},{10,11... | collective-permute-start | bytes 245768 | tf_op jit(solution)/shard_map/ppermute | solution.py:341
  48.8 3.3 %copy-start = (bf16[3,3,3,256,256]{4,3,2,1,0:T(8,128)(2,1)S(1)}, bf16[3,3,3,256,256]{4,3,2,1,0:T(8,128)(2,1)}, u32[]{:S(2)}) copy-start(bf16[3,3,3,256,256]{4,3,2,1,0:T(8,128)(2,1)} %param.5) | copy-start | bytes 10616836
  49.4 7.1 %collective-permute-start.20 = (bf16[480,128]{1,0:T(8,128)(2,1)S(1)}, bf16[480,128]{1,0:T(8,128)(2,1)S(1)}, u32[]{:S(2)}, u32[]{:S(2)}) collective-permute-start(bf16[480,128]{1,0:T(8,128)(2,1)S(1)} %get-tuple-element.85), channel_id=1, source_target_pairs={{0,4},{1,5},{2,6},{3,7},{4,0},{5,1},{6,2},{7,3},{8,12},{9,13},{10,... | collective-permute-start | bytes 368648 | tf_op jit(solution)/shard_map/ppermute | solution.py:341
  52.1 5.8 %collective-permute-start.21 = (f32[480,128]{1,0:T(8,128)S(1)}, f32[480,128]{1,0:T(8,128)S(1)}, u32[]{:S(2)}, u32[]{:S(2)}) collective-permute-start(f32[480,128]{1,0:T(8,128)S(1)} %get-tuple-element.84.refs_1_), channel_id=1, source_target_pairs={{0,8},{8,0},{16,24},{24,16},{1,9},{9,1},{17,25},{25,17},{2,10},{10... | collective-permute-start | bytes 737288 | tf_op jit(solution)/shard_map/ppermute | solution.py:341
  56.6 1.3 %collective-permute-start.22 = (bf16[480,128]{1,0:T(8,128)(2,1)S(1)}, bf16[480,128]{1,0:T(8,128)(2,1)S(1)}, u32[]{:S(2)}, u32[]{:S(2)}) collective-permute-start(bf16[480,128]{1,0:T(8,128)(2,1)S(1)} %collective-permute-done.20.refs_2_), channel_id=1, source_target_pairs={{0,8},{8,0},{16,24},{24,16},{1,9},{9,1},{17,25},{25,17},{2,10},{10... | collective-permute-start | bytes 368648 | tf_op jit(solution)/shard_map/ppermute | solution.py:341

commit v9 on v8

--- a/solution.py
+++ b/solution.py
@@ -266,17 +266,25 @@
     done_ref[...] = jnp.zeros_like(done_ref)
 
 
-def input_kernel(plan, spot_ref, clip_ref, grads, weight_ref, out_ref, done_ref):
+def tap_sum(plan, side, grads, weight_ref, cells, c):
+    cols, chans = plan.cols, plan.chans
+    taps = [(a, slot, b) for a in range(3) for slot, b in enumerate((1, side, 2 - side))]
+    left = jnp.concatenate([grads[slot, (2 - a) * cols : (2 - a) * cols + cells] for a, slot, _ in taps], axis=1)
+    right = jnp.concatenate([weight_ref[a * 3 + b, c * chans : (c + 1) * chans] for a, _, b in taps], axis=1)
+    return dot_nt(left, right)
+
+
+def middle_kernel(plan, spot_ref, grads, weight_ref, middle_ref, done_ref):
+    middle_ref[...] = tap_sum(plan, 2 * (spot_ref[1] & 1), grads, weight_ref, middle_ref.shape[0], 1)
+    done_ref[...] = jnp.zeros_like(done_ref)
+
+
+def input_kernel(plan, spot_ref, clip_ref, grads, middle_ref, weight_ref, out_ref, done_ref):
     cols, chans = plan.cols, plan.chans
     cells = clip_ref.shape[0]
     side = 2 * (spot_ref[1] & 1)
-    taps = [(a, slot, b) for a in range(3) for slot, b in enumerate((1, side, 2 - side))]
-    left = jnp.concatenate([grads[slot, (2 - a) * cols : (2 - a) * cols + cells] for a, slot, _ in taps], axis=1)
-    acc = []
-    for c in range(3):
-        right = jnp.concatenate([weight_ref[a * 3 + b, c * chans : (c + 1) * chans] for a, _, b in taps], axis=1)
-        acc.append(dot_nt(left, right))
-    grad_act = acc[1]
+    acc = {c: tap_sum(plan, side, grads, weight_ref, cells, c) for c in (0, 2)}
+    grad_act = middle_ref[...]
     for c in (0, 2):
         grad_act = grad_act + shifted_rows(acc[c], 1 - c, cols)
     value = clip_ref[...].astype(F32)
@@ -413,8 +421,12 @@
         [mine, here_other, side, side_other, far, far_other, following, spread],
         [shape((3, (2 * half + 2) * ncols, chans), BF16), shape((8, part), F32)], us=1, limit=16,
     )
+    middle, begun = call(
+        functools.partial(middle_kernel, plan), [spot], [grads, weight],
+        [shape((cells, chans), F32), shape((8, part), F32)], us=1, limit=16,
+    )
     grad_input, done = call(
-        functools.partial(input_kernel, plan), [spot], [flat, grads, weight],
+        functools.partial(input_kernel, plan), [spot], [flat, grads, middle, weight],
         [shape((cells, chans), BF16), shape((8, part), F32)], us=2, limit=24,
     )
     held = [held[:2] + down_held, held[2:4], held[4:6]]
@@ -424,7 +436,7 @@
             dims = lead[step + 1 :] + (rows, part)
             send, keep = call(
                 functools.partial(single_kernel, plan, g, step), [spot], held[g], [shape(dims, BF16), shape(dims, F32)],
-                us=1, limit=8, after=[ready] if (g, step) == (2, 2) else (),
+                us=2.5, limit=8, after=[ready] if (g, step) == (2, 2) else (),
             )
             held[g] = [keep, swapped(send, plan.orders[g][step])]
     held = sum(held, [])
@@ -432,6 +444,7 @@
         dims = lead[step + 1 :] + (plan.rows + plan.down_rows, part)
         send, keep = call(
             functools.partial(merge_kernel, plan, step), [spot], held, [shape(dims, BF16), shape(dims, F32)], limit=8,
+            after=[begun] if step == 3 else (),
         )
         held = [keep, swapped(send, plan.orders[0][step])]
     arrived, done = lax.optimization_barrier((held[1], done))

time: 59.6 us -> 59.4 us (level); the launches traced: 59.4 us -> 58.5 us
  waiting for transfers between devices: 9.98 us -> 8.51 us
  starting transfers between devices: 27 us -> 26.1 us
  Pallas kernels: 21.4 us -> 22.2 us
  local copies, waits for them, and re-layouts: 0.02 us -> 0.75 us
    ppermute x19, waiting for transfers between devices: 9.92 us -> 8.45 us  [swapped(): lax.ppermute(value, axis, [(i, i ^ 1 << link[1]) for i in range(lax.axis_...]
    ppermute x19, starting transfers between devices: 18.8 us -> 17.9 us  [swapped(): lax.ppermute(value, axis, [(i, i ^ 1 << link[1]) for i in range(lax.axis_...]
    pallas_call x15 -> x16, Pallas kernels: 21.4 us -> 22.2 us  [call(): pl.pallas_call(run, out_shape=outs, in_specs=[smem] * len(scalars) + [hbm...]
    unnamed x6, local copies, waits for them, and re-layouts: 0.02 us -> 0.75 us
  transfers between devices with their start and end apart: 23 -> 23, of which waited for: 7 -> 8; matrix products, arithmetic and copies ran while one was open for 0% -> 0% of each run, Pallas kernels for 28% -> 30%
where the time goes in v9:
time: 59.4 us; the launch traced here: 58.5 us
  starting transfers between devices  26.1 us (44%)
  Pallas kernels  22.2 us (37%)
  waiting for transfers between devices  8.51 us (14%)
  between operations  0.86 us (1%)
  local copies, waits for them, and re-layouts  0.75 us (1%)
    pallas_call x16, Pallas kernels, call(): pl.pallas_call(run, out_shape=outs, in_specs=[smem] * len(scalars) + [hbm...  22.2 us
    ppermute x19, starting transfers between devices, swapped(): lax.ppermute(value, axis, [(i, i ^ 1 << link[1]) for i in range(lax.axis_...  17.9 us
    ppermute x19, waiting for transfers between devices, swapped(): lax.ppermute(value, axis, [(i, i ^ 1 << link[1]) for i in range(lax.axis_...  8.45 us
    ppermute x1, starting transfers between devices, body(): lax.ppermute(side, 'height', [(i, i + (2 if i % 2 == 0 else -2)) for i in...  3.49 us
    ppermute x1, starting transfers between devices, body(): lax.ppermute(clip_other, 'tm', [(i, i + 3) for i in range(0, tm_count - 3...  3.38 us
  transfers between devices with their start and end apart: 23, of which 8 were waited for; matrix products, arithmetic and copies ran while one was open for 0% of the time, Pallas kernels for 30%

profile of v9, /device:TPU:0, one launch (start us, length us, event | category | flops | bytes accessed | tf_op | source)
XLA Modules:
  0.0 58.5 jit_solution(12701436989788368054)
XLA Ops:
  0.6 0.5 collective-permute-start.4
  1.1 2.6 %collective-permute-start.1 = (bf16[256,256]{1,0:T(8,128)(2,1)}, bf16[256,256]{1,0:T(8,128)(2,1)S(1)}, u32[]{:S(2)}, u32[]{:S(2)}) collective-permute-start(bf16[256,256]{1,0:T(8,128)(2,1)} %bitcast.18), channel_id=1, source_target_pairs={{0,1},{1,0},{2,3},{3,2},{4,5},{5,4},{6,7},{7,6},{8,9},{9,8},{10,11... | collective-permute-start | bytes 393224 | tf_op jit(solution)/shard_map/ppermute | solution.py:349
  3.7 0.2 collective-permute-start
  3.9 0.7 %collective-permute-start.5 = (bf16[512,256]{1,0:T(8,128)(2,1)}, bf16[512,256]{1,0:T(8,128)(2,1)S(1)}, u32[]{:S(2)}, u32[]{:S(2)}) collective-permute-start(bf16[512,256]{1,0:T(8,128)(2,1)} %bitcast.15), channel_id=1, source_target_pairs={{8,16},{9,17},{10,18},{11,19},{12,20},{13,21},{14,22},{15,23}} | collective-permute-start | bytes 786440 | tf_op jit(solution)/shard_map/ppermute | solution.py:371
  4.6 0.1 pad_add_fusion.refs_0_
  4.6 3.4 %collective-permute-start.6 = (bf16[512,256]{1,0:T(8,128)(2,1)S(1)}, bf16[512,256]{1,0:T(8,128)(2,1)S(1)}, u32[]{:S(2)}, u32[]{:S(2)}) collective-permute-start(bf16[512,256]{1,0:T(8,128)(2,1)S(1)} %collective-permute-done.4.refs_2_), channel_id=1, source_target_pairs={{0,24},{1,25},{2,26},{3,27},{4,28},{5,29},{6,30},{7,31}} | collective-permute-start | bytes 786440 | tf_op jit(solution)/shard_map/ppermute | solution.py:372
  8.0 2.7 %shard_map.67 = (bf16[9,256,384]{2,1,0:T(8,128)(2,1)S(1)}, bf16[768,256]{1,0:T(8,128)(2,1)S(1)}) custom-call(s32[2]{0:T(128)S(1)} %pad_add_fusion.refs_0_, bf16[9,3,8,2,16,256]{5,4,3,2,1,0:T(8,128)(2,1)} %bitcast.11, bf16[3,256,256]{2,1,0:T(8,128)(2,1)} %refs_2_.1), custom_call_target="tpu_custom_call" | custom-call | flops 3449999872 | bytes 3932160 | tf_op jit(solution)/shard_map/pallas_call | solution.py:312
  10.8 3.5 %collective-permute-start.3 = (bf16[256,256]{1,0:T(8,128)(2,1)S(1)}, bf16[256,256]{1,0:T(8,128)(2,1)S(1)}, u32[]{:S(2)}, u32[]{:S(2)}) collective-permute-start(bf16[256,256]{1,0:T(8,128)(2,1)S(1)} %collective-permute-done.1.refs_1_.refs_2_.refs_3_), channel_id=1, source_target_pairs={{0,2},{2,4},{3,1},{4,6},{5,3},{7,5},{8,10},{10,12},{11,9},{12,14},... | collective-permute-start | bytes 393224 | tf_op jit(solution)/shard_map/ppermute | solution.py:380
  14.3 0.1 collective-permute-start.2
  14.4 2.9 %shard_map.68 = (bf16[384,768]{1,0:T(8,128)(2,1)S(1)}, bf16[384,768]{1,0:T(8,128)(2,1)S(1)}, f32[3,384,256]{2,1,0:T(8,128)S(1)}, f32[256,768]{1,0:T(8,128)S(1)}, f32[128,768]{1,0:T(8,128)S(1)}) custom-call(s32[2]{0:T(128)S(1)} %pad_add_fusion.refs_0_, bf16[512,256]{1,0:T(8,128)(2,1)S(1)} %bitcast.16, bf16[512,256]{1,0:T(8,128)(2,1)S(1)} %collective-permute-done.4.refs_2_, ...), custom_call_target="tpu_custom_call" | custom-call | flops 6899999744 | bytes 3473408 | tf_op jit(solution)/shard_map/pallas_call | solution.py:312
  17.4 0.5 collective-permute-start.7
  17.9 2.2 %shard_map.69 = (f32[3,384,256]{2,1,0:T(8,128)S(1)}, f32[256,768]{1,0:T(8,128)S(1)}) custom-call(s32[2]{0:T(128)S(1)} %pad_add_fusion.refs_0_, bf16[256,256]{1,0:T(8,128)(2,1)S(1)} %collective-permute-done.1.refs_1_.refs_2_.refs_3_, bf16[256,256]{1,0:T(8,128)(2,1)S(1)} %collective-permute-done.2.refs_2_.refs_4_, ...), custom_call_target="tpu_custom_call" | custom-call | flops 2300000000 | bytes 3604480 | tf_op jit(solution)/shard_map/pallas_call | solution.py:312
  20.1 2.8 %shard_map.70 = (bf16[3,256,256]{2,1,0:T(8,128)(2,1)S(1)}, bf16[2,2,2,112,128]{4,3,2,1,0:T(8,128)(2,1)S(1)}, f32[2,2,2,112,128]{4,3,2,1,0:T(8,128)S(1)}, bf16[2,...) custom-call(s32[2]{0:T(128)S(1)} %pad_add_fusion.refs_0_, ...), custom_call_target="tpu_custom_call" | custom-call | flops 3449999872 | bytes 8192000 | tf_op jit(solution)/shard_map/pallas_call | solution.py:312
  22.9 0.1 collective-permute-start.10
  23.0 1.1 %collective-permute-start.9 = (bf16[2,2,2,112,128]{4,3,2,1,0:T(8,128)(2,1)S(1)}, bf16[2,2,2,112,128]{4,3,2,1,0:T(8,128)(2,1)S(1)}, u32[]{:S(2)}, u32[]{:S(2)}) collective-permute-start(bf16[2,2,2,112,128]{4,3,2,1,0:T(8,128)(2,1)S(1)} %get-tuple-element.65), channel_id=1, source_target_pairs={{0,16},{8,24},{16,0},{24,8},{1,17},{9,25},{17,1},{25,9},{2,18},{10... | collective-permute-start | bytes 688136 | tf_op jit(solution)/shard_map/ppermute | solution.py:349
  24.1 0.3 collective-permute-done.10.refs_2_
  24.4 0.6 shard_map.74
  25.0 1.1 %collective-permute-start.11 = (bf16[2,2,2,48,128]{4,3,2,1,0:T(8,128)(2,1)S(1)}, bf16[2,2,2,48,128]{4,3,2,1,0:T(8,128)(2,1)S(1)}, u32[]{:S(2)}, u32[]{:S(2)}) collective-permute-start(bf16[2,2,2,48,128]{4,3,2,1,0:T(8,128)(2,1)S(1)} %get-tuple-element.69), channel_id=1, source_target_pairs={{0,16},{8,24},{16,0},{24,8},{1,17},{9,25},{17,1},{25,9},{2,18},{10... | collective-permute-start | bytes 294920 | tf_op jit(solution)/shard_map/ppermute | solution.py:349
  26.1 1.0 %collective-permute-start.14 = (bf16[2,2,2,160,128]{4,3,2,1,0:T(8,128)(2,1)S(1)}, bf16[2,2,2,160,128]{4,3,2,1,0:T(8,128)(2,1)S(1)}, u32[]{:S(2)}, u32[]{:S(2)}) collective-permute-start(bf16[2,2,2,160,128]{4,3,2,1,0:T(8,128)(2,1)S(1)} %get-tuple-element.75), channel_id=1, source_target_pairs={{0,1},{1,0},{2,3},{3,2},{4,5},{5,4},{6,7},{7,6},{8,9},{9,8},{10,11... | collective-permute-start | bytes 983048 | tf_op jit(solution)/shard_map/ppermute | solution.py:349
  27.1 1.6 %collective-permute-start.17 = (bf16[2,2,2,160,128]{4,3,2,1,0:T(8,128)(2,1)S(1)}, bf16[2,2,2,160,128]{4,3,2,1,0:T(8,128)(2,1)S(1)}, u32[]{:S(2)}, u32[]{:S(2)}) collective-permute-start(bf16[2,2,2,160,128]{4,3,2,1,0:T(8,128)(2,1)S(1)} %get-tuple-element.81), channel_id=1, source_target_pairs={{0,2},{1,3},{2,0},{3,1},{4,6},{5,7},{6,4},{7,5},{8,10},{9,11},{10,... | collective-permute-start | bytes 983048 | tf_op jit(solution)/shard_map/ppermute | solution.py:349
  28.7 0.7 %collective-permute-start.8 = (bf16[3,256,256]{2,1,0:T(8,128)(2,1)S(1)}, bf16[3,256,256]{2,1,0:T(8,128)(2,1)S(1)}, u32[]{:S(2)}, u32[]{:S(2)}) collective-permute-start(bf16[3,256,256]{2,1,0:T(8,128)(2,1)S(1)} %get-tuple-element.60), channel_id=1, source_target_pairs={{16,8},{17,9},{18,10},{19,11},{20,12},{21,13},{22,14},{23,15}} | collective-permute-start | bytes 1179656 | tf_op jit(solution)/shard_map/ppermute | solution.py:418
  29.4 2.1 %collective-permute-done.9.refs_2_ = bf16[2,2,2,112,128]{4,3,2,1,0:T(8,128)(2,1)S(1)} collective-permute-done((bf16[2,2,2,112,128]{4,3,2,1,0:T(8,128)(2,1)S(1)}, bf16[2,2,2,112,128]{4,3,2,1,0:T(8,128)(2,1)S(1)}, u32[]{:S(2)}, u32[]{:S(2)}) %collective-permute-start.9) | collective-permute-done | bytes 229408 | tf_op jit(solution)/shard_map/ppermute | solution.py:349
  31.5 1.7 %collective-permute-done.11.refs_4_ = bf16[2,2,2,48,128]{4,3,2,1,0:T(8,128)(2,1)S(1)} collective-permute-done((bf16[2,2,2,48,128]{4,3,2,1,0:T(8,128)(2,1)S(1)}, bf16[2,2,2,48,128]{4,3,2,1,0:T(8,128)(2,1)S(1)}, u32[]{:S(2)}, u32[]{:S(2)}) %collective-permute-start.11) | collective-permute-done | bytes 98336 | tf_op jit(solution)/shard_map/ppermute | solution.py:349
  33.1 0.6 %shard_map.75 = (bf16[2,2,160,128]{3,2,1,0:T(8,128)(2,1)S(1)}, f32[2,2,160,128]{3,2,1,0:T(8,128)S(1)}) custom-call(s32[2]{0:T(128)S(1)} %pad_add_fusion.refs_0_, f32[2,2,2,112,128]{4,3,2,1,0:T(8,128)S(1)} %get-tuple-element.64.refs_1_, bf16[2,2,2,112,128]{4,3,2,1,0:T(8,128)(2,1)S(1)} %collective-permute-done.9.refs_2_, ...), custom_call_target="tpu_custom_call" | custom-call | flops 2875000064 | bytes 983040 | tf_op jit(solution)/shard_map/pallas_call | solution.py:312
  33.8 1.1 %collective-permute-start.12 = (bf16[2,2,160,128]{3,2,1,0:T(8,128)(2,1)S(1)}, bf16[2,2,160,128]{3,2,1,0:T(8,128)(2,1)S(1)}, u32[]{:S(2)}, u32[]{:S(2)}) collective-permute-start(bf16[2,2,160,128]{3,2,1,0:T(8,128)(2,1)S(1)} %get-tuple-element.71), channel_id=1, source_target_pairs={{0,1},{1,0},{2,3},{3,2},{4,5},{5,4},{6,7},{7,6},{8,9},{9,8},{10,11... | collective-permute-start | bytes 491528 | tf_op jit(solution)/shard_map/ppermute | solution.py:349
  34.8 0.8 %collective-permute-done.14.refs_2_ = bf16[2,2,2,160,128]{4,3,2,1,0:T(8,128)(2,1)S(1)} collective-permute-done((bf16[2,2,2,160,128]{4,3,2,1,0:T(8,128)(2,1)S(1)}, bf16[2,2,2,160,128]{4,3,2,1,0:T(8,128)(2,1)S(1)}, u32[]{:S(2)}, u32[]{:S(2)}) %collective-permute-start.14) | collective-permute-done | bytes 327712 | tf_op jit(solution)/shard_map/ppermute | solution.py:349
  35.6 0.6 %shard_map.77 = (bf16[2,2,160,128]{3,2,1,0:T(8,128)(2,1)S(1)}, f32[2,2,160,128]{3,2,1,0:T(8,128)S(1)}) custom-call(s32[2]{0:T(128)S(1)} %pad_add_fusion.refs_0_, f32[2,2,2,160,128]{4,3,2,1,0:T(8,128)S(1)} %get-tuple-element.74.refs_1_, bf16[2,2,2,160,128]{4,3,2,1,0:T(8,128)(2,1)S(1)} %collective-permute-done.14.refs_2_), custom_call_target="tpu_custom_call" | custom-call | flops 2875000064 | bytes 983040 | tf_op jit(solution)/shard_map/pallas_call | solution.py:312
  36.2 1.9 %collective-permute-start.15 = (bf16[2,2,160,128]{3,2,1,0:T(8,128)(2,1)S(1)}, bf16[2,2,160,128]{3,2,1,0:T(8,128)(2,1)S(1)}, u32[]{:S(2)}, u32[]{:S(2)}) collective-permute-start(bf16[2,2,160,128]{3,2,1,0:T(8,128)(2,1)S(1)} %get-tuple-element.77), channel_id=1, source_target_pairs={{0,2},{1,3},{2,0},{3,1},{4,6},{5,7},{6,4},{7,5},{8,10},{9,11},{10,... | collective-permute-start | bytes 491528 | tf_op jit(solution)/shard_map/ppermute | solution.py:349
  38.1 0.6 %shard_map.79 = (bf16[2,2,160,128]{3,2,1,0:T(8,128)(2,1)S(1)}, f32[2,2,160,128]{3,2,1,0:T(8,128)S(1)}) custom-call(s32[2]{0:T(128)S(1)} %pad_add_fusion.refs_0_, f32[2,2,2,160,128]{4,3,2,1,0:T(8,128)S(1)} %get-tuple-element.80.refs_1_, bf16[2,2,2,160,128]{4,3,2,1,0:T(8,128)(2,1)S(1)} %collective-permute-done.17.refs_2_), custom_call_target="tpu_custom_call" | custom-call | flops 2875000064 | bytes 983040 | tf_op jit(solution)/shard_map/pallas_call | solution.py:312
  38.7 1.5 %collective-permute-start.18 = (bf16[2,2,160,128]{3,2,1,0:T(8,128)(2,1)S(1)}, bf16[2,2,160,128]{3,2,1,0:T(8,128)(2,1)S(1)}, u32[]{:S(2)}, u32[]{:S(2)}) collective-permute-start(bf16[2,2,160,128]{3,2,1,0:T(8,128)(2,1)S(1)} %get-tuple-element.83), channel_id=1, source_target_pairs={{0,16},{8,24},{16,0},{24,8},{1,17},{9,25},{17,1},{25,9},{2,18},{10... | collective-permute-start | bytes 491528 | tf_op jit(solution)/shard_map/ppermute | solution.py:349
  40.3 1.2 %shard_map.71 = (bf16[3,768,256]{2,1,0:T(8,128)(2,1)S(1)}, f32[8,128]{1,0:T(8,128)S(1)}) custom-call(s32[2]{0:T(128)S(1)} %pad_add_fusion.refs_0_, bf16[256,256]{1,0:T(8,128)(2,1)S(1)} %bitcast.22, bf16[256,256]{1,0:T(8,128)(2,1)S(1)} %collective-permute-done.refs_6_.refs_2_, bf16[256,256]{1,0:T(8,128)(2,1)S(1)} %collective-permute-done.1.refs_1_.refs_2_.refs_3_, ...), custom_call_target="tpu_custom_call" | custom-call | flops 1150000000 | bytes 1572864 | tf_op jit(solution)/shard_map/pallas_call | solution.py:312
  41.5 0.6 shard_map.76
  42.1 0.1 collective-permute-start.13
  42.2 0.6 shard_map.78
  42.8 1.1 %collective-permute-start.16 = (bf16[2,160,128]{2,1,0:T(8,128)(2,1)S(1)}, bf16[2,160,128]{2,1,0:T(8,128)(2,1)S(1)}, u32[]{:S(2)}, u32[]{:S(2)}) collective-permute-start(bf16[2,160,128]{2,1,0:T(8,128)(2,1)S(1)} %get-tuple-element.79), channel_id=1, source_target_pairs={{0,16},{8,24},{16,0},{24,8},{1,17},{9,25},{17,1},{25,9},{2,18},{10... | collective-permute-start | bytes 245768 | tf_op jit(solution)/shard_map/ppermute | solution.py:349
  43.9 0.3 collective-permute-done.18.refs_2_
  44.1 0.6 shard_map.80
  44.7 0.7 %collective-permute-start.19 = (bf16[2,160,128]{2,1,0:T(8,128)(2,1)S(1)}, bf16[2,160,128]{2,1,0:T(8,128)(2,1)S(1)}, u32[]{:S(2)}, u32[]{:S(2)}) collective-permute-start(bf16[2,160,128]{2,1,0:T(8,128)(2,1)S(1)} %get-tuple-element.86), channel_id=1, source_target_pairs={{0,1},{1,0},{2,3},{3,2},{4,5},{5,4},{6,7},{7,6},{8,9},{9,8},{10,11... | collective-permute-start | bytes 245768 | tf_op jit(solution)/shard_map/ppermute | solution.py:349
  45.4 0.7 %copy-done = bf16[3,3,3,256,256]{4,3,2,1,0:T(8,128)(2,1)S(1)} copy-done((bf16[3,3,3,256,256]{4,3,2,1,0:T(8,128)(2,1)S(1)}, bf16[3,3,3,256,256]{4,3,2,1,0:T(8,128)(2,1)}, u32[]{:S(2)}) %copy-start) | copy-done | bytes 3538968
  46.1 1.3 %shard_map.72 = (f32[512,256]{1,0:T(8,128)S(1)}, f32[8,128]{1,0:T(8,128)S(1)}) custom-call(s32[2]{0:T(128)S(1)} %pad_add_fusion.refs_0_, bf16[3,768,256]{2,1,0:T(8,128)(2,1)S(1)} %get-tuple-element.61.refs_1_.refs_2_, bf16[9,768,256]{2,1,0:T(8,128)(2,1)S(1)} %bitcast.12), custom_call_target="tpu_custom_call" | custom-call | flops 1150000000 | bytes 4718592 | tf_op jit(solution)/shard_map/pallas_call | solution.py:312
  47.5 1.7 %collective-permute-done.19.refs_6_ = bf16[2,160,128]{2,1,0:T(8,128)(2,1)S(1)} collective-permute-done((bf16[2,160,128]{2,1,0:T(8,128)(2,1)S(1)}, bf16[2,160,128]{2,1,0:T(8,128)(2,1)S(1)}, u32[]{:S(2)}, u32[]{:S(2)}) %collective-permute-start.19) | collective-permute-done | bytes 81952 | tf_op jit(solution)/shard_map/ppermute | solution.py:349
  49.2 0.6 %shard_map.81 = (bf16[480,128]{1,0:T(8,128)(2,1)S(1)}, f32[480,128]{1,0:T(8,128)S(1)}) custom-call(s32[2]{0:T(128)S(1)} %pad_add_fusion.refs_0_, f32[2,160,128]{2,1,0:T(8,128)S(1)} %get-tuple-element.72.refs_1_, bf16[2,160,128]{2,1,0:T(8,128)(2,1)S(1)} %collective-permute-done.13.refs_2_, f32[2,160,128]{2,1,0:T(8,128)S(1)} %get-tuple-element.78.refs_3_, ...), custom_call_target="tpu_custom_call" | custom-call | flops 1150000000 | bytes 737280 | tf_op jit(solution)/shard_map/pallas_call | solution.py:312
  49.8 2.7 %collective-permute-start.20 = (bf16[480,128]{1,0:T(8,128)(2,1)S(1)}, bf16[480,128]{1,0:T(8,128)(2,1)S(1)}, u32[]{:S(2)}, u32[]{:S(2)}) collective-permute-start(bf16[480,128]{1,0:T(8,128)(2,1)S(1)} %get-tuple-element.89), channel_id=1, source_target_pairs={{0,4},{1,5},{2,6},{3,7},{4,0},{5,1},{6,2},{7,3},{8,12},{9,13},{10,... | collective-permute-start | bytes 368648 | tf_op jit(solution)/shard_map/ppermute | solution.py:349
  52.5 2.8 %shard_map.73 = (bf16[512,256]{1,0:T(8,128)(2,1)}, f32[8,128]{1,0:T(8,128)S(1)}) custom-call(s32[2]{0:T(128)S(1)} %pad_add_fusion.refs_0_, bf16[512,256]{1,0:T(8,128)(2,1)S(1)} %bitcast.17, bf16[3,768,256]{2,1,0:T(8,128)(2,1)S(1)} %get-tuple-element.61.refs_1_.refs_2_, f32[512,256]{1,0:T(8,128)S(1)} %get-tuple-element.62.refs_3_, ...), custom_call_target="tpu_custom_call" | custom-call | flops 2300000000 | bytes 5505024 | tf_op jit(solution)/shard_map/pallas_call | solution.py:312
  55.3 0.4 collective-permute-done.20.refs_2_
  55.7 0.1 collective-permute-start.22
  55.8 1.2 %collective-permute-done.22.refs_4_ = bf16[480,128]{1,0:T(8,128)(2,1)S(1)} collective-permute-done((bf16[480,128]{1,0:T(8,128)(2,1)S(1)}, bf16[480,128]{1,0:T(8,128)(2,1)S(1)}, u32[]{:S(2)}, u32[]{:S(2)}) %collective-permute-start.22) | collective-permute-done | bytes 122912 | tf_op jit(solution)/shard_map/ppermute | solution.py:349
  57.0 1.5 %shard_map.82 = (f32[64,864]{1,0:T(8,128)}, f32[64,96]{1,0:T(8,128)}) custom-call(s32[2]{0:T(128)S(1)} %pad_add_fusion.refs_0_, f32[480,128]{1,0:T(8,128)S(1)} %get-tuple-element.88.refs_1_, bf16[480,128]{1,0:T(8,128)(2,1)S(1)} %collective-permute-done.20.refs_2_, f32[480,128]{1,0:T(8,128)S(1)} %collective-permute-done.21.refs_3_, ...), custom_call_target="tpu_custom_call" | custom-call | flops 1150000000 | bytes 737280 | tf_op jit(solution)/shard_map/pallas_call | solution.py:312
  (21 shorter events, 0.1 us)
Async XLA Ops:
  0.6 4.0 %collective-permute-start.4 = (bf16[512,256]{1,0:T(8,128)(2,1)}, bf16[512,256]{1,0:T(8,128)(2,1)S(1)}, u32[]{:S(2)}, u32[]{:S(2)}) collective-permute-start(bf16[512,256]{1,0:T(8,128)(2,1)} %bitcast.14), channel_id=1, source_target_pairs={{0,8},{8,0},{16,24},{24,16},{1,9},{9,1},{17,25},{25,17},{2,10},{10... | collective-permute-start | bytes 786440 | tf_op jit(solution)/shard_map/ppermute | solution.py:349
  1.1 9.6 %collective-permute-start.1 = (bf16[256,256]{1,0:T(8,128)(2,1)}, bf16[256,256]{1,0:T(8,128)(2,1)S(1)}, u32[]{:S(2)}, u32[]{:S(2)}) collective-permute-start(bf16[256,256]{1,0:T(8,128)(2,1)} %bitcast.18), channel_id=1, source_target_pairs={{0,1},{1,0},{2,3},{3,2},{4,5},{5,4},{6,7},{7,6},{8,9},{9,8},{10,11... | collective-permute-start | bytes 393224 | tf_op jit(solution)/shard_map/ppermute | solution.py:349
  3.7 10.7 %collective-permute-start = (bf16[256,256]{1,0:T(8,128)(2,1)}, bf16[256,256]{1,0:T(8,128)(2,1)S(1)}, u32[]{:S(2)}, u32[]{:S(2)}) collective-permute-start(bf16[256,256]{1,0:T(8,128)(2,1)} %bitcast.19), channel_id=1, source_target_pairs={{0,8},{8,0},{16,24},{24,16},{1,9},{9,1},{17,25},{25,17},{2,10},{10... | collective-permute-start | bytes 393224 | tf_op jit(solution)/shard_map/ppermute | solution.py:349
  3.9 10.5 %collective-permute-start.5 = (bf16[512,256]{1,0:T(8,128)(2,1)}, bf16[512,256]{1,0:T(8,128)(2,1)S(1)}, u32[]{:S(2)}, u32[]{:S(2)}) collective-permute-start(bf16[512,256]{1,0:T(8,128)(2,1)} %bitcast.15), channel_id=1, source_target_pairs={{8,16},{9,17},{10,18},{11,19},{12,20},{13,21},{14,22},{15,23}} | collective-permute-start | bytes 786440 | tf_op jit(solution)/shard_map/ppermute | solution.py:371
  4.6 9.8 %collective-permute-start.6 = (bf16[512,256]{1,0:T(8,128)(2,1)S(1)}, bf16[512,256]{1,0:T(8,128)(2,1)S(1)}, u32[]{:S(2)}, u32[]{:S(2)}) collective-permute-start(bf16[512,256]{1,0:T(8,128)(2,1)S(1)} %collective-permute-done.4.refs_2_), channel_id=1, source_target_pairs={{0,24},{1,25},{2,26},{3,27},{4,28},{5,29},{6,30},{7,31}} | collective-permute-start | bytes 786440 | tf_op jit(solution)/shard_map/ppermute | solution.py:372
  8.0 6.4 %copy-start.1 = (bf16[4,1,128,256]{3,2,1,0:T(8,128)(2,1)S(1)}, bf16[4,1,128,256]{3,2,1,0:T(8,128)(2,1)}, u32[]{:S(2)}) copy-start(bf16[4,1,128,256]{3,2,1,0:T(8,128)(2,1)} %param.4) | copy-start | bytes 786436
  8.0 6.4 %copy-start.2 = (bf16[2,1,128,256]{3,2,1,0:T(8,128)(2,1)S(1)}, bf16[2,1,128,256]{3,2,1,0:T(8,128)(2,1)}, u32[]{:S(2)}) copy-start(bf16[2,1,128,256]{3,2,1,0:T(8,128)(2,1)} %param.7) | copy-start | bytes 393220
  10.8 6.6 %collective-permute-start.3 = (bf16[256,256]{1,0:T(8,128)(2,1)S(1)}, bf16[256,256]{1,0:T(8,128)(2,1)S(1)}, u32[]{:S(2)}, u32[]{:S(2)}) collective-permute-start(bf16[256,256]{1,0:T(8,128)(2,1)S(1)} %collective-permute-done.1.refs_1_.refs_2_.refs_3_), channel_id=1, source_target_pairs={{0,2},{2,4},{3,1},{4,6},{5,3},{7,5},{8,10},{10,12},{11,9},{12,14},... | collective-permute-start | bytes 393224 | tf_op jit(solution)/shard_map/ppermute | solution.py:380
  14.3 3.6 %collective-permute-start.2 = (bf16[256,256]{1,0:T(8,128)(2,1)S(1)}, bf16[256,256]{1,0:T(8,128)(2,1)S(1)}, u32[]{:S(2)}, u32[]{:S(2)}) collective-permute-start(bf16[256,256]{1,0:T(8,128)(2,1)S(1)} %collective-permute-done.1.refs_1_.refs_2_.refs_3_), channel_id=1, source_target_pairs={{0,8},{8,0},{16,24},{24,16},{1,9},{9,1},{17,25},{25,17},{2,10},{10... | collective-permute-start | bytes 393224 | tf_op jit(solution)/shard_map/ppermute | solution.py:349
  17.4 2.7 %collective-permute-start.7 = (bf16[256,256]{1,0:T(8,128)(2,1)S(1)}, bf16[256,256]{1,0:T(8,128)(2,1)S(1)}, u32[]{:S(2)}, u32[]{:S(2)}) collective-permute-start(bf16[256,256]{1,0:T(8,128)(2,1)S(1)} %collective-permute-done.3.refs_3_.refs_5_), channel_id=1, source_target_pairs={{0,8},{8,0},{16,24},{24,16},{1,9},{9,1},{17,25},{25,17},{2,10},{10... | collective-permute-start | bytes 393224 | tf_op jit(solution)/shard_map/ppermute | solution.py:349
  22.9 1.5 %collective-permute-start.10 = (bf16[2,2,2,2,48,128]{5,4,3,2,1,0:T(8,128)(2,1)S(1)}, bf16[2,2,2,2,48,128]{5,4,3,2,1,0:T(8,128)(2,1)S(1)}, u32[]{:S(2)}, u32[]{:S(2)}) collective-permute-start(bf16[2,2,2,2,48,128]{5,4,3,2,1,0:T(8,128)(2,1)S(1)} %get-tuple-element.67), channel_id=1, source_target_pairs={{0,8},{8,0},{16,24},{24,16},{1,9},{9,1},{17,25},{25,17},{2,10},{10... | collective-permute-start | bytes 589832 | tf_op jit(solution)/shard_map/ppermute | solution.py:349
  23.0 8.5 %collective-permute-start.9 = (bf16[2,2,2,112,128]{4,3,2,1,0:T(8,128)(2,1)S(1)}, bf16[2,2,2,112,128]{4,3,2,1,0:T(8,128)(2,1)S(1)}, u32[]{:S(2)}, u32[]{:S(2)}) collective-permute-start(bf16[2,2,2,112,128]{4,3,2,1,0:T(8,128)(2,1)S(1)} %get-tuple-element.65), channel_id=1, source_target_pairs={{0,16},{8,24},{16,0},{24,8},{1,17},{9,25},{17,1},{25,9},{2,18},{10... | collective-permute-start | bytes 688136 | tf_op jit(solution)/shard_map/ppermute | solution.py:349
  25.0 8.1 %collective-permute-start.11 = (bf16[2,2,2,48,128]{4,3,2,1,0:T(8,128)(2,1)S(1)}, bf16[2,2,2,48,128]{4,3,2,1,0:T(8,128)(2,1)S(1)}, u32[]{:S(2)}, u32[]{:S(2)}) collective-permute-start(bf16[2,2,2,48,128]{4,3,2,1,0:T(8,128)(2,1)S(1)} %get-tuple-element.69), channel_id=1, source_target_pairs={{0,16},{8,24},{16,0},{24,8},{1,17},{9,25},{17,1},{25,9},{2,18},{10... | collective-permute-start | bytes 294920 | tf_op jit(solution)/shard_map/ppermute | solution.py:349
  26.1 9.5 %collective-permute-start.14 = (bf16[2,2,2,160,128]{4,3,2,1,0:T(8,128)(2,1)S(1)}, bf16[2,2,2,160,128]{4,3,2,1,0:T(8,128)(2,1)S(1)}, u32[]{:S(2)}, u32[]{:S(2)}) collective-permute-start(bf16[2,2,2,160,128]{4,3,2,1,0:T(8,128)(2,1)S(1)} %get-tuple-element.75), channel_id=1, source_target_pairs={{0,1},{1,0},{2,3},{3,2},{4,5},{5,4},{6,7},{7,6},{8,9},{9,8},{10,11... | collective-permute-start | bytes 983048 | tf_op jit(solution)/shard_map/ppermute | solution.py:349
  27.1 11.0 %collective-permute-start.17 = (bf16[2,2,2,160,128]{4,3,2,1,0:T(8,128)(2,1)S(1)}, bf16[2,2,2,160,128]{4,3,2,1,0:T(8,128)(2,1)S(1)}, u32[]{:S(2)}, u32[]{:S(2)}) collective-permute-start(bf16[2,2,2,160,128]{4,3,2,1,0:T(8,128)(2,1)S(1)} %get-tuple-element.81), channel_id=1, source_target_pairs={{0,2},{1,3},{2,0},{3,1},{4,6},{5,7},{6,4},{7,5},{8,10},{9,11},{10,... | collective-permute-start | bytes 983048 | tf_op jit(solution)/shard_map/ppermute | solution.py:349
  28.7 11.6 %collective-permute-start.8 = (bf16[3,256,256]{2,1,0:T(8,128)(2,1)S(1)}, bf16[3,256,256]{2,1,0:T(8,128)(2,1)S(1)}, u32[]{:S(2)}, u32[]{:S(2)}) collective-permute-start(bf16[3,256,256]{2,1,0:T(8,128)(2,1)S(1)} %get-tuple-element.60), channel_id=1, source_target_pairs={{16,8},{17,9},{18,10},{19,11},{20,12},{21,13},{22,14},{23,15}} | collective-permute-start | bytes 1179656 | tf_op jit(solution)/shard_map/ppermute | solution.py:418
  33.8 7.7 %collective-permute-start.12 = (bf16[2,2,160,128]{3,2,1,0:T(8,128)(2,1)S(1)}, bf16[2,2,160,128]{3,2,1,0:T(8,128)(2,1)S(1)}, u32[]{:S(2)}, u32[]{:S(2)}) collective-permute-start(bf16[2,2,160,128]{3,2,1,0:T(8,128)(2,1)S(1)} %get-tuple-element.71), channel_id=1, source_target_pairs={{0,1},{1,0},{2,3},{3,2},{4,5},{5,4},{6,7},{7,6},{8,9},{9,8},{10,11... | collective-permute-start | bytes 491528 | tf_op jit(solution)/shard_map/ppermute | solution.py:349
  36.2 6.0 %collective-permute-start.15 = (bf16[2,2,160,128]{3,2,1,0:T(8,128)(2,1)S(1)}, bf16[2,2,160,128]{3,2,1,0:T(8,128)(2,1)S(1)}, u32[]{:S(2)}, u32[]{:S(2)}) collective-permute-start(bf16[2,2,160,128]{3,2,1,0:T(8,128)(2,1)S(1)} %get-tuple-element.77), channel_id=1, source_target_pairs={{0,2},{1,3},{2,0},{3,1},{4,6},{5,7},{6,4},{7,5},{8,10},{9,11},{10,... | collective-permute-start | bytes 491528 | tf_op jit(solution)/shard_map/ppermute | solution.py:349
  38.7 5.4 %collective-permute-start.18 = (bf16[2,2,160,128]{3,2,1,0:T(8,128)(2,1)S(1)}, bf16[2,2,160,128]{3,2,1,0:T(8,128)(2,1)S(1)}, u32[]{:S(2)}, u32[]{:S(2)}) collective-permute-start(bf16[2,2,160,128]{3,2,1,0:T(8,128)(2,1)S(1)} %get-tuple-element.83), channel_id=1, source_target_pairs={{0,16},{8,24},{16,0},{24,8},{1,17},{9,25},{17,1},{25,9},{2,18},{10... | collective-permute-start | bytes 491528 | tf_op jit(solution)/shard_map/ppermute | solution.py:349
  42.1 5.4 %collective-permute-start.13 = (bf16[2,160,128]{2,1,0:T(8,128)(2,1)S(1)}, bf16[2,160,128]{2,1,0:T(8,128)(2,1)S(1)}, u32[]{:S(2)}, u32[]{:S(2)}) collective-permute-start(bf16[2,160,128]{2,1,0:T(8,128)(2,1)S(1)} %get-tuple-element.73), channel_id=1, source_target_pairs={{0,2},{1,3},{2,0},{3,1},{4,6},{5,7},{6,4},{7,5},{8,10},{9,11},{10,... | collective-permute-start | bytes 245768 | tf_op jit(solution)/shard_map/ppermute | solution.py:349
  42.8 4.7 %collective-permute-start.16 = (bf16[2,160,128]{2,1,0:T(8,128)(2,1)S(1)}, bf16[2,160,128]{2,1,0:T(8,128)(2,1)S(1)}, u32[]{:S(2)}, u32[]{:S(2)}) collective-permute-start(bf16[2,160,128]{2,1,0:T(8,128)(2,1)S(1)} %get-tuple-element.79), channel_id=1, source_target_pairs={{0,16},{8,24},{16,0},{24,8},{1,17},{9,25},{17,1},{25,9},{2,18},{10... | collective-permute-start | bytes 245768 | tf_op jit(solution)/shard_map/ppermute | solution.py:349
  44.1 2.0 %copy-start = (bf16[3,3,3,256,256]{4,3,2,1,0:T(8,128)(2,1)S(1)}, bf16[3,3,3,256,256]{4,3,2,1,0:T(8,128)(2,1)}, u32[]{:S(2)}) copy-start(bf16[3,3,3,256,256]{4,3,2,1,0:T(8,128)(2,1)} %param.5) | copy-start | bytes 10616836
  44.7 4.5 %collective-permute-start.19 = (bf16[2,160,128]{2,1,0:T(8,128)(2,1)S(1)}, bf16[2,160,128]{2,1,0:T(8,128)(2,1)S(1)}, u32[]{:S(2)}, u32[]{:S(2)}) collective-permute-start(bf16[2,160,128]{2,1,0:T(8,128)(2,1)S(1)} %get-tuple-element.86), channel_id=1, source_target_pairs={{0,1},{1,0},{2,3},{3,2},{4,5},{5,4},{6,7},{7,6},{8,9},{9,8},{10,11... | collective-permute-start | bytes 245768 | tf_op jit(solution)/shard_map/ppermute | solution.py:349
  49.8 5.8 %collective-permute-start.20 = (bf16[480,128]{1,0:T(8,128)(2,1)S(1)}, bf16[480,128]{1,0:T(8,128)(2,1)S(1)}, u32[]{:S(2)}, u32[]{:S(2)}) collective-permute-start(bf16[480,128]{1,0:T(8,128)(2,1)S(1)} %get-tuple-element.89), channel_id=1, source_target_pairs={{0,4},{1,5},{2,6},{3,7},{4,0},{5,1},{6,2},{7,3},{8,12},{9,13},{10,... | collective-permute-start | bytes 368648 | tf_op jit(solution)/shard_map/ppermute | solution.py:349
  52.5 4.5 %collective-permute-start.21 = (f32[480,128]{1,0:T(8,128)S(1)}, f32[480,128]{1,0:T(8,128)S(1)}, u32[]{:S(2)}, u32[]{:S(2)}) collective-permute-start(f32[480,128]{1,0:T(8,128)S(1)} %get-tuple-element.88.refs_1_), channel_id=1, source_target_pairs={{0,8},{8,0},{16,24},{24,16},{1,9},{9,1},{17,25},{25,17},{2,10},{10... | collective-permute-start | bytes 737288 | tf_op jit(solution)/shard_map/ppermute | solution.py:349
  55.7 1.3 %collective-permute-start.22 = (bf16[480,128]{1,0:T(8,128)(2,1)S(1)}, bf16[480,128]{1,0:T(8,128)(2,1)S(1)}, u32[]{:S(2)}, u32[]{:S(2)}) collective-permute-start(bf16[480,128]{1,0:T(8,128)(2,1)S(1)} %collective-permute-done.20.refs_2_), channel_id=1, source_target_pairs={{0,8},{8,0},{16,24},{24,16},{1,9},{9,1},{17,25},{25,17},{2,10},{10... | collective-permute-start | bytes 368648 | tf_op jit(solution)/shard_map/ppermute | solution.py:349
